TPU v7x, 32 devices: a whole 2x2x4 slice. The times are simulated.
32 devices in a mesh: seq: 8 (over y, x, core), head: 4 (over z).
Axes of the slice: x: 2, y: 2, z: 4, core: 2. Of those that a mesh axis runs over, the one named last changes fastest.
Arguments:
- queries: bfloat16 [8192, 40, 128], P(('seq', 'head')), may hold values from -6 to 6
- key_vectors: bfloat16 [8192, 40, 128], P(('seq', 'head')), may hold values from -6 to 6
- value_vectors: bfloat16 [8192, 40, 128], P(('seq', 'head')), may hold values from -6 to 6
- key_tiles: int32 [64, 10], replicated, may hold values from 0 to 63, as said below
Outputs:
- attended: bfloat16 [8192, 40, 128], P(('seq', 'head'))
Inputs may be any that keep to these rules, and one draw needn't show every extreme that they name: `key_tiles`: shard s holds tiles s * 8 to (s + 1) * 8 - 1. In each list the first 2 entries are distinct tiles of the query tile's own shard, the first being the query tile itself; the other 8 are distinct tiles of other shards. Over the lists of one shard's query tiles, an owner shard at distance 1 to 4 contributes exactly 2 distinct tiles, one at a greater distance at most 1.
All inputs are finite; a program needn't handle non-finite values.
Results may differ from a plain program's by a relative error of at most 0.0048.
Values may be sent and summed in bfloat16 or wider, within the bound.
No kernel may reach another device: no remote copies, remote signals or barrier semaphores. Data moves between devices by JAX's collectives and lax.ppermute only.
A program may use at most 192 MiB of HBM per device.

v0:
```python
import math

import jax
import jax.numpy as jnp
from jax import lax
from jax.sharding import PartitionSpec as P

TILE = 128
CAP = 2


def select_tiles(choose, tile_data):
    return jnp.einsum(
        "...t,tx->...x", choose.astype(jnp.bfloat16), tile_data, preferred_element_type=jnp.float32
    ).astype(jnp.bfloat16)


def attend_block(query_group, index_group, key_pool, value_pool, list_length, score_scale):
    group_size, tile_rows, head_count, head_size = query_group.shape
    gathered_keys = key_pool[index_group].reshape(
        group_size, list_length * tile_rows, head_count, head_size
    )
    gathered_values = value_pool[index_group].reshape(
        group_size, list_length * tile_rows, head_count, head_size
    )
    scores = jnp.einsum(
        "gqhd,gkhd->ghqk", query_group, gathered_keys, preferred_element_type=jnp.float32
    )
    row_top = jnp.max(scores, axis=-1, keepdims=True)
    weights = jnp.exp((scores - row_top) * score_scale)
    row_total = jnp.sum(weights, axis=-1, keepdims=True)
    rounded = weights.astype(jnp.bfloat16)
    mixed = (
        jnp.einsum("ghqk,gkhd->ghqd", rounded, gathered_values, preferred_element_type=jnp.float32)
        / row_total
    )
    return jnp.transpose(mixed, (0, 2, 1, 3)).astype(jnp.bfloat16)


def attend(query_block, key_block, value_block, key_tiles):
    seg_tokens = query_block.shape[0]
    head_count = query_block.shape[2]
    head_size = query_block.shape[3]
    queries = query_block.reshape(seg_tokens, head_count, head_size)
    key_vectors = key_block.reshape(seg_tokens, head_count, head_size)
    value_vectors = value_block.reshape(seg_tokens, head_count, head_size)
    shard_count = lax.axis_size("seq")
    my_shard = lax.axis_index("seq")
    tiles_here = seg_tokens // TILE
    list_length = key_tiles.shape[1]
    tile_width = TILE * head_count * head_size
    key_rows = key_vectors.reshape(tiles_here, tile_width)
    value_rows = value_vectors.reshape(tiles_here, tile_width)
    own_ids = my_shard * tiles_here + jnp.arange(tiles_here, dtype=jnp.int32)
    reader_lists = key_tiles.reshape(shard_count, tiles_here * list_length)
    readers = jnp.arange(shard_count, dtype=jnp.int32)
    wanted = (
        jnp.any(reader_lists[:, :, None] == own_ids[None, None, :], axis=1)
        & (readers != my_shard)[:, None]
    )
    send_rank = jnp.cumsum(wanted.astype(jnp.int32), axis=1) - 1
    my_lists = lax.dynamic_slice_in_dim(key_tiles, my_shard * tiles_here, tiles_here, 0).reshape(-1)
    all_ids = jnp.arange(shard_count * tiles_here, dtype=jnp.int32)
    matches = my_lists[:, None] == all_ids[None, :]
    needed = jnp.any(matches, axis=0).reshape(shard_count, tiles_here)
    recv_rank = (jnp.cumsum(needed.astype(jnp.int32), axis=1) - 1).reshape(-1)
    entry_rank = jnp.sum(jnp.where(matches, recv_rank[None, :], 0), axis=1)
    owners = my_lists // tiles_here
    within = my_lists % tiles_here
    distance = owners - my_shard
    slot_ids = jnp.arange(CAP, dtype=jnp.int32)
    choose = wanted[:, None, :] & (send_rank[:, None, :] == slot_ids[None, :, None])
    got_keys, got_values = (
        lax.all_to_all(
            select_tiles(choose, key_rows), "seq", split_axis=0, concat_axis=0, tiled=True
        ),
        lax.all_to_all(
            select_tiles(choose, value_rows), "seq", split_axis=0, concat_axis=0, tiled=True
        ),
    )
    key_pool = jnp.concatenate([key_rows, got_keys.reshape(-1, tile_width)], axis=0)
    value_pool = jnp.concatenate([value_rows, got_values.reshape(-1, tile_width)], axis=0)
    pool_index = jnp.where(distance == 0, within, tiles_here + owners * CAP + entry_rank)
    key_pool = key_pool.reshape(-1, TILE, head_count, head_size)
    value_pool = value_pool.reshape(-1, TILE, head_count, head_size)
    group_size = math.gcd(tiles_here, max(1, 512 // TILE))
    index_groups = pool_index.reshape(tiles_here // group_size, group_size, list_length)
    query_groups = queries.reshape(
        tiles_here // group_size, group_size, TILE, head_count, head_size
    )
    score_scale = 1.0 / math.sqrt(head_size)

    def per_group(pair):
        return attend_block(pair[0], pair[1], key_pool, value_pool, list_length, score_scale)

    outputs = lax.map(per_group, (query_groups, index_groups))
    outputs = outputs.reshape(seg_tokens, 1, head_count, head_size)
    return lax.all_to_all(outputs, "head", split_axis=0, concat_axis=1, tiled=True)


def shards(queries, key_vectors, value_vectors, key_tiles):
    group_count = lax.axis_size("head")
    row_count, head_total, head_size = queries.shape
    per_group_heads = head_total // group_count
    query_split = queries.reshape(row_count, group_count, per_group_heads, head_size)
    key_split = key_vectors.reshape(row_count, group_count, per_group_heads, head_size)
    value_split = value_vectors.reshape(row_count, group_count, per_group_heads, head_size)
    regrouped = (
        lax.all_to_all(query_split, "head", split_axis=1, concat_axis=0, tiled=True),
        lax.all_to_all(key_split, "head", split_axis=1, concat_axis=0, tiled=True),
        lax.all_to_all(value_split, "head", split_axis=1, concat_axis=0, tiled=True),
    )
    result = attend(regrouped[0], regrouped[1], regrouped[2], key_tiles)
    return result.reshape(result.shape[0], result.shape[1] * result.shape[2], result.shape[3])


def solution(mesh):
    return jax.shard_map(
        shards,
        mesh=mesh,
        in_specs=(
            P(("seq", "head"), None, None),
            P(("seq", "head"), None, None),
            P(("seq", "head"), None, None),
            P(),
        ),
        out_specs=P(("seq", "head"), None, None),
        check_vma=False,
    )
```

profile of v0, /device:TPU:10, one launch (start us, length us, event | category | flops | bytes accessed | tf_op | source)
XLA Modules:
  0.0 628.7 jit_solution(5059718666587023929)
XLA Ops:
  0.0 3.9 copy.73
  3.9 5.3 all-to-all-start.1
  9.2 3.9 copy.79
  13.0 52.3 %all-to-all-done.1 = bf16[256,4,10,128]{3,0,2,1:T(8,128)(2,1)S(1)} async-done(((bf16[256,4,10,128]{3,0,2,1:T(8,128)(2,1)}), bf16[256,4,10,128]{3,0,2,1:T(8,128)(2,1)S(1)}, u32[]{:S(2)}, u32[]{:S(2)}) %all-to-all-start.1) | async-done | bytes 2621472 | tf_op jit(solution)/shard_map/all_to_all | solution.py:110
  65.3 7.8 %all-to-all-start.3 = ((bf16[256,4,10,128]{3,0,2,1:T(8,128)(2,1)}), bf16[256,4,10,128]{3,0,2,1:T(8,128)(2,1)}, u32[]{:S(2)}, u32[]{:S(2)}) async-start(bf16[256,4,10,128]{3,0,2,1:T(8,128)(2,1)} %bitcast.74), calls=%async_computation.3 | async-start | bytes 5242880 | tf_op jit(solution)/shard_map/all_to_all | solution.py:111
  73.1 0.0 copy-start
  73.1 3.9 copy.70
  77.0 51.8 %all-to-all-done.3 = bf16[256,4,10,128]{3,0,2,1:T(8,128)(2,1)} async-done(((bf16[256,4,10,128]{3,0,2,1:T(8,128)(2,1)}), bf16[256,4,10,128]{3,0,2,1:T(8,128)(2,1)}, u32[]{:S(2)}, u32[]{:S(2)}) %all-to-all-start.3) | async-done | bytes 2621472 | tf_op jit(solution)/shard_map/all_to_all | solution.py:111
  128.8 7.9 %all-to-all-start = ((bf16[256,4,10,128]{3,0,2,1:T(8,128)(2,1)}), bf16[256,4,10,128]{3,0,2,1:T(8,128)(2,1)}, u32[]{:S(2)}, u32[]{:S(2)}) async-start(bf16[256,4,10,128]{3,0,2,1:T(8,128)(2,1)} %bitcast.73), calls=%async_computation | async-start | bytes 5242880 | tf_op jit(solution)/shard_map/all_to_all | solution.py:109
  136.6 0.0 copy-done
  136.6 0.1 copy.72
  136.7 0.1 eq.55
  136.8 0.3 compare_reduce_fusion
  137.1 0.1 fusion.31
  137.2 0.2 reduce_window_sum.18
  137.4 3.8 copy.76
  141.2 5.2 reshape.153
  146.4 3.2 convolution_convert_fusion.1
  149.6 13.3 %copy.77 = bf16[8,2,163840]{2,1,0:T(2,128)(2,1)} copy(bf16[8,2,163840]{2,0,1:T(8,128)(2,1)S(1)} %convolution_convert_fusion.1) | data formatting | bytes 10485760 | tf_op jit(solution)/shard_map/convert_element_type | solution.py:15
  162.9 29.4 %all-to-all-done = bf16[256,4,10,128]{3,0,2,1:T(8,128)(2,1)} async-done(((bf16[256,4,10,128]{3,0,2,1:T(8,128)(2,1)}), bf16[256,4,10,128]{3,0,2,1:T(8,128)(2,1)}, u32[]{:S(2)}, u32[]{:S(2)}) %all-to-all-start) | async-done | bytes 2621472 | tf_op jit(solution)/shard_map/all_to_all | solution.py:109
  192.3 5.3 all-to-all-start.2
  197.6 5.6 copy.81
  203.2 5.2 reshape.154
  208.4 3.2 convolution_convert_fusion
  211.7 13.3 %copy.82 = bf16[8,2,163840]{2,1,0:T(2,128)(2,1)} copy(bf16[8,2,163840]{2,0,1:T(8,128)(2,1)S(1)} %convolution_convert_fusion) | data formatting | bytes 10485760 | tf_op jit(solution)/shard_map/convert_element_type | solution.py:15
  225.0 31.5 %all-to-all-done.2 = bf16[8,2,163840]{2,1,0:T(2,128)(2,1)} async-done(((bf16[8,2,163840]{2,1,0:T(2,128)(2,1)}), bf16[8,2,163840]{2,1,0:T(2,128)(2,1)}, u32[]{:S(2)}, u32[]{:S(2)}) %all-to-all-start.2) | async-done | bytes 5242912 | tf_op jit(solution)/shard_map/all_to_all | solution.py:74
  256.5 6.1 all-to-all-start.4
  262.6 0.1 eq.51
  262.7 0.1 fusion.20
  262.8 0.1 reshape.132
  262.9 0.2 reduce_window_sum.17
  263.1 0.1 sub.33
  263.2 0.1 select_reduce_fusion
  263.3 0.1 reduce_sum.21
  263.4 0.2 copy.74
  263.6 2.0 copy.80
  265.6 4.0 copy.78
  269.6 4.0 copy.83
  273.6 3.5 copy.71
  277.2 9.3 %concatenate.17 = bf16[16,128,10,128]{3,2,1,0:T(8,128)(2,1)} reshape(bf16[8,2,163840]{2,1,0:T(2,128)(2,1)} %all-to-all-done.2) | data formatting | bytes 10485760 | tf_op jit(solution)/shard_map/concatenate | solution.py:81
  286.4 11.0 %pad_maximum_fusion = bf16[24,128,10,128]{3,2,1,0:T(8,128)(2,1)} fusion(bf16[16,128,10,128]{3,2,1,0:T(8,128)(2,1)} %concatenate.17, bf16[8,128,10,128]{3,2,1,0:T(8,128)(2,1)} %copy.78), kind=kLoop, calls=%fused_computation.21 | loop fusion | flops 3932160 | bytes 15728640 | tf_op jit(solution)/shard_map/concatenate | solution.py:81
  297.4 24.1 %all-to-all-done.4 = bf16[8,2,163840]{2,1,0:T(2,128)(2,1)} async-done(((bf16[8,2,163840]{2,1,0:T(2,128)(2,1)}), bf16[8,2,163840]{2,1,0:T(2,128)(2,1)}, u32[]{:S(2)}, u32[]{:S(2)}) %all-to-all-start.4) | async-done | bytes 5242912 | tf_op jit(solution)/shard_map/all_to_all | solution.py:77
  321.6 9.3 %concatenate.20 = bf16[16,128,10,128]{3,2,1,0:T(8,128)(2,1)} reshape(bf16[8,2,163840]{2,1,0:T(2,128)(2,1)} %all-to-all-done.4) | data formatting | bytes 10485760 | tf_op jit(solution)/shard_map/concatenate | solution.py:82
  330.9 11.0 %pad_maximum_fusion.1 = bf16[24,128,10,128]{3,2,1,0:T(8,128)(2,1)} fusion(bf16[16,128,10,128]{3,2,1,0:T(8,128)(2,1)} %concatenate.20, bf16[8,128,10,128]{3,2,1,0:T(8,128)(2,1)} %copy.83), kind=kLoop, calls=%fused_computation.22 | loop fusion | flops 3932160 | bytes 15728640 | tf_op jit(solution)/shard_map/concatenate | solution.py:82
  341.9 180.8 %while.10 = (s32[]{:T(128)}, bf16[2,4,128,10,128]{4,2,1,0,3:T(8,128)(2,1)}, bf16[2,4,128,10,128]{4,2,1,0,3:T(8,128)(2,1)}, s32[2,4,10]{2,1,0:T(4,128)S(1)}, bf16...) while((s32[]{:T(128)}, bf16[2,4,128,10,128]{4,2,1,0,3:T(8,128)(2,1)}, ...), condition=%wide.region_8.9_spmd, body=%wide.region_5.8_spmd.sunk | while | flops 5073806336 | bytes 166509232 | solution.py:96
  342.1 0.1 reshape.166
  342.2 13.3 %gather_fusion.1 = bf16[40,128,10,128]{3,2,1,0:T(8,128)(2,1)} fusion(bf16[24,128,10,128]{3,2,1,0:T(8,128)(2,1)} %get-tuple-element.131, s32[1024]{0:T(1024)S(1)} %pad_clamp_fusion.2), kind=kCustom, calls=%fused_computation.clone.1 | custom fusion | bytes 26214560 | tf_op jit(solution)/shard_map/while/body/eval_jaxpr/gather | solution.py:20
  355.5 18.7 %fusion.51 = f32[4,10,128,1280]{3,2,1,0:T(8,128)} fusion(bf16[4,1280,10,128]{3,2,1,0:T(8,128)(2,1)} %bitcast.68, bf16[2,4,128,10,128]{4,2,1,0,3:T(8,128)(2,1)} %get-tuple-element.129, s32[]{:T(128)} %get-tuple-element.120), kind=kOutput, calls=%fused_computation.6.clone.2 | convolution fusion | flops 1677721600 | bytes 48497152 | tf_op jit(solution)/shard_map/while/body/eval_jaxpr/gqhd,gkhd->ghqk/dot_general | solution.py:26
  374.2 16.1 %fusion.52 = f32[4,10,128]{2,1,0:T(8,128)S(1)} fusion(bf16[4,1280,10,128]{3,2,1,0:T(8,128)(2,1)} %bitcast.69, bf16[2,4,128,10,128]{4,2,1,0,3:T(8,128)(2,1)} %get-tuple-element.129, s32[]{:T(128)} %get-tuple-element.120), kind=kOutput, calls=%fused_computation.50.clone.1 | convolution fusion | flops 1697383680 | bytes 22303232 | tf_op jit(solution)/shard_map/while/body/eval_jaxpr/sub | solution.py:30
  390.3 13.3 %gather_fusion = bf16[40,128,10,128]{3,2,1,0:T(8,128)(2,1)} fusion(bf16[24,128,10,128]{3,2,1,0:T(8,128)(2,1)} %get-tuple-element.132, s32[1024]{0:T(1024)S(1)} %pad_clamp_fusion.2), kind=kCustom, calls=%fused_computation.1.clone.1 | custom fusion | bytes 26214560 | tf_op jit(solution)/shard_map/while/body/eval_jaxpr/gather | solution.py:23
  403.6 27.4 %fusion.53 = bf16[1,4,128,10,128]{4,2,3,1,0:T(8,128)(2,1)S(1)} fusion(bf16[4,1280,10,128]{3,2,1,0:T(8,128)(2,1)} %bitcast.70, f32[4,10,128,1280]{3,2,1,0:T(8,128)} %fusion.51, f32[4,128,10]{1,2,0:T(8,128)S(1)} %bitcast.82), kind=kOutput, calls=%fused_computation.11.clone.1 | convolution fusion | flops 1698699520 | bytes 40652800 | tf_op jit(solution)/shard_map/while/body/eval_jaxpr/ghqk,gkhd->ghqd/dot_general | solution.py:34
  431.0 1.3 copy_dynamic-update-slice_fusion.2
  432.3 0.1 reshape.166
  432.4 13.3 %gather_fusion.1 = bf16[40,128,10,128]{3,2,1,0:T(8,128)(2,1)} fusion(bf16[24,128,10,128]{3,2,1,0:T(8,128)(2,1)} %get-tuple-element.131, s32[1024]{0:T(1024)S(1)} %pad_clamp_fusion.2), kind=kCustom, calls=%fused_computation.clone.1 | custom fusion | bytes 26214560 | tf_op jit(solution)/shard_map/while/body/eval_jaxpr/gather | solution.py:20
  445.7 18.7 %fusion.51 = f32[4,10,128,1280]{3,2,1,0:T(8,128)} fusion(bf16[4,1280,10,128]{3,2,1,0:T(8,128)(2,1)} %bitcast.68, bf16[2,4,128,10,128]{4,2,1,0,3:T(8,128)(2,1)} %get-tuple-element.129, s32[]{:T(128)} %get-tuple-element.120), kind=kOutput, calls=%fused_computation.6.clone.2 | convolution fusion | flops 1677721600 | bytes 48497152 | tf_op jit(solution)/shard_map/while/body/eval_jaxpr/gqhd,gkhd->ghqk/dot_general | solution.py:26
  464.4 16.1 %fusion.52 = f32[4,10,128]{2,1,0:T(8,128)S(1)} fusion(bf16[4,1280,10,128]{3,2,1,0:T(8,128)(2,1)} %bitcast.69, bf16[2,4,128,10,128]{4,2,1,0,3:T(8,128)(2,1)} %get-tuple-element.129, s32[]{:T(128)} %get-tuple-element.120), kind=kOutput, calls=%fused_computation.50.clone.1 | convolution fusion | flops 1697383680 | bytes 22303232 | tf_op jit(solution)/shard_map/while/body/eval_jaxpr/sub | solution.py:30
  480.5 13.3 %gather_fusion = bf16[40,128,10,128]{3,2,1,0:T(8,128)(2,1)} fusion(bf16[24,128,10,128]{3,2,1,0:T(8,128)(2,1)} %get-tuple-element.132, s32[1024]{0:T(1024)S(1)} %pad_clamp_fusion.2), kind=kCustom, calls=%fused_computation.1.clone.1 | custom fusion | bytes 26214560 | tf_op jit(solution)/shard_map/while/body/eval_jaxpr/gather | solution.py:23
  493.8 27.4 %fusion.53 = bf16[1,4,128,10,128]{4,2,3,1,0:T(8,128)(2,1)S(1)} fusion(bf16[4,1280,10,128]{3,2,1,0:T(8,128)(2,1)} %bitcast.70, f32[4,10,128,1280]{3,2,1,0:T(8,128)} %fusion.51, f32[4,128,10]{1,2,0:T(8,128)S(1)} %bitcast.82), kind=kOutput, calls=%fused_computation.11.clone.1 | convolution fusion | flops 1698699520 | bytes 40652800 | tf_op jit(solution)/shard_map/while/body/eval_jaxpr/ghqk,gkhd->ghqd/dot_general | solution.py:34
  521.2 1.3 copy_dynamic-update-slice_fusion.2
  522.7 3.6 copy.86
  526.4 97.8 %all_to_all.70 = bf16[1024,1,10,128]{3,2,1,0:T(8,128)(2,1)S(1)} all-to-all(bf16[1024,1,10,128]{3,2,1,0:T(8,128)(2,1)S(1)} %copy.86), channel_id=1, replica_groups=mesh['seq'=8,'head'=4] {'head'}, dimensions={0} | all-to-all | bytes 5242880 | tf_op jit(solution)/shard_map/all_to_all | solution.py:98
  624.1 0.7 copy.87
  624.8 0.3 copy.88
  625.1 3.2 copy.89
  (12 shorter events, 0.1 us)
Async XLA Ops:
  3.9 61.5 %all-to-all-start.1 = ((bf16[256,4,10,128]{3,0,2,1:T(8,128)(2,1)}), bf16[256,4,10,128]{3,0,2,1:T(8,128)(2,1)S(1)}, u32[]{:S(2)}, u32[]{:S(2)}) async-start(bf16[256,4,10,128]{3,0,2,1:T(8,128)(2,1)} %bitcast.75), calls=%async_computation.1 | async-start | bytes 5242880 | tf_op jit(solution)/shard_map/all_to_all | solution.py:110
  65.3 63.4 %all-to-all-start.3 = ((bf16[256,4,10,128]{3,0,2,1:T(8,128)(2,1)}), bf16[256,4,10,128]{3,0,2,1:T(8,128)(2,1)}, u32[]{:S(2)}, u32[]{:S(2)}) async-start(bf16[256,4,10,128]{3,0,2,1:T(8,128)(2,1)} %bitcast.74), calls=%async_computation.3 | async-start | bytes 5242880 | tf_op jit(solution)/shard_map/all_to_all | solution.py:111
  73.1 63.6 %copy-start = (s32[64,10]{0,1:T(8,128)S(1)}, s32[64,10]{0,1:T(8,128)}, u32[]{:S(2)}) copy-start(s32[64,10]{0,1:T(8,128)} %param.9) | copy-start | bytes 7684
  128.8 63.5 %all-to-all-start = ((bf16[256,4,10,128]{3,0,2,1:T(8,128)(2,1)}), bf16[256,4,10,128]{3,0,2,1:T(8,128)(2,1)}, u32[]{:S(2)}, u32[]{:S(2)}) async-start(bf16[256,4,10,128]{3,0,2,1:T(8,128)(2,1)} %bitcast.73), calls=%async_computation | async-start | bytes 5242880 | tf_op jit(solution)/shard_map/all_to_all | solution.py:109
  192.3 64.2 %all-to-all-start.2 = ((bf16[8,2,163840]{2,1,0:T(2,128)(2,1)}), bf16[8,2,163840]{2,1,0:T(2,128)(2,1)}, u32[]{:S(2)}, u32[]{:S(2)}) async-start(bf16[8,2,163840]{2,1,0:T(2,128)(2,1)} %copy.77), calls=%async_computation.2 | async-start | bytes 10485760 | tf_op jit(solution)/shard_map/all_to_all | solution.py:74
  256.5 65.1 %all-to-all-start.4 = ((bf16[8,2,163840]{2,1,0:T(2,128)(2,1)}), bf16[8,2,163840]{2,1,0:T(2,128)(2,1)}, u32[]{:S(2)}, u32[]{:S(2)}) async-start(bf16[8,2,163840]{2,1,0:T(2,128)(2,1)} %copy.82), calls=%async_computation.4 | async-start | bytes 10485760 | tf_op jit(solution)/shard_map/all_to_all | solution.py:77
where the time goes:
time: 638 us; the launch traced here: 629 us
  waiting for transfers between devices  189 us (30%)
  local copies, waits for them, and re-layouts  155 us (24%)
  matrix products  131 us (21%)
  blocking collectives  97.8 us (15%)
  starting transfers between devices  32.4 us (5%)
  other arithmetic  23 us (4%)
    all_to_all x1, blocking collectives, attend(): lax.all_to_all(outputs, 'head', split_axis=0, concat_axis=1, tiled=True)  97.8 us
    dot_general x2, matrix products, attend_block(): jnp.einsum('ghqk,gkhd->ghqd', rounded, gathered_values, preferred_element...  54.7 us
    all_to_all x1, waiting for transfers between devices, shards(): lax.all_to_all(key_split, 'head', split_axis=1, concat_axis=0, tiled=True)  52.3 us
    all_to_all x1, waiting for transfers between devices, shards(): lax.all_to_all(value_split, 'head', split_axis=1, concat_axis=0, tiled=True)  51.8 us
    dot_general x2, matrix products, attend_block(): jnp.einsum('gqhd,gkhd->ghqk', query_group, gathered_keys, preferred_eleme...  37.3 us
    sub x2, matrix products, attend_block(): weights = jnp.exp((scores - row_top) * score_scale)  32.2 us
    all_to_all x1, waiting for transfers between devices, attend(): lax.all_to_all(select_tiles(choose, key_rows), 'seq', split_axis=0, conca...  31.5 us
    all_to_all x1, waiting for transfers between devices, shards(): lax.all_to_all(query_split, 'head', split_axis=1, concat_axis=0, tiled=True)  29.4 us
  transfers between devices with their start and end apart: 5, of which 5 were waited for; matrix products, arithmetic and copies ran while one was open for 15% of the time, Pallas kernels for 0%

commit v1 on v0

v1 whole, which is shorter than its diff:
```python
import math

import jax
import jax.numpy as jnp
from jax import lax
from jax.experimental import pallas as pl
from jax.experimental.pallas import tpu as pltpu
from jax.sharding import PartitionSpec as P

TILE = 128
CAP = 2
CHUNKS = 2
BF16 = jnp.bfloat16
F32 = jnp.float32


def split_heads(own_heads):
    count = min(CHUNKS, own_heads)
    sizes = [own_heads // count + (i < own_heads % count) for i in range(count)]
    return [(sum(sizes[:i]), size) for i, size in enumerate(sizes)]


def row_block(rows):
    return TILE if rows % TILE == 0 else rows


def by_partner(array, here, partners, chunks):
    rows, heads, size = array.shape
    own_heads = heads // partners
    block = row_block(rows)

    def kernel(here_ref, in_ref, *refs):
        outs, turned = refs[:-1], refs[-1]
        turned[...] = jnp.swapaxes(in_ref[...], 0, 1)
        for k in range(partners):
            first = (here_ref[0] ^ k) * own_heads
            for c, (start, count) in enumerate(chunks):
                outs[k * len(chunks) + c][...] = turned[pl.ds(first + start, count)]

    parts = [count for _ in range(partners) for _, count in chunks]
    outs = pl.pallas_call(
        kernel,
        grid_spec=pltpu.PrefetchScalarGridSpec(
            num_scalar_prefetch=1,
            grid=(rows // block,),
            in_specs=[pl.BlockSpec((block, heads, size), lambda i, _: (i, 0, 0))],
            out_specs=[pl.BlockSpec((count, block, size), lambda i, _: (0, i, 0)) for count in parts],
            scratch_shapes=[pltpu.VMEM((heads, block, size), array.dtype)],
        ),
        out_shape=[jax.ShapeDtypeStruct((count, rows, size), array.dtype) for count in parts],
    )(here, array)
    return [outs[k * len(chunks) : (k + 1) * len(chunks)] for k in range(partners)]


def from_partners(pieces, here, chunks, heads):
    partners = len(pieces)
    own_heads = heads // partners
    rows, size = pieces[0][0].shape[1:]
    block = row_block(rows)

    def kernel(here_ref, *refs):
        ins, out, turned = refs[:-2], refs[-2], refs[-1]
        for k in range(partners):
            first = (here_ref[0] ^ k) * own_heads
            for c, (start, count) in enumerate(chunks):
                turned[pl.ds(first + start, count)] = ins[k * len(chunks) + c][...]
        out[...] = jnp.swapaxes(turned[...], 0, 1)

    flat = [piece for group in pieces for piece in group]
    return pl.pallas_call(
        kernel,
        grid_spec=pltpu.PrefetchScalarGridSpec(
            num_scalar_prefetch=1,
            grid=(rows // block,),
            in_specs=[pl.BlockSpec((piece.shape[0], block, size), lambda i, _: (0, i, 0)) for piece in flat],
            out_specs=pl.BlockSpec((block, heads, size), lambda i, _: (i, 0, 0)),
            scratch_shapes=[pltpu.VMEM((heads, block, size), BF16)],
        ),
        out_shape=jax.ShapeDtypeStruct((rows, heads, size), BF16),
    )(here, *flat)


def pick_tiles(pieces, picks):
    count, rows, size = pieces[0].shape
    readers = picks.shape[0]
    tiles = rows // TILE

    def kernel(pick_ref, *refs):
        ins, out, pool = refs[:-2], refs[-2], refs[-1]
        for k, piece in enumerate(ins):
            pool[k * tiles : (k + 1) * tiles] = piece[0].reshape(tiles, TILE, size)
        for reader in range(readers):
            for slot in range(CAP):
                out[reader, slot, 0] = pool[pick_ref[reader, slot]]

    return pl.pallas_call(
        kernel,
        grid_spec=pltpu.PrefetchScalarGridSpec(
            num_scalar_prefetch=1,
            grid=(count,),
            in_specs=[pl.BlockSpec((1, rows, size), lambda h, _: (h, 0, 0))] * len(pieces),
            out_specs=pl.BlockSpec((readers, CAP, 1, TILE, size), lambda h, _: (0, 0, h, 0, 0)),
            scratch_shapes=[pltpu.VMEM((len(pieces) * tiles, TILE, size), BF16)],
        ),
        out_shape=jax.ShapeDtypeStruct((readers, CAP, count, TILE, size), BF16),
    )(picks, *pieces)


def attend(queries, keys, values, far_keys, far_values, places):
    partners = len(queries)
    count, rows, size = queries[0].shape
    owners = far_keys.shape[0]
    tiles = rows // TILE
    near = partners * tiles
    listed = places.shape[1]
    factor = math.log2(math.e) / math.sqrt(size)

    def kernel(place_ref, *refs):
        q_refs, k_refs, v_refs = refs[:partners], refs[partners : 2 * partners], refs[2 * partners : 3 * partners]
        far_k, far_v = refs[3 * partners : 3 * partners + 2]
        outs = refs[3 * partners + 2 : 4 * partners + 2]
        k_pool, v_pool = refs[4 * partners + 2 :]
        for k in range(partners):
            k_pool[k * tiles : (k + 1) * tiles] = k_refs[k][0].reshape(tiles, TILE, size)
            v_pool[k * tiles : (k + 1) * tiles] = v_refs[k][0].reshape(tiles, TILE, size)
        k_pool[near:] = far_k[:, :, 0].reshape(owners * CAP, TILE, size)
        v_pool[near:] = far_v[:, :, 0].reshape(owners * CAP, TILE, size)
        for k in range(partners):
            for tile in range(tiles):
                at = pl.ds(tile * TILE, TILE)
                ids = [place_ref[k * tiles + tile, j] for j in range(listed)]
                key_rows = jnp.concatenate([k_pool[i] for i in ids], axis=0)
                scores = lax.dot_general(
                    q_refs[k][0, at, :], key_rows, (((1,), (1,)), ((), ())), preferred_element_type=F32
                )
                row_top = jnp.max(scores, axis=-1, keepdims=True)
                weights = jnp.exp2((scores - row_top) * factor)
                row_total = jnp.sum(weights, axis=-1, keepdims=True)
                value_rows = jnp.concatenate([v_pool[i] for i in ids], axis=0)
                mixed = jnp.dot(weights.astype(BF16), value_rows, preferred_element_type=F32)
                outs[k][0, at, :] = (mixed / row_total).astype(BF16)

    head_spec = pl.BlockSpec((1, rows, size), lambda h, _: (h, 0, 0))
    far_spec = pl.BlockSpec((owners, CAP, 1, TILE, size), lambda h, _: (0, 0, h, 0, 0))
    pool_size = near + owners * CAP
    pairs = count * partners * tiles * listed
    return pl.pallas_call(
        kernel,
        grid_spec=pltpu.PrefetchScalarGridSpec(
            num_scalar_prefetch=1,
            grid=(count,),
            in_specs=[head_spec] * (3 * partners) + [far_spec] * 2,
            out_specs=[head_spec] * partners,
            scratch_shapes=[pltpu.VMEM((pool_size, TILE, size), BF16)] * 2,
        ),
        out_shape=[jax.ShapeDtypeStruct((count, rows, size), BF16)] * partners,
        cost_estimate=pl.CostEstimate(
            flops=pairs * 4 * TILE * TILE * size,
            bytes_accessed=count * 2 * TILE * size * (2 * near + 2 * pool_size),
            transcendentals=pairs * TILE * TILE,
        ),
    )(places, *queries, *keys, *values, far_keys, far_values)


def plan(key_tiles, my_shard, here, shards, partners, tiles):
    shard_tiles = partners * tiles
    listed = key_tiles.shape[1]
    own = jnp.arange(shard_tiles, dtype=jnp.int32)
    place_of = ((own // tiles) ^ here) * tiles + own % tiles
    by_reader = key_tiles.reshape(shards, shard_tiles * listed)
    wanted = jnp.any(by_reader[:, :, None] == (my_shard * shard_tiles + own)[None, None, :], axis=1)
    rank = jnp.cumsum(wanted.astype(jnp.int32), axis=1) - 1
    slots = jnp.arange(CAP, dtype=jnp.int32)
    chosen = wanted[:, None, :] & (rank[:, None, :] == slots[None, :, None])
    picks = jnp.sum(jnp.where(chosen, place_of[None, None, :], 0), axis=2)
    lists = lax.dynamic_slice_in_dim(key_tiles, my_shard * shard_tiles, shard_tiles, 0)
    matches = lists[:, :, None] == jnp.arange(shards * shard_tiles, dtype=jnp.int32)[None, None, :]
    needed = jnp.any(matches, axis=(0, 1)).reshape(shards, shard_tiles)
    need_rank = jnp.cumsum(needed.astype(jnp.int32), axis=1) - 1
    far_place = shard_tiles + jnp.arange(shards, dtype=jnp.int32)[:, None] * CAP + need_rank
    is_own = (jnp.arange(shards, dtype=jnp.int32) == my_shard)[:, None]
    place = jnp.where(is_own, place_of[None, :], far_place).reshape(-1)
    places = jnp.sum(jnp.where(matches, place[None, None, :], 0), axis=2)
    places = places.reshape(partners, tiles, listed)
    order = jnp.arange(partners, dtype=jnp.int32) ^ here
    places = jnp.take(places, order, axis=0).reshape(shard_tiles, listed)
    return picks.astype(jnp.int32), places.astype(jnp.int32)


def shards(queries, key_vectors, value_vectors, key_tiles):
    partners = lax.axis_size("head")
    shard_count = lax.axis_size("seq")
    here = lax.axis_index("head").astype(jnp.int32)
    my_shard = lax.axis_index("seq").astype(jnp.int32)
    here_arg = here.reshape(1)
    rows, heads, _ = queries.shape
    chunks = split_heads(heads // partners)
    tiles = rows // TILE

    def swap(piece, k):
        return piece if k == 0 else lax.ppermute(piece, "head", [(i, i ^ k) for i in range(partners)])

    def exchange(parts, c):
        return [swap(parts[k][c], k) for k in range(partners)]

    key_parts = by_partner(key_vectors, here_arg, partners, chunks)
    value_parts = by_partner(value_vectors, here_arg, partners, chunks)
    query_parts = by_partner(queries, here_arg, partners, chunks)
    picks, places = plan(key_tiles, my_shard, here, shard_count, partners, tiles)

    ready = []
    for c in range(len(chunks)):
        keys = exchange(key_parts, c)
        far_keys = lax.all_to_all(pick_tiles(keys, picks), "seq", 0, 0, tiled=True)
        values = exchange(value_parts, c)
        far_values = lax.all_to_all(pick_tiles(values, picks), "seq", 0, 0, tiled=True)
        ready.append((keys, values, far_keys, far_values))
    asked = [exchange(query_parts, c) for c in range(len(chunks))]
    answers = []
    for c in range(len(chunks)):
        outs = attend(asked[c], *ready[c], places)
        answers.append([swap(outs[k], k) for k in range(partners)])
    return from_partners([[answers[c][k] for c in range(len(chunks))] for k in range(partners)], here_arg, chunks, heads)


def solution(mesh):
    return jax.shard_map(
        shards,
        mesh=mesh,
        in_specs=(
            P(("seq", "head"), None, None),
            P(("seq", "head"), None, None),
            P(("seq", "head"), None, None),
            P(),
        ),
        out_specs=P(("seq", "head"), None, None),
        check_vma=False,
    )
```

time: 638 us -> 301 us (0.47); the launches traced: 629 us -> 299 us
  local copies, waits for them, and re-layouts: 155 us -> 7.19 us
  matrix products: 131 us -> 0 us
  blocking collectives: 97.8 us -> 0 us
  Pallas kernels: 0 us -> 73.6 us
  other arithmetic: 23 us -> 1.96 us
  waiting for transfers between devices: 189 us -> 168 us
  starting transfers between devices: 32.4 us -> 47.8 us
    all_to_all x5 -> x4, waiting for transfers between devices: 189 us -> 0.01 us  [the longest x2 0.01 us: shards(): far_keys = lax.all_to_all(pick_tiles(keys, picks), 'seq', 0, 0, tiled=True)]
    ppermute x0 -> x24, waiting for transfers between devices: none -> 168 us  [swap(): lax.ppermute(piece, 'head', [(i, i ^ k) for i in range(partners)])]
    dot_general x6 -> x0, matrix products: 98.5 us -> none  [the longest x2 54.7 us: attend_block(): jnp.einsum('ghqk,gkhd->ghqd', rounded, gathered_values, preferred_element...]
    all_to_all x1 -> x0, blocking collectives: 97.8 us -> none  [attend(): lax.all_to_all(outputs, 'head', split_axis=0, concat_axis=1, tiled=True)]
    pallas_call x0 -> x10, Pallas kernels: none -> 73.6 us  [the longest x2 40.1 us: attend(): pl.pallas_call(kernel, grid_spec=pltpu.PrefetchScalarGridSpec(num_scalar_...]
    gather x4 -> x1, local copies, waits for them, and re-layouts: 53.3 us -> 0.57 us  [plan(): places = jnp.take(places, order, axis=0).reshape(shard_tiles, listed)]
    sub x2 -> x0, matrix products: 32.2 us -> none  [attend_block(): weights = jnp.exp((scores - row_top) * score_scale)]
    ppermute x0 -> x24, starting transfers between devices: none -> 30.1 us  [swap(): lax.ppermute(piece, 'head', [(i, i ^ k) for i in range(partners)])]
  transfers between devices with their start and end apart: 5 -> 28, of which waited for: 5 -> 19; matrix products, arithmetic and copies ran while one was open for 15% -> 1% of each run, Pallas kernels for 0% -> 21%
where the time goes in v1:
time: 301 us; the launch traced here: 299 us
  waiting for transfers between devices  168 us (56%)
  Pallas kernels  73.6 us (24%)
  starting transfers between devices  47.8 us (16%)
  local copies, waits for them, and re-layouts  7.19 us (2%)
    ppermute x24, waiting for transfers between devices, swap(): lax.ppermute(piece, 'head', [(i, i ^ k) for i in range(partners)])  168 us
    pallas_call x2, Pallas kernels, attend(): pl.pallas_call(kernel, grid_spec=pltpu.PrefetchScalarGridSpec(num_scalar_...  40.1 us
    ppermute x24, starting transfers between devices, swap(): lax.ppermute(piece, 'head', [(i, i ^ k) for i in range(partners)])  30.1 us
    pallas_call x4, Pallas kernels, pick_tiles(): pl.pallas_call(kernel, grid_spec=pltpu.PrefetchScalarGridSpec(num_scalar_...  20.4 us
    pallas_call x3, Pallas kernels, by_partner(): pl.pallas_call(kernel, grid_spec=pltpu.PrefetchScalarGridSpec(num_scalar_...  9.81 us
    all_to_all x2, starting transfers between devices, shards(): far_keys = lax.all_to_all(pick_tiles(keys, picks), 'seq', 0, 0, tiled=True)  8.89 us
    all_to_all x2, starting transfers between devices, shards(): lax.all_to_all(pick_tiles(values, picks), 'seq', 0, 0, tiled=True)  8.89 us
  transfers between devices with their start and end apart: 28, of which 19 were waited for; matrix products, arithmetic and copies ran while one was open for 1% of the time, Pallas kernels for 21%

profile of v1, /device:TPU:10, one launch (start us, length us, event | category | flops | bytes accessed | tf_op | source)
XLA Modules:
  0.0 299.2 jit_solution(4052094487123361455)
XLA Ops:
  0.0 3.2 %shard_map.47 = (bf16[5,256,128]{2,1,0:T(8,128)(2,1)}, bf16[5,256,128]{2,1,0:T(8,128)(2,1)}, bf16[5,256,128]{2,1,0:T(8,128)(2,1)}, bf16[5,256,128]{2,1,0:T(8,128...) custom-call(s32[1]{0:T(128)} %bitcast.here_ref, ...), custom_call_target="tpu_custom_call" | custom-call | tf_op jit(solution)/shard_map/pallas_call | solution.py:41
  3.2 0.4 collective-permute-start.12
  3.7 2.6 collective-permute-start.13
  6.3 0.5 collective-permute-start.14
  6.9 0.3 compare_reduce_fusion
  7.2 0.2 reduce_window_sum.18
  7.4 0.2 select_reduce_fusion.1
  7.5 0.7 copy.10.pick_ref
  8.2 9.0 %collective-permute-done.12.refs_1_.refs_5_ = bf16[5,256,128]{2,1,0:T(8,128)(2,1)S(1)} collective-permute-done((bf16[5,256,128]{2,1,0:T(8,128)(2,1)}, bf16[5,256,128]{2,1,0:T(8,128)(2,1)S(1)}, u32[]{:S(2)}, u32[]{:S(2)}) %collective-permute-start.12) | collective-permute-done | bytes 327712 | tf_op jit(solution)/shard_map/ppermute | solution.py:201
  17.2 11.6 %collective-permute-done.13.refs_2_.refs_6_ = bf16[5,256,128]{2,1,0:T(8,128)(2,1)S(1)} collective-permute-done((bf16[5,256,128]{2,1,0:T(8,128)(2,1)}, bf16[5,256,128]{2,1,0:T(8,128)(2,1)S(1)}, u32[]{:S(2)}, u32[]{:S(2)}) %collective-permute-start.13) | collective-permute-done | bytes 327712 | tf_op jit(solution)/shard_map/ppermute | solution.py:201
  28.8 6.4 %collective-permute-done.14.refs_3_.refs_7_ = bf16[5,256,128]{2,1,0:T(8,128)(2,1)S(1)} collective-permute-done((bf16[5,256,128]{2,1,0:T(8,128)(2,1)}, bf16[5,256,128]{2,1,0:T(8,128)(2,1)S(1)}, u32[]{:S(2)}, u32[]{:S(2)}) %collective-permute-start.14) | collective-permute-done | bytes 327712 | tf_op jit(solution)/shard_map/ppermute | solution.py:201
  35.2 0.7 copy-done.4
  35.9 5.1 %shard_map.52 = bf16[8,2,5,128,128]{4,3,2,1,0:T(8,128)(2,1)} custom-call(s32[8,2]{1,0:T(8,128)} %copy.10.pick_ref, bf16[5,256,128]{2,1,0:T(8,128)(2,1)} %get-tuple-element.54.refs_0_.refs_4_, bf16[5,256,128]{2,1,0:T(8,128)(2,1)} %copy-done.2, bf16[5,256,128]{2,1,0:T(8,128)(2,1)} %copy-done.3, bf16[5,256,128]{2,1,0:T(8,128)(2,1)} %copy-done.4), custom_call_target="tpu_custom_call" | custom-call | tf_op jit(solution)/shard_map/pallas_call | solution.py:96
  41.0 4.3 %all-to-all-start.2 = ((bf16[8,2,5,128,128]{4,3,2,1,0:T(8,128)(2,1)}), bf16[8,2,5,128,128]{4,3,2,1,0:T(8,128)(2,1)S(1)}, u32[]{:S(2)}, u32[]{:S(2)}) async-start(bf16[8,2,5,128,128]{4,3,2,1,0:T(8,128)(2,1)} %shard_map.52), calls=%async_computation.2 | async-start | bytes 5242880 | tf_op jit(solution)/shard_map/all_to_all | solution.py:214
  45.3 3.3 %shard_map.48 = (bf16[5,256,128]{2,1,0:T(8,128)(2,1)}, bf16[5,256,128]{2,1,0:T(8,128)(2,1)}, bf16[5,256,128]{2,1,0:T(8,128)(2,1)}, bf16[5,256,128]{2,1,0:T(8,128...) custom-call(s32[1]{0:T(128)} %bitcast.here_ref, ...), custom_call_target="tpu_custom_call" | custom-call | tf_op jit(solution)/shard_map/pallas_call | solution.py:41
  48.6 3.0 %collective-permute-start.16 = (bf16[5,256,128]{2,1,0:T(8,128)(2,1)}, bf16[5,256,128]{2,1,0:T(8,128)(2,1)S(1)}, u32[]{:S(2)}, u32[]{:S(2)}) collective-permute-start(bf16[5,256,128]{2,1,0:T(8,128)(2,1)} %get-tuple-element.60), channel_id=1, source_target_pairs={{0,2},{1,3},{2,0},{3,1},{4,6},{5,7},{6,4},{7,5},{8,10},{9,11},{10,... | collective-permute-start | bytes 983048 | tf_op jit(solution)/shard_map/ppermute | solution.py:201
  51.6 0.4 collective-permute-start.17
  52.1 10.8 %collective-permute-done.15.refs_1_.refs_9_ = bf16[5,256,128]{2,1,0:T(8,128)(2,1)S(1)} collective-permute-done((bf16[5,256,128]{2,1,0:T(8,128)(2,1)}, bf16[5,256,128]{2,1,0:T(8,128)(2,1)S(1)}, u32[]{:S(2)}, u32[]{:S(2)}) %collective-permute-start.15) | collective-permute-done | bytes 327712 | tf_op jit(solution)/shard_map/ppermute | solution.py:201
  62.9 11.2 %collective-permute-done.16.refs_2_.refs_10_ = bf16[5,256,128]{2,1,0:T(8,128)(2,1)S(1)} collective-permute-done((bf16[5,256,128]{2,1,0:T(8,128)(2,1)}, bf16[5,256,128]{2,1,0:T(8,128)(2,1)S(1)}, u32[]{:S(2)}, u32[]{:S(2)}) %collective-permute-start.16) | collective-permute-done | bytes 327712 | tf_op jit(solution)/shard_map/ppermute | solution.py:201
  74.1 6.9 %collective-permute-done.17.refs_3_.refs_11_ = bf16[5,256,128]{2,1,0:T(8,128)(2,1)} collective-permute-done((bf16[5,256,128]{2,1,0:T(8,128)(2,1)}, bf16[5,256,128]{2,1,0:T(8,128)(2,1)}, u32[]{:S(2)}, u32[]{:S(2)}) %collective-permute-start.17) | collective-permute-done | bytes 327712 | tf_op jit(solution)/shard_map/ppermute | solution.py:201
  81.0 5.1 %shard_map.53 = bf16[8,2,5,128,128]{4,3,2,1,0:T(8,128)(2,1)} custom-call(s32[8,2]{1,0:T(8,128)} %copy.10.pick_ref, bf16[5,256,128]{2,1,0:T(8,128)(2,1)} %get-tuple-element.58.refs_0_.refs_8_, bf16[5,256,128]{2,1,0:T(8,128)(2,1)} %copy-done.8, bf16[5,256,128]{2,1,0:T(8,128)(2,1)} %copy-done.9, bf16[5,256,128]{2,1,0:T(8,128)(2,1)} %collective-permute-done.17.refs_3_.refs_11_), custom_call_target="tpu_custom_call" | custom-call | tf_op jit(solution)/shard_map/pallas_call | solution.py:96
  86.0 4.7 %all-to-all-start.3 = ((bf16[8,2,5,128,128]{4,3,2,1,0:T(8,128)(2,1)}), bf16[8,2,5,128,128]{4,3,2,1,0:T(8,128)(2,1)}, u32[]{:S(2)}, u32[]{:S(2)}) async-start(bf16[8,2,5,128,128]{4,3,2,1,0:T(8,128)(2,1)} %shard_map.53), calls=%async_computation.3 | async-start | bytes 5242880 | tf_op jit(solution)/shard_map/all_to_all | solution.py:216
  90.7 3.0 %collective-permute-start.7 = (bf16[5,256,128]{2,1,0:T(8,128)(2,1)}, bf16[5,256,128]{2,1,0:T(8,128)(2,1)S(1)}, u32[]{:S(2)}, u32[]{:S(2)}) collective-permute-start(bf16[5,256,128]{2,1,0:T(8,128)(2,1)} %get-tuple-element.47), channel_id=1, source_target_pairs={{0,2},{1,3},{2,0},{3,1},{4,6},{5,7},{6,4},{7,5},{8,10},{9,11},{10,... | collective-permute-start | bytes 983048 | tf_op jit(solution)/shard_map/ppermute | solution.py:201
  93.8 0.4 collective-permute-start.8
  94.2 10.8 %collective-permute-done.6.refs_1_.refs_9_ = bf16[5,256,128]{2,1,0:T(8,128)(2,1)S(1)} collective-permute-done((bf16[5,256,128]{2,1,0:T(8,128)(2,1)}, bf16[5,256,128]{2,1,0:T(8,128)(2,1)S(1)}, u32[]{:S(2)}, u32[]{:S(2)}) %collective-permute-start.6) | collective-permute-done | bytes 327712 | tf_op jit(solution)/shard_map/ppermute | solution.py:201
  105.0 11.2 %collective-permute-done.7.refs_2_.refs_10_ = bf16[5,256,128]{2,1,0:T(8,128)(2,1)S(1)} collective-permute-done((bf16[5,256,128]{2,1,0:T(8,128)(2,1)}, bf16[5,256,128]{2,1,0:T(8,128)(2,1)S(1)}, u32[]{:S(2)}, u32[]{:S(2)}) %collective-permute-start.7) | collective-permute-done | bytes 327712 | tf_op jit(solution)/shard_map/ppermute | solution.py:201
  116.2 6.8 %collective-permute-done.8.refs_3_.refs_11_ = bf16[5,256,128]{2,1,0:T(8,128)(2,1)S(1)} collective-permute-done((bf16[5,256,128]{2,1,0:T(8,128)(2,1)}, bf16[5,256,128]{2,1,0:T(8,128)(2,1)S(1)}, u32[]{:S(2)}, u32[]{:S(2)}) %collective-permute-start.8) | collective-permute-done | bytes 327712 | tf_op jit(solution)/shard_map/ppermute | solution.py:201
  123.0 0.8 copy-done.7
  123.7 5.1 %shard_map.50 = bf16[8,2,5,128,128]{4,3,2,1,0:T(8,128)(2,1)} custom-call(s32[8,2]{1,0:T(8,128)} %copy.10.pick_ref, bf16[5,256,128]{2,1,0:T(8,128)(2,1)} %get-tuple-element.45.refs_0_.refs_8_, bf16[5,256,128]{2,1,0:T(8,128)(2,1)} %copy-done.5, bf16[5,256,128]{2,1,0:T(8,128)(2,1)} %copy-done.6, bf16[5,256,128]{2,1,0:T(8,128)(2,1)} %copy-done.7), custom_call_target="tpu_custom_call" | custom-call | tf_op jit(solution)/shard_map/pallas_call | solution.py:96
  128.9 4.2 %all-to-all-start.1 = ((bf16[8,2,5,128,128]{4,3,2,1,0:T(8,128)(2,1)}), bf16[8,2,5,128,128]{4,3,2,1,0:T(8,128)(2,1)S(1)}, u32[]{:S(2)}, u32[]{:S(2)}) async-start(bf16[8,2,5,128,128]{4,3,2,1,0:T(8,128)(2,1)} %shard_map.50), calls=%async_computation.1 | async-start | bytes 5242880 | tf_op jit(solution)/shard_map/all_to_all | solution.py:216
  133.1 3.0 %collective-permute-start.4 = (bf16[5,256,128]{2,1,0:T(8,128)(2,1)}, bf16[5,256,128]{2,1,0:T(8,128)(2,1)S(1)}, u32[]{:S(2)}, u32[]{:S(2)}) collective-permute-start(bf16[5,256,128]{2,1,0:T(8,128)(2,1)} %get-tuple-element.43), channel_id=1, source_target_pairs={{0,2},{1,3},{2,0},{3,1},{4,6},{5,7},{6,4},{7,5},{8,10},{9,11},{10,... | collective-permute-start | bytes 983048 | tf_op jit(solution)/shard_map/ppermute | solution.py:201
  136.1 0.4 collective-permute-start.5
  136.6 10.8 %collective-permute-done.3.refs_1_.refs_5_ = bf16[5,256,128]{2,1,0:T(8,128)(2,1)S(1)} collective-permute-done((bf16[5,256,128]{2,1,0:T(8,128)(2,1)}, bf16[5,256,128]{2,1,0:T(8,128)(2,1)S(1)}, u32[]{:S(2)}, u32[]{:S(2)}) %collective-permute-start.3) | collective-permute-done | bytes 327712 | tf_op jit(solution)/shard_map/ppermute | solution.py:201
  147.4 11.2 %collective-permute-done.4.refs_2_.refs_6_ = bf16[5,256,128]{2,1,0:T(8,128)(2,1)S(1)} collective-permute-done((bf16[5,256,128]{2,1,0:T(8,128)(2,1)}, bf16[5,256,128]{2,1,0:T(8,128)(2,1)S(1)}, u32[]{:S(2)}, u32[]{:S(2)}) %collective-permute-start.4) | collective-permute-done | bytes 327712 | tf_op jit(solution)/shard_map/ppermute | solution.py:201
  158.6 6.9 %collective-permute-done.5.refs_3_.refs_7_ = bf16[5,256,128]{2,1,0:T(8,128)(2,1)} collective-permute-done((bf16[5,256,128]{2,1,0:T(8,128)(2,1)}, bf16[5,256,128]{2,1,0:T(8,128)(2,1)}, u32[]{:S(2)}, u32[]{:S(2)}) %collective-permute-start.5) | collective-permute-done | bytes 327712 | tf_op jit(solution)/shard_map/ppermute | solution.py:201
  165.5 5.1 %shard_map.49 = bf16[8,2,5,128,128]{4,3,2,1,0:T(8,128)(2,1)} custom-call(s32[8,2]{1,0:T(8,128)} %copy.10.pick_ref, bf16[5,256,128]{2,1,0:T(8,128)(2,1)} %get-tuple-element.41.refs_0_.refs_4_, bf16[5,256,128]{2,1,0:T(8,128)(2,1)} %copy-done.10, bf16[5,256,128]{2,1,0:T(8,128)(2,1)} %copy-done.11, bf16[5,256,128]{2,1,0:T(8,128)(2,1)} %collective-permute-done.5.refs_3_.refs_7_), custom_call_target="tpu_custom_call" | custom-call | tf_op jit(solution)/shard_map/pallas_call | solution.py:96
  170.6 1.5 copy-done.1
  172.1 4.6 %all-to-all-start = ((bf16[8,2,5,128,128]{4,3,2,1,0:T(8,128)(2,1)}), bf16[8,2,5,128,128]{4,3,2,1,0:T(8,128)(2,1)}, u32[]{:S(2)}, u32[]{:S(2)}) async-start(bf16[8,2,5,128,128]{4,3,2,1,0:T(8,128)(2,1)} %shard_map.49), calls=%async_computation | async-start | bytes 5242880 | tf_op jit(solution)/shard_map/all_to_all | solution.py:214
  176.7 3.3 %shard_map.46 = (bf16[5,256,128]{2,1,0:T(8,128)(2,1)}, bf16[5,256,128]{2,1,0:T(8,128)(2,1)}, bf16[5,256,128]{2,1,0:T(8,128)(2,1)}, bf16[5,256,128]{2,1,0:T(8,128...) custom-call(s32[1]{0:T(128)} %bitcast.here_ref, ...), custom_call_target="tpu_custom_call" | custom-call | tf_op jit(solution)/shard_map/pallas_call | solution.py:41
  180.0 1.6 collective-permute-start.11
  181.6 2.7 collective-permute-start.9
  184.4 3.0 %collective-permute-start.1 = (bf16[5,256,128]{2,1,0:T(8,128)(2,1)}, bf16[5,256,128]{2,1,0:T(8,128)(2,1)S(1)}, u32[]{:S(2)}, u32[]{:S(2)}) collective-permute-start(bf16[5,256,128]{2,1,0:T(8,128)(2,1)} %get-tuple-element.39), channel_id=1, source_target_pairs={{0,2},{1,3},{2,0},{3,1},{4,6},{5,7},{6,4},{7,5},{8,10},{9,11},{10,... | collective-permute-start | bytes 983048 | tf_op jit(solution)/shard_map/ppermute | solution.py:201
  187.7 0.2 reduce_window_sum.17
  188.0 0.3 select_reduce_fusion
  188.6 0.6 gather_fusion
  189.2 13.2 %collective-permute-done.10.refs_2_ = bf16[5,256,128]{2,1,0:T(8,128)(2,1)S(1)} collective-permute-done((bf16[5,256,128]{2,1,0:T(8,128)(2,1)}, bf16[5,256,128]{2,1,0:T(8,128)(2,1)S(1)}, u32[]{:S(2)}, u32[]{:S(2)}) %collective-permute-start.10) | collective-permute-done | bytes 327712 | tf_op jit(solution)/shard_map/ppermute | solution.py:201
  202.4 1.6 collective-permute-start.2
  204.0 0.7 broadcast_select_fusion.place_ref
  204.7 6.9 %collective-permute-done.11.refs_3_ = bf16[5,256,128]{2,1,0:T(8,128)(2,1)S(1)} collective-permute-done((bf16[5,256,128]{2,1,0:T(8,128)(2,1)}, bf16[5,256,128]{2,1,0:T(8,128)(2,1)S(1)}, u32[]{:S(2)}, u32[]{:S(2)}) %collective-permute-start.11) | collective-permute-done | bytes 327712 | tf_op jit(solution)/shard_map/ppermute | solution.py:201
  211.5 0.7 copy-done.22
  212.4 20.0 %shard_map.54 = (bf16[5,256,128]{2,1,0:T(8,128)(2,1)}, bf16[5,256,128]{2,1,0:T(8,128)(2,1)}, bf16[5,256,128]{2,1,0:T(8,128)(2,1)}, bf16[5,256,128]{2,1,0:T(8,128)(2,1)}) custom-call(s32[8,10]{1,0:T(8,128)} %broadcast_select_fusion.place_ref, bf16[5,256,128]{2,1,0:T(8,128)(2,1)} %get-tuple-element.50.refs_0_, bf16[5,256,128]{2,1,0:T(8,128)(2,1)} %copy-done.23, ...), custom_call_target="tpu_custom_call" | custom-call | flops 3355443200 | bytes 10485760 | tf_op jit(solution)/shard_map/pallas_call | solution.py:147
  232.5 1.7 collective-permute-start.21
  234.2 1.7 collective-permute-start.23
  236.0 3.6 %collective-permute-done.2.refs_3_ = bf16[5,256,128]{2,1,0:T(8,128)(2,1)S(1)} collective-permute-done((bf16[5,256,128]{2,1,0:T(8,128)(2,1)}, bf16[5,256,128]{2,1,0:T(8,128)(2,1)S(1)}, u32[]{:S(2)}, u32[]{:S(2)}) %collective-permute-start.2) | collective-permute-done | bytes 327712 | tf_op jit(solution)/shard_map/ppermute | solution.py:201
  239.6 0.7 copy-done.24
  240.3 20.0 %shard_map.51 = (bf16[5,256,128]{2,1,0:T(8,128)(2,1)}, bf16[5,256,128]{2,1,0:T(8,128)(2,1)}, bf16[5,256,128]{2,1,0:T(8,128)(2,1)}, bf16[5,256,128]{2,1,0:T(8,128)(2,1)}) custom-call(s32[8,10]{1,0:T(8,128)} %broadcast_select_fusion.place_ref, bf16[5,256,128]{2,1,0:T(8,128)(2,1)} %get-tuple-element.37.refs_0_, bf16[5,256,128]{2,1,0:T(8,128)(2,1)} %copy-done.19, ...), custom_call_target="tpu_custom_call" | custom-call | flops 3355443200 | bytes 10485760 | tf_op jit(solution)/shard_map/pallas_call | solution.py:147
  260.5 1.8 collective-permute-start.20
  262.3 1.7 collective-permute-start.22
  264.0 3.8 %collective-permute-done.23.refs_7_ = bf16[5,256,128]{2,1,0:T(8,128)(2,1)S(1)} collective-permute-done((bf16[5,256,128]{2,1,0:T(8,128)(2,1)}, bf16[5,256,128]{2,1,0:T(8,128)(2,1)S(1)}, u32[]{:S(2)}, u32[]{:S(2)}) %collective-permute-start.23) | collective-permute-done | bytes 327712 | tf_op jit(solution)/shard_map/ppermute | solution.py:201
  267.7 3.6 %collective-permute-done.18.refs_2_ = bf16[5,256,128]{2,1,0:T(8,128)(2,1)S(1)} collective-permute-done((bf16[5,256,128]{2,1,0:T(8,128)(2,1)}, bf16[5,256,128]{2,1,0:T(8,128)(2,1)S(1)}, u32[]{:S(2)}, u32[]{:S(2)}) %collective-permute-start.18) | collective-permute-done | bytes 327712 | tf_op jit(solution)/shard_map/ppermute | solution.py:201
  271.3 15.4 %collective-permute-done.20.refs_4_ = bf16[5,256,128]{2,1,0:T(8,128)(2,1)S(1)} collective-permute-done((bf16[5,256,128]{2,1,0:T(8,128)(2,1)}, bf16[5,256,128]{2,1,0:T(8,128)(2,1)S(1)}, u32[]{:S(2)}, u32[]{:S(2)}) %collective-permute-start.20) | collective-permute-done | bytes 327712 | tf_op jit(solution)/shard_map/ppermute | solution.py:201
  286.7 8.5 %collective-permute-done.22.refs_6_ = bf16[5,256,128]{2,1,0:T(8,128)(2,1)S(1)} collective-permute-done((bf16[5,256,128]{2,1,0:T(8,128)(2,1)}, bf16[5,256,128]{2,1,0:T(8,128)(2,1)S(1)}, u32[]{:S(2)}, u32[]{:S(2)}) %collective-permute-start.22) | collective-permute-done | bytes 327712 | tf_op jit(solution)/shard_map/ppermute | solution.py:201
  295.2 0.7 copy-done.17
  295.9 3.3 %shard_map.55 = bf16[256,40,128]{2,1,0:T(8,128)(2,1)} custom-call(s32[1]{0:T(128)} %bitcast.here_ref, bf16[5,256,128]{2,1,0:T(8,128)(2,1)} %get-tuple-element.49.refs_0_, bf16[5,256,128]{2,1,0:T(8,128)(2,1)} %get-tuple-element.62.refs_1_, bf16[5,256,128]{2,1,0:T(8,128)(2,1)} %copy-done.15, bf16[5,256,128]{2,1,0:T(8,128)(2,1)} %copy-done.12, ...), custom_call_target="tpu_custom_call" | custom-call | tf_op jit(solution)/shard_map/pallas_call | solution.py:70
  (79 shorter events, 1.3 us)
Async XLA Ops:
  0.0 6.7 %copy-start.18 = (s32[64,10]{0,1:T(8,128)S(1)}, s32[64,10]{0,1:T(8,128)}, u32[]{:S(2)}) copy-start(s32[64,10]{0,1:T(8,128)} %param.7) | copy-start | bytes 7684
  3.2 14.0 %collective-permute-start.12 = (bf16[5,256,128]{2,1,0:T(8,128)(2,1)}, bf16[5,256,128]{2,1,0:T(8,128)(2,1)S(1)}, u32[]{:S(2)}, u32[]{:S(2)}) collective-permute-start(bf16[5,256,128]{2,1,0:T(8,128)(2,1)} %get-tuple-element.55), channel_id=1, source_target_pairs={{0,1},{1,0},{2,3},{3,2},{4,5},{5,4},{6,7},{7,6},{8,9},{9,8},{10,11... | collective-permute-start | bytes 983048 | tf_op jit(solution)/shard_map/ppermute | solution.py:201
  3.7 25.1 %collective-permute-start.13 = (bf16[5,256,128]{2,1,0:T(8,128)(2,1)}, bf16[5,256,128]{2,1,0:T(8,128)(2,1)S(1)}, u32[]{:S(2)}, u32[]{:S(2)}) collective-permute-start(bf16[5,256,128]{2,1,0:T(8,128)(2,1)} %get-tuple-element.56), channel_id=1, source_target_pairs={{0,2},{1,3},{2,0},{3,1},{4,6},{5,7},{6,4},{7,5},{8,10},{9,11},{10,... | collective-permute-start | bytes 983048 | tf_op jit(solution)/shard_map/ppermute | solution.py:201
  6.3 28.9 %collective-permute-start.14 = (bf16[5,256,128]{2,1,0:T(8,128)(2,1)}, bf16[5,256,128]{2,1,0:T(8,128)(2,1)S(1)}, u32[]{:S(2)}, u32[]{:S(2)}) collective-permute-start(bf16[5,256,128]{2,1,0:T(8,128)(2,1)} %get-tuple-element.57), channel_id=1, source_target_pairs={{0,3},{1,2},{2,1},{3,0},{4,7},{5,6},{6,5},{7,4},{8,11},{9,10},{10,... | collective-permute-start | bytes 983048 | tf_op jit(solution)/shard_map/ppermute | solution.py:201
  17.2 18.0 %copy-start.2 = (bf16[5,256,128]{2,1,0:T(8,128)(2,1)}, bf16[5,256,128]{2,1,0:T(8,128)(2,1)S(1)}, u32[]{:S(2)}) copy-start(bf16[5,256,128]{2,1,0:T(8,128)(2,1)S(1)} %collective-permute-done.12.refs_1_.refs_5_) | copy-start | bytes 983044
  28.8 6.4 %copy-start.3 = (bf16[5,256,128]{2,1,0:T(8,128)(2,1)}, bf16[5,256,128]{2,1,0:T(8,128)(2,1)S(1)}, u32[]{:S(2)}) copy-start(bf16[5,256,128]{2,1,0:T(8,128)(2,1)S(1)} %collective-permute-done.13.refs_2_.refs_6_) | copy-start | bytes 983044
  35.2 0.7 copy-start.4
  41.0 45.0 %all-to-all-start.2 = ((bf16[8,2,5,128,128]{4,3,2,1,0:T(8,128)(2,1)}), bf16[8,2,5,128,128]{4,3,2,1,0:T(8,128)(2,1)S(1)}, u32[]{:S(2)}, u32[]{:S(2)}) async-start(bf16[8,2,5,128,128]{4,3,2,1,0:T(8,128)(2,1)} %shard_map.52), calls=%async_computation.2 | async-start | bytes 5242880 | tf_op jit(solution)/shard_map/all_to_all | solution.py:214
  48.6 14.3 %collective-permute-start.15 = (bf16[5,256,128]{2,1,0:T(8,128)(2,1)}, bf16[5,256,128]{2,1,0:T(8,128)(2,1)S(1)}, u32[]{:S(2)}, u32[]{:S(2)}) collective-permute-start(bf16[5,256,128]{2,1,0:T(8,128)(2,1)} %get-tuple-element.59), channel_id=1, source_target_pairs={{0,1},{1,0},{2,3},{3,2},{4,5},{5,4},{6,7},{7,6},{8,9},{9,8},{10,11... | collective-permute-start | bytes 983048 | tf_op jit(solution)/shard_map/ppermute | solution.py:201
  48.6 25.5 %collective-permute-start.16 = (bf16[5,256,128]{2,1,0:T(8,128)(2,1)}, bf16[5,256,128]{2,1,0:T(8,128)(2,1)S(1)}, u32[]{:S(2)}, u32[]{:S(2)}) collective-permute-start(bf16[5,256,128]{2,1,0:T(8,128)(2,1)} %get-tuple-element.60), channel_id=1, source_target_pairs={{0,2},{1,3},{2,0},{3,1},{4,6},{5,7},{6,4},{7,5},{8,10},{9,11},{10,... | collective-permute-start | bytes 983048 | tf_op jit(solution)/shard_map/ppermute | solution.py:201
  51.6 29.3 %collective-permute-start.17 = (bf16[5,256,128]{2,1,0:T(8,128)(2,1)}, bf16[5,256,128]{2,1,0:T(8,128)(2,1)}, u32[]{:S(2)}, u32[]{:S(2)}) collective-permute-start(bf16[5,256,128]{2,1,0:T(8,128)(2,1)} %get-tuple-element.61), channel_id=1, source_target_pairs={{0,3},{1,2},{2,1},{3,0},{4,7},{5,6},{6,5},{7,4},{8,11},{9,10},{10,... | collective-permute-start | bytes 983048 | tf_op jit(solution)/shard_map/ppermute | solution.py:201
  62.9 18.1 %copy-start.8 = (bf16[5,256,128]{2,1,0:T(8,128)(2,1)}, bf16[5,256,128]{2,1,0:T(8,128)(2,1)S(1)}, u32[]{:S(2)}) copy-start(bf16[5,256,128]{2,1,0:T(8,128)(2,1)S(1)} %collective-permute-done.15.refs_1_.refs_9_) | copy-start | bytes 983044
  74.1 6.9 %copy-start.9 = (bf16[5,256,128]{2,1,0:T(8,128)(2,1)}, bf16[5,256,128]{2,1,0:T(8,128)(2,1)S(1)}, u32[]{:S(2)}) copy-start(bf16[5,256,128]{2,1,0:T(8,128)(2,1)S(1)} %collective-permute-done.16.refs_2_.refs_10_) | copy-start | bytes 983044
  86.0 4.7 %copy-start = (bf16[8,2,5,128,128]{4,3,2,1,0:T(8,128)(2,1)}, bf16[8,2,5,128,128]{4,3,2,1,0:T(8,128)(2,1)S(1)}, u32[]{:S(2)}) copy-start(bf16[8,2,5,128,128]{4,3,2,1,0:T(8,128)(2,1)S(1)} %all-to-all-done.2.refs_12_) | copy-start | bytes 7864324
  86.0 42.8 %all-to-all-start.3 = ((bf16[8,2,5,128,128]{4,3,2,1,0:T(8,128)(2,1)}), bf16[8,2,5,128,128]{4,3,2,1,0:T(8,128)(2,1)}, u32[]{:S(2)}, u32[]{:S(2)}) async-start(bf16[8,2,5,128,128]{4,3,2,1,0:T(8,128)(2,1)} %shard_map.53), calls=%async_computation.3 | async-start | bytes 5242880 | tf_op jit(solution)/shard_map/all_to_all | solution.py:216
  90.7 14.3 %collective-permute-start.6 = (bf16[5,256,128]{2,1,0:T(8,128)(2,1)}, bf16[5,256,128]{2,1,0:T(8,128)(2,1)S(1)}, u32[]{:S(2)}, u32[]{:S(2)}) collective-permute-start(bf16[5,256,128]{2,1,0:T(8,128)(2,1)} %get-tuple-element.46), channel_id=1, source_target_pairs={{0,1},{1,0},{2,3},{3,2},{4,5},{5,4},{6,7},{7,6},{8,9},{9,8},{10,11... | collective-permute-start | bytes 983048 | tf_op jit(solution)/shard_map/ppermute | solution.py:201
  90.7 25.5 %collective-permute-start.7 = (bf16[5,256,128]{2,1,0:T(8,128)(2,1)}, bf16[5,256,128]{2,1,0:T(8,128)(2,1)S(1)}, u32[]{:S(2)}, u32[]{:S(2)}) collective-permute-start(bf16[5,256,128]{2,1,0:T(8,128)(2,1)} %get-tuple-element.47), channel_id=1, source_target_pairs={{0,2},{1,3},{2,0},{3,1},{4,6},{5,7},{6,4},{7,5},{8,10},{9,11},{10,... | collective-permute-start | bytes 983048 | tf_op jit(solution)/shard_map/ppermute | solution.py:201
  93.8 29.2 %collective-permute-start.8 = (bf16[5,256,128]{2,1,0:T(8,128)(2,1)}, bf16[5,256,128]{2,1,0:T(8,128)(2,1)S(1)}, u32[]{:S(2)}, u32[]{:S(2)}) collective-permute-start(bf16[5,256,128]{2,1,0:T(8,128)(2,1)} %get-tuple-element.48), channel_id=1, source_target_pairs={{0,3},{1,2},{2,1},{3,0},{4,7},{5,6},{6,5},{7,4},{8,11},{9,10},{10,... | collective-permute-start | bytes 983048 | tf_op jit(solution)/shard_map/ppermute | solution.py:201
  105.0 18.0 %copy-start.5 = (bf16[5,256,128]{2,1,0:T(8,128)(2,1)}, bf16[5,256,128]{2,1,0:T(8,128)(2,1)S(1)}, u32[]{:S(2)}) copy-start(bf16[5,256,128]{2,1,0:T(8,128)(2,1)S(1)} %collective-permute-done.6.refs_1_.refs_9_) | copy-start | bytes 983044
  116.2 6.8 %copy-start.6 = (bf16[5,256,128]{2,1,0:T(8,128)(2,1)}, bf16[5,256,128]{2,1,0:T(8,128)(2,1)S(1)}, u32[]{:S(2)}) copy-start(bf16[5,256,128]{2,1,0:T(8,128)(2,1)S(1)} %collective-permute-done.7.refs_2_.refs_10_) | copy-start | bytes 983044
  123.0 0.8 copy-start.7
  128.9 41.7 %all-to-all-start.1 = ((bf16[8,2,5,128,128]{4,3,2,1,0:T(8,128)(2,1)}), bf16[8,2,5,128,128]{4,3,2,1,0:T(8,128)(2,1)S(1)}, u32[]{:S(2)}, u32[]{:S(2)}) async-start(bf16[8,2,5,128,128]{4,3,2,1,0:T(8,128)(2,1)} %shard_map.50), calls=%async_computation.1 | async-start | bytes 5242880 | tf_op jit(solution)/shard_map/all_to_all | solution.py:216
  133.1 14.3 %collective-permute-start.3 = (bf16[5,256,128]{2,1,0:T(8,128)(2,1)}, bf16[5,256,128]{2,1,0:T(8,128)(2,1)S(1)}, u32[]{:S(2)}, u32[]{:S(2)}) collective-permute-start(bf16[5,256,128]{2,1,0:T(8,128)(2,1)} %get-tuple-element.42), channel_id=1, source_target_pairs={{0,1},{1,0},{2,3},{3,2},{4,5},{5,4},{6,7},{7,6},{8,9},{9,8},{10,11... | collective-permute-start | bytes 983048 | tf_op jit(solution)/shard_map/ppermute | solution.py:201
  133.1 25.5 %collective-permute-start.4 = (bf16[5,256,128]{2,1,0:T(8,128)(2,1)}, bf16[5,256,128]{2,1,0:T(8,128)(2,1)S(1)}, u32[]{:S(2)}, u32[]{:S(2)}) collective-permute-start(bf16[5,256,128]{2,1,0:T(8,128)(2,1)} %get-tuple-element.43), channel_id=1, source_target_pairs={{0,2},{1,3},{2,0},{3,1},{4,6},{5,7},{6,4},{7,5},{8,10},{9,11},{10,... | collective-permute-start | bytes 983048 | tf_op jit(solution)/shard_map/ppermute | solution.py:201
  136.1 29.3 %collective-permute-start.5 = (bf16[5,256,128]{2,1,0:T(8,128)(2,1)}, bf16[5,256,128]{2,1,0:T(8,128)(2,1)}, u32[]{:S(2)}, u32[]{:S(2)}) collective-permute-start(bf16[5,256,128]{2,1,0:T(8,128)(2,1)} %get-tuple-element.44), channel_id=1, source_target_pairs={{0,3},{1,2},{2,1},{3,0},{4,7},{5,6},{6,5},{7,4},{8,11},{9,10},{10,... | collective-permute-start | bytes 983048 | tf_op jit(solution)/shard_map/ppermute | solution.py:201
  147.4 18.1 %copy-start.10 = (bf16[5,256,128]{2,1,0:T(8,128)(2,1)}, bf16[5,256,128]{2,1,0:T(8,128)(2,1)S(1)}, u32[]{:S(2)}) copy-start(bf16[5,256,128]{2,1,0:T(8,128)(2,1)S(1)} %collective-permute-done.3.refs_1_.refs_5_) | copy-start | bytes 983044
  158.6 6.9 %copy-start.11 = (bf16[5,256,128]{2,1,0:T(8,128)(2,1)}, bf16[5,256,128]{2,1,0:T(8,128)(2,1)S(1)}, u32[]{:S(2)}) copy-start(bf16[5,256,128]{2,1,0:T(8,128)(2,1)S(1)} %collective-permute-done.4.refs_2_.refs_6_) | copy-start | bytes 983044
  170.6 1.5 copy-start.1
  172.1 67.5 %all-to-all-start = ((bf16[8,2,5,128,128]{4,3,2,1,0:T(8,128)(2,1)}), bf16[8,2,5,128,128]{4,3,2,1,0:T(8,128)(2,1)}, u32[]{:S(2)}, u32[]{:S(2)}) async-start(bf16[8,2,5,128,128]{4,3,2,1,0:T(8,128)(2,1)} %shard_map.49), calls=%async_computation | async-start | bytes 5242880 | tf_op jit(solution)/shard_map/all_to_all | solution.py:214
  180.0 22.4 %collective-permute-start.10 = (bf16[5,256,128]{2,1,0:T(8,128)(2,1)}, bf16[5,256,128]{2,1,0:T(8,128)(2,1)S(1)}, u32[]{:S(2)}, u32[]{:S(2)}) collective-permute-start(bf16[5,256,128]{2,1,0:T(8,128)(2,1)} %get-tuple-element.52), channel_id=1, source_target_pairs={{0,2},{1,3},{2,0},{3,1},{4,6},{5,7},{6,4},{7,5},{8,10},{9,11},{10,... | collective-permute-start | bytes 983048 | tf_op jit(solution)/shard_map/ppermute | solution.py:201
  180.0 31.5 %collective-permute-start.11 = (bf16[5,256,128]{2,1,0:T(8,128)(2,1)}, bf16[5,256,128]{2,1,0:T(8,128)(2,1)S(1)}, u32[]{:S(2)}, u32[]{:S(2)}) collective-permute-start(bf16[5,256,128]{2,1,0:T(8,128)(2,1)} %get-tuple-element.53), channel_id=1, source_target_pairs={{0,3},{1,2},{2,1},{3,0},{4,7},{5,6},{6,5},{7,4},{8,11},{9,10},{10,... | collective-permute-start | bytes 983048 | tf_op jit(solution)/shard_map/ppermute | solution.py:201
  181.6 29.9 %collective-permute-start.9 = (bf16[5,256,128]{2,1,0:T(8,128)(2,1)}, bf16[5,256,128]{2,1,0:T(8,128)(2,1)S(1)}, u32[]{:S(2)}, u32[]{:S(2)}) collective-permute-start(bf16[5,256,128]{2,1,0:T(8,128)(2,1)} %get-tuple-element.51), channel_id=1, source_target_pairs={{0,1},{1,0},{2,3},{3,2},{4,5},{5,4},{6,7},{7,6},{8,9},{9,8},{10,11... | collective-permute-start | bytes 983048 | tf_op jit(solution)/shard_map/ppermute | solution.py:201
  184.4 49.9 %collective-permute-start = (bf16[5,256,128]{2,1,0:T(8,128)(2,1)}, bf16[5,256,128]{2,1,0:T(8,128)(2,1)S(1)}, u32[]{:S(2)}, u32[]{:S(2)}) collective-permute-start(bf16[5,256,128]{2,1,0:T(8,128)(2,1)} %get-tuple-element.38), channel_id=1, source_target_pairs={{0,1},{1,0},{2,3},{3,2},{4,5},{5,4},{6,7},{7,6},{8,9},{9,8},{10,11... | collective-permute-start | bytes 983048 | tf_op jit(solution)/shard_map/ppermute | solution.py:201
  184.4 51.6 %collective-permute-start.1 = (bf16[5,256,128]{2,1,0:T(8,128)(2,1)}, bf16[5,256,128]{2,1,0:T(8,128)(2,1)S(1)}, u32[]{:S(2)}, u32[]{:S(2)}) collective-permute-start(bf16[5,256,128]{2,1,0:T(8,128)(2,1)} %get-tuple-element.39), channel_id=1, source_target_pairs={{0,2},{1,3},{2,0},{3,1},{4,6},{5,7},{6,4},{7,5},{8,10},{9,11},{10,... | collective-permute-start | bytes 983048 | tf_op jit(solution)/shard_map/ppermute | solution.py:201
  202.4 9.1 %copy-start.21 = (bf16[5,256,128]{2,1,0:T(8,128)(2,1)}, bf16[5,256,128]{2,1,0:T(8,128)(2,1)S(1)}, u32[]{:S(2)}) copy-start(bf16[5,256,128]{2,1,0:T(8,128)(2,1)S(1)} %collective-permute-done.10.refs_2_) | copy-start | bytes 983044
  202.4 37.2 %collective-permute-start.2 = (bf16[5,256,128]{2,1,0:T(8,128)(2,1)}, bf16[5,256,128]{2,1,0:T(8,128)(2,1)S(1)}, u32[]{:S(2)}, u32[]{:S(2)}) collective-permute-start(bf16[5,256,128]{2,1,0:T(8,128)(2,1)} %get-tuple-element.40), channel_id=1, source_target_pairs={{0,3},{1,2},{2,1},{3,0},{4,7},{5,6},{6,5},{7,4},{8,11},{9,10},{10,... | collective-permute-start | bytes 983048 | tf_op jit(solution)/shard_map/ppermute | solution.py:201
  211.5 0.7 copy-start.22
  211.5 0.8 copy-start.23
  232.4 29.8 %collective-permute-start.19 = (bf16[5,256,128]{2,1,0:T(8,128)(2,1)}, bf16[5,256,128]{2,1,0:T(8,128)(2,1)S(1)}, u32[]{:S(2)}, u32[]{:S(2)}) collective-permute-start(bf16[5,256,128]{2,1,0:T(8,128)(2,1)} %get-tuple-element.64), channel_id=1, source_target_pairs={{0,1},{1,0},{2,3},{3,2},{4,5},{5,4},{6,7},{7,6},{8,9},{9,8},{10,11... | collective-permute-start | bytes 983048 | tf_op jit(solution)/shard_map/ppermute | solution.py:201
  232.5 31.5 %collective-permute-start.21 = (bf16[5,256,128]{2,1,0:T(8,128)(2,1)}, bf16[5,256,128]{2,1,0:T(8,128)(2,1)S(1)}, u32[]{:S(2)}, u32[]{:S(2)}) collective-permute-start(bf16[5,256,128]{2,1,0:T(8,128)(2,1)} %get-tuple-element.66), channel_id=1, source_target_pairs={{0,2},{1,3},{2,0},{3,1},{4,6},{5,7},{6,4},{7,5},{8,10},{9,11},{10,... | collective-permute-start | bytes 983048 | tf_op jit(solution)/shard_map/ppermute | solution.py:201
  234.2 5.4 %copy-start.19 = (bf16[5,256,128]{2,1,0:T(8,128)(2,1)}, bf16[5,256,128]{2,1,0:T(8,128)(2,1)S(1)}, u32[]{:S(2)}) copy-start(bf16[5,256,128]{2,1,0:T(8,128)(2,1)S(1)} %collective-permute-done.refs_1_) | copy-start | bytes 983044
  234.2 33.5 %collective-permute-start.23 = (bf16[5,256,128]{2,1,0:T(8,128)(2,1)}, bf16[5,256,128]{2,1,0:T(8,128)(2,1)S(1)}, u32[]{:S(2)}, u32[]{:S(2)}) collective-permute-start(bf16[5,256,128]{2,1,0:T(8,128)(2,1)} %get-tuple-element.68), channel_id=1, source_target_pairs={{0,3},{1,2},{2,1},{3,0},{4,7},{5,6},{6,5},{7,4},{8,11},{9,10},{10,... | collective-permute-start | bytes 983048 | tf_op jit(solution)/shard_map/ppermute | solution.py:201
  236.0 3.6 %copy-start.20 = (bf16[5,256,128]{2,1,0:T(8,128)(2,1)}, bf16[5,256,128]{2,1,0:T(8,128)(2,1)S(1)}, u32[]{:S(2)}) copy-start(bf16[5,256,128]{2,1,0:T(8,128)(2,1)S(1)} %collective-permute-done.1.refs_2_) | copy-start | bytes 983044
  239.6 0.7 copy-start.24
  260.4 10.9 %collective-permute-start.18 = (bf16[5,256,128]{2,1,0:T(8,128)(2,1)}, bf16[5,256,128]{2,1,0:T(8,128)(2,1)S(1)}, u32[]{:S(2)}, u32[]{:S(2)}) collective-permute-start(bf16[5,256,128]{2,1,0:T(8,128)(2,1)} %get-tuple-element.63), channel_id=1, source_target_pairs={{0,1},{1,0},{2,3},{3,2},{4,5},{5,4},{6,7},{7,6},{8,9},{9,8},{10,11... | collective-permute-start | bytes 983048 | tf_op jit(solution)/shard_map/ppermute | solution.py:201
  260.5 26.2 %collective-permute-start.20 = (bf16[5,256,128]{2,1,0:T(8,128)(2,1)}, bf16[5,256,128]{2,1,0:T(8,128)(2,1)S(1)}, u32[]{:S(2)}, u32[]{:S(2)}) collective-permute-start(bf16[5,256,128]{2,1,0:T(8,128)(2,1)} %get-tuple-element.65), channel_id=1, source_target_pairs={{0,2},{1,3},{2,0},{3,1},{4,6},{5,7},{6,4},{7,5},{8,10},{9,11},{10,... | collective-permute-start | bytes 983048 | tf_op jit(solution)/shard_map/ppermute | solution.py:201
  262.3 32.9 %copy-start.12 = (bf16[5,256,128]{2,1,0:T(8,128)(2,1)}, bf16[5,256,128]{2,1,0:T(8,128)(2,1)S(1)}, u32[]{:S(2)}) copy-start(bf16[5,256,128]{2,1,0:T(8,128)(2,1)S(1)} %collective-permute-done.19.refs_3_) | copy-start | bytes 983044
  262.3 32.9 %collective-permute-start.22 = (bf16[5,256,128]{2,1,0:T(8,128)(2,1)}, bf16[5,256,128]{2,1,0:T(8,128)(2,1)S(1)}, u32[]{:S(2)}, u32[]{:S(2)}) collective-permute-start(bf16[5,256,128]{2,1,0:T(8,128)(2,1)} %get-tuple-element.67), channel_id=1, source_target_pairs={{0,3},{1,2},{2,1},{3,0},{4,7},{5,6},{6,5},{7,4},{8,11},{9,10},{10,... | collective-permute-start | bytes 983048 | tf_op jit(solution)/shard_map/ppermute | solution.py:201
  264.0 31.2 %copy-start.13 = (bf16[5,256,128]{2,1,0:T(8,128)(2,1)}, bf16[5,256,128]{2,1,0:T(8,128)(2,1)S(1)}, u32[]{:S(2)}) copy-start(bf16[5,256,128]{2,1,0:T(8,128)(2,1)S(1)} %collective-permute-done.21.refs_5_) | copy-start | bytes 983044
  267.7 27.4 %copy-start.14 = (bf16[5,256,128]{2,1,0:T(8,128)(2,1)}, bf16[5,256,128]{2,1,0:T(8,128)(2,1)S(1)}, u32[]{:S(2)}) copy-start(bf16[5,256,128]{2,1,0:T(8,128)(2,1)S(1)} %collective-permute-done.23.refs_7_) | copy-start | bytes 983044
  271.3 23.9 %copy-start.15 = (bf16[5,256,128]{2,1,0:T(8,128)(2,1)}, bf16[5,256,128]{2,1,0:T(8,128)(2,1)S(1)}, u32[]{:S(2)}) copy-start(bf16[5,256,128]{2,1,0:T(8,128)(2,1)S(1)} %collective-permute-done.18.refs_2_) | copy-start | bytes 983044
  286.7 8.5 %copy-start.16 = (bf16[5,256,128]{2,1,0:T(8,128)(2,1)}, bf16[5,256,128]{2,1,0:T(8,128)(2,1)S(1)}, u32[]{:S(2)}) copy-start(bf16[5,256,128]{2,1,0:T(8,128)(2,1)S(1)} %collective-permute-done.20.refs_4_) | copy-start | bytes 983044
  295.2 0.8 copy-start.17

commit v2 on v1

--- a/solution.py
+++ b/solution.py
@@ -80,36 +80,41 @@
     )(here, *flat)
 
 
-def pick_tiles(pieces, picks):
-    count, rows, size = pieces[0].shape
-    readers = picks.shape[0]
+def pick_tiles(keys, values, picks, groups):
+    count, rows, size = keys[0].shape
     tiles = rows // TILE
+    partners = len(keys)
 
     def kernel(pick_ref, *refs):
-        ins, out, pool = refs[:-2], refs[-2], refs[-1]
-        for k, piece in enumerate(ins):
-            pool[k * tiles : (k + 1) * tiles] = piece[0].reshape(tiles, TILE, size)
-        for reader in range(readers):
-            for slot in range(CAP):
-                out[reader, slot, 0] = pool[pick_ref[reader, slot]]
+        ins, outs, pools = refs[: 2 * partners], refs[2 * partners : -2], refs[-2:]
+        for kind, pool in enumerate(pools):
+            for k in range(partners):
+                pool[k * tiles : (k + 1) * tiles] = ins[kind * partners + k][0].reshape(tiles, TILE, size)
+            for group, out in zip(groups, outs):
+                for at, reader in enumerate(group):
+                    for slot in range(CAP):
+                        out[at, kind, slot, 0] = pool[pick_ref[reader, slot]]
 
     return pl.pallas_call(
         kernel,
         grid_spec=pltpu.PrefetchScalarGridSpec(
             num_scalar_prefetch=1,
             grid=(count,),
-            in_specs=[pl.BlockSpec((1, rows, size), lambda h, _: (h, 0, 0))] * len(pieces),
-            out_specs=pl.BlockSpec((readers, CAP, 1, TILE, size), lambda h, _: (0, 0, h, 0, 0)),
-            scratch_shapes=[pltpu.VMEM((len(pieces) * tiles, TILE, size), BF16)],
-        ),
-        out_shape=jax.ShapeDtypeStruct((readers, CAP, count, TILE, size), BF16),
-    )(picks, *pieces)
-
-
-def attend(queries, keys, values, far_keys, far_values, places):
+            in_specs=[pl.BlockSpec((1, rows, size), lambda h, _: (h, 0, 0))] * (2 * partners),
+            out_specs=[
+                pl.BlockSpec((len(group), 2, CAP, 1, TILE, size), lambda h, _: (0, 0, 0, h, 0, 0)) for group in groups
+            ],
+            scratch_shapes=[pltpu.VMEM((partners * tiles, TILE, size), BF16)] * 2,
+        ),
+        out_shape=[jax.ShapeDtypeStruct((len(group), 2, CAP, count, TILE, size), BF16) for group in groups],
+    )(picks, *keys, *values)
+
+
+def attend(queries, keys, values, far, places):
     partners = len(queries)
     count, rows, size = queries[0].shape
-    owners = far_keys.shape[0]
+    far_count = len(far)
+    far_tiles = [part.shape[0] * CAP for part in far]
     tiles = rows // TILE
     near = partners * tiles
     listed = places.shape[1]
@@ -117,14 +122,16 @@
 
     def kernel(place_ref, *refs):
         q_refs, k_refs, v_refs = refs[:partners], refs[partners : 2 * partners], refs[2 * partners : 3 * partners]
-        far_k, far_v = refs[3 * partners : 3 * partners + 2]
-        outs = refs[3 * partners + 2 : 4 * partners + 2]
-        k_pool, v_pool = refs[4 * partners + 2 :]
+        far_refs = refs[3 * partners : 3 * partners + far_count]
+        outs, (k_pool, v_pool) = refs[3 * partners + far_count : -2], refs[-2:]
         for k in range(partners):
             k_pool[k * tiles : (k + 1) * tiles] = k_refs[k][0].reshape(tiles, TILE, size)
             v_pool[k * tiles : (k + 1) * tiles] = v_refs[k][0].reshape(tiles, TILE, size)
-        k_pool[near:] = far_k[:, :, 0].reshape(owners * CAP, TILE, size)
-        v_pool[near:] = far_v[:, :, 0].reshape(owners * CAP, TILE, size)
+        place = near
+        for k, many in enumerate(far_tiles):
+            k_pool[place : place + many] = far_refs[k][:, 0, :, 0].reshape(many, TILE, size)
+            v_pool[place : place + many] = far_refs[k][:, 1, :, 0].reshape(many, TILE, size)
+            place += many
         for k in range(partners):
             for tile in range(tiles):
                 at = pl.ds(tile * TILE, TILE)
@@ -141,15 +148,17 @@
                 outs[k][0, at, :] = (mixed / row_total).astype(BF16)
 
     head_spec = pl.BlockSpec((1, rows, size), lambda h, _: (h, 0, 0))
-    far_spec = pl.BlockSpec((owners, CAP, 1, TILE, size), lambda h, _: (0, 0, h, 0, 0))
-    pool_size = near + owners * CAP
+    far_specs = [
+        pl.BlockSpec((part.shape[0], 2, CAP, 1, TILE, size), lambda h, _: (0, 0, 0, h, 0, 0)) for part in far
+    ]
+    pool_size = near + sum(far_tiles)
     pairs = count * partners * tiles * listed
     return pl.pallas_call(
         kernel,
         grid_spec=pltpu.PrefetchScalarGridSpec(
             num_scalar_prefetch=1,
             grid=(count,),
-            in_specs=[head_spec] * (3 * partners) + [far_spec] * 2,
+            in_specs=[head_spec] * (3 * partners) + far_specs,
             out_specs=[head_spec] * partners,
             scratch_shapes=[pltpu.VMEM((pool_size, TILE, size), BF16)] * 2,
         ),
@@ -159,10 +168,10 @@
             bytes_accessed=count * 2 * TILE * size * (2 * near + 2 * pool_size),
             transcendentals=pairs * TILE * TILE,
         ),
-    )(places, *queries, *keys, *values, far_keys, far_values)
-
-
-def plan(key_tiles, my_shard, here, shards, partners, tiles):
+    )(places, *queries, *keys, *values, *far)
+
+
+def plan(key_tiles, my_shard, here, shards, partners, tiles, pairwise):
     shard_tiles = partners * tiles
     listed = key_tiles.shape[1]
     own = jnp.arange(shard_tiles, dtype=jnp.int32)
@@ -177,7 +186,11 @@
     matches = lists[:, :, None] == jnp.arange(shards * shard_tiles, dtype=jnp.int32)[None, None, :]
     needed = jnp.any(matches, axis=(0, 1)).reshape(shards, shard_tiles)
     need_rank = jnp.cumsum(needed.astype(jnp.int32), axis=1) - 1
-    far_place = shard_tiles + jnp.arange(shards, dtype=jnp.int32)[:, None] * CAP + need_rank
+    far_at = jnp.arange(shards, dtype=jnp.int32)
+    if pairwise:
+        picks = jnp.take(picks, far_at ^ my_shard, axis=0)
+        far_at = (far_at ^ my_shard) - 1
+    far_place = shard_tiles + far_at[:, None] * CAP + need_rank
     is_own = (jnp.arange(shards, dtype=jnp.int32) == my_shard)[:, None]
     place = jnp.where(is_own, place_of[None, :], far_place).reshape(-1)
     places = jnp.sum(jnp.where(matches, place[None, None, :], 0), axis=2)
@@ -196,6 +209,7 @@
     rows, heads, _ = queries.shape
     chunks = split_heads(heads // partners)
     tiles = rows // TILE
+    pairwise = False
 
     def swap(piece, k):
         return piece if k == 0 else lax.ppermute(piece, "head", [(i, i ^ k) for i in range(partners)])
@@ -206,15 +220,22 @@
     key_parts = by_partner(key_vectors, here_arg, partners, chunks)
     value_parts = by_partner(value_vectors, here_arg, partners, chunks)
     query_parts = by_partner(queries, here_arg, partners, chunks)
-    picks, places = plan(key_tiles, my_shard, here, shard_count, partners, tiles)
+    picks, places = plan(key_tiles, my_shard, here, shard_count, partners, tiles, pairwise)
+
+    def share(keys, values):
+        if not pairwise:
+            sent = pick_tiles(keys, values, picks, [range(shard_count)])[0]
+            return [lax.all_to_all(sent, "seq", 0, 0, tiled=True)]
+        sent = pick_tiles(keys, values, picks, [[k] for k in range(1, shard_count)])
+        return [
+            lax.ppermute(part, "seq", [(i, i ^ k) for i in range(shard_count)]) for k, part in enumerate(sent, start=1)
+        ]
 
     ready = []
     for c in range(len(chunks)):
         keys = exchange(key_parts, c)
-        far_keys = lax.all_to_all(pick_tiles(keys, picks), "seq", 0, 0, tiled=True)
         values = exchange(value_parts, c)
-        far_values = lax.all_to_all(pick_tiles(values, picks), "seq", 0, 0, tiled=True)
-        ready.append((keys, values, far_keys, far_values))
+        ready.append((keys, values, share(keys, values)))
     asked = [exchange(query_parts, c) for c in range(len(chunks))]
     answers = []
     for c in range(len(chunks)):

time: 301 us -> 271 us (0.900)
  waiting for transfers between devices: 168 us -> 153 us
  Pallas kernels: 73.6 us -> 65.7 us
  starting transfers between devices: 47.8 us -> 43.4 us
    ppermute x24, waiting for transfers between devices: 168 us -> 153 us  [swap(): lax.ppermute(piece, 'head', [(i, i ^ k) for i in range(partners)])]
    pallas_call x4 -> x2, Pallas kernels: 20.4 us -> 12.4 us  [pick_tiles(): pl.pallas_call(kernel, grid_spec=pltpu.PrefetchScalarGridSpec(num_scalar_...]
    all_to_all x4 -> x2, starting transfers between devices: 17.8 us -> 10.1 us  [share(): return [lax.all_to_all(sent, 'seq', 0, 0, tiled=True)]]
    ppermute x24, starting transfers between devices: 30.1 us -> 33.3 us  [swap(): lax.ppermute(piece, 'head', [(i, i ^ k) for i in range(partners)])]
  transfers between devices with their start and end apart: 28 -> 26, of which waited for: 19 -> 17; matrix products, arithmetic and copies ran while one was open for 1% -> 1% of each run, Pallas kernels for 21% -> 20%
where the time goes in v2:
time: 271 us; the launch traced here: 270 us
  waiting for transfers between devices  153 us (56%)
  Pallas kernels  65.7 us (24%)
  starting transfers between devices  43.4 us (16%)
  local copies, waits for them, and re-layouts  5.72 us (2%)
    ppermute x24, waiting for transfers between devices, swap(): lax.ppermute(piece, 'head', [(i, i ^ k) for i in range(partners)])  153 us
    pallas_call x2, Pallas kernels, attend(): pl.pallas_call(kernel, grid_spec=pltpu.PrefetchScalarGridSpec(num_scalar_...  40.1 us
    ppermute x24, starting transfers between devices, swap(): lax.ppermute(piece, 'head', [(i, i ^ k) for i in range(partners)])  33.3 us
    pallas_call x2, Pallas kernels, pick_tiles(): pl.pallas_call(kernel, grid_spec=pltpu.PrefetchScalarGridSpec(num_scalar_...  12.4 us
    all_to_all x2, starting transfers between devices, share(): return [lax.all_to_all(sent, 'seq', 0, 0, tiled=True)]  10.1 us
    pallas_call x3, Pallas kernels, by_partner(): pl.pallas_call(kernel, grid_spec=pltpu.PrefetchScalarGridSpec(num_scalar_...  9.86 us
  transfers between devices with their start and end apart: 26, of which 17 were waited for; matrix products, arithmetic and copies ran while one was open for 1% of the time, Pallas kernels for 20%

profile of v2, /device:TPU:10, one launch (start us, length us, event | category | flops | bytes accessed | tf_op | source)
XLA Modules:
  0.0 270.0 jit_solution(3245265416472845831)
XLA Ops:
  0.0 3.3 %shard_map.47 = (bf16[5,256,128]{2,1,0:T(8,128)(2,1)}, bf16[5,256,128]{2,1,0:T(8,128)(2,1)}, bf16[5,256,128]{2,1,0:T(8,128)(2,1)}, bf16[5,256,128]{2,1,0:T(8,128...) custom-call(s32[1]{0:T(128)} %bitcast.here_ref, ...), custom_call_target="tpu_custom_call" | custom-call | tf_op jit(solution)/shard_map/pallas_call | solution.py:41
  3.3 0.4 collective-permute-start.12
  3.7 2.6 collective-permute-start.13
  6.3 0.5 collective-permute-start.14
  6.7 3.4 %shard_map.48 = (bf16[5,256,128]{2,1,0:T(8,128)(2,1)}, bf16[5,256,128]{2,1,0:T(8,128)(2,1)}, bf16[5,256,128]{2,1,0:T(8,128)(2,1)}, bf16[5,256,128]{2,1,0:T(8,128...) custom-call(s32[1]{0:T(128)} %bitcast.here_ref, ...), custom_call_target="tpu_custom_call" | custom-call | tf_op jit(solution)/shard_map/pallas_call | solution.py:41
  10.1 1.3 collective-permute-start.15
  11.5 2.2 collective-permute-start.16
  13.7 0.1 copy.9
  13.8 0.3 compare_reduce_fusion
  14.1 0.2 reduce_window_sum.18
  14.3 4.1 %collective-permute-done.12.refs_1_.refs_5_ = bf16[5,256,128]{2,1,0:T(8,128)(2,1)S(1)} collective-permute-done((bf16[5,256,128]{2,1,0:T(8,128)(2,1)}, bf16[5,256,128]{2,1,0:T(8,128)(2,1)S(1)}, u32[]{:S(2)}, u32[]{:S(2)}) %collective-permute-start.12) | collective-permute-done | bytes 327712 | tf_op jit(solution)/shard_map/ppermute | solution.py:215
  18.4 2.7 %collective-permute-start.17 = (bf16[5,256,128]{2,1,0:T(8,128)(2,1)}, bf16[5,256,128]{2,1,0:T(8,128)(2,1)S(1)}, u32[]{:S(2)}, u32[]{:S(2)}) collective-permute-start(bf16[5,256,128]{2,1,0:T(8,128)(2,1)} %get-tuple-element.61), channel_id=1, source_target_pairs={{0,3},{1,2},{2,1},{3,0},{4,7},{5,6},{6,5},{7,4},{8,11},{9,10},{10,... | collective-permute-start | bytes 983048 | tf_op jit(solution)/shard_map/ppermute | solution.py:215
  21.1 0.1 select_reduce_fusion.1
  21.3 0.7 copy.10.pick_ref
  21.9 6.9 %collective-permute-done.13.refs_2_.refs_6_ = bf16[5,256,128]{2,1,0:T(8,128)(2,1)S(1)} collective-permute-done((bf16[5,256,128]{2,1,0:T(8,128)(2,1)}, bf16[5,256,128]{2,1,0:T(8,128)(2,1)S(1)}, u32[]{:S(2)}, u32[]{:S(2)}) %collective-permute-start.13) | collective-permute-done | bytes 327712 | tf_op jit(solution)/shard_map/ppermute | solution.py:215
  28.9 21.9 %collective-permute-done.14.refs_3_.refs_7_ = bf16[5,256,128]{2,1,0:T(8,128)(2,1)S(1)} collective-permute-done((bf16[5,256,128]{2,1,0:T(8,128)(2,1)}, bf16[5,256,128]{2,1,0:T(8,128)(2,1)S(1)}, u32[]{:S(2)}, u32[]{:S(2)}) %collective-permute-start.14) | collective-permute-done | bytes 327712 | tf_op jit(solution)/shard_map/ppermute | solution.py:215
  50.7 6.2 %collective-permute-done.16.refs_6_.refs_10_ = bf16[5,256,128]{2,1,0:T(8,128)(2,1)S(1)} collective-permute-done((bf16[5,256,128]{2,1,0:T(8,128)(2,1)}, bf16[5,256,128]{2,1,0:T(8,128)(2,1)S(1)}, u32[]{:S(2)}, u32[]{:S(2)}) %collective-permute-start.16) | collective-permute-done | bytes 327712 | tf_op jit(solution)/shard_map/ppermute | solution.py:215
  56.9 6.4 %collective-permute-done.17.refs_7_.refs_11_ = bf16[5,256,128]{2,1,0:T(8,128)(2,1)S(1)} collective-permute-done((bf16[5,256,128]{2,1,0:T(8,128)(2,1)}, bf16[5,256,128]{2,1,0:T(8,128)(2,1)S(1)}, u32[]{:S(2)}, u32[]{:S(2)}) %collective-permute-start.17) | collective-permute-done | bytes 327712 | tf_op jit(solution)/shard_map/ppermute | solution.py:215
  63.4 0.7 copy-done.7
  64.1 6.2 %shard_map.51 = bf16[8,2,2,5,128,128]{5,4,3,2,1,0:T(8,128)(2,1)} custom-call(s32[8,2]{1,0:T(8,128)} %copy.10.pick_ref, bf16[5,256,128]{2,1,0:T(8,128)(2,1)} %get-tuple-element.54.refs_0_.refs_4_, bf16[5,256,128]{2,1,0:T(8,128)(2,1)} %copy-done, bf16[5,256,128]{2,1,0:T(8,128)(2,1)} %copy-done.1, bf16[5,256,128]{2,1,0:T(8,128)(2,1)} %copy-done.2, ...), custom_call_target="tpu_custom_call" | custom-call | tf_op jit(solution)/shard_map/pallas_call | solution.py:98
  70.3 5.2 %all-to-all-start.1 = ((bf16[8,2,2,5,128,128]{5,4,3,2,1,0:T(8,128)(2,1)}), bf16[8,2,2,5,128,128]{5,4,3,2,1,0:T(8,128)(2,1)}, u32[]{:S(2)}, u32[]{:S(2)}) async-start(bf16[8,2,2,5,128,128]{5,4,3,2,1,0:T(8,128)(2,1)} %shard_map.51), calls=%async_computation.1 | async-start | bytes 10485760 | tf_op jit(solution)/shard_map/all_to_all | solution.py:228
  75.5 3.0 %collective-permute-start.4 = (bf16[5,256,128]{2,1,0:T(8,128)(2,1)S(1)}, bf16[5,256,128]{2,1,0:T(8,128)(2,1)S(1)}, u32[]{:S(2)}, u32[]{:S(2)}) collective-permute-start(bf16[5,256,128]{2,1,0:T(8,128)(2,1)S(1)} %copy-done.22), channel_id=1, source_target_pairs={{0,2},{1,3},{2,0},{3,1},{4,6},{5,7},{6,4},{7,5},{8,10},{9,11},{10,... | collective-permute-start | bytes 983048 | tf_op jit(solution)/shard_map/ppermute | solution.py:215
  78.6 0.4 collective-permute-start.5
  79.0 1.1 collective-permute-start.6
  80.1 2.0 collective-permute-start.7
  82.1 7.9 %collective-permute-done.3.refs_1_.refs_5_ = bf16[5,256,128]{2,1,0:T(8,128)(2,1)S(1)} collective-permute-done((bf16[5,256,128]{2,1,0:T(8,128)(2,1)S(1)}, bf16[5,256,128]{2,1,0:T(8,128)(2,1)S(1)}, u32[]{:S(2)}, u32[]{:S(2)}) %collective-permute-start.3) | collective-permute-done | bytes 327712 | tf_op jit(solution)/shard_map/ppermute | solution.py:215
  90.0 0.9 collective-permute-start.8
  90.9 9.8 %collective-permute-done.4.refs_2_.refs_6_ = bf16[5,256,128]{2,1,0:T(8,128)(2,1)S(1)} collective-permute-done((bf16[5,256,128]{2,1,0:T(8,128)(2,1)S(1)}, bf16[5,256,128]{2,1,0:T(8,128)(2,1)S(1)}, u32[]{:S(2)}, u32[]{:S(2)}) %collective-permute-start.4) | collective-permute-done | bytes 327712 | tf_op jit(solution)/shard_map/ppermute | solution.py:215
  100.8 22.0 %collective-permute-done.5.refs_3_.refs_7_ = bf16[5,256,128]{2,1,0:T(8,128)(2,1)S(1)} collective-permute-done((bf16[5,256,128]{2,1,0:T(8,128)(2,1)S(1)}, bf16[5,256,128]{2,1,0:T(8,128)(2,1)S(1)}, u32[]{:S(2)}, u32[]{:S(2)}) %collective-permute-start.5) | collective-permute-done | bytes 327712 | tf_op jit(solution)/shard_map/ppermute | solution.py:215
  122.7 6.1 %collective-permute-done.7.refs_6_.refs_10_ = bf16[5,256,128]{2,1,0:T(8,128)(2,1)S(1)} collective-permute-done((bf16[5,256,128]{2,1,0:T(8,128)(2,1)S(1)}, bf16[5,256,128]{2,1,0:T(8,128)(2,1)S(1)}, u32[]{:S(2)}, u32[]{:S(2)}) %collective-permute-start.7) | collective-permute-done | bytes 327712 | tf_op jit(solution)/shard_map/ppermute | solution.py:215
  128.9 6.9 %collective-permute-done.8.refs_7_.refs_11_ = bf16[5,256,128]{2,1,0:T(8,128)(2,1)S(1)} collective-permute-done((bf16[5,256,128]{2,1,0:T(8,128)(2,1)S(1)}, bf16[5,256,128]{2,1,0:T(8,128)(2,1)S(1)}, u32[]{:S(2)}, u32[]{:S(2)}) %collective-permute-start.8) | collective-permute-done | bytes 327712 | tf_op jit(solution)/shard_map/ppermute | solution.py:215
  135.8 0.7 copy-done.11
  136.5 6.2 %shard_map.49 = bf16[8,2,2,5,128,128]{5,4,3,2,1,0:T(8,128)(2,1)} custom-call(s32[8,2]{1,0:T(8,128)} %copy.10.pick_ref, bf16[5,256,128]{2,1,0:T(8,128)(2,1)} %get-tuple-element.41.refs_0_.refs_4_, bf16[5,256,128]{2,1,0:T(8,128)(2,1)} %copy-done.5, bf16[5,256,128]{2,1,0:T(8,128)(2,1)} %copy-done.6, bf16[5,256,128]{2,1,0:T(8,128)(2,1)} %copy-done.8, ...), custom_call_target="tpu_custom_call" | custom-call | tf_op jit(solution)/shard_map/pallas_call | solution.py:98
  142.6 4.9 %all-to-all-start = ((bf16[8,2,2,5,128,128]{5,4,3,2,1,0:T(8,128)(2,1)}), bf16[8,2,2,5,128,128]{5,4,3,2,1,0:T(8,128)(2,1)}, u32[]{:S(2)}, u32[]{:S(2)}) async-start(bf16[8,2,2,5,128,128]{5,4,3,2,1,0:T(8,128)(2,1)} %shard_map.49), calls=%async_computation | async-start | bytes 10485760 | tf_op jit(solution)/shard_map/all_to_all | solution.py:228
  147.5 3.2 %shard_map.46 = (bf16[5,256,128]{2,1,0:T(8,128)(2,1)}, bf16[5,256,128]{2,1,0:T(8,128)(2,1)}, bf16[5,256,128]{2,1,0:T(8,128)(2,1)}, bf16[5,256,128]{2,1,0:T(8,128...) custom-call(s32[1]{0:T(128)} %bitcast.here_ref, ...), custom_call_target="tpu_custom_call" | custom-call | tf_op jit(solution)/shard_map/pallas_call | solution.py:41
  150.8 1.6 collective-permute-start.11
  152.5 2.7 %collective-permute-start.9 = (bf16[5,256,128]{2,1,0:T(8,128)(2,1)}, bf16[5,256,128]{2,1,0:T(8,128)(2,1)S(1)}, u32[]{:S(2)}, u32[]{:S(2)}) collective-permute-start(bf16[5,256,128]{2,1,0:T(8,128)(2,1)} %get-tuple-element.51), channel_id=1, source_target_pairs={{0,1},{1,0},{2,3},{3,2},{4,5},{5,4},{6,7},{7,6},{8,9},{9,8},{10,11... | collective-permute-start | bytes 983048 | tf_op jit(solution)/shard_map/ppermute | solution.py:215
  155.2 3.0 %collective-permute-start.1 = (bf16[5,256,128]{2,1,0:T(8,128)(2,1)}, bf16[5,256,128]{2,1,0:T(8,128)(2,1)S(1)}, u32[]{:S(2)}, u32[]{:S(2)}) collective-permute-start(bf16[5,256,128]{2,1,0:T(8,128)(2,1)} %get-tuple-element.39), channel_id=1, source_target_pairs={{0,2},{1,3},{2,0},{3,1},{4,6},{5,7},{6,4},{7,5},{8,10},{9,11},{10,... | collective-permute-start | bytes 983048 | tf_op jit(solution)/shard_map/ppermute | solution.py:215
  158.3 0.1 fusion
  158.5 0.2 reduce_window_sum.17
  158.7 0.1 select_n.76
  158.8 0.3 select_reduce_fusion
  159.3 0.1 broadcast_in_dim.65
  159.4 0.6 gather_fusion
  160.0 13.3 %collective-permute-done.10.refs_2_ = bf16[5,256,128]{2,1,0:T(8,128)(2,1)S(1)} collective-permute-done((bf16[5,256,128]{2,1,0:T(8,128)(2,1)}, bf16[5,256,128]{2,1,0:T(8,128)(2,1)S(1)}, u32[]{:S(2)}, u32[]{:S(2)}) %collective-permute-start.10) | collective-permute-done | bytes 327712 | tf_op jit(solution)/shard_map/ppermute | solution.py:215
  173.2 1.6 collective-permute-start.2
  174.8 0.7 broadcast_select_fusion.place_ref
  175.5 6.9 %collective-permute-done.11.refs_3_ = bf16[5,256,128]{2,1,0:T(8,128)(2,1)S(1)} collective-permute-done((bf16[5,256,128]{2,1,0:T(8,128)(2,1)}, bf16[5,256,128]{2,1,0:T(8,128)(2,1)S(1)}, u32[]{:S(2)}, u32[]{:S(2)}) %collective-permute-start.11) | collective-permute-done | bytes 327712 | tf_op jit(solution)/shard_map/ppermute | solution.py:215
  182.4 0.7 copy-done.27
  183.1 0.2 copy-done.28
  183.3 20.1 %shard_map.52 = (bf16[5,256,128]{2,1,0:T(8,128)(2,1)}, bf16[5,256,128]{2,1,0:T(8,128)(2,1)}, bf16[5,256,128]{2,1,0:T(8,128)(2,1)}, bf16[5,256,128]{2,1,0:T(8,128)(2,1)}) custom-call(s32[8,10]{1,0:T(8,128)} %broadcast_select_fusion.place_ref, bf16[5,256,128]{2,1,0:T(8,128)(2,1)} %get-tuple-element.50.refs_0_, bf16[5,256,128]{2,1,0:T(8,128)(2,1)} %copy-done.28, ...), custom_call_target="tpu_custom_call" | custom-call | flops 3355443200 | bytes 10485760 | tf_op jit(solution)/shard_map/pallas_call | solution.py:156
  203.4 1.7 collective-permute-start.21
  205.2 1.7 collective-permute-start.23
  206.9 3.4 %collective-permute-done.2.refs_3_ = bf16[5,256,128]{2,1,0:T(8,128)(2,1)S(1)} collective-permute-done((bf16[5,256,128]{2,1,0:T(8,128)(2,1)}, bf16[5,256,128]{2,1,0:T(8,128)(2,1)S(1)}, u32[]{:S(2)}, u32[]{:S(2)}) %collective-permute-start.2) | collective-permute-done | bytes 327712 | tf_op jit(solution)/shard_map/ppermute | solution.py:215
  210.3 0.7 copy-done.29
  211.0 20.1 %shard_map.50 = (bf16[5,256,128]{2,1,0:T(8,128)(2,1)}, bf16[5,256,128]{2,1,0:T(8,128)(2,1)}, bf16[5,256,128]{2,1,0:T(8,128)(2,1)}, bf16[5,256,128]{2,1,0:T(8,128)(2,1)}) custom-call(s32[8,10]{1,0:T(8,128)} %broadcast_select_fusion.place_ref, bf16[5,256,128]{2,1,0:T(8,128)(2,1)} %get-tuple-element.37.refs_0_, bf16[5,256,128]{2,1,0:T(8,128)(2,1)} %copy-done.19, ...), custom_call_target="tpu_custom_call" | custom-call | flops 3355443200 | bytes 10485760 | tf_op jit(solution)/shard_map/pallas_call | solution.py:156
  231.2 1.9 collective-permute-start.20
  233.1 1.6 collective-permute-start.22
  234.6 3.9 %collective-permute-done.23.refs_7_ = bf16[5,256,128]{2,1,0:T(8,128)(2,1)S(1)} collective-permute-done((bf16[5,256,128]{2,1,0:T(8,128)(2,1)}, bf16[5,256,128]{2,1,0:T(8,128)(2,1)S(1)}, u32[]{:S(2)}, u32[]{:S(2)}) %collective-permute-start.23) | collective-permute-done | bytes 327712 | tf_op jit(solution)/shard_map/ppermute | solution.py:215
  238.6 3.4 %collective-permute-done.18.refs_2_ = bf16[5,256,128]{2,1,0:T(8,128)(2,1)S(1)} collective-permute-done((bf16[5,256,128]{2,1,0:T(8,128)(2,1)}, bf16[5,256,128]{2,1,0:T(8,128)(2,1)S(1)}, u32[]{:S(2)}, u32[]{:S(2)}) %collective-permute-start.18) | collective-permute-done | bytes 327712 | tf_op jit(solution)/shard_map/ppermute | solution.py:215
  242.0 15.6 %collective-permute-done.20.refs_4_ = bf16[5,256,128]{2,1,0:T(8,128)(2,1)S(1)} collective-permute-done((bf16[5,256,128]{2,1,0:T(8,128)(2,1)}, bf16[5,256,128]{2,1,0:T(8,128)(2,1)S(1)}, u32[]{:S(2)}, u32[]{:S(2)}) %collective-permute-start.20) | collective-permute-done | bytes 327712 | tf_op jit(solution)/shard_map/ppermute | solution.py:215
  257.6 8.4 %collective-permute-done.22.refs_6_ = bf16[5,256,128]{2,1,0:T(8,128)(2,1)S(1)} collective-permute-done((bf16[5,256,128]{2,1,0:T(8,128)(2,1)}, bf16[5,256,128]{2,1,0:T(8,128)(2,1)S(1)}, u32[]{:S(2)}, u32[]{:S(2)}) %collective-permute-start.22) | collective-permute-done | bytes 327712 | tf_op jit(solution)/shard_map/ppermute | solution.py:215
  266.0 0.7 copy-done.17
  266.7 3.3 %shard_map.53 = bf16[256,40,128]{2,1,0:T(8,128)(2,1)} custom-call(s32[1]{0:T(128)} %bitcast.here_ref, bf16[5,256,128]{2,1,0:T(8,128)(2,1)} %get-tuple-element.49.refs_0_, bf16[5,256,128]{2,1,0:T(8,128)(2,1)} %get-tuple-element.62.refs_1_, bf16[5,256,128]{2,1,0:T(8,128)(2,1)} %copy-done.15, bf16[5,256,128]{2,1,0:T(8,128)(2,1)} %copy-done.12, ...), custom_call_target="tpu_custom_call" | custom-call | tf_op jit(solution)/shard_map/pallas_call | solution.py:70
  (83 shorter events, 0.8 us)
Async XLA Ops:
  0.0 13.7 %copy-start.18 = (s32[64,10]{0,1:T(8,128)S(1)}, s32[64,10]{0,1:T(8,128)}, u32[]{:S(2)}) copy-start(s32[64,10]{0,1:T(8,128)} %param.7) | copy-start | bytes 7684
  3.3 15.1 %collective-permute-start.12 = (bf16[5,256,128]{2,1,0:T(8,128)(2,1)}, bf16[5,256,128]{2,1,0:T(8,128)(2,1)S(1)}, u32[]{:S(2)}, u32[]{:S(2)}) collective-permute-start(bf16[5,256,128]{2,1,0:T(8,128)(2,1)} %get-tuple-element.55), channel_id=1, source_target_pairs={{0,1},{1,0},{2,3},{3,2},{4,5},{5,4},{6,7},{7,6},{8,9},{9,8},{10,11... | collective-permute-start | bytes 983048 | tf_op jit(solution)/shard_map/ppermute | solution.py:215
  3.7 25.1 %collective-permute-start.13 = (bf16[5,256,128]{2,1,0:T(8,128)(2,1)}, bf16[5,256,128]{2,1,0:T(8,128)(2,1)S(1)}, u32[]{:S(2)}, u32[]{:S(2)}) collective-permute-start(bf16[5,256,128]{2,1,0:T(8,128)(2,1)} %get-tuple-element.56), channel_id=1, source_target_pairs={{0,2},{1,3},{2,0},{3,1},{4,6},{5,7},{6,4},{7,5},{8,10},{9,11},{10,... | collective-permute-start | bytes 983048 | tf_op jit(solution)/shard_map/ppermute | solution.py:215
  6.3 44.4 %collective-permute-start.14 = (bf16[5,256,128]{2,1,0:T(8,128)(2,1)}, bf16[5,256,128]{2,1,0:T(8,128)(2,1)S(1)}, u32[]{:S(2)}, u32[]{:S(2)}) collective-permute-start(bf16[5,256,128]{2,1,0:T(8,128)(2,1)} %get-tuple-element.57), channel_id=1, source_target_pairs={{0,3},{1,2},{2,1},{3,0},{4,7},{5,6},{6,5},{7,4},{8,11},{9,10},{10,... | collective-permute-start | bytes 983048 | tf_op jit(solution)/shard_map/ppermute | solution.py:215
  10.1 40.6 %collective-permute-start.15 = (bf16[5,256,128]{2,1,0:T(8,128)(2,1)}, bf16[5,256,128]{2,1,0:T(8,128)(2,1)S(1)}, u32[]{:S(2)}, u32[]{:S(2)}) collective-permute-start(bf16[5,256,128]{2,1,0:T(8,128)(2,1)} %get-tuple-element.59), channel_id=1, source_target_pairs={{0,1},{1,0},{2,3},{3,2},{4,5},{5,4},{6,7},{7,6},{8,9},{9,8},{10,11... | collective-permute-start | bytes 983048 | tf_op jit(solution)/shard_map/ppermute | solution.py:215
  11.5 45.5 %collective-permute-start.16 = (bf16[5,256,128]{2,1,0:T(8,128)(2,1)}, bf16[5,256,128]{2,1,0:T(8,128)(2,1)S(1)}, u32[]{:S(2)}, u32[]{:S(2)}) collective-permute-start(bf16[5,256,128]{2,1,0:T(8,128)(2,1)} %get-tuple-element.60), channel_id=1, source_target_pairs={{0,2},{1,3},{2,0},{3,1},{4,6},{5,7},{6,4},{7,5},{8,10},{9,11},{10,... | collective-permute-start | bytes 983048 | tf_op jit(solution)/shard_map/ppermute | solution.py:215
  18.4 45.0 %copy-start = (bf16[5,256,128]{2,1,0:T(8,128)(2,1)}, bf16[5,256,128]{2,1,0:T(8,128)(2,1)S(1)}, u32[]{:S(2)}) copy-start(bf16[5,256,128]{2,1,0:T(8,128)(2,1)S(1)} %collective-permute-done.12.refs_1_.refs_5_) | copy-start | bytes 983044
  18.4 44.9 %collective-permute-start.17 = (bf16[5,256,128]{2,1,0:T(8,128)(2,1)}, bf16[5,256,128]{2,1,0:T(8,128)(2,1)S(1)}, u32[]{:S(2)}, u32[]{:S(2)}) collective-permute-start(bf16[5,256,128]{2,1,0:T(8,128)(2,1)} %get-tuple-element.61), channel_id=1, source_target_pairs={{0,3},{1,2},{2,1},{3,0},{4,7},{5,6},{6,5},{7,4},{8,11},{9,10},{10,... | collective-permute-start | bytes 983048 | tf_op jit(solution)/shard_map/ppermute | solution.py:215
  28.9 34.5 %copy-start.1 = (bf16[5,256,128]{2,1,0:T(8,128)(2,1)}, bf16[5,256,128]{2,1,0:T(8,128)(2,1)S(1)}, u32[]{:S(2)}) copy-start(bf16[5,256,128]{2,1,0:T(8,128)(2,1)S(1)} %collective-permute-done.13.refs_2_.refs_6_) | copy-start | bytes 983044
  50.7 12.6 %copy-start.2 = (bf16[5,256,128]{2,1,0:T(8,128)(2,1)}, bf16[5,256,128]{2,1,0:T(8,128)(2,1)S(1)}, u32[]{:S(2)}) copy-start(bf16[5,256,128]{2,1,0:T(8,128)(2,1)S(1)} %collective-permute-done.14.refs_3_.refs_7_) | copy-start | bytes 983044
  50.7 12.6 %copy-start.3 = (bf16[5,256,128]{2,1,0:T(8,128)(2,1)}, bf16[5,256,128]{2,1,0:T(8,128)(2,1)S(1)}, u32[]{:S(2)}) copy-start(bf16[5,256,128]{2,1,0:T(8,128)(2,1)S(1)} %collective-permute-done.15.refs_5_.refs_9_) | copy-start | bytes 983044
  56.9 6.4 %copy-start.4 = (bf16[5,256,128]{2,1,0:T(8,128)(2,1)}, bf16[5,256,128]{2,1,0:T(8,128)(2,1)S(1)}, u32[]{:S(2)}) copy-start(bf16[5,256,128]{2,1,0:T(8,128)(2,1)S(1)} %collective-permute-done.16.refs_6_.refs_10_) | copy-start | bytes 983044
  63.3 0.8 copy-start.7
  70.3 5.3 %copy-start.24 = (bf16[5,256,128]{2,1,0:T(8,128)(2,1)S(1)}, bf16[5,256,128]{2,1,0:T(8,128)(2,1)}, u32[]{:S(2)}) copy-start(bf16[5,256,128]{2,1,0:T(8,128)(2,1)} %get-tuple-element.42) | copy-start | bytes 983044
  70.3 5.3 %copy-start.22 = (bf16[5,256,128]{2,1,0:T(8,128)(2,1)S(1)}, bf16[5,256,128]{2,1,0:T(8,128)(2,1)}, u32[]{:S(2)}) copy-start(bf16[5,256,128]{2,1,0:T(8,128)(2,1)} %get-tuple-element.43) | copy-start | bytes 983044
  70.3 8.3 %copy-start.20 = (bf16[5,256,128]{2,1,0:T(8,128)(2,1)S(1)}, bf16[5,256,128]{2,1,0:T(8,128)(2,1)}, u32[]{:S(2)}) copy-start(bf16[5,256,128]{2,1,0:T(8,128)(2,1)} %get-tuple-element.44) | copy-start | bytes 983044
  70.3 9.8 %copy-start.25 = (bf16[5,256,128]{2,1,0:T(8,128)(2,1)S(1)}, bf16[5,256,128]{2,1,0:T(8,128)(2,1)}, u32[]{:S(2)}) copy-start(bf16[5,256,128]{2,1,0:T(8,128)(2,1)} %get-tuple-element.47) | copy-start | bytes 983044
  70.3 19.7 %copy-start.23 = (bf16[5,256,128]{2,1,0:T(8,128)(2,1)S(1)}, bf16[5,256,128]{2,1,0:T(8,128)(2,1)}, u32[]{:S(2)}) copy-start(bf16[5,256,128]{2,1,0:T(8,128)(2,1)} %get-tuple-element.48) | copy-start | bytes 983044
  70.3 72.3 %all-to-all-start.1 = ((bf16[8,2,2,5,128,128]{5,4,3,2,1,0:T(8,128)(2,1)}), bf16[8,2,2,5,128,128]{5,4,3,2,1,0:T(8,128)(2,1)}, u32[]{:S(2)}, u32[]{:S(2)}) async-start(bf16[8,2,2,5,128,128]{5,4,3,2,1,0:T(8,128)(2,1)} %shard_map.51), calls=%async_computation.1 | async-start | bytes 10485760 | tf_op jit(solution)/shard_map/all_to_all | solution.py:228
  75.5 14.5 %collective-permute-start.3 = (bf16[5,256,128]{2,1,0:T(8,128)(2,1)S(1)}, bf16[5,256,128]{2,1,0:T(8,128)(2,1)S(1)}, u32[]{:S(2)}, u32[]{:S(2)}) collective-permute-start(bf16[5,256,128]{2,1,0:T(8,128)(2,1)S(1)} %copy-done.24), channel_id=1, source_target_pairs={{0,1},{1,0},{2,3},{3,2},{4,5},{5,4},{6,7},{7,6},{8,9},{9,8},{10,11... | collective-permute-start | bytes 983048 | tf_op jit(solution)/shard_map/ppermute | solution.py:215
  75.5 25.2 %collective-permute-start.4 = (bf16[5,256,128]{2,1,0:T(8,128)(2,1)S(1)}, bf16[5,256,128]{2,1,0:T(8,128)(2,1)S(1)}, u32[]{:S(2)}, u32[]{:S(2)}) collective-permute-start(bf16[5,256,128]{2,1,0:T(8,128)(2,1)S(1)} %copy-done.22), channel_id=1, source_target_pairs={{0,2},{1,3},{2,0},{3,1},{4,6},{5,7},{6,4},{7,5},{8,10},{9,11},{10,... | collective-permute-start | bytes 983048 | tf_op jit(solution)/shard_map/ppermute | solution.py:215
  78.6 44.2 %collective-permute-start.5 = (bf16[5,256,128]{2,1,0:T(8,128)(2,1)S(1)}, bf16[5,256,128]{2,1,0:T(8,128)(2,1)S(1)}, u32[]{:S(2)}, u32[]{:S(2)}) collective-permute-start(bf16[5,256,128]{2,1,0:T(8,128)(2,1)S(1)} %copy-done.20), channel_id=1, source_target_pairs={{0,3},{1,2},{2,1},{3,0},{4,7},{5,6},{6,5},{7,4},{8,11},{9,10},{10,... | collective-permute-start | bytes 983048 | tf_op jit(solution)/shard_map/ppermute | solution.py:215
  79.0 43.7 %collective-permute-start.6 = (bf16[5,256,128]{2,1,0:T(8,128)(2,1)}, bf16[5,256,128]{2,1,0:T(8,128)(2,1)S(1)}, u32[]{:S(2)}, u32[]{:S(2)}) collective-permute-start(bf16[5,256,128]{2,1,0:T(8,128)(2,1)} %get-tuple-element.46), channel_id=1, source_target_pairs={{0,1},{1,0},{2,3},{3,2},{4,5},{5,4},{6,7},{7,6},{8,9},{9,8},{10,11... | collective-permute-start | bytes 983048 | tf_op jit(solution)/shard_map/ppermute | solution.py:215
  80.1 48.7 %collective-permute-start.7 = (bf16[5,256,128]{2,1,0:T(8,128)(2,1)S(1)}, bf16[5,256,128]{2,1,0:T(8,128)(2,1)S(1)}, u32[]{:S(2)}, u32[]{:S(2)}) collective-permute-start(bf16[5,256,128]{2,1,0:T(8,128)(2,1)S(1)} %copy-done.25), channel_id=1, source_target_pairs={{0,2},{1,3},{2,0},{3,1},{4,6},{5,7},{6,4},{7,5},{8,10},{9,11},{10,... | collective-permute-start | bytes 983048 | tf_op jit(solution)/shard_map/ppermute | solution.py:215
  90.0 45.7 %copy-start.5 = (bf16[5,256,128]{2,1,0:T(8,128)(2,1)}, bf16[5,256,128]{2,1,0:T(8,128)(2,1)S(1)}, u32[]{:S(2)}) copy-start(bf16[5,256,128]{2,1,0:T(8,128)(2,1)S(1)} %collective-permute-done.3.refs_1_.refs_5_) | copy-start | bytes 983044
  90.0 45.7 %collective-permute-start.8 = (bf16[5,256,128]{2,1,0:T(8,128)(2,1)S(1)}, bf16[5,256,128]{2,1,0:T(8,128)(2,1)S(1)}, u32[]{:S(2)}, u32[]{:S(2)}) collective-permute-start(bf16[5,256,128]{2,1,0:T(8,128)(2,1)S(1)} %copy-done.23), channel_id=1, source_target_pairs={{0,3},{1,2},{2,1},{3,0},{4,7},{5,6},{6,5},{7,4},{8,11},{9,10},{10,... | collective-permute-start | bytes 983048 | tf_op jit(solution)/shard_map/ppermute | solution.py:215
  100.8 35.0 %copy-start.6 = (bf16[5,256,128]{2,1,0:T(8,128)(2,1)}, bf16[5,256,128]{2,1,0:T(8,128)(2,1)S(1)}, u32[]{:S(2)}) copy-start(bf16[5,256,128]{2,1,0:T(8,128)(2,1)S(1)} %collective-permute-done.4.refs_2_.refs_6_) | copy-start | bytes 983044
  122.7 13.0 %copy-start.8 = (bf16[5,256,128]{2,1,0:T(8,128)(2,1)}, bf16[5,256,128]{2,1,0:T(8,128)(2,1)S(1)}, u32[]{:S(2)}) copy-start(bf16[5,256,128]{2,1,0:T(8,128)(2,1)S(1)} %collective-permute-done.5.refs_3_.refs_7_) | copy-start | bytes 983044
  122.7 13.0 %copy-start.9 = (bf16[5,256,128]{2,1,0:T(8,128)(2,1)}, bf16[5,256,128]{2,1,0:T(8,128)(2,1)S(1)}, u32[]{:S(2)}) copy-start(bf16[5,256,128]{2,1,0:T(8,128)(2,1)S(1)} %collective-permute-done.6.refs_5_.refs_9_) | copy-start | bytes 983044
  128.9 6.9 %copy-start.10 = (bf16[5,256,128]{2,1,0:T(8,128)(2,1)}, bf16[5,256,128]{2,1,0:T(8,128)(2,1)S(1)}, u32[]{:S(2)}) copy-start(bf16[5,256,128]{2,1,0:T(8,128)(2,1)S(1)} %collective-permute-done.7.refs_6_.refs_10_) | copy-start | bytes 983044
  135.7 0.7 copy-start.11
  142.6 67.7 %all-to-all-start = ((bf16[8,2,2,5,128,128]{5,4,3,2,1,0:T(8,128)(2,1)}), bf16[8,2,2,5,128,128]{5,4,3,2,1,0:T(8,128)(2,1)}, u32[]{:S(2)}, u32[]{:S(2)}) async-start(bf16[8,2,2,5,128,128]{5,4,3,2,1,0:T(8,128)(2,1)} %shard_map.49), calls=%async_computation | async-start | bytes 10485760 | tf_op jit(solution)/shard_map/all_to_all | solution.py:228
  150.8 22.5 %collective-permute-start.10 = (bf16[5,256,128]{2,1,0:T(8,128)(2,1)}, bf16[5,256,128]{2,1,0:T(8,128)(2,1)S(1)}, u32[]{:S(2)}, u32[]{:S(2)}) collective-permute-start(bf16[5,256,128]{2,1,0:T(8,128)(2,1)} %get-tuple-element.52), channel_id=1, source_target_pairs={{0,2},{1,3},{2,0},{3,1},{4,6},{5,7},{6,4},{7,5},{8,10},{9,11},{10,... | collective-permute-start | bytes 983048 | tf_op jit(solution)/shard_map/ppermute | solution.py:215
  150.8 31.5 %collective-permute-start.11 = (bf16[5,256,128]{2,1,0:T(8,128)(2,1)}, bf16[5,256,128]{2,1,0:T(8,128)(2,1)S(1)}, u32[]{:S(2)}, u32[]{:S(2)}) collective-permute-start(bf16[5,256,128]{2,1,0:T(8,128)(2,1)} %get-tuple-element.53), channel_id=1, source_target_pairs={{0,3},{1,2},{2,1},{3,0},{4,7},{5,6},{6,5},{7,4},{8,11},{9,10},{10,... | collective-permute-start | bytes 983048 | tf_op jit(solution)/shard_map/ppermute | solution.py:215
  152.5 29.9 %collective-permute-start.9 = (bf16[5,256,128]{2,1,0:T(8,128)(2,1)}, bf16[5,256,128]{2,1,0:T(8,128)(2,1)S(1)}, u32[]{:S(2)}, u32[]{:S(2)}) collective-permute-start(bf16[5,256,128]{2,1,0:T(8,128)(2,1)} %get-tuple-element.51), channel_id=1, source_target_pairs={{0,1},{1,0},{2,3},{3,2},{4,5},{5,4},{6,7},{7,6},{8,9},{9,8},{10,11... | collective-permute-start | bytes 983048 | tf_op jit(solution)/shard_map/ppermute | solution.py:215
  155.2 50.0 %collective-permute-start = (bf16[5,256,128]{2,1,0:T(8,128)(2,1)}, bf16[5,256,128]{2,1,0:T(8,128)(2,1)S(1)}, u32[]{:S(2)}, u32[]{:S(2)}) collective-permute-start(bf16[5,256,128]{2,1,0:T(8,128)(2,1)} %get-tuple-element.38), channel_id=1, source_target_pairs={{0,1},{1,0},{2,3},{3,2},{4,5},{5,4},{6,7},{7,6},{8,9},{9,8},{10,11... | collective-permute-start | bytes 983048 | tf_op jit(solution)/shard_map/ppermute | solution.py:215
  155.2 51.7 %collective-permute-start.1 = (bf16[5,256,128]{2,1,0:T(8,128)(2,1)}, bf16[5,256,128]{2,1,0:T(8,128)(2,1)S(1)}, u32[]{:S(2)}, u32[]{:S(2)}) collective-permute-start(bf16[5,256,128]{2,1,0:T(8,128)(2,1)} %get-tuple-element.39), channel_id=1, source_target_pairs={{0,2},{1,3},{2,0},{3,1},{4,6},{5,7},{6,4},{7,5},{8,10},{9,11},{10,... | collective-permute-start | bytes 983048 | tf_op jit(solution)/shard_map/ppermute | solution.py:215
  173.2 9.1 %copy-start.26 = (bf16[5,256,128]{2,1,0:T(8,128)(2,1)}, bf16[5,256,128]{2,1,0:T(8,128)(2,1)S(1)}, u32[]{:S(2)}) copy-start(bf16[5,256,128]{2,1,0:T(8,128)(2,1)S(1)} %collective-permute-done.10.refs_2_) | copy-start | bytes 983044
  173.2 37.0 %collective-permute-start.2 = (bf16[5,256,128]{2,1,0:T(8,128)(2,1)}, bf16[5,256,128]{2,1,0:T(8,128)(2,1)S(1)}, u32[]{:S(2)}, u32[]{:S(2)}) collective-permute-start(bf16[5,256,128]{2,1,0:T(8,128)(2,1)} %get-tuple-element.40), channel_id=1, source_target_pairs={{0,3},{1,2},{2,1},{3,0},{4,7},{5,6},{6,5},{7,4},{8,11},{9,10},{10,... | collective-permute-start | bytes 983048 | tf_op jit(solution)/shard_map/ppermute | solution.py:215
  182.3 0.7 copy-start.27
  182.4 0.9 copy-start.28
  203.3 29.7 %collective-permute-start.19 = (bf16[5,256,128]{2,1,0:T(8,128)(2,1)}, bf16[5,256,128]{2,1,0:T(8,128)(2,1)S(1)}, u32[]{:S(2)}, u32[]{:S(2)}) collective-permute-start(bf16[5,256,128]{2,1,0:T(8,128)(2,1)} %get-tuple-element.64), channel_id=1, source_target_pairs={{0,1},{1,0},{2,3},{3,2},{4,5},{5,4},{6,7},{7,6},{8,9},{9,8},{10,11... | collective-permute-start | bytes 983048 | tf_op jit(solution)/shard_map/ppermute | solution.py:215
  203.4 31.2 %collective-permute-start.21 = (bf16[5,256,128]{2,1,0:T(8,128)(2,1)}, bf16[5,256,128]{2,1,0:T(8,128)(2,1)S(1)}, u32[]{:S(2)}, u32[]{:S(2)}) collective-permute-start(bf16[5,256,128]{2,1,0:T(8,128)(2,1)} %get-tuple-element.66), channel_id=1, source_target_pairs={{0,2},{1,3},{2,0},{3,1},{4,6},{5,7},{6,4},{7,5},{8,10},{9,11},{10,... | collective-permute-start | bytes 983048 | tf_op jit(solution)/shard_map/ppermute | solution.py:215
  205.2 5.1 %copy-start.19 = (bf16[5,256,128]{2,1,0:T(8,128)(2,1)}, bf16[5,256,128]{2,1,0:T(8,128)(2,1)S(1)}, u32[]{:S(2)}) copy-start(bf16[5,256,128]{2,1,0:T(8,128)(2,1)S(1)} %collective-permute-done.refs_1_) | copy-start | bytes 983044
  205.2 33.4 %collective-permute-start.23 = (bf16[5,256,128]{2,1,0:T(8,128)(2,1)}, bf16[5,256,128]{2,1,0:T(8,128)(2,1)S(1)}, u32[]{:S(2)}, u32[]{:S(2)}) collective-permute-start(bf16[5,256,128]{2,1,0:T(8,128)(2,1)} %get-tuple-element.68), channel_id=1, source_target_pairs={{0,3},{1,2},{2,1},{3,0},{4,7},{5,6},{6,5},{7,4},{8,11},{9,10},{10,... | collective-permute-start | bytes 983048 | tf_op jit(solution)/shard_map/ppermute | solution.py:215
  206.9 3.4 %copy-start.21 = (bf16[5,256,128]{2,1,0:T(8,128)(2,1)}, bf16[5,256,128]{2,1,0:T(8,128)(2,1)S(1)}, u32[]{:S(2)}) copy-start(bf16[5,256,128]{2,1,0:T(8,128)(2,1)S(1)} %collective-permute-done.1.refs_2_) | copy-start | bytes 983044
  210.3 0.7 copy-start.29
  231.1 10.9 %collective-permute-start.18 = (bf16[5,256,128]{2,1,0:T(8,128)(2,1)}, bf16[5,256,128]{2,1,0:T(8,128)(2,1)S(1)}, u32[]{:S(2)}, u32[]{:S(2)}) collective-permute-start(bf16[5,256,128]{2,1,0:T(8,128)(2,1)} %get-tuple-element.63), channel_id=1, source_target_pairs={{0,1},{1,0},{2,3},{3,2},{4,5},{5,4},{6,7},{7,6},{8,9},{9,8},{10,11... | collective-permute-start | bytes 983048 | tf_op jit(solution)/shard_map/ppermute | solution.py:215
  231.2 26.4 %collective-permute-start.20 = (bf16[5,256,128]{2,1,0:T(8,128)(2,1)}, bf16[5,256,128]{2,1,0:T(8,128)(2,1)S(1)}, u32[]{:S(2)}, u32[]{:S(2)}) collective-permute-start(bf16[5,256,128]{2,1,0:T(8,128)(2,1)} %get-tuple-element.65), channel_id=1, source_target_pairs={{0,2},{1,3},{2,0},{3,1},{4,6},{5,7},{6,4},{7,5},{8,10},{9,11},{10,... | collective-permute-start | bytes 983048 | tf_op jit(solution)/shard_map/ppermute | solution.py:215
  233.1 32.9 %copy-start.12 = (bf16[5,256,128]{2,1,0:T(8,128)(2,1)}, bf16[5,256,128]{2,1,0:T(8,128)(2,1)S(1)}, u32[]{:S(2)}) copy-start(bf16[5,256,128]{2,1,0:T(8,128)(2,1)S(1)} %collective-permute-done.19.refs_3_) | copy-start | bytes 983044
  233.1 32.9 %collective-permute-start.22 = (bf16[5,256,128]{2,1,0:T(8,128)(2,1)}, bf16[5,256,128]{2,1,0:T(8,128)(2,1)S(1)}, u32[]{:S(2)}, u32[]{:S(2)}) collective-permute-start(bf16[5,256,128]{2,1,0:T(8,128)(2,1)} %get-tuple-element.67), channel_id=1, source_target_pairs={{0,3},{1,2},{2,1},{3,0},{4,7},{5,6},{6,5},{7,4},{8,11},{9,10},{10,... | collective-permute-start | bytes 983048 | tf_op jit(solution)/shard_map/ppermute | solution.py:215
  234.6 31.4 %copy-start.13 = (bf16[5,256,128]{2,1,0:T(8,128)(2,1)}, bf16[5,256,128]{2,1,0:T(8,128)(2,1)S(1)}, u32[]{:S(2)}) copy-start(bf16[5,256,128]{2,1,0:T(8,128)(2,1)S(1)} %collective-permute-done.21.refs_5_) | copy-start | bytes 983044
  238.6 27.4 %copy-start.14 = (bf16[5,256,128]{2,1,0:T(8,128)(2,1)}, bf16[5,256,128]{2,1,0:T(8,128)(2,1)S(1)}, u32[]{:S(2)}) copy-start(bf16[5,256,128]{2,1,0:T(8,128)(2,1)S(1)} %collective-permute-done.23.refs_7_) | copy-start | bytes 983044
  242.0 24.0 %copy-start.15 = (bf16[5,256,128]{2,1,0:T(8,128)(2,1)}, bf16[5,256,128]{2,1,0:T(8,128)(2,1)S(1)}, u32[]{:S(2)}) copy-start(bf16[5,256,128]{2,1,0:T(8,128)(2,1)S(1)} %collective-permute-done.18.refs_2_) | copy-start | bytes 983044
  257.6 8.4 %copy-start.16 = (bf16[5,256,128]{2,1,0:T(8,128)(2,1)}, bf16[5,256,128]{2,1,0:T(8,128)(2,1)S(1)}, u32[]{:S(2)}) copy-start(bf16[5,256,128]{2,1,0:T(8,128)(2,1)S(1)} %collective-permute-done.20.refs_4_) | copy-start | bytes 983044
  266.0 0.7 copy-start.17

commit v3 on v2

--- a/solution.py
+++ b/solution.py
@@ -80,34 +80,46 @@
     )(here, *flat)
 
 
-def pick_tiles(keys, values, picks, groups):
-    count, rows, size = keys[0].shape
+def pick_tiles(pieces, picks, kind, buffer):
+    count, rows, size = pieces[0].shape
+    readers = picks.shape[0]
     tiles = rows // TILE
-    partners = len(keys)
+    partners = len(pieces)
 
     def kernel(pick_ref, *refs):
-        ins, outs, pools = refs[: 2 * partners], refs[2 * partners : -2], refs[-2:]
-        for kind, pool in enumerate(pools):
-            for k in range(partners):
-                pool[k * tiles : (k + 1) * tiles] = ins[kind * partners + k][0].reshape(tiles, TILE, size)
-            for group, out in zip(groups, outs):
-                for at, reader in enumerate(group):
-                    for slot in range(CAP):
-                        out[at, kind, slot, 0] = pool[pick_ref[reader, slot]]
-
+        out, pool, sems = refs[-3:]
+        for k in range(partners):
+            for tile in range(tiles):
+                pool[k * tiles + tile] = refs[k][:, tile * TILE : (tile + 1) * TILE, :]
+        copies = [
+            pltpu.make_async_copy(
+                pool.at[pick_ref[reader, slot]], out.at[reader, kind, slot], sems.at[reader * CAP + slot]
+            )
+            for reader in range(readers)
+            for slot in range(CAP)
+        ]
+        for copy in copies:
+            copy.start()
+        for copy in copies:
+            copy.wait()
+
+    held = [] if buffer is None else [buffer]
     return pl.pallas_call(
         kernel,
         grid_spec=pltpu.PrefetchScalarGridSpec(
             num_scalar_prefetch=1,
-            grid=(count,),
-            in_specs=[pl.BlockSpec((1, rows, size), lambda h, _: (h, 0, 0))] * (2 * partners),
-            out_specs=[
-                pl.BlockSpec((len(group), 2, CAP, 1, TILE, size), lambda h, _: (0, 0, 0, h, 0, 0)) for group in groups
+            grid=(1,),
+            in_specs=[pl.BlockSpec((count, rows, size), lambda i, _: (0, 0, 0))] * partners
+            + [pl.BlockSpec(memory_space=pl.ANY)] * len(held),
+            out_specs=pl.BlockSpec(memory_space=pl.ANY),
+            scratch_shapes=[
+                pltpu.VMEM((partners * tiles, count, TILE, size), BF16),
+                pltpu.SemaphoreType.DMA((readers * CAP,)),
             ],
-            scratch_shapes=[pltpu.VMEM((partners * tiles, TILE, size), BF16)] * 2,
-        ),
-        out_shape=[jax.ShapeDtypeStruct((len(group), 2, CAP, count, TILE, size), BF16) for group in groups],
-    )(picks, *keys, *values)
+        ),
+        out_shape=jax.ShapeDtypeStruct((readers, 2, CAP, count, TILE, size), BF16),
+        input_output_aliases={1 + partners: 0} if held else {},
+    )(picks, *pieces, *held)
 
 
 def attend(queries, keys, values, far, places):
@@ -171,7 +183,7 @@
     )(places, *queries, *keys, *values, *far)
 
 
-def plan(key_tiles, my_shard, here, shards, partners, tiles, pairwise):
+def plan(key_tiles, my_shard, here, shards, partners, tiles):
     shard_tiles = partners * tiles
     listed = key_tiles.shape[1]
     own = jnp.arange(shard_tiles, dtype=jnp.int32)
@@ -187,9 +199,6 @@
     needed = jnp.any(matches, axis=(0, 1)).reshape(shards, shard_tiles)
     need_rank = jnp.cumsum(needed.astype(jnp.int32), axis=1) - 1
     far_at = jnp.arange(shards, dtype=jnp.int32)
-    if pairwise:
-        picks = jnp.take(picks, far_at ^ my_shard, axis=0)
-        far_at = (far_at ^ my_shard) - 1
     far_place = shard_tiles + far_at[:, None] * CAP + need_rank
     is_own = (jnp.arange(shards, dtype=jnp.int32) == my_shard)[:, None]
     place = jnp.where(is_own, place_of[None, :], far_place).reshape(-1)
@@ -209,7 +218,6 @@
     rows, heads, _ = queries.shape
     chunks = split_heads(heads // partners)
     tiles = rows // TILE
-    pairwise = False
 
     def swap(piece, k):
         return piece if k == 0 else lax.ppermute(piece, "head", [(i, i ^ k) for i in range(partners)])
@@ -220,17 +228,13 @@
     key_parts = by_partner(key_vectors, here_arg, partners, chunks)
     value_parts = by_partner(value_vectors, here_arg, partners, chunks)
     query_parts = by_partner(queries, here_arg, partners, chunks)
-    picks, places = plan(key_tiles, my_shard, here, shard_count, partners, tiles, pairwise)
+    picks, places = plan(key_tiles, my_shard, here, shard_count, partners, tiles)
 
     def share(keys, values):
-        if not pairwise:
-            sent = pick_tiles(keys, values, picks, [range(shard_count)])[0]
-            return [lax.all_to_all(sent, "seq", 0, 0, tiled=True)]
-        sent = pick_tiles(keys, values, picks, [[k] for k in range(1, shard_count)])
-        return [
-            lax.ppermute(part, "seq", [(i, i ^ k) for i in range(shard_count)]) for k, part in enumerate(sent, start=1)
-        ]
-
+        sent = pick_tiles(values, picks, 1, pick_tiles(keys, picks, 0, None))
+        return [lax.all_to_all(sent, "seq", 0, 0, tiled=True)]
+
+    picks, query_parts = lax.optimization_barrier((picks, query_parts))
     ready = []
     for c in range(len(chunks)):
         keys = exchange(key_parts, c)

time: 271 us -> 263 us (0.970)
  waiting for transfers between devices: 153 us -> 142 us
    ppermute x24, waiting for transfers between devices: 153 us -> 142 us  [swap(): lax.ppermute(piece, 'head', [(i, i ^ k) for i in range(partners)])]
    pallas_call x2 -> x4, Pallas kernels: 12.4 us -> 14.9 us  [pick_tiles(): pl.pallas_call(kernel, grid_spec=pltpu.PrefetchScalarGridSpec(num_scalar_...]
  transfers between devices with their start and end apart: 26 -> 26, of which waited for: 17 -> 17; matrix products, arithmetic and copies ran while one was open for 1% -> 1% of each run, Pallas kernels for 20% -> 22%
where the time goes in v3:
time: 263 us; the launch traced here: 262 us
  waiting for transfers between devices  142 us (54%)
  Pallas kernels  68.3 us (26%)
  starting transfers between devices  43.6 us (17%)
  local copies, waits for them, and re-layouts  6.28 us (2%)
    ppermute x24, waiting for transfers between devices, swap(): lax.ppermute(piece, 'head', [(i, i ^ k) for i in range(partners)])  142 us
    pallas_call x2, Pallas kernels, attend(): pl.pallas_call(kernel, grid_spec=pltpu.PrefetchScalarGridSpec(num_scalar_...  40.1 us
    ppermute x24, starting transfers between devices, swap(): lax.ppermute(piece, 'head', [(i, i ^ k) for i in range(partners)])  33.3 us
    pallas_call x4, Pallas kernels, pick_tiles(): pl.pallas_call(kernel, grid_spec=pltpu.PrefetchScalarGridSpec(num_scalar_...  14.9 us
    all_to_all x2, starting transfers between devices, share(): return [lax.all_to_all(sent, 'seq', 0, 0, tiled=True)]  10.3 us
    pallas_call x3, Pallas kernels, by_partner(): pl.pallas_call(kernel, grid_spec=pltpu.PrefetchScalarGridSpec(num_scalar_...  9.87 us
  transfers between devices with their start and end apart: 26, of which 17 were waited for; matrix products, arithmetic and copies ran while one was open for 1% of the time, Pallas kernels for 22%

profile of v3, /device:TPU:10, one launch (start us, length us, event | category | flops | bytes accessed | tf_op | source)
XLA Modules:
  0.0 261.9 jit_solution(11830860400431705973)
XLA Ops:
  0.0 3.3 %shard_map.47 = (bf16[5,256,128]{2,1,0:T(8,128)(2,1)}, bf16[5,256,128]{2,1,0:T(8,128)(2,1)}, bf16[5,256,128]{2,1,0:T(8,128)(2,1)}, bf16[5,256,128]{2,1,0:T(8,128...) custom-call(s32[1]{0:T(128)} %bitcast.here_ref, ...), custom_call_target="tpu_custom_call" | custom-call | tf_op jit(solution)/shard_map/pallas_call | solution.py:41
  3.3 0.4 collective-permute-start.12
  3.8 2.6 collective-permute-start.13
  6.4 0.5 collective-permute-start.14
  6.8 3.3 %shard_map.48 = (bf16[5,256,128]{2,1,0:T(8,128)(2,1)}, bf16[5,256,128]{2,1,0:T(8,128)(2,1)}, bf16[5,256,128]{2,1,0:T(8,128)(2,1)}, bf16[5,256,128]{2,1,0:T(8,128...) custom-call(s32[1]{0:T(128)} %bitcast.here_ref, ...), custom_call_target="tpu_custom_call" | custom-call | tf_op jit(solution)/shard_map/pallas_call | solution.py:41
  10.1 1.3 collective-permute-start.15
  11.4 2.2 collective-permute-start.16
  13.7 0.1 copy.11
  13.8 0.3 compare_reduce_fusion
  14.1 3.3 %shard_map.46 = (bf16[5,256,128]{2,1,0:T(8,128)(2,1)}, bf16[5,256,128]{2,1,0:T(8,128)(2,1)}, bf16[5,256,128]{2,1,0:T(8,128)(2,1)}, bf16[5,256,128]{2,1,0:T(8,128...) custom-call(s32[1]{0:T(128)} %bitcast.here_ref, ...), custom_call_target="tpu_custom_call" | custom-call | tf_op jit(solution)/shard_map/pallas_call | solution.py:41
  17.4 0.2 reduce_window_sum.18
  17.6 0.9 collective-permute-done.12.refs_1_.refs_5_
  18.5 2.7 %collective-permute-start.17 = (bf16[5,256,128]{2,1,0:T(8,128)(2,1)}, bf16[5,256,128]{2,1,0:T(8,128)(2,1)S(1)}, u32[]{:S(2)}, u32[]{:S(2)}) collective-permute-start(bf16[5,256,128]{2,1,0:T(8,128)(2,1)} %get-tuple-element.79), channel_id=1, source_target_pairs={{0,3},{1,2},{2,1},{3,0},{4,7},{5,6},{6,5},{7,4},{8,11},{9,10},{10,... | collective-permute-start | bytes 983048 | tf_op jit(solution)/shard_map/ppermute | solution.py:223
  21.2 0.1 select_reduce_fusion.1
  21.3 0.7 copy.13.pick_ref
  22.0 6.9 %collective-permute-done.13.refs_2_.refs_6_ = bf16[5,256,128]{2,1,0:T(8,128)(2,1)S(1)} collective-permute-done((bf16[5,256,128]{2,1,0:T(8,128)(2,1)}, bf16[5,256,128]{2,1,0:T(8,128)(2,1)S(1)}, u32[]{:S(2)}, u32[]{:S(2)}) %collective-permute-start.13) | collective-permute-done | bytes 327712 | tf_op jit(solution)/shard_map/ppermute | solution.py:223
  28.9 21.9 %collective-permute-done.14.refs_3_.refs_7_ = bf16[5,256,128]{2,1,0:T(8,128)(2,1)S(1)} collective-permute-done((bf16[5,256,128]{2,1,0:T(8,128)(2,1)}, bf16[5,256,128]{2,1,0:T(8,128)(2,1)S(1)}, u32[]{:S(2)}, u32[]{:S(2)}) %collective-permute-start.14) | collective-permute-done | bytes 327712 | tf_op jit(solution)/shard_map/ppermute | solution.py:223
  50.8 0.7 copy-done.2
  51.5 3.8 %shard_map.52.refs_4_ = bf16[8,2,2,5,128,128]{5,4,3,2,1,0:T(8,128)(2,1)} custom-call(s32[8,2]{1,0:T(8,128)} %copy.13.pick_ref, bf16[5,256,128]{2,1,0:T(8,128)(2,1)} %get-tuple-element.72.refs_0_.refs_4_, bf16[5,256,128]{2,1,0:T(8,128)(2,1)} %copy-done, bf16[5,256,128]{2,1,0:T(8,128)(2,1)} %copy-done.1, bf16[5,256,128]{2,1,0:T(8,128)(2,1)} %copy-done.2), custom_call_target="tpu_custom_call" | custom-call | tf_op jit(solution)/shard_map/pallas_call | solution.py:107
  55.3 1.7 collective-permute-done.16.refs_2_.refs_10_
  57.0 6.4 %collective-permute-done.17.refs_3_.refs_11_ = bf16[5,256,128]{2,1,0:T(8,128)(2,1)S(1)} collective-permute-done((bf16[5,256,128]{2,1,0:T(8,128)(2,1)}, bf16[5,256,128]{2,1,0:T(8,128)(2,1)S(1)}, u32[]{:S(2)}, u32[]{:S(2)}) %collective-permute-start.17) | collective-permute-done | bytes 327712 | tf_op jit(solution)/shard_map/ppermute | solution.py:223
  63.4 0.7 copy-done.6
  64.1 3.7 %shard_map.53 = bf16[8,2,2,5,128,128]{5,4,3,2,1,0:T(8,128)(2,1)} custom-call(s32[8,2]{1,0:T(8,128)} %copy.13.pick_ref, bf16[5,256,128]{2,1,0:T(8,128)(2,1)} %get-tuple-element.76.refs_0_.refs_8_, bf16[5,256,128]{2,1,0:T(8,128)(2,1)} %copy-done.3, bf16[5,256,128]{2,1,0:T(8,128)(2,1)} %copy-done.4, ...), custom_call_target="tpu_custom_call", output_to_operand_aliasing={{}: (5, {})} | custom-call | tf_op jit(solution)/shard_map/pallas_call | solution.py:107
  67.9 5.2 %all-to-all-start.1 = ((bf16[8,2,2,5,128,128]{5,4,3,2,1,0:T(8,128)(2,1)}), bf16[8,2,2,5,128,128]{5,4,3,2,1,0:T(8,128)(2,1)}, u32[]{:S(2)}, u32[]{:S(2)}) async-start(bf16[8,2,2,5,128,128]{5,4,3,2,1,0:T(8,128)(2,1)} %shard_map.53), calls=%async_computation.1 | async-start | bytes 10485760 | tf_op jit(solution)/shard_map/all_to_all | solution.py:235
  73.1 3.0 %collective-permute-start.4 = (bf16[5,256,128]{2,1,0:T(8,128)(2,1)S(1)}, bf16[5,256,128]{2,1,0:T(8,128)(2,1)S(1)}, u32[]{:S(2)}, u32[]{:S(2)}) collective-permute-start(bf16[5,256,128]{2,1,0:T(8,128)(2,1)S(1)} %copy-done.26), channel_id=1, source_target_pairs={{0,2},{1,3},{2,0},{3,1},{4,6},{5,7},{6,4},{7,5},{8,10},{9,11},{10,... | collective-permute-start | bytes 983048 | tf_op jit(solution)/shard_map/ppermute | solution.py:223
  76.2 0.4 collective-permute-start.5
  76.6 1.1 collective-permute-start.6
  77.7 2.0 collective-permute-start.7
  79.6 7.9 %collective-permute-done.3.refs_1_.refs_5_ = bf16[5,256,128]{2,1,0:T(8,128)(2,1)S(1)} collective-permute-done((bf16[5,256,128]{2,1,0:T(8,128)(2,1)S(1)}, bf16[5,256,128]{2,1,0:T(8,128)(2,1)S(1)}, u32[]{:S(2)}, u32[]{:S(2)}) %collective-permute-start.3) | collective-permute-done | bytes 327712 | tf_op jit(solution)/shard_map/ppermute | solution.py:223
  87.6 0.9 collective-permute-start.8
  88.5 9.8 %collective-permute-done.4.refs_2_.refs_6_ = bf16[5,256,128]{2,1,0:T(8,128)(2,1)S(1)} collective-permute-done((bf16[5,256,128]{2,1,0:T(8,128)(2,1)S(1)}, bf16[5,256,128]{2,1,0:T(8,128)(2,1)S(1)}, u32[]{:S(2)}, u32[]{:S(2)}) %collective-permute-start.4) | collective-permute-done | bytes 327712 | tf_op jit(solution)/shard_map/ppermute | solution.py:223
  98.4 22.0 %collective-permute-done.5.refs_3_.refs_7_ = bf16[5,256,128]{2,1,0:T(8,128)(2,1)S(1)} collective-permute-done((bf16[5,256,128]{2,1,0:T(8,128)(2,1)S(1)}, bf16[5,256,128]{2,1,0:T(8,128)(2,1)S(1)}, u32[]{:S(2)}, u32[]{:S(2)}) %collective-permute-start.5) | collective-permute-done | bytes 327712 | tf_op jit(solution)/shard_map/ppermute | solution.py:223
  120.3 0.7 copy-done.8
  121.0 3.8 %shard_map.49.refs_4_ = bf16[8,2,2,5,128,128]{5,4,3,2,1,0:T(8,128)(2,1)} custom-call(s32[8,2]{1,0:T(8,128)} %copy.13.pick_ref, bf16[5,256,128]{2,1,0:T(8,128)(2,1)} %get-tuple-element.58.refs_0_.refs_4_, bf16[5,256,128]{2,1,0:T(8,128)(2,1)} %copy-done.5, bf16[5,256,128]{2,1,0:T(8,128)(2,1)} %copy-done.7, bf16[5,256,128]{2,1,0:T(8,128)(2,1)} %copy-done.8), custom_call_target="tpu_custom_call" | custom-call | tf_op jit(solution)/shard_map/pallas_call | solution.py:107
  124.8 1.6 collective-permute-done.7.refs_2_.refs_10_
  126.4 6.9 %collective-permute-done.8.refs_3_.refs_11_ = bf16[5,256,128]{2,1,0:T(8,128)(2,1)S(1)} collective-permute-done((bf16[5,256,128]{2,1,0:T(8,128)(2,1)S(1)}, bf16[5,256,128]{2,1,0:T(8,128)(2,1)S(1)}, u32[]{:S(2)}, u32[]{:S(2)}) %collective-permute-start.8) | collective-permute-done | bytes 327712 | tf_op jit(solution)/shard_map/ppermute | solution.py:223
  133.3 0.7 copy-done.11
  134.0 3.7 %shard_map.50 = bf16[8,2,2,5,128,128]{5,4,3,2,1,0:T(8,128)(2,1)} custom-call(s32[8,2]{1,0:T(8,128)} %copy.13.pick_ref, bf16[5,256,128]{2,1,0:T(8,128)(2,1)} %get-tuple-element.62.refs_0_.refs_8_, bf16[5,256,128]{2,1,0:T(8,128)(2,1)} %copy-done.9, bf16[5,256,128]{2,1,0:T(8,128)(2,1)} %copy-done.10, ...), custom_call_target="tpu_custom_call", output_to_operand_aliasing={{}: (5, {})} | custom-call | tf_op jit(solution)/shard_map/pallas_call | solution.py:107
  137.8 5.1 %all-to-all-start = ((bf16[8,2,2,5,128,128]{5,4,3,2,1,0:T(8,128)(2,1)}), bf16[8,2,2,5,128,128]{5,4,3,2,1,0:T(8,128)(2,1)}, u32[]{:S(2)}, u32[]{:S(2)}) async-start(bf16[8,2,2,5,128,128]{5,4,3,2,1,0:T(8,128)(2,1)} %shard_map.50), calls=%async_computation | async-start | bytes 10485760 | tf_op jit(solution)/shard_map/all_to_all | solution.py:235
  142.9 1.6 collective-permute-start.11
  144.5 2.7 %collective-permute-start.9 = (bf16[5,256,128]{2,1,0:T(8,128)(2,1)S(1)}, bf16[5,256,128]{2,1,0:T(8,128)(2,1)}, u32[]{:S(2)}, u32[]{:S(2)}) collective-permute-start(bf16[5,256,128]{2,1,0:T(8,128)(2,1)S(1)} %copy-done.22), channel_id=1, source_target_pairs={{0,1},{1,0},{2,3},{3,2},{4,5},{5,4},{6,7},{7,6},{8,9},{9,8},{10,11... | collective-permute-start | bytes 983048 | tf_op jit(solution)/shard_map/ppermute | solution.py:223
  147.3 3.0 %collective-permute-start.1 = (bf16[5,256,128]{2,1,0:T(8,128)(2,1)S(1)}, bf16[5,256,128]{2,1,0:T(8,128)(2,1)S(1)}, u32[]{:S(2)}, u32[]{:S(2)}) collective-permute-start(bf16[5,256,128]{2,1,0:T(8,128)(2,1)S(1)} %copy-done.20), channel_id=1, source_target_pairs={{0,2},{1,3},{2,0},{3,1},{4,6},{5,7},{6,4},{7,5},{8,10},{9,11},{10,... | collective-permute-start | bytes 983048 | tf_op jit(solution)/shard_map/ppermute | solution.py:223
  150.4 0.1 fusion
  150.6 0.2 reduce_window_sum.17
  150.9 0.3 select_reduce_fusion
  151.5 0.6 gather_fusion
  152.1 12.9 %collective-permute-done.10.refs_2_ = bf16[5,256,128]{2,1,0:T(8,128)(2,1)S(1)} collective-permute-done((bf16[5,256,128]{2,1,0:T(8,128)(2,1)S(1)}, bf16[5,256,128]{2,1,0:T(8,128)(2,1)S(1)}, u32[]{:S(2)}, u32[]{:S(2)}) %collective-permute-start.10) | collective-permute-done | bytes 327712 | tf_op jit(solution)/shard_map/ppermute | solution.py:223
  165.0 1.6 collective-permute-start.2
  166.6 0.7 broadcast_select_fusion.place_ref
  167.2 7.1 %collective-permute-done.11.refs_3_ = bf16[5,256,128]{2,1,0:T(8,128)(2,1)} collective-permute-done((bf16[5,256,128]{2,1,0:T(8,128)(2,1)S(1)}, bf16[5,256,128]{2,1,0:T(8,128)(2,1)}, u32[]{:S(2)}, u32[]{:S(2)}) %collective-permute-start.11) | collective-permute-done | bytes 327712 | tf_op jit(solution)/shard_map/ppermute | solution.py:223
  174.3 20.1 %shard_map.54 = (bf16[5,256,128]{2,1,0:T(8,128)(2,1)}, bf16[5,256,128]{2,1,0:T(8,128)(2,1)}, bf16[5,256,128]{2,1,0:T(8,128)(2,1)}, bf16[5,256,128]{2,1,0:T(8,128)(2,1)}) custom-call(s32[8,10]{1,0:T(8,128)} %broadcast_select_fusion.place_ref, bf16[5,256,128]{2,1,0:T(8,128)(2,1)} %get-tuple-element.68.refs_0_, ...), custom_call_target="tpu_custom_call" | custom-call | flops 3355443200 | bytes 10485760 | tf_op jit(solution)/shard_map/pallas_call | solution.py:168
  194.5 1.7 collective-permute-start.21
  196.2 1.7 collective-permute-start.23
  198.0 5.0 %collective-permute-done.2.refs_3_ = bf16[5,256,128]{2,1,0:T(8,128)(2,1)S(1)} collective-permute-done((bf16[5,256,128]{2,1,0:T(8,128)(2,1)S(1)}, bf16[5,256,128]{2,1,0:T(8,128)(2,1)S(1)}, u32[]{:S(2)}, u32[]{:S(2)}) %collective-permute-start.2) | collective-permute-done | bytes 327712 | tf_op jit(solution)/shard_map/ppermute | solution.py:223
  203.0 0.7 copy-done.33
  203.7 20.1 %shard_map.51 = (bf16[5,256,128]{2,1,0:T(8,128)(2,1)}, bf16[5,256,128]{2,1,0:T(8,128)(2,1)}, bf16[5,256,128]{2,1,0:T(8,128)(2,1)}, bf16[5,256,128]{2,1,0:T(8,128)(2,1)}) custom-call(s32[8,10]{1,0:T(8,128)} %broadcast_select_fusion.place_ref, bf16[5,256,128]{2,1,0:T(8,128)(2,1)} %get-tuple-element.54.refs_0_, bf16[5,256,128]{2,1,0:T(8,128)(2,1)} %copy-done.30, ...), custom_call_target="tpu_custom_call" | custom-call | flops 3355443200 | bytes 10485760 | tf_op jit(solution)/shard_map/pallas_call | solution.py:168
  223.8 1.2 collective-permute-start.20
  225.0 2.3 collective-permute-start.22
  227.3 2.9 %collective-permute-done.23.refs_7_ = bf16[5,256,128]{2,1,0:T(8,128)(2,1)S(1)} collective-permute-done((bf16[5,256,128]{2,1,0:T(8,128)(2,1)}, bf16[5,256,128]{2,1,0:T(8,128)(2,1)S(1)}, u32[]{:S(2)}, u32[]{:S(2)}) %collective-permute-start.23) | collective-permute-done | bytes 327712 | tf_op jit(solution)/shard_map/ppermute | solution.py:223
  230.2 4.4 %collective-permute-done.18.refs_2_ = bf16[5,256,128]{2,1,0:T(8,128)(2,1)S(1)} collective-permute-done((bf16[5,256,128]{2,1,0:T(8,128)(2,1)}, bf16[5,256,128]{2,1,0:T(8,128)(2,1)S(1)}, u32[]{:S(2)}, u32[]{:S(2)}) %collective-permute-start.18) | collective-permute-done | bytes 327712 | tf_op jit(solution)/shard_map/ppermute | solution.py:223
  234.7 14.7 %collective-permute-done.20.refs_4_ = bf16[5,256,128]{2,1,0:T(8,128)(2,1)S(1)} collective-permute-done((bf16[5,256,128]{2,1,0:T(8,128)(2,1)}, bf16[5,256,128]{2,1,0:T(8,128)(2,1)S(1)}, u32[]{:S(2)}, u32[]{:S(2)}) %collective-permute-start.20) | collective-permute-done | bytes 327712 | tf_op jit(solution)/shard_map/ppermute | solution.py:223
  249.4 8.5 %collective-permute-done.22.refs_6_ = bf16[5,256,128]{2,1,0:T(8,128)(2,1)S(1)} collective-permute-done((bf16[5,256,128]{2,1,0:T(8,128)(2,1)}, bf16[5,256,128]{2,1,0:T(8,128)(2,1)S(1)}, u32[]{:S(2)}, u32[]{:S(2)}) %collective-permute-start.22) | collective-permute-done | bytes 327712 | tf_op jit(solution)/shard_map/ppermute | solution.py:223
  257.9 0.7 copy-done.17
  258.6 3.3 %shard_map.55 = bf16[256,40,128]{2,1,0:T(8,128)(2,1)} custom-call(s32[1]{0:T(128)} %bitcast.here_ref, bf16[5,256,128]{2,1,0:T(8,128)(2,1)} %get-tuple-element.67.refs_0_, bf16[5,256,128]{2,1,0:T(8,128)(2,1)} %get-tuple-element.80.refs_1_, bf16[5,256,128]{2,1,0:T(8,128)(2,1)} %copy-done.15, bf16[5,256,128]{2,1,0:T(8,128)(2,1)} %copy-done.12, ...), custom_call_target="tpu_custom_call" | custom-call | tf_op jit(solution)/shard_map/pallas_call | solution.py:70
  (93 shorter events, 1.0 us)
Async XLA Ops:
  0.0 13.7 %copy-start.18 = (s32[64,10]{0,1:T(8,128)S(1)}, s32[64,10]{0,1:T(8,128)}, u32[]{:S(2)}) copy-start(s32[64,10]{0,1:T(8,128)} %param.7) | copy-start | bytes 7684
  3.3 15.1 %collective-permute-start.12 = (bf16[5,256,128]{2,1,0:T(8,128)(2,1)}, bf16[5,256,128]{2,1,0:T(8,128)(2,1)S(1)}, u32[]{:S(2)}, u32[]{:S(2)}) collective-permute-start(bf16[5,256,128]{2,1,0:T(8,128)(2,1)} %get-tuple-element.73), channel_id=1, source_target_pairs={{0,1},{1,0},{2,3},{3,2},{4,5},{5,4},{6,7},{7,6},{8,9},{9,8},{10,11... | collective-permute-start | bytes 983048 | tf_op jit(solution)/shard_map/ppermute | solution.py:223
  3.8 25.1 %collective-permute-start.13 = (bf16[5,256,128]{2,1,0:T(8,128)(2,1)}, bf16[5,256,128]{2,1,0:T(8,128)(2,1)S(1)}, u32[]{:S(2)}, u32[]{:S(2)}) collective-permute-start(bf16[5,256,128]{2,1,0:T(8,128)(2,1)} %get-tuple-element.74), channel_id=1, source_target_pairs={{0,2},{1,3},{2,0},{3,1},{4,6},{5,7},{6,4},{7,5},{8,10},{9,11},{10,... | collective-permute-start | bytes 983048 | tf_op jit(solution)/shard_map/ppermute | solution.py:223
  6.4 44.4 %collective-permute-start.14 = (bf16[5,256,128]{2,1,0:T(8,128)(2,1)}, bf16[5,256,128]{2,1,0:T(8,128)(2,1)S(1)}, u32[]{:S(2)}, u32[]{:S(2)}) collective-permute-start(bf16[5,256,128]{2,1,0:T(8,128)(2,1)} %get-tuple-element.75), channel_id=1, source_target_pairs={{0,3},{1,2},{2,1},{3,0},{4,7},{5,6},{6,5},{7,4},{8,11},{9,10},{10,... | collective-permute-start | bytes 983048 | tf_op jit(solution)/shard_map/ppermute | solution.py:223
  10.1 45.2 %collective-permute-start.15 = (bf16[5,256,128]{2,1,0:T(8,128)(2,1)}, bf16[5,256,128]{2,1,0:T(8,128)(2,1)S(1)}, u32[]{:S(2)}, u32[]{:S(2)}) collective-permute-start(bf16[5,256,128]{2,1,0:T(8,128)(2,1)} %get-tuple-element.77), channel_id=1, source_target_pairs={{0,1},{1,0},{2,3},{3,2},{4,5},{5,4},{6,7},{7,6},{8,9},{9,8},{10,11... | collective-permute-start | bytes 983048 | tf_op jit(solution)/shard_map/ppermute | solution.py:223
  11.4 45.6 %collective-permute-start.16 = (bf16[5,256,128]{2,1,0:T(8,128)(2,1)}, bf16[5,256,128]{2,1,0:T(8,128)(2,1)S(1)}, u32[]{:S(2)}, u32[]{:S(2)}) collective-permute-start(bf16[5,256,128]{2,1,0:T(8,128)(2,1)} %get-tuple-element.78), channel_id=1, source_target_pairs={{0,2},{1,3},{2,0},{3,1},{4,6},{5,7},{6,4},{7,5},{8,10},{9,11},{10,... | collective-permute-start | bytes 983048 | tf_op jit(solution)/shard_map/ppermute | solution.py:223
  18.5 32.3 %copy-start = (bf16[5,256,128]{2,1,0:T(8,128)(2,1)}, bf16[5,256,128]{2,1,0:T(8,128)(2,1)S(1)}, u32[]{:S(2)}) copy-start(bf16[5,256,128]{2,1,0:T(8,128)(2,1)S(1)} %collective-permute-done.12.refs_1_.refs_5_) | copy-start | bytes 983044
  18.5 44.9 %collective-permute-start.17 = (bf16[5,256,128]{2,1,0:T(8,128)(2,1)}, bf16[5,256,128]{2,1,0:T(8,128)(2,1)S(1)}, u32[]{:S(2)}, u32[]{:S(2)}) collective-permute-start(bf16[5,256,128]{2,1,0:T(8,128)(2,1)} %get-tuple-element.79), channel_id=1, source_target_pairs={{0,3},{1,2},{2,1},{3,0},{4,7},{5,6},{6,5},{7,4},{8,11},{9,10},{10,... | collective-permute-start | bytes 983048 | tf_op jit(solution)/shard_map/ppermute | solution.py:223
  28.9 21.9 %copy-start.1 = (bf16[5,256,128]{2,1,0:T(8,128)(2,1)}, bf16[5,256,128]{2,1,0:T(8,128)(2,1)S(1)}, u32[]{:S(2)}) copy-start(bf16[5,256,128]{2,1,0:T(8,128)(2,1)S(1)} %collective-permute-done.13.refs_2_.refs_6_) | copy-start | bytes 983044
  50.8 0.7 copy-start.2
  55.3 8.1 %copy-start.3 = (bf16[5,256,128]{2,1,0:T(8,128)(2,1)}, bf16[5,256,128]{2,1,0:T(8,128)(2,1)S(1)}, u32[]{:S(2)}) copy-start(bf16[5,256,128]{2,1,0:T(8,128)(2,1)S(1)} %collective-permute-done.15.refs_1_.refs_9_) | copy-start | bytes 983044
  57.0 6.4 %copy-start.4 = (bf16[5,256,128]{2,1,0:T(8,128)(2,1)}, bf16[5,256,128]{2,1,0:T(8,128)(2,1)S(1)}, u32[]{:S(2)}) copy-start(bf16[5,256,128]{2,1,0:T(8,128)(2,1)S(1)} %collective-permute-done.16.refs_2_.refs_10_) | copy-start | bytes 983044
  63.4 0.7 copy-start.6
  67.8 5.3 %copy-start.28 = (bf16[5,256,128]{2,1,0:T(8,128)(2,1)S(1)}, bf16[5,256,128]{2,1,0:T(8,128)(2,1)}, u32[]{:S(2)}) copy-start(bf16[5,256,128]{2,1,0:T(8,128)(2,1)} %get-tuple-element.59) | copy-start | bytes 983044
  67.8 5.3 %copy-start.26 = (bf16[5,256,128]{2,1,0:T(8,128)(2,1)S(1)}, bf16[5,256,128]{2,1,0:T(8,128)(2,1)}, u32[]{:S(2)}) copy-start(bf16[5,256,128]{2,1,0:T(8,128)(2,1)} %get-tuple-element.60) | copy-start | bytes 983044
  67.9 8.3 %copy-start.25 = (bf16[5,256,128]{2,1,0:T(8,128)(2,1)S(1)}, bf16[5,256,128]{2,1,0:T(8,128)(2,1)}, u32[]{:S(2)}) copy-start(bf16[5,256,128]{2,1,0:T(8,128)(2,1)} %get-tuple-element.61) | copy-start | bytes 983044
  67.9 9.8 %copy-start.29 = (bf16[5,256,128]{2,1,0:T(8,128)(2,1)S(1)}, bf16[5,256,128]{2,1,0:T(8,128)(2,1)}, u32[]{:S(2)}) copy-start(bf16[5,256,128]{2,1,0:T(8,128)(2,1)} %get-tuple-element.64) | copy-start | bytes 983044
  67.9 19.7 %copy-start.27 = (bf16[5,256,128]{2,1,0:T(8,128)(2,1)S(1)}, bf16[5,256,128]{2,1,0:T(8,128)(2,1)}, u32[]{:S(2)}) copy-start(bf16[5,256,128]{2,1,0:T(8,128)(2,1)} %get-tuple-element.65) | copy-start | bytes 983044
  67.9 69.9 %all-to-all-start.1 = ((bf16[8,2,2,5,128,128]{5,4,3,2,1,0:T(8,128)(2,1)}), bf16[8,2,2,5,128,128]{5,4,3,2,1,0:T(8,128)(2,1)}, u32[]{:S(2)}, u32[]{:S(2)}) async-start(bf16[8,2,2,5,128,128]{5,4,3,2,1,0:T(8,128)(2,1)} %shard_map.53), calls=%async_computation.1 | async-start | bytes 10485760 | tf_op jit(solution)/shard_map/all_to_all | solution.py:235
  73.1 14.5 %collective-permute-start.3 = (bf16[5,256,128]{2,1,0:T(8,128)(2,1)S(1)}, bf16[5,256,128]{2,1,0:T(8,128)(2,1)S(1)}, u32[]{:S(2)}, u32[]{:S(2)}) collective-permute-start(bf16[5,256,128]{2,1,0:T(8,128)(2,1)S(1)} %copy-done.28), channel_id=1, source_target_pairs={{0,1},{1,0},{2,3},{3,2},{4,5},{5,4},{6,7},{7,6},{8,9},{9,8},{10,11... | collective-permute-start | bytes 983048 | tf_op jit(solution)/shard_map/ppermute | solution.py:223
  73.1 25.2 %collective-permute-start.4 = (bf16[5,256,128]{2,1,0:T(8,128)(2,1)S(1)}, bf16[5,256,128]{2,1,0:T(8,128)(2,1)S(1)}, u32[]{:S(2)}, u32[]{:S(2)}) collective-permute-start(bf16[5,256,128]{2,1,0:T(8,128)(2,1)S(1)} %copy-done.26), channel_id=1, source_target_pairs={{0,2},{1,3},{2,0},{3,1},{4,6},{5,7},{6,4},{7,5},{8,10},{9,11},{10,... | collective-permute-start | bytes 983048 | tf_op jit(solution)/shard_map/ppermute | solution.py:223
  76.2 44.2 %collective-permute-start.5 = (bf16[5,256,128]{2,1,0:T(8,128)(2,1)S(1)}, bf16[5,256,128]{2,1,0:T(8,128)(2,1)S(1)}, u32[]{:S(2)}, u32[]{:S(2)}) collective-permute-start(bf16[5,256,128]{2,1,0:T(8,128)(2,1)S(1)} %copy-done.25), channel_id=1, source_target_pairs={{0,3},{1,2},{2,1},{3,0},{4,7},{5,6},{6,5},{7,4},{8,11},{9,10},{10,... | collective-permute-start | bytes 983048 | tf_op jit(solution)/shard_map/ppermute | solution.py:223
  76.6 48.2 %collective-permute-start.6 = (bf16[5,256,128]{2,1,0:T(8,128)(2,1)}, bf16[5,256,128]{2,1,0:T(8,128)(2,1)S(1)}, u32[]{:S(2)}, u32[]{:S(2)}) collective-permute-start(bf16[5,256,128]{2,1,0:T(8,128)(2,1)} %get-tuple-element.63), channel_id=1, source_target_pairs={{0,1},{1,0},{2,3},{3,2},{4,5},{5,4},{6,7},{7,6},{8,9},{9,8},{10,11... | collective-permute-start | bytes 983048 | tf_op jit(solution)/shard_map/ppermute | solution.py:223
  77.7 48.7 %collective-permute-start.7 = (bf16[5,256,128]{2,1,0:T(8,128)(2,1)S(1)}, bf16[5,256,128]{2,1,0:T(8,128)(2,1)S(1)}, u32[]{:S(2)}, u32[]{:S(2)}) collective-permute-start(bf16[5,256,128]{2,1,0:T(8,128)(2,1)S(1)} %copy-done.29), channel_id=1, source_target_pairs={{0,2},{1,3},{2,0},{3,1},{4,6},{5,7},{6,4},{7,5},{8,10},{9,11},{10,... | collective-permute-start | bytes 983048 | tf_op jit(solution)/shard_map/ppermute | solution.py:223
  87.6 32.7 %copy-start.5 = (bf16[5,256,128]{2,1,0:T(8,128)(2,1)}, bf16[5,256,128]{2,1,0:T(8,128)(2,1)S(1)}, u32[]{:S(2)}) copy-start(bf16[5,256,128]{2,1,0:T(8,128)(2,1)S(1)} %collective-permute-done.3.refs_1_.refs_5_) | copy-start | bytes 983044
  87.6 45.7 %collective-permute-start.8 = (bf16[5,256,128]{2,1,0:T(8,128)(2,1)S(1)}, bf16[5,256,128]{2,1,0:T(8,128)(2,1)S(1)}, u32[]{:S(2)}, u32[]{:S(2)}) collective-permute-start(bf16[5,256,128]{2,1,0:T(8,128)(2,1)S(1)} %copy-done.27), channel_id=1, source_target_pairs={{0,3},{1,2},{2,1},{3,0},{4,7},{5,6},{6,5},{7,4},{8,11},{9,10},{10,... | collective-permute-start | bytes 983048 | tf_op jit(solution)/shard_map/ppermute | solution.py:223
  98.3 22.0 %copy-start.7 = (bf16[5,256,128]{2,1,0:T(8,128)(2,1)}, bf16[5,256,128]{2,1,0:T(8,128)(2,1)S(1)}, u32[]{:S(2)}) copy-start(bf16[5,256,128]{2,1,0:T(8,128)(2,1)S(1)} %collective-permute-done.4.refs_2_.refs_6_) | copy-start | bytes 983044
  120.3 0.7 copy-start.8
  124.8 8.5 %copy-start.9 = (bf16[5,256,128]{2,1,0:T(8,128)(2,1)}, bf16[5,256,128]{2,1,0:T(8,128)(2,1)S(1)}, u32[]{:S(2)}) copy-start(bf16[5,256,128]{2,1,0:T(8,128)(2,1)S(1)} %collective-permute-done.6.refs_1_.refs_9_) | copy-start | bytes 983044
  126.4 6.9 %copy-start.10 = (bf16[5,256,128]{2,1,0:T(8,128)(2,1)}, bf16[5,256,128]{2,1,0:T(8,128)(2,1)S(1)}, u32[]{:S(2)}) copy-start(bf16[5,256,128]{2,1,0:T(8,128)(2,1)S(1)} %collective-permute-done.7.refs_2_.refs_10_) | copy-start | bytes 983044
  133.3 0.7 copy-start.11
  137.7 5.1 %copy-start.24 = (bf16[5,256,128]{2,1,0:T(8,128)(2,1)S(1)}, bf16[5,256,128]{2,1,0:T(8,128)(2,1)}, u32[]{:S(2)}) copy-start(bf16[5,256,128]{2,1,0:T(8,128)(2,1)} %get-tuple-element.70) | copy-start | bytes 983044
  137.7 5.1 %copy-start.23 = (bf16[5,256,128]{2,1,0:T(8,128)(2,1)S(1)}, bf16[5,256,128]{2,1,0:T(8,128)(2,1)}, u32[]{:S(2)}) copy-start(bf16[5,256,128]{2,1,0:T(8,128)(2,1)} %get-tuple-element.71) | copy-start | bytes 983044
  137.7 6.8 %copy-start.22 = (bf16[5,256,128]{2,1,0:T(8,128)(2,1)S(1)}, bf16[5,256,128]{2,1,0:T(8,128)(2,1)}, u32[]{:S(2)}) copy-start(bf16[5,256,128]{2,1,0:T(8,128)(2,1)} %get-tuple-element.69) | copy-start | bytes 983044
  137.8 9.5 %copy-start.21 = (bf16[5,256,128]{2,1,0:T(8,128)(2,1)S(1)}, bf16[5,256,128]{2,1,0:T(8,128)(2,1)}, u32[]{:S(2)}) copy-start(bf16[5,256,128]{2,1,0:T(8,128)(2,1)} %get-tuple-element.55) | copy-start | bytes 983044
  137.8 9.6 %copy-start.20 = (bf16[5,256,128]{2,1,0:T(8,128)(2,1)S(1)}, bf16[5,256,128]{2,1,0:T(8,128)(2,1)}, u32[]{:S(2)}) copy-start(bf16[5,256,128]{2,1,0:T(8,128)(2,1)} %get-tuple-element.56) | copy-start | bytes 983044
  137.8 27.2 %copy-start.19 = (bf16[5,256,128]{2,1,0:T(8,128)(2,1)S(1)}, bf16[5,256,128]{2,1,0:T(8,128)(2,1)}, u32[]{:S(2)}) copy-start(bf16[5,256,128]{2,1,0:T(8,128)(2,1)} %get-tuple-element.57) | copy-start | bytes 983044
  137.8 65.2 %all-to-all-start = ((bf16[8,2,2,5,128,128]{5,4,3,2,1,0:T(8,128)(2,1)}), bf16[8,2,2,5,128,128]{5,4,3,2,1,0:T(8,128)(2,1)}, u32[]{:S(2)}, u32[]{:S(2)}) async-start(bf16[8,2,2,5,128,128]{5,4,3,2,1,0:T(8,128)(2,1)} %shard_map.50), calls=%async_computation | async-start | bytes 10485760 | tf_op jit(solution)/shard_map/all_to_all | solution.py:235
  142.9 22.1 %collective-permute-start.10 = (bf16[5,256,128]{2,1,0:T(8,128)(2,1)S(1)}, bf16[5,256,128]{2,1,0:T(8,128)(2,1)S(1)}, u32[]{:S(2)}, u32[]{:S(2)}) collective-permute-start(bf16[5,256,128]{2,1,0:T(8,128)(2,1)S(1)} %copy-done.24), channel_id=1, source_target_pairs={{0,2},{1,3},{2,0},{3,1},{4,6},{5,7},{6,4},{7,5},{8,10},{9,11},{10,... | collective-permute-start | bytes 983048 | tf_op jit(solution)/shard_map/ppermute | solution.py:223
  142.9 31.4 %collective-permute-start.11 = (bf16[5,256,128]{2,1,0:T(8,128)(2,1)S(1)}, bf16[5,256,128]{2,1,0:T(8,128)(2,1)}, u32[]{:S(2)}, u32[]{:S(2)}) collective-permute-start(bf16[5,256,128]{2,1,0:T(8,128)(2,1)S(1)} %copy-done.23), channel_id=1, source_target_pairs={{0,3},{1,2},{2,1},{3,0},{4,7},{5,6},{6,5},{7,4},{8,11},{9,10},{10,... | collective-permute-start | bytes 983048 | tf_op jit(solution)/shard_map/ppermute | solution.py:223
  144.5 29.8 %collective-permute-start.9 = (bf16[5,256,128]{2,1,0:T(8,128)(2,1)S(1)}, bf16[5,256,128]{2,1,0:T(8,128)(2,1)}, u32[]{:S(2)}, u32[]{:S(2)}) collective-permute-start(bf16[5,256,128]{2,1,0:T(8,128)(2,1)S(1)} %copy-done.22), channel_id=1, source_target_pairs={{0,1},{1,0},{2,3},{3,2},{4,5},{5,4},{6,7},{7,6},{8,9},{9,8},{10,11... | collective-permute-start | bytes 983048 | tf_op jit(solution)/shard_map/ppermute | solution.py:223
  147.3 49.0 %collective-permute-start = (bf16[5,256,128]{2,1,0:T(8,128)(2,1)S(1)}, bf16[5,256,128]{2,1,0:T(8,128)(2,1)S(1)}, u32[]{:S(2)}, u32[]{:S(2)}) collective-permute-start(bf16[5,256,128]{2,1,0:T(8,128)(2,1)S(1)} %copy-done.21), channel_id=1, source_target_pairs={{0,1},{1,0},{2,3},{3,2},{4,5},{5,4},{6,7},{7,6},{8,9},{9,8},{10,11... | collective-permute-start | bytes 983048 | tf_op jit(solution)/shard_map/ppermute | solution.py:223
  147.3 50.6 %collective-permute-start.1 = (bf16[5,256,128]{2,1,0:T(8,128)(2,1)S(1)}, bf16[5,256,128]{2,1,0:T(8,128)(2,1)S(1)}, u32[]{:S(2)}, u32[]{:S(2)}) collective-permute-start(bf16[5,256,128]{2,1,0:T(8,128)(2,1)S(1)} %copy-done.20), channel_id=1, source_target_pairs={{0,2},{1,3},{2,0},{3,1},{4,6},{5,7},{6,4},{7,5},{8,10},{9,11},{10,... | collective-permute-start | bytes 983048 | tf_op jit(solution)/shard_map/ppermute | solution.py:223
  165.0 9.3 %copy-start.32 = (bf16[5,256,128]{2,1,0:T(8,128)(2,1)}, bf16[5,256,128]{2,1,0:T(8,128)(2,1)S(1)}, u32[]{:S(2)}) copy-start(bf16[5,256,128]{2,1,0:T(8,128)(2,1)S(1)} %collective-permute-done.10.refs_2_) | copy-start | bytes 983044
  165.0 38.0 %collective-permute-start.2 = (bf16[5,256,128]{2,1,0:T(8,128)(2,1)S(1)}, bf16[5,256,128]{2,1,0:T(8,128)(2,1)S(1)}, u32[]{:S(2)}, u32[]{:S(2)}) collective-permute-start(bf16[5,256,128]{2,1,0:T(8,128)(2,1)S(1)} %copy-done.19), channel_id=1, source_target_pairs={{0,3},{1,2},{2,1},{3,0},{4,7},{5,6},{6,5},{7,4},{8,11},{9,10},{10,... | collective-permute-start | bytes 983048 | tf_op jit(solution)/shard_map/ppermute | solution.py:223
  194.4 30.6 %collective-permute-start.19 = (bf16[5,256,128]{2,1,0:T(8,128)(2,1)}, bf16[5,256,128]{2,1,0:T(8,128)(2,1)S(1)}, u32[]{:S(2)}, u32[]{:S(2)}) collective-permute-start(bf16[5,256,128]{2,1,0:T(8,128)(2,1)} %get-tuple-element.82), channel_id=1, source_target_pairs={{0,1},{1,0},{2,3},{3,2},{4,5},{5,4},{6,7},{7,6},{8,9},{9,8},{10,11... | collective-permute-start | bytes 983048 | tf_op jit(solution)/shard_map/ppermute | solution.py:223
  194.5 32.8 %collective-permute-start.21 = (bf16[5,256,128]{2,1,0:T(8,128)(2,1)}, bf16[5,256,128]{2,1,0:T(8,128)(2,1)S(1)}, u32[]{:S(2)}, u32[]{:S(2)}) collective-permute-start(bf16[5,256,128]{2,1,0:T(8,128)(2,1)} %get-tuple-element.84), channel_id=1, source_target_pairs={{0,2},{1,3},{2,0},{3,1},{4,6},{5,7},{6,4},{7,5},{8,10},{9,11},{10,... | collective-permute-start | bytes 983048 | tf_op jit(solution)/shard_map/ppermute | solution.py:223
  196.2 6.7 %copy-start.30 = (bf16[5,256,128]{2,1,0:T(8,128)(2,1)}, bf16[5,256,128]{2,1,0:T(8,128)(2,1)S(1)}, u32[]{:S(2)}) copy-start(bf16[5,256,128]{2,1,0:T(8,128)(2,1)S(1)} %collective-permute-done.refs_1_) | copy-start | bytes 983044
  196.2 34.0 %collective-permute-start.23 = (bf16[5,256,128]{2,1,0:T(8,128)(2,1)}, bf16[5,256,128]{2,1,0:T(8,128)(2,1)S(1)}, u32[]{:S(2)}, u32[]{:S(2)}) collective-permute-start(bf16[5,256,128]{2,1,0:T(8,128)(2,1)} %get-tuple-element.86), channel_id=1, source_target_pairs={{0,3},{1,2},{2,1},{3,0},{4,7},{5,6},{6,5},{7,4},{8,11},{9,10},{10,... | collective-permute-start | bytes 983048 | tf_op jit(solution)/shard_map/ppermute | solution.py:223
  198.0 5.0 %copy-start.31 = (bf16[5,256,128]{2,1,0:T(8,128)(2,1)}, bf16[5,256,128]{2,1,0:T(8,128)(2,1)S(1)}, u32[]{:S(2)}) copy-start(bf16[5,256,128]{2,1,0:T(8,128)(2,1)S(1)} %collective-permute-done.1.refs_2_) | copy-start | bytes 983044
  202.9 0.7 copy-start.33
  223.7 10.9 %collective-permute-start.18 = (bf16[5,256,128]{2,1,0:T(8,128)(2,1)}, bf16[5,256,128]{2,1,0:T(8,128)(2,1)S(1)}, u32[]{:S(2)}, u32[]{:S(2)}) collective-permute-start(bf16[5,256,128]{2,1,0:T(8,128)(2,1)} %get-tuple-element.81), channel_id=1, source_target_pairs={{0,1},{1,0},{2,3},{3,2},{4,5},{5,4},{6,7},{7,6},{8,9},{9,8},{10,11... | collective-permute-start | bytes 983048 | tf_op jit(solution)/shard_map/ppermute | solution.py:223
  223.8 25.6 %collective-permute-start.20 = (bf16[5,256,128]{2,1,0:T(8,128)(2,1)}, bf16[5,256,128]{2,1,0:T(8,128)(2,1)S(1)}, u32[]{:S(2)}, u32[]{:S(2)}) collective-permute-start(bf16[5,256,128]{2,1,0:T(8,128)(2,1)} %get-tuple-element.83), channel_id=1, source_target_pairs={{0,2},{1,3},{2,0},{3,1},{4,6},{5,7},{6,4},{7,5},{8,10},{9,11},{10,... | collective-permute-start | bytes 983048 | tf_op jit(solution)/shard_map/ppermute | solution.py:223
  225.0 32.9 %copy-start.12 = (bf16[5,256,128]{2,1,0:T(8,128)(2,1)}, bf16[5,256,128]{2,1,0:T(8,128)(2,1)S(1)}, u32[]{:S(2)}) copy-start(bf16[5,256,128]{2,1,0:T(8,128)(2,1)S(1)} %collective-permute-done.19.refs_3_) | copy-start | bytes 983044
  225.0 32.9 %collective-permute-start.22 = (bf16[5,256,128]{2,1,0:T(8,128)(2,1)}, bf16[5,256,128]{2,1,0:T(8,128)(2,1)S(1)}, u32[]{:S(2)}, u32[]{:S(2)}) collective-permute-start(bf16[5,256,128]{2,1,0:T(8,128)(2,1)} %get-tuple-element.85), channel_id=1, source_target_pairs={{0,3},{1,2},{2,1},{3,0},{4,7},{5,6},{6,5},{7,4},{8,11},{9,10},{10,... | collective-permute-start | bytes 983048 | tf_op jit(solution)/shard_map/ppermute | solution.py:223
  227.3 30.6 %copy-start.13 = (bf16[5,256,128]{2,1,0:T(8,128)(2,1)}, bf16[5,256,128]{2,1,0:T(8,128)(2,1)S(1)}, u32[]{:S(2)}) copy-start(bf16[5,256,128]{2,1,0:T(8,128)(2,1)S(1)} %collective-permute-done.21.refs_5_) | copy-start | bytes 983044
  230.2 27.7 %copy-start.14 = (bf16[5,256,128]{2,1,0:T(8,128)(2,1)}, bf16[5,256,128]{2,1,0:T(8,128)(2,1)S(1)}, u32[]{:S(2)}) copy-start(bf16[5,256,128]{2,1,0:T(8,128)(2,1)S(1)} %collective-permute-done.23.refs_7_) | copy-start | bytes 983044
  234.7 23.2 %copy-start.15 = (bf16[5,256,128]{2,1,0:T(8,128)(2,1)}, bf16[5,256,128]{2,1,0:T(8,128)(2,1)S(1)}, u32[]{:S(2)}) copy-start(bf16[5,256,128]{2,1,0:T(8,128)(2,1)S(1)} %collective-permute-done.18.refs_2_) | copy-start | bytes 983044
  249.4 8.5 %copy-start.16 = (bf16[5,256,128]{2,1,0:T(8,128)(2,1)}, bf16[5,256,128]{2,1,0:T(8,128)(2,1)S(1)}, u32[]{:S(2)}) copy-start(bf16[5,256,128]{2,1,0:T(8,128)(2,1)S(1)} %collective-permute-done.20.refs_4_) | copy-start | bytes 983044
  257.9 0.7 copy-start.17

commit v4 on v3

--- a/solution.py
+++ b/solution.py
@@ -87,38 +87,37 @@
     partners = len(pieces)
 
     def kernel(pick_ref, *refs):
-        out, pool, sems = refs[-3:]
-        for k in range(partners):
-            for tile in range(tiles):
-                pool[k * tiles + tile] = refs[k][:, tile * TILE : (tile + 1) * TILE, :]
-        copies = [
-            pltpu.make_async_copy(
-                pool.at[pick_ref[reader, slot]], out.at[reader, kind, slot], sems.at[reader * CAP + slot]
-            )
-            for reader in range(readers)
-            for slot in range(CAP)
-        ]
-        for copy in copies:
-            copy.start()
-        for copy in copies:
-            copy.wait()
+        ins = refs[:partners]
+        out, sems = refs[-2:]
+
+        def copy_of(k, row, reader, slot):
+            source = ins[k].at[:, pl.ds(row, TILE), :]
+            return pltpu.make_async_copy(source, out.at[reader, kind, slot], sems.at[reader * CAP + slot])
+
+        wanted = [(reader, slot) for reader in range(readers) for slot in range(CAP)]
+        for reader, slot in wanted:
+            place = pick_ref[reader, slot]
+            row = pl.multiple_of(lax.rem(place, tiles) * TILE, TILE)
+            for k in range(partners):
+
+                @pl.when(lax.div(place, tiles) == k)
+                def _(k=k, row=row, reader=reader, slot=slot):
+                    copy_of(k, row, reader, slot).start()
+
+        for reader, slot in wanted:
+            copy_of(0, 0, reader, slot).wait()
 
     held = [] if buffer is None else [buffer]
     return pl.pallas_call(
         kernel,
-        grid_spec=pltpu.PrefetchScalarGridSpec(
-            num_scalar_prefetch=1,
-            grid=(1,),
-            in_specs=[pl.BlockSpec((count, rows, size), lambda i, _: (0, 0, 0))] * partners
-            + [pl.BlockSpec(memory_space=pl.ANY)] * len(held),
-            out_specs=pl.BlockSpec(memory_space=pl.ANY),
-            scratch_shapes=[
-                pltpu.VMEM((partners * tiles, count, TILE, size), BF16),
-                pltpu.SemaphoreType.DMA((readers * CAP,)),
-            ],
-        ),
+        in_specs=[pl.BlockSpec(memory_space=pltpu.SMEM)]
+        + [pl.BlockSpec(memory_space=pl.ANY)] * partners
+        + [pl.BlockSpec(memory_space=pltpu.HBM)] * len(held),
+        out_specs=pl.BlockSpec(memory_space=pltpu.HBM),
+        scratch_shapes=[pltpu.SemaphoreType.DMA((readers * CAP,))],
         out_shape=jax.ShapeDtypeStruct((readers, 2, CAP, count, TILE, size), BF16),
         input_output_aliases={1 + partners: 0} if held else {},
+        compiler_params=pltpu.CompilerParams(vmem_limit_bytes=50 * 2**20),
     )(picks, *pieces, *held)
 
 
@@ -154,10 +153,10 @@
                 )
                 row_top = jnp.max(scores, axis=-1, keepdims=True)
                 weights = jnp.exp2((scores - row_top) * factor)
-                row_total = jnp.sum(weights, axis=-1, keepdims=True)
                 value_rows = jnp.concatenate([v_pool[i] for i in ids], axis=0)
-                mixed = jnp.dot(weights.astype(BF16), value_rows, preferred_element_type=F32)
-                outs[k][0, at, :] = (mixed / row_total).astype(BF16)
+                beside = jnp.concatenate([value_rows, jnp.ones_like(value_rows)], axis=1)
+                mixed = jnp.dot(weights.astype(BF16), beside, preferred_element_type=F32)
+                outs[k][0, at, :] = (mixed[:, :size] / mixed[:, size:]).astype(BF16)
 
     head_spec = pl.BlockSpec((1, rows, size), lambda h, _: (h, 0, 0))
     far_specs = [
@@ -243,7 +242,7 @@
     asked = [exchange(query_parts, c) for c in range(len(chunks))]
     answers = []
     for c in range(len(chunks)):
-        outs = attend(asked[c], *ready[c], places)
+        outs, _ = lax.optimization_barrier((attend(asked[c], *ready[c], places), [pieces[2] for pieces in asked]))
         answers.append([swap(outs[k], k) for k in range(partners)])
     return from_partners([[answers[c][k] for c in range(len(chunks))] for k in range(partners)], here_arg, chunks, heads)
 

time: 263 us -> 258 us (0.981)
  waiting for transfers between devices: 142 us -> 162 us
  Pallas kernels: 68.3 us -> 48.8 us
  local copies, waits for them, and re-layouts: 6.28 us -> 2.17 us
    ppermute x24, waiting for transfers between devices: 142 us -> 162 us  [swap(): lax.ppermute(piece, 'head', [(i, i ^ k) for i in range(partners)])]
    pallas_call x2, Pallas kernels: 40.1 us -> 26.5 us  [attend(): pl.pallas_call(kernel, grid_spec=pltpu.PrefetchScalarGridSpec(num_scalar_...]
    pallas_call x4, Pallas kernels: 14.9 us -> 9.07 us  [pick_tiles(): pl.pallas_call(kernel, in_specs=[pl.BlockSpec(memory_space=pltpu.SMEM)] +...]
    unnamed x69, local copies, waits for them, and re-layouts: 4.47 us -> 0.96 us
  transfers between devices with their start and end apart: 26 -> 26, of which waited for: 17 -> 18; matrix products, arithmetic and copies ran while one was open for 1% -> 1% of each run, Pallas kernels for 22% -> 16%
where the time goes in v4:
time: 258 us
  waiting for transfers between devices  162 us (63%)
  Pallas kernels  48.8 us (19%)
  starting transfers between devices  42.9 us (17%)
    ppermute x24, waiting for transfers between devices, swap(): lax.ppermute(piece, 'head', [(i, i ^ k) for i in range(partners)])  162 us
    ppermute x24, starting transfers between devices, swap(): lax.ppermute(piece, 'head', [(i, i ^ k) for i in range(partners)])  32.6 us
    pallas_call x2, Pallas kernels, attend(): pl.pallas_call(kernel, grid_spec=pltpu.PrefetchScalarGridSpec(num_scalar_...  26.5 us
    all_to_all x2, starting transfers between devices, share(): return [lax.all_to_all(sent, 'seq', 0, 0, tiled=True)]  10.3 us
    pallas_call x3, Pallas kernels, by_partner(): pl.pallas_call(kernel, grid_spec=pltpu.PrefetchScalarGridSpec(num_scalar_...  9.97 us
    pallas_call x4, Pallas kernels, pick_tiles(): pl.pallas_call(kernel, in_specs=[pl.BlockSpec(memory_space=pltpu.SMEM)] +...  9.07 us
  transfers between devices with their start and end apart: 26, of which 18 were waited for; matrix products, arithmetic and copies ran while one was open for 1% of the time, Pallas kernels for 16%

profile of v4, /device:TPU:10, one launch (start us, length us, event | category | flops | bytes accessed | tf_op | source)
XLA Modules:
  0.0 257.8 jit_solution(14207089780087752748)
XLA Ops:
  0.0 3.3 %shard_map.47 = (bf16[5,256,128]{2,1,0:T(8,128)(2,1)}, bf16[5,256,128]{2,1,0:T(8,128)(2,1)}, bf16[5,256,128]{2,1,0:T(8,128)(2,1)}, bf16[5,256,128]{2,1,0:T(8,128...) custom-call(s32[1]{0:T(128)} %bitcast.here_ref, ...), custom_call_target="tpu_custom_call" | custom-call | tf_op jit(solution)/shard_map/pallas_call | solution.py:41
  3.3 0.5 collective-permute-start.12
  3.8 2.6 %collective-permute-start.13 = (bf16[5,256,128]{2,1,0:T(8,128)(2,1)}, bf16[5,256,128]{2,1,0:T(8,128)(2,1)S(1)}, u32[]{:S(2)}, u32[]{:S(2)}) collective-permute-start(bf16[5,256,128]{2,1,0:T(8,128)(2,1)} %get-tuple-element.86), channel_id=1, source_target_pairs={{0,2},{1,3},{2,0},{3,1},{4,6},{5,7},{6,4},{7,5},{8,10},{9,11},{10,... | collective-permute-start | bytes 983048 | tf_op jit(solution)/shard_map/ppermute | solution.py:222
  6.4 0.5 collective-permute-start.14
  6.9 3.3 %shard_map.48 = (bf16[5,256,128]{2,1,0:T(8,128)(2,1)}, bf16[5,256,128]{2,1,0:T(8,128)(2,1)}, bf16[5,256,128]{2,1,0:T(8,128)(2,1)}, bf16[5,256,128]{2,1,0:T(8,128...) custom-call(s32[1]{0:T(128)} %bitcast.here_ref, ...), custom_call_target="tpu_custom_call" | custom-call | tf_op jit(solution)/shard_map/pallas_call | solution.py:41
  10.2 1.4 collective-permute-start.15
  11.6 2.2 collective-permute-start.16
  13.8 0.1 copy.11
  14.0 0.3 compare_reduce_fusion
  14.3 3.3 %shard_map.46 = (bf16[5,256,128]{2,1,0:T(8,128)(2,1)}, bf16[5,256,128]{2,1,0:T(8,128)(2,1)}, bf16[5,256,128]{2,1,0:T(8,128)(2,1)}, bf16[5,256,128]{2,1,0:T(8,128...) custom-call(s32[1]{0:T(128)} %bitcast.here_ref, ...), custom_call_target="tpu_custom_call" | custom-call | tf_op jit(solution)/shard_map/pallas_call | solution.py:41
  17.6 0.2 reduce_window_sum.18
  17.8 0.7 collective-permute-done.12.refs_1_.refs_5_
  18.5 2.7 %collective-permute-start.17 = (bf16[5,256,128]{2,1,0:T(8,128)(2,1)}, bf16[5,256,128]{2,1,0:T(8,128)(2,1)S(1)}, u32[]{:S(2)}, u32[]{:S(2)}) collective-permute-start(bf16[5,256,128]{2,1,0:T(8,128)(2,1)} %get-tuple-element.91), channel_id=1, source_target_pairs={{0,3},{1,2},{2,1},{3,0},{4,7},{5,6},{6,5},{7,4},{8,11},{9,10},{10,... | collective-permute-start | bytes 983048 | tf_op jit(solution)/shard_map/ppermute | solution.py:222
  21.2 0.1 select_reduce_fusion.1
  21.4 0.1 copy.13.pick_ref
  21.5 7.5 %collective-permute-done.13.refs_2_.refs_6_ = bf16[5,256,128]{2,1,0:T(8,128)(2,1)S(1)} collective-permute-done((bf16[5,256,128]{2,1,0:T(8,128)(2,1)}, bf16[5,256,128]{2,1,0:T(8,128)(2,1)S(1)}, u32[]{:S(2)}, u32[]{:S(2)}) %collective-permute-start.13) | collective-permute-done | bytes 327712 | tf_op jit(solution)/shard_map/ppermute | solution.py:222
  29.0 21.9 %collective-permute-done.14.refs_3_.refs_7_ = bf16[5,256,128]{2,1,0:T(8,128)(2,1)S(1)} collective-permute-done((bf16[5,256,128]{2,1,0:T(8,128)(2,1)}, bf16[5,256,128]{2,1,0:T(8,128)(2,1)S(1)}, u32[]{:S(2)}, u32[]{:S(2)}) %collective-permute-start.14) | collective-permute-done | bytes 327712 | tf_op jit(solution)/shard_map/ppermute | solution.py:222
  50.8 2.3 shard_map.52.refs_4_
  53.2 3.9 %collective-permute-done.16.refs_2_.refs_10_ = bf16[5,256,128]{2,1,0:T(8,128)(2,1)S(1)} collective-permute-done((bf16[5,256,128]{2,1,0:T(8,128)(2,1)}, bf16[5,256,128]{2,1,0:T(8,128)(2,1)S(1)}, u32[]{:S(2)}, u32[]{:S(2)}) %collective-permute-start.16) | collective-permute-done | bytes 327712 | tf_op jit(solution)/shard_map/ppermute | solution.py:222
  57.1 6.4 %collective-permute-done.17.refs_3_.refs_11_ = bf16[5,256,128]{2,1,0:T(8,128)(2,1)S(1)} collective-permute-done((bf16[5,256,128]{2,1,0:T(8,128)(2,1)}, bf16[5,256,128]{2,1,0:T(8,128)(2,1)S(1)}, u32[]{:S(2)}, u32[]{:S(2)}) %collective-permute-start.17) | collective-permute-done | bytes 327712 | tf_op jit(solution)/shard_map/ppermute | solution.py:222
  63.5 2.2 shard_map.53
  65.8 5.2 %all-to-all-start.1 = ((bf16[8,2,2,5,128,128]{5,4,3,2,1,0:T(8,128)(2,1)}), bf16[8,2,2,5,128,128]{5,4,3,2,1,0:T(8,128)(2,1)}, u32[]{:S(2)}, u32[]{:S(2)}) async-start(bf16[8,2,2,5,128,128]{5,4,3,2,1,0:T(8,128)(2,1)} %shard_map.53), calls=%async_computation.1 | async-start | bytes 10485760 | tf_op jit(solution)/shard_map/all_to_all | solution.py:234
  71.0 3.0 %collective-permute-start.4 = (bf16[5,256,128]{2,1,0:T(8,128)(2,1)S(1)}, bf16[5,256,128]{2,1,0:T(8,128)(2,1)S(1)}, u32[]{:S(2)}, u32[]{:S(2)}) collective-permute-start(bf16[5,256,128]{2,1,0:T(8,128)(2,1)S(1)} %copy-done.30), channel_id=1, source_target_pairs={{0,2},{1,3},{2,0},{3,1},{4,6},{5,7},{6,4},{7,5},{8,10},{9,11},{10,... | collective-permute-start | bytes 983048 | tf_op jit(solution)/shard_map/ppermute | solution.py:222
  74.1 0.4 collective-permute-start.5
  74.5 1.1 collective-permute-start.6
  75.6 2.0 collective-permute-start.7
  77.6 8.4 %collective-permute-done.3.refs_1_.refs_5_ = bf16[5,256,128]{2,1,0:T(8,128)(2,1)S(1)} collective-permute-done((bf16[5,256,128]{2,1,0:T(8,128)(2,1)}, bf16[5,256,128]{2,1,0:T(8,128)(2,1)S(1)}, u32[]{:S(2)}, u32[]{:S(2)}) %collective-permute-start.3) | collective-permute-done | bytes 327712 | tf_op jit(solution)/shard_map/ppermute | solution.py:222
  85.9 1.0 collective-permute-start.8
  86.9 9.3 %collective-permute-done.4.refs_2_.refs_6_ = bf16[5,256,128]{2,1,0:T(8,128)(2,1)S(1)} collective-permute-done((bf16[5,256,128]{2,1,0:T(8,128)(2,1)S(1)}, bf16[5,256,128]{2,1,0:T(8,128)(2,1)S(1)}, u32[]{:S(2)}, u32[]{:S(2)}) %collective-permute-start.4) | collective-permute-done | bytes 327712 | tf_op jit(solution)/shard_map/ppermute | solution.py:222
  96.3 22.0 %collective-permute-done.5.refs_3_.refs_7_ = bf16[5,256,128]{2,1,0:T(8,128)(2,1)S(1)} collective-permute-done((bf16[5,256,128]{2,1,0:T(8,128)(2,1)S(1)}, bf16[5,256,128]{2,1,0:T(8,128)(2,1)S(1)}, u32[]{:S(2)}, u32[]{:S(2)}) %collective-permute-start.5) | collective-permute-done | bytes 327712 | tf_op jit(solution)/shard_map/ppermute | solution.py:222
  118.2 2.3 shard_map.49.refs_4_
  120.6 3.9 %collective-permute-done.7.refs_2_.refs_10_ = bf16[5,256,128]{2,1,0:T(8,128)(2,1)S(1)} collective-permute-done((bf16[5,256,128]{2,1,0:T(8,128)(2,1)}, bf16[5,256,128]{2,1,0:T(8,128)(2,1)S(1)}, u32[]{:S(2)}, u32[]{:S(2)}) %collective-permute-start.7) | collective-permute-done | bytes 327712 | tf_op jit(solution)/shard_map/ppermute | solution.py:222
  124.5 6.7 %collective-permute-done.8.refs_3_.refs_11_ = bf16[5,256,128]{2,1,0:T(8,128)(2,1)S(1)} collective-permute-done((bf16[5,256,128]{2,1,0:T(8,128)(2,1)}, bf16[5,256,128]{2,1,0:T(8,128)(2,1)S(1)}, u32[]{:S(2)}, u32[]{:S(2)}) %collective-permute-start.8) | collective-permute-done | bytes 327712 | tf_op jit(solution)/shard_map/ppermute | solution.py:222
  131.2 2.2 shard_map.50
  133.6 5.1 %all-to-all-start = ((bf16[8,2,2,5,128,128]{5,4,3,2,1,0:T(8,128)(2,1)}), bf16[8,2,2,5,128,128]{5,4,3,2,1,0:T(8,128)(2,1)}, u32[]{:S(2)}, u32[]{:S(2)}) async-start(bf16[8,2,2,5,128,128]{5,4,3,2,1,0:T(8,128)(2,1)} %shard_map.50), calls=%async_computation | async-start | bytes 10485760 | tf_op jit(solution)/shard_map/all_to_all | solution.py:234
  138.7 3.0 %collective-permute-start.10 = (bf16[5,256,128]{2,1,0:T(8,128)(2,1)S(1)}, bf16[5,256,128]{2,1,0:T(8,128)(2,1)}, u32[]{:S(2)}, u32[]{:S(2)}) collective-permute-start(bf16[5,256,128]{2,1,0:T(8,128)(2,1)S(1)} %copy-done.27), channel_id=1, source_target_pairs={{0,1},{1,0},{2,3},{3,2},{4,5},{5,4},{6,7},{7,6},{8,9},{9,8},{10,11... | collective-permute-start | bytes 983048 | tf_op jit(solution)/shard_map/ppermute | solution.py:222
  141.7 0.4 collective-permute-start.11
  142.1 2.0 collective-permute-start.1
  144.1 1.1 collective-permute-start
  145.3 0.1 fusion
  145.4 0.1 reshape.137
  145.5 0.2 reduce_window_sum.17
  145.7 0.1 select_n.76
  145.8 0.3 select_reduce_fusion
  146.3 0.1 broadcast_in_dim.65
  146.4 0.6 gather_fusion
  147.0 6.8 %collective-permute-done.9.refs_2_ = bf16[5,256,128]{2,1,0:T(8,128)(2,1)S(1)} collective-permute-done((bf16[5,256,128]{2,1,0:T(8,128)(2,1)S(1)}, bf16[5,256,128]{2,1,0:T(8,128)(2,1)S(1)}, u32[]{:S(2)}, u32[]{:S(2)}) %collective-permute-start.9) | collective-permute-done | bytes 327712 | tf_op jit(solution)/shard_map/ppermute | solution.py:222
  153.8 1.6 collective-permute-start.2
  155.3 0.7 broadcast_select_fusion.place_ref
  156.0 1.4 collective-permute-done.10.refs_1_
  157.4 19.7 %collective-permute-done.11.refs_3_ = bf16[5,256,128]{2,1,0:T(8,128)(2,1)} collective-permute-done((bf16[5,256,128]{2,1,0:T(8,128)(2,1)S(1)}, bf16[5,256,128]{2,1,0:T(8,128)(2,1)}, u32[]{:S(2)}, u32[]{:S(2)}) %collective-permute-start.11) | collective-permute-done | bytes 327712 | tf_op jit(solution)/shard_map/ppermute | solution.py:222
  177.1 13.2 %shard_map.54 = (bf16[5,256,128]{2,1,0:T(8,128)(2,1)}, bf16[5,256,128]{2,1,0:T(8,128)(2,1)}, bf16[5,256,128]{2,1,0:T(8,128)(2,1)}, bf16[5,256,128]{2,1,0:T(8,128)(2,1)}) custom-call(s32[8,10]{1,0:T(8,128)} %broadcast_select_fusion.place_ref, bf16[5,256,128]{2,1,0:T(8,128)(2,1)} %get-tuple-element.81.refs_0_, ...), custom_call_target="tpu_custom_call" | custom-call | flops 3355443200 | bytes 10485760 | tf_op jit(solution)/shard_map/pallas_call | solution.py:167
  190.4 2.0 collective-permute-start.19
  192.4 1.6 collective-permute-start.23
  193.9 4.1 %collective-permute-done.2.refs_3_ = bf16[5,256,128]{2,1,0:T(8,128)(2,1)} collective-permute-done((bf16[5,256,128]{2,1,0:T(8,128)(2,1)S(1)}, bf16[5,256,128]{2,1,0:T(8,128)(2,1)}, u32[]{:S(2)}, u32[]{:S(2)}) %collective-permute-start.2) | collective-permute-done | bytes 327712 | tf_op jit(solution)/shard_map/ppermute | solution.py:222
  198.1 13.2 %shard_map.51 = (bf16[5,256,128]{2,1,0:T(8,128)(2,1)}, bf16[5,256,128]{2,1,0:T(8,128)(2,1)}, bf16[5,256,128]{2,1,0:T(8,128)(2,1)}, bf16[5,256,128]{2,1,0:T(8,128)(2,1)}) custom-call(s32[8,10]{1,0:T(8,128)} %broadcast_select_fusion.place_ref, bf16[5,256,128]{2,1,0:T(8,128)(2,1)} %get-tuple-element.62.refs_0_, bf16[5,256,128]{2,1,0:T(8,128)(2,1)} %copy-done.32, ...), custom_call_target="tpu_custom_call" | custom-call | flops 3355443200 | bytes 10485760 | tf_op jit(solution)/shard_map/pallas_call | solution.py:167
  211.4 2.6 collective-permute-start.20
  214.0 0.9 collective-permute-start.22
  214.9 2.3 collective-permute-done.21.refs_5_
  217.1 23.0 %collective-permute-done.23.refs_7_ = bf16[5,256,128]{2,1,0:T(8,128)(2,1)S(1)} collective-permute-done((bf16[5,256,128]{2,1,0:T(8,128)(2,1)}, bf16[5,256,128]{2,1,0:T(8,128)(2,1)S(1)}, u32[]{:S(2)}, u32[]{:S(2)}) %collective-permute-start.23) | collective-permute-done | bytes 327712 | tf_op jit(solution)/shard_map/ppermute | solution.py:222
  240.1 5.1 %collective-permute-done.20.refs_4_ = bf16[5,256,128]{2,1,0:T(8,128)(2,1)S(1)} collective-permute-done((bf16[5,256,128]{2,1,0:T(8,128)(2,1)}, bf16[5,256,128]{2,1,0:T(8,128)(2,1)S(1)}, u32[]{:S(2)}, u32[]{:S(2)}) %collective-permute-start.20) | collective-permute-done | bytes 327712 | tf_op jit(solution)/shard_map/ppermute | solution.py:222
  245.2 8.4 %collective-permute-done.22.refs_6_ = bf16[5,256,128]{2,1,0:T(8,128)(2,1)S(1)} collective-permute-done((bf16[5,256,128]{2,1,0:T(8,128)(2,1)}, bf16[5,256,128]{2,1,0:T(8,128)(2,1)S(1)}, u32[]{:S(2)}, u32[]{:S(2)}) %collective-permute-start.22) | collective-permute-done | bytes 327712 | tf_op jit(solution)/shard_map/ppermute | solution.py:222
  253.7 0.7 copy-done.21
  254.4 3.3 %shard_map.55 = bf16[256,40,128]{2,1,0:T(8,128)(2,1)} custom-call(s32[1]{0:T(128)} %bitcast.here_ref, bf16[5,256,128]{2,1,0:T(8,128)(2,1)} %get-tuple-element.80.refs_0_, bf16[5,256,128]{2,1,0:T(8,128)(2,1)} %get-tuple-element.96.refs_1_, bf16[5,256,128]{2,1,0:T(8,128)(2,1)} %copy-done.19, bf16[5,256,128]{2,1,0:T(8,128)(2,1)} %copy-done.16, ...), custom_call_target="tpu_custom_call" | custom-call | tf_op jit(solution)/shard_map/pallas_call | solution.py:70
  (93 shorter events, 0.7 us)
Async XLA Ops:
  0.0 13.8 %copy-start.22 = (s32[64,10]{0,1:T(8,128)S(1)}, s32[64,10]{0,1:T(8,128)}, u32[]{:S(2)}) copy-start(s32[64,10]{0,1:T(8,128)} %param.7) | copy-start | bytes 7684
  3.3 47.5 %copy-start.2 = (bf16[5,256,128]{2,1,0:T(8,128)(2,1)S(1)}, bf16[5,256,128]{2,1,0:T(8,128)(2,1)}, u32[]{:S(2)}) copy-start(bf16[5,256,128]{2,1,0:T(8,128)(2,1)} %get-tuple-element.84.refs_0_.refs_4_) | copy-start | bytes 983044
  3.3 15.2 %collective-permute-start.12 = (bf16[5,256,128]{2,1,0:T(8,128)(2,1)}, bf16[5,256,128]{2,1,0:T(8,128)(2,1)S(1)}, u32[]{:S(2)}, u32[]{:S(2)}) collective-permute-start(bf16[5,256,128]{2,1,0:T(8,128)(2,1)} %get-tuple-element.85), channel_id=1, source_target_pairs={{0,1},{1,0},{2,3},{3,2},{4,5},{5,4},{6,7},{7,6},{8,9},{9,8},{10,11... | collective-permute-start | bytes 983048 | tf_op jit(solution)/shard_map/ppermute | solution.py:222
  3.8 25.1 %collective-permute-start.13 = (bf16[5,256,128]{2,1,0:T(8,128)(2,1)}, bf16[5,256,128]{2,1,0:T(8,128)(2,1)S(1)}, u32[]{:S(2)}, u32[]{:S(2)}) collective-permute-start(bf16[5,256,128]{2,1,0:T(8,128)(2,1)} %get-tuple-element.86), channel_id=1, source_target_pairs={{0,2},{1,3},{2,0},{3,1},{4,6},{5,7},{6,4},{7,5},{8,10},{9,11},{10,... | collective-permute-start | bytes 983048 | tf_op jit(solution)/shard_map/ppermute | solution.py:222
  6.4 44.4 %collective-permute-start.14 = (bf16[5,256,128]{2,1,0:T(8,128)(2,1)}, bf16[5,256,128]{2,1,0:T(8,128)(2,1)S(1)}, u32[]{:S(2)}, u32[]{:S(2)}) collective-permute-start(bf16[5,256,128]{2,1,0:T(8,128)(2,1)} %get-tuple-element.87), channel_id=1, source_target_pairs={{0,3},{1,2},{2,1},{3,0},{4,7},{5,6},{6,5},{7,4},{8,11},{9,10},{10,... | collective-permute-start | bytes 983048 | tf_op jit(solution)/shard_map/ppermute | solution.py:222
  10.2 53.3 %copy-start.6 = (bf16[5,256,128]{2,1,0:T(8,128)(2,1)S(1)}, bf16[5,256,128]{2,1,0:T(8,128)(2,1)}, u32[]{:S(2)}) copy-start(bf16[5,256,128]{2,1,0:T(8,128)(2,1)} %get-tuple-element.88.refs_0_.refs_8_) | copy-start | bytes 983044
  10.2 43.0 %collective-permute-start.15 = (bf16[5,256,128]{2,1,0:T(8,128)(2,1)}, bf16[5,256,128]{2,1,0:T(8,128)(2,1)S(1)}, u32[]{:S(2)}, u32[]{:S(2)}) collective-permute-start(bf16[5,256,128]{2,1,0:T(8,128)(2,1)} %get-tuple-element.89), channel_id=1, source_target_pairs={{0,1},{1,0},{2,3},{3,2},{4,5},{5,4},{6,7},{7,6},{8,9},{9,8},{10,11... | collective-permute-start | bytes 983048 | tf_op jit(solution)/shard_map/ppermute | solution.py:222
  11.6 45.4 %collective-permute-start.16 = (bf16[5,256,128]{2,1,0:T(8,128)(2,1)}, bf16[5,256,128]{2,1,0:T(8,128)(2,1)S(1)}, u32[]{:S(2)}, u32[]{:S(2)}) collective-permute-start(bf16[5,256,128]{2,1,0:T(8,128)(2,1)} %get-tuple-element.90), channel_id=1, source_target_pairs={{0,2},{1,3},{2,0},{3,1},{4,6},{5,7},{6,4},{7,5},{8,10},{9,11},{10,... | collective-permute-start | bytes 983048 | tf_op jit(solution)/shard_map/ppermute | solution.py:222
  18.5 47.2 %copy-start.3 = (bf16[5,256,128]{2,1,0:T(8,128)(2,1)}, bf16[5,256,128]{2,1,0:T(8,128)(2,1)S(1)}, u32[]{:S(2)}) copy-start(bf16[5,256,128]{2,1,0:T(8,128)(2,1)S(1)} %collective-permute-done.12.refs_1_.refs_5_) | copy-start | bytes 983044
  18.5 44.9 %collective-permute-start.17 = (bf16[5,256,128]{2,1,0:T(8,128)(2,1)}, bf16[5,256,128]{2,1,0:T(8,128)(2,1)S(1)}, u32[]{:S(2)}, u32[]{:S(2)}) collective-permute-start(bf16[5,256,128]{2,1,0:T(8,128)(2,1)} %get-tuple-element.91), channel_id=1, source_target_pairs={{0,3},{1,2},{2,1},{3,0},{4,7},{5,6},{6,5},{7,4},{8,11},{9,10},{10,... | collective-permute-start | bytes 983048 | tf_op jit(solution)/shard_map/ppermute | solution.py:222
  29.0 36.7 %copy-start.4 = (bf16[5,256,128]{2,1,0:T(8,128)(2,1)}, bf16[5,256,128]{2,1,0:T(8,128)(2,1)S(1)}, u32[]{:S(2)}) copy-start(bf16[5,256,128]{2,1,0:T(8,128)(2,1)S(1)} %collective-permute-done.13.refs_2_.refs_6_) | copy-start | bytes 983044
  50.8 14.9 %copy-start.5 = (bf16[5,256,128]{2,1,0:T(8,128)(2,1)}, bf16[5,256,128]{2,1,0:T(8,128)(2,1)S(1)}, u32[]{:S(2)}) copy-start(bf16[5,256,128]{2,1,0:T(8,128)(2,1)S(1)} %collective-permute-done.14.refs_3_.refs_7_) | copy-start | bytes 983044
  53.2 12.6 %copy-start.7 = (bf16[5,256,128]{2,1,0:T(8,128)(2,1)}, bf16[5,256,128]{2,1,0:T(8,128)(2,1)S(1)}, u32[]{:S(2)}) copy-start(bf16[5,256,128]{2,1,0:T(8,128)(2,1)S(1)} %collective-permute-done.15.refs_1_.refs_9_) | copy-start | bytes 983044
  57.1 8.7 %copy-start.8 = (bf16[5,256,128]{2,1,0:T(8,128)(2,1)}, bf16[5,256,128]{2,1,0:T(8,128)(2,1)S(1)}, u32[]{:S(2)}) copy-start(bf16[5,256,128]{2,1,0:T(8,128)(2,1)S(1)} %collective-permute-done.16.refs_2_.refs_10_) | copy-start | bytes 983044
  63.5 2.3 copy-start.10
  65.8 5.3 %copy-start.30 = (bf16[5,256,128]{2,1,0:T(8,128)(2,1)S(1)}, bf16[5,256,128]{2,1,0:T(8,128)(2,1)}, u32[]{:S(2)}) copy-start(bf16[5,256,128]{2,1,0:T(8,128)(2,1)} %get-tuple-element.68) | copy-start | bytes 983044
  65.8 8.3 %copy-start.29 = (bf16[5,256,128]{2,1,0:T(8,128)(2,1)S(1)}, bf16[5,256,128]{2,1,0:T(8,128)(2,1)}, u32[]{:S(2)}) copy-start(bf16[5,256,128]{2,1,0:T(8,128)(2,1)} %get-tuple-element.69) | copy-start | bytes 983044
  65.8 52.4 %copy-start = (bf16[5,256,128]{2,1,0:T(8,128)(2,1)S(1)}, bf16[5,256,128]{2,1,0:T(8,128)(2,1)}, u32[]{:S(2)}) copy-start(bf16[5,256,128]{2,1,0:T(8,128)(2,1)} %get-tuple-element.66.refs_0_.refs_4_) | copy-start | bytes 983044
  65.8 67.8 %all-to-all-start.1 = ((bf16[8,2,2,5,128,128]{5,4,3,2,1,0:T(8,128)(2,1)}), bf16[8,2,2,5,128,128]{5,4,3,2,1,0:T(8,128)(2,1)}, u32[]{:S(2)}, u32[]{:S(2)}) async-start(bf16[8,2,2,5,128,128]{5,4,3,2,1,0:T(8,128)(2,1)} %shard_map.53), calls=%async_computation.1 | async-start | bytes 10485760 | tf_op jit(solution)/shard_map/all_to_all | solution.py:234
  71.0 60.2 %copy-start.1 = (bf16[5,256,128]{2,1,0:T(8,128)(2,1)S(1)}, bf16[5,256,128]{2,1,0:T(8,128)(2,1)}, u32[]{:S(2)}) copy-start(bf16[5,256,128]{2,1,0:T(8,128)(2,1)} %get-tuple-element.70.refs_0_.refs_8_) | copy-start | bytes 983044
  71.0 14.9 %collective-permute-start.3 = (bf16[5,256,128]{2,1,0:T(8,128)(2,1)}, bf16[5,256,128]{2,1,0:T(8,128)(2,1)S(1)}, u32[]{:S(2)}, u32[]{:S(2)}) collective-permute-start(bf16[5,256,128]{2,1,0:T(8,128)(2,1)} %get-tuple-element.67), channel_id=1, source_target_pairs={{0,1},{1,0},{2,3},{3,2},{4,5},{5,4},{6,7},{7,6},{8,9},{9,8},{10,11... | collective-permute-start | bytes 983048 | tf_op jit(solution)/shard_map/ppermute | solution.py:222
  71.0 25.2 %collective-permute-start.4 = (bf16[5,256,128]{2,1,0:T(8,128)(2,1)S(1)}, bf16[5,256,128]{2,1,0:T(8,128)(2,1)S(1)}, u32[]{:S(2)}, u32[]{:S(2)}) collective-permute-start(bf16[5,256,128]{2,1,0:T(8,128)(2,1)S(1)} %copy-done.30), channel_id=1, source_target_pairs={{0,2},{1,3},{2,0},{3,1},{4,6},{5,7},{6,4},{7,5},{8,10},{9,11},{10,... | collective-permute-start | bytes 983048 | tf_op jit(solution)/shard_map/ppermute | solution.py:222
  74.1 44.2 %collective-permute-start.5 = (bf16[5,256,128]{2,1,0:T(8,128)(2,1)S(1)}, bf16[5,256,128]{2,1,0:T(8,128)(2,1)S(1)}, u32[]{:S(2)}, u32[]{:S(2)}) collective-permute-start(bf16[5,256,128]{2,1,0:T(8,128)(2,1)S(1)} %copy-done.29), channel_id=1, source_target_pairs={{0,3},{1,2},{2,1},{3,0},{4,7},{5,6},{6,5},{7,4},{8,11},{9,10},{10,... | collective-permute-start | bytes 983048 | tf_op jit(solution)/shard_map/ppermute | solution.py:222
  74.5 46.0 %collective-permute-start.6 = (bf16[5,256,128]{2,1,0:T(8,128)(2,1)}, bf16[5,256,128]{2,1,0:T(8,128)(2,1)S(1)}, u32[]{:S(2)}, u32[]{:S(2)}) collective-permute-start(bf16[5,256,128]{2,1,0:T(8,128)(2,1)} %get-tuple-element.71), channel_id=1, source_target_pairs={{0,1},{1,0},{2,3},{3,2},{4,5},{5,4},{6,7},{7,6},{8,9},{9,8},{10,11... | collective-permute-start | bytes 983048 | tf_op jit(solution)/shard_map/ppermute | solution.py:222
  75.6 48.9 %collective-permute-start.7 = (bf16[5,256,128]{2,1,0:T(8,128)(2,1)}, bf16[5,256,128]{2,1,0:T(8,128)(2,1)S(1)}, u32[]{:S(2)}, u32[]{:S(2)}) collective-permute-start(bf16[5,256,128]{2,1,0:T(8,128)(2,1)} %get-tuple-element.72), channel_id=1, source_target_pairs={{0,2},{1,3},{2,0},{3,1},{4,6},{5,7},{6,4},{7,5},{8,10},{9,11},{10,... | collective-permute-start | bytes 983048 | tf_op jit(solution)/shard_map/ppermute | solution.py:222
  85.9 47.5 %copy-start.9 = (bf16[5,256,128]{2,1,0:T(8,128)(2,1)}, bf16[5,256,128]{2,1,0:T(8,128)(2,1)S(1)}, u32[]{:S(2)}) copy-start(bf16[5,256,128]{2,1,0:T(8,128)(2,1)S(1)} %collective-permute-done.3.refs_1_.refs_5_) | copy-start | bytes 983044
  85.9 45.3 %collective-permute-start.8 = (bf16[5,256,128]{2,1,0:T(8,128)(2,1)}, bf16[5,256,128]{2,1,0:T(8,128)(2,1)S(1)}, u32[]{:S(2)}, u32[]{:S(2)}) collective-permute-start(bf16[5,256,128]{2,1,0:T(8,128)(2,1)} %get-tuple-element.73), channel_id=1, source_target_pairs={{0,3},{1,2},{2,1},{3,0},{4,7},{5,6},{6,5},{7,4},{8,11},{9,10},{10,... | collective-permute-start | bytes 983048 | tf_op jit(solution)/shard_map/ppermute | solution.py:222
  96.3 37.2 %copy-start.11 = (bf16[5,256,128]{2,1,0:T(8,128)(2,1)}, bf16[5,256,128]{2,1,0:T(8,128)(2,1)S(1)}, u32[]{:S(2)}) copy-start(bf16[5,256,128]{2,1,0:T(8,128)(2,1)S(1)} %collective-permute-done.4.refs_2_.refs_6_) | copy-start | bytes 983044
  118.2 15.3 %copy-start.12 = (bf16[5,256,128]{2,1,0:T(8,128)(2,1)}, bf16[5,256,128]{2,1,0:T(8,128)(2,1)S(1)}, u32[]{:S(2)}) copy-start(bf16[5,256,128]{2,1,0:T(8,128)(2,1)S(1)} %collective-permute-done.5.refs_3_.refs_7_) | copy-start | bytes 983044
  120.5 12.9 %copy-start.13 = (bf16[5,256,128]{2,1,0:T(8,128)(2,1)}, bf16[5,256,128]{2,1,0:T(8,128)(2,1)S(1)}, u32[]{:S(2)}) copy-start(bf16[5,256,128]{2,1,0:T(8,128)(2,1)S(1)} %collective-permute-done.6.refs_1_.refs_9_) | copy-start | bytes 983044
  124.5 9.0 %copy-start.14 = (bf16[5,256,128]{2,1,0:T(8,128)(2,1)}, bf16[5,256,128]{2,1,0:T(8,128)(2,1)S(1)}, u32[]{:S(2)}) copy-start(bf16[5,256,128]{2,1,0:T(8,128)(2,1)S(1)} %collective-permute-done.7.refs_2_.refs_10_) | copy-start | bytes 983044
  131.2 2.3 copy-start.15
  133.5 8.2 %copy-start.26 = (bf16[5,256,128]{2,1,0:T(8,128)(2,1)S(1)}, bf16[5,256,128]{2,1,0:T(8,128)(2,1)}, u32[]{:S(2)}) copy-start(bf16[5,256,128]{2,1,0:T(8,128)(2,1)} %get-tuple-element.83) | copy-start | bytes 983044
  133.5 8.6 %copy-start.25 = (bf16[5,256,128]{2,1,0:T(8,128)(2,1)S(1)}, bf16[5,256,128]{2,1,0:T(8,128)(2,1)}, u32[]{:S(2)}) copy-start(bf16[5,256,128]{2,1,0:T(8,128)(2,1)} %get-tuple-element.64) | copy-start | bytes 983044
  133.5 10.6 %copy-start.24 = (bf16[5,256,128]{2,1,0:T(8,128)(2,1)S(1)}, bf16[5,256,128]{2,1,0:T(8,128)(2,1)}, u32[]{:S(2)}) copy-start(bf16[5,256,128]{2,1,0:T(8,128)(2,1)} %get-tuple-element.63) | copy-start | bytes 983044
  133.5 20.2 %copy-start.23 = (bf16[5,256,128]{2,1,0:T(8,128)(2,1)S(1)}, bf16[5,256,128]{2,1,0:T(8,128)(2,1)}, u32[]{:S(2)}) copy-start(bf16[5,256,128]{2,1,0:T(8,128)(2,1)} %get-tuple-element.65) | copy-start | bytes 983044
  133.6 5.1 %copy-start.28 = (bf16[5,256,128]{2,1,0:T(8,128)(2,1)S(1)}, bf16[5,256,128]{2,1,0:T(8,128)(2,1)}, u32[]{:S(2)}) copy-start(bf16[5,256,128]{2,1,0:T(8,128)(2,1)} %get-tuple-element.79) | copy-start | bytes 983044
  133.6 5.1 %copy-start.27 = (bf16[5,256,128]{2,1,0:T(8,128)(2,1)S(1)}, bf16[5,256,128]{2,1,0:T(8,128)(2,1)}, u32[]{:S(2)}) copy-start(bf16[5,256,128]{2,1,0:T(8,128)(2,1)} %get-tuple-element.82) | copy-start | bytes 983044
  133.6 64.5 %all-to-all-start = ((bf16[8,2,2,5,128,128]{5,4,3,2,1,0:T(8,128)(2,1)}), bf16[8,2,2,5,128,128]{5,4,3,2,1,0:T(8,128)(2,1)}, u32[]{:S(2)}, u32[]{:S(2)}) async-start(bf16[8,2,2,5,128,128]{5,4,3,2,1,0:T(8,128)(2,1)} %shard_map.50), calls=%async_computation | async-start | bytes 10485760 | tf_op jit(solution)/shard_map/all_to_all | solution.py:234
  138.6 15.1 %collective-permute-start.9 = (bf16[5,256,128]{2,1,0:T(8,128)(2,1)S(1)}, bf16[5,256,128]{2,1,0:T(8,128)(2,1)S(1)}, u32[]{:S(2)}, u32[]{:S(2)}) collective-permute-start(bf16[5,256,128]{2,1,0:T(8,128)(2,1)S(1)} %copy-done.28), channel_id=1, source_target_pairs={{0,2},{1,3},{2,0},{3,1},{4,6},{5,7},{6,4},{7,5},{8,10},{9,11},{10,... | collective-permute-start | bytes 983048 | tf_op jit(solution)/shard_map/ppermute | solution.py:222
  138.7 18.7 %collective-permute-start.10 = (bf16[5,256,128]{2,1,0:T(8,128)(2,1)S(1)}, bf16[5,256,128]{2,1,0:T(8,128)(2,1)}, u32[]{:S(2)}, u32[]{:S(2)}) collective-permute-start(bf16[5,256,128]{2,1,0:T(8,128)(2,1)S(1)} %copy-done.27), channel_id=1, source_target_pairs={{0,1},{1,0},{2,3},{3,2},{4,5},{5,4},{6,7},{7,6},{8,9},{9,8},{10,11... | collective-permute-start | bytes 983048 | tf_op jit(solution)/shard_map/ppermute | solution.py:222
  141.7 35.4 %collective-permute-start.11 = (bf16[5,256,128]{2,1,0:T(8,128)(2,1)S(1)}, bf16[5,256,128]{2,1,0:T(8,128)(2,1)}, u32[]{:S(2)}, u32[]{:S(2)}) collective-permute-start(bf16[5,256,128]{2,1,0:T(8,128)(2,1)S(1)} %copy-done.26), channel_id=1, source_target_pairs={{0,3},{1,2},{2,1},{3,0},{4,7},{5,6},{6,5},{7,4},{8,11},{9,10},{10,... | collective-permute-start | bytes 983048 | tf_op jit(solution)/shard_map/ppermute | solution.py:222
  142.1 48.2 %collective-permute-start.1 = (bf16[5,256,128]{2,1,0:T(8,128)(2,1)S(1)}, bf16[5,256,128]{2,1,0:T(8,128)(2,1)S(1)}, u32[]{:S(2)}, u32[]{:S(2)}) collective-permute-start(bf16[5,256,128]{2,1,0:T(8,128)(2,1)S(1)} %copy-done.25), channel_id=1, source_target_pairs={{0,2},{1,3},{2,0},{3,1},{4,6},{5,7},{6,4},{7,5},{8,10},{9,11},{10,... | collective-permute-start | bytes 983048 | tf_op jit(solution)/shard_map/ppermute | solution.py:222
  144.1 49.8 %collective-permute-start = (bf16[5,256,128]{2,1,0:T(8,128)(2,1)S(1)}, bf16[5,256,128]{2,1,0:T(8,128)(2,1)S(1)}, u32[]{:S(2)}, u32[]{:S(2)}) collective-permute-start(bf16[5,256,128]{2,1,0:T(8,128)(2,1)S(1)} %copy-done.24), channel_id=1, source_target_pairs={{0,1},{1,0},{2,3},{3,2},{4,5},{5,4},{6,7},{7,6},{8,9},{9,8},{10,11... | collective-permute-start | bytes 983048 | tf_op jit(solution)/shard_map/ppermute | solution.py:222
  153.8 23.4 %copy-start.33 = (bf16[5,256,128]{2,1,0:T(8,128)(2,1)}, bf16[5,256,128]{2,1,0:T(8,128)(2,1)S(1)}, u32[]{:S(2)}) copy-start(bf16[5,256,128]{2,1,0:T(8,128)(2,1)S(1)} %collective-permute-done.9.refs_2_) | copy-start | bytes 983044
  153.8 44.3 %collective-permute-start.2 = (bf16[5,256,128]{2,1,0:T(8,128)(2,1)S(1)}, bf16[5,256,128]{2,1,0:T(8,128)(2,1)}, u32[]{:S(2)}, u32[]{:S(2)}) collective-permute-start(bf16[5,256,128]{2,1,0:T(8,128)(2,1)S(1)} %copy-done.23), channel_id=1, source_target_pairs={{0,3},{1,2},{2,1},{3,0},{4,7},{5,6},{6,5},{7,4},{8,11},{9,10},{10,... | collective-permute-start | bytes 983048 | tf_op jit(solution)/shard_map/ppermute | solution.py:222
  190.4 7.7 %copy-start.31 = (bf16[5,256,128]{2,1,0:T(8,128)(2,1)}, bf16[5,256,128]{2,1,0:T(8,128)(2,1)S(1)}, u32[]{:S(2)}) copy-start(bf16[5,256,128]{2,1,0:T(8,128)(2,1)S(1)} %collective-permute-done.1.refs_2_) | copy-start | bytes 983044
  190.4 23.6 %collective-permute-start.19 = (bf16[5,256,128]{2,1,0:T(8,128)(2,1)}, bf16[5,256,128]{2,1,0:T(8,128)(2,1)S(1)}, u32[]{:S(2)}, u32[]{:S(2)}) collective-permute-start(bf16[5,256,128]{2,1,0:T(8,128)(2,1)} %get-tuple-element.98), channel_id=1, source_target_pairs={{0,1},{1,0},{2,3},{3,2},{4,5},{5,4},{6,7},{7,6},{8,9},{9,8},{10,11... | collective-permute-start | bytes 983048 | tf_op jit(solution)/shard_map/ppermute | solution.py:222
  192.4 24.8 %collective-permute-start.21 = (bf16[5,256,128]{2,1,0:T(8,128)(2,1)}, bf16[5,256,128]{2,1,0:T(8,128)(2,1)S(1)}, u32[]{:S(2)}, u32[]{:S(2)}) collective-permute-start(bf16[5,256,128]{2,1,0:T(8,128)(2,1)} %get-tuple-element.100), channel_id=1, source_target_pairs={{0,2},{1,3},{2,0},{3,1},{4,6},{5,7},{6,4},{7,5},{8,10},{9,11},{10,... | collective-permute-start | bytes 983048 | tf_op jit(solution)/shard_map/ppermute | solution.py:222
  192.4 47.7 %collective-permute-start.23 = (bf16[5,256,128]{2,1,0:T(8,128)(2,1)}, bf16[5,256,128]{2,1,0:T(8,128)(2,1)S(1)}, u32[]{:S(2)}, u32[]{:S(2)}) collective-permute-start(bf16[5,256,128]{2,1,0:T(8,128)(2,1)} %get-tuple-element.102), channel_id=1, source_target_pairs={{0,3},{1,2},{2,1},{3,0},{4,7},{5,6},{6,5},{7,4},{8,11},{9,10},{10,... | collective-permute-start | bytes 983048 | tf_op jit(solution)/shard_map/ppermute | solution.py:222
  193.9 4.1 %copy-start.32 = (bf16[5,256,128]{2,1,0:T(8,128)(2,1)}, bf16[5,256,128]{2,1,0:T(8,128)(2,1)S(1)}, u32[]{:S(2)}) copy-start(bf16[5,256,128]{2,1,0:T(8,128)(2,1)S(1)} %collective-permute-done.refs_1_) | copy-start | bytes 983044
  211.3 28.8 %collective-permute-start.18 = (bf16[5,256,128]{2,1,0:T(8,128)(2,1)}, bf16[5,256,128]{2,1,0:T(8,128)(2,1)S(1)}, u32[]{:S(2)}, u32[]{:S(2)}) collective-permute-start(bf16[5,256,128]{2,1,0:T(8,128)(2,1)} %get-tuple-element.97), channel_id=1, source_target_pairs={{0,1},{1,0},{2,3},{3,2},{4,5},{5,4},{6,7},{7,6},{8,9},{9,8},{10,11... | collective-permute-start | bytes 983048 | tf_op jit(solution)/shard_map/ppermute | solution.py:222
  211.4 33.8 %collective-permute-start.20 = (bf16[5,256,128]{2,1,0:T(8,128)(2,1)}, bf16[5,256,128]{2,1,0:T(8,128)(2,1)S(1)}, u32[]{:S(2)}, u32[]{:S(2)}) collective-permute-start(bf16[5,256,128]{2,1,0:T(8,128)(2,1)} %get-tuple-element.99), channel_id=1, source_target_pairs={{0,2},{1,3},{2,0},{3,1},{4,6},{5,7},{6,4},{7,5},{8,10},{9,11},{10,... | collective-permute-start | bytes 983048 | tf_op jit(solution)/shard_map/ppermute | solution.py:222
  214.0 39.7 %copy-start.16 = (bf16[5,256,128]{2,1,0:T(8,128)(2,1)}, bf16[5,256,128]{2,1,0:T(8,128)(2,1)S(1)}, u32[]{:S(2)}) copy-start(bf16[5,256,128]{2,1,0:T(8,128)(2,1)S(1)} %collective-permute-done.19.refs_3_) | copy-start | bytes 983044
  214.0 39.7 %collective-permute-start.22 = (bf16[5,256,128]{2,1,0:T(8,128)(2,1)}, bf16[5,256,128]{2,1,0:T(8,128)(2,1)S(1)}, u32[]{:S(2)}, u32[]{:S(2)}) collective-permute-start(bf16[5,256,128]{2,1,0:T(8,128)(2,1)} %get-tuple-element.101), channel_id=1, source_target_pairs={{0,3},{1,2},{2,1},{3,0},{4,7},{5,6},{6,5},{7,4},{8,11},{9,10},{10,... | collective-permute-start | bytes 983048 | tf_op jit(solution)/shard_map/ppermute | solution.py:222
  217.1 36.5 %copy-start.17 = (bf16[5,256,128]{2,1,0:T(8,128)(2,1)}, bf16[5,256,128]{2,1,0:T(8,128)(2,1)S(1)}, u32[]{:S(2)}) copy-start(bf16[5,256,128]{2,1,0:T(8,128)(2,1)S(1)} %collective-permute-done.21.refs_5_) | copy-start | bytes 983044
  240.1 13.6 %copy-start.18 = (bf16[5,256,128]{2,1,0:T(8,128)(2,1)}, bf16[5,256,128]{2,1,0:T(8,128)(2,1)S(1)}, u32[]{:S(2)}) copy-start(bf16[5,256,128]{2,1,0:T(8,128)(2,1)S(1)} %collective-permute-done.23.refs_7_) | copy-start | bytes 983044
  240.1 13.6 %copy-start.19 = (bf16[5,256,128]{2,1,0:T(8,128)(2,1)}, bf16[5,256,128]{2,1,0:T(8,128)(2,1)S(1)}, u32[]{:S(2)}) copy-start(bf16[5,256,128]{2,1,0:T(8,128)(2,1)S(1)} %collective-permute-done.18.refs_2_) | copy-start | bytes 983044
  245.2 8.5 %copy-start.20 = (bf16[5,256,128]{2,1,0:T(8,128)(2,1)}, bf16[5,256,128]{2,1,0:T(8,128)(2,1)S(1)}, u32[]{:S(2)}) copy-start(bf16[5,256,128]{2,1,0:T(8,128)(2,1)S(1)} %collective-permute-done.20.refs_4_) | copy-start | bytes 983044
  253.7 0.7 copy-start.21

commit v5 on v4

--- a/solution.py
+++ b/solution.py
@@ -77,6 +77,7 @@
             scratch_shapes=[pltpu.VMEM((heads, block, size), BF16)],
         ),
         out_shape=jax.ShapeDtypeStruct((rows, heads, size), BF16),
+        compiler_params=pltpu.CompilerParams(vmem_limit_bytes=16 * 2**20),
     )(here, *flat)
 
 
@@ -87,7 +88,7 @@
     partners = len(pieces)
 
     def kernel(pick_ref, *refs):
-        ins = refs[:partners]
+        ins = refs[:partners][::-1]
         out, sems = refs[-2:]
 
         def copy_of(k, row, reader, slot):
@@ -118,10 +119,10 @@
         out_shape=jax.ShapeDtypeStruct((readers, 2, CAP, count, TILE, size), BF16),
         input_output_aliases={1 + partners: 0} if held else {},
         compiler_params=pltpu.CompilerParams(vmem_limit_bytes=50 * 2**20),
-    )(picks, *pieces, *held)
-
-
-def attend(queries, keys, values, far, places):
+    )(picks, *pieces[::-1], *held)
+
+
+def attend(queries, keys, values, far, places, turn):
     partners = len(queries)
     count, rows, size = queries[0].shape
     far_count = len(far)
@@ -132,7 +133,8 @@
     factor = math.log2(math.e) / math.sqrt(size)
 
     def kernel(place_ref, *refs):
-        q_refs, k_refs, v_refs = refs[:partners], refs[partners : 2 * partners], refs[2 * partners : 3 * partners]
+        q_refs = refs[:partners][::turn]
+        k_refs, v_refs = refs[partners : 2 * partners][::-1], refs[2 * partners : 3 * partners]
         far_refs = refs[3 * partners : 3 * partners + far_count]
         outs, (k_pool, v_pool) = refs[3 * partners + far_count : -2], refs[-2:]
         for k in range(partners):
@@ -179,7 +181,7 @@
             bytes_accessed=count * 2 * TILE * size * (2 * near + 2 * pool_size),
             transcendentals=pairs * TILE * TILE,
         ),
-    )(places, *queries, *keys, *values, *far)
+    )(places, *queries[::turn], *keys[::-1], *values, *far)
 
 
 def plan(key_tiles, my_shard, here, shards, partners, tiles):
@@ -242,7 +244,7 @@
     asked = [exchange(query_parts, c) for c in range(len(chunks))]
     answers = []
     for c in range(len(chunks)):
-        outs, _ = lax.optimization_barrier((attend(asked[c], *ready[c], places), [pieces[2] for pieces in asked]))
+        outs, _ = lax.optimization_barrier((attend(asked[c], *ready[c], places, -1 if c else 1), [pieces[-1] for pieces in asked]))
         answers.append([swap(outs[k], k) for k in range(partners)])
     return from_partners([[answers[c][k] for c in range(len(chunks))] for k in range(partners)], here_arg, chunks, heads)
 

time: 258 us -> 250 us (0.969)
  waiting for transfers between devices: 162 us -> 155 us
    ppermute x24, waiting for transfers between devices: 162 us -> 148 us  [swap(): lax.ppermute(piece, 'head', [(i, i ^ k) for i in range(partners)])]
    all_to_all x2, waiting for transfers between devices: 0.01 us -> 6.58 us  [share(): return [lax.all_to_all(sent, 'seq', 0, 0, tiled=True)]]
where the time goes in v5:
time: 250 us; the launch traced here: 249 us
  waiting for transfers between devices  155 us (62%)
  Pallas kernels  47.6 us (19%)
  starting transfers between devices  41.7 us (17%)
    ppermute x24, waiting for transfers between devices, swap(): lax.ppermute(piece, 'head', [(i, i ^ k) for i in range(partners)])  148 us
    ppermute x24, starting transfers between devices, swap(): lax.ppermute(piece, 'head', [(i, i ^ k) for i in range(partners)])  30.3 us
    pallas_call x2, Pallas kernels, attend(): pl.pallas_call(kernel, grid_spec=pltpu.PrefetchScalarGridSpec(num_scalar_...  26.5 us
    all_to_all x2, starting transfers between devices, share(): return [lax.all_to_all(sent, 'seq', 0, 0, tiled=True)]  11.4 us
    pallas_call x3, Pallas kernels, by_partner(): pl.pallas_call(kernel, grid_spec=pltpu.PrefetchScalarGridSpec(num_scalar_...  9.88 us
    pallas_call x4, Pallas kernels, pick_tiles(): pl.pallas_call(kernel, in_specs=[pl.BlockSpec(memory_space=pltpu.SMEM)] +...  9.08 us
    all_to_all x2, waiting for transfers between devices, share(): return [lax.all_to_all(sent, 'seq', 0, 0, tiled=True)]  6.58 us
  transfers between devices with their start and end apart: 26, of which 18 were waited for; matrix products, arithmetic and copies ran while one was open for 1% of the time, Pallas kernels for 16%

profile of v5, /device:TPU:10, one launch (start us, length us, event | category | flops | bytes accessed | tf_op | source)
XLA Modules:
  0.0 249.0 jit_solution(1183471401040914042)
XLA Ops:
  0.0 3.3 %shard_map.47 = (bf16[5,256,128]{2,1,0:T(8,128)(2,1)}, bf16[5,256,128]{2,1,0:T(8,128)(2,1)}, bf16[5,256,128]{2,1,0:T(8,128)(2,1)}, bf16[5,256,128]{2,1,0:T(8,128...) custom-call(s32[1]{0:T(128)} %bitcast.here_ref, ...), custom_call_target="tpu_custom_call" | custom-call | tf_op jit(solution)/shard_map/pallas_call | solution.py:41
  3.3 1.6 collective-permute-start.12
  4.9 1.2 collective-permute-start.13
  6.2 1.2 collective-permute-start.14
  7.4 3.3 %shard_map.48 = (bf16[5,256,128]{2,1,0:T(8,128)(2,1)}, bf16[5,256,128]{2,1,0:T(8,128)(2,1)}, bf16[5,256,128]{2,1,0:T(8,128)(2,1)}, bf16[5,256,128]{2,1,0:T(8,128...) custom-call(s32[1]{0:T(128)} %bitcast.here_ref, ...), custom_call_target="tpu_custom_call" | custom-call | tf_op jit(solution)/shard_map/pallas_call | solution.py:41
  10.7 0.8 collective-permute-start.15
  11.6 2.2 collective-permute-start.16
  13.8 0.1 copy.11
  14.0 0.3 compare_reduce_fusion
  14.3 3.3 %shard_map.46 = (bf16[5,256,128]{2,1,0:T(8,128)(2,1)}, bf16[5,256,128]{2,1,0:T(8,128)(2,1)}, bf16[5,256,128]{2,1,0:T(8,128)(2,1)}, bf16[5,256,128]{2,1,0:T(8,128...) custom-call(s32[1]{0:T(128)} %bitcast.here_ref, ...), custom_call_target="tpu_custom_call" | custom-call | tf_op jit(solution)/shard_map/pallas_call | solution.py:41
  17.5 0.2 reduce_window_sum.18
  17.7 10.3 %collective-permute-done.12.refs_0_.refs_4_ = bf16[5,256,128]{2,1,0:T(8,128)(2,1)S(1)} collective-permute-done((bf16[5,256,128]{2,1,0:T(8,128)(2,1)}, bf16[5,256,128]{2,1,0:T(8,128)(2,1)S(1)}, u32[]{:S(2)}, u32[]{:S(2)}) %collective-permute-start.12) | collective-permute-done | bytes 327712 | tf_op jit(solution)/shard_map/ppermute | solution.py:224
  28.0 1.8 collective-permute-start.17
  29.8 0.1 select_reduce_fusion.1
  29.9 0.1 copy.13.pick_ref
  30.0 4.4 %collective-permute-done.13.refs_1_.refs_5_ = bf16[5,256,128]{2,1,0:T(8,128)(2,1)S(1)} collective-permute-done((bf16[5,256,128]{2,1,0:T(8,128)(2,1)}, bf16[5,256,128]{2,1,0:T(8,128)(2,1)S(1)}, u32[]{:S(2)}, u32[]{:S(2)}) %collective-permute-start.13) | collective-permute-done | bytes 327712 | tf_op jit(solution)/shard_map/ppermute | solution.py:224
  34.4 2.3 shard_map.52.refs_4_
  36.7 0.6 collective-permute-done.15.refs_2_.refs_9_
  37.3 18.2 %collective-permute-done.16.refs_1_.refs_10_ = bf16[5,256,128]{2,1,0:T(8,128)(2,1)S(1)} collective-permute-done((bf16[5,256,128]{2,1,0:T(8,128)(2,1)}, bf16[5,256,128]{2,1,0:T(8,128)(2,1)S(1)}, u32[]{:S(2)}, u32[]{:S(2)}) %collective-permute-start.16) | collective-permute-done | bytes 327712 | tf_op jit(solution)/shard_map/ppermute | solution.py:224
  55.6 6.7 %collective-permute-done.17.refs_0_.refs_11_ = bf16[5,256,128]{2,1,0:T(8,128)(2,1)S(1)} collective-permute-done((bf16[5,256,128]{2,1,0:T(8,128)(2,1)}, bf16[5,256,128]{2,1,0:T(8,128)(2,1)S(1)}, u32[]{:S(2)}, u32[]{:S(2)}) %collective-permute-start.17) | collective-permute-done | bytes 327712 | tf_op jit(solution)/shard_map/ppermute | solution.py:224
  62.2 2.3 shard_map.53
  64.6 5.2 %all-to-all-start.1 = ((bf16[8,2,2,5,128,128]{5,4,3,2,1,0:T(8,128)(2,1)}), bf16[8,2,2,5,128,128]{5,4,3,2,1,0:T(8,128)(2,1)}, u32[]{:S(2)}, u32[]{:S(2)}) async-start(bf16[8,2,2,5,128,128]{5,4,3,2,1,0:T(8,128)(2,1)} %shard_map.53), calls=%async_computation.1 | async-start | bytes 10485760 | tf_op jit(solution)/shard_map/all_to_all | solution.py:236
  69.8 1.6 collective-permute-start.3
  71.4 1.9 collective-permute-start.5
  73.3 0.2 collective-permute-start.6
  73.5 2.9 %collective-permute-start.7 = (bf16[5,256,128]{2,1,0:T(8,128)(2,1)}, bf16[5,256,128]{2,1,0:T(8,128)(2,1)S(1)}, u32[]{:S(2)}, u32[]{:S(2)}) collective-permute-start(bf16[5,256,128]{2,1,0:T(8,128)(2,1)} %get-tuple-element.72), channel_id=1, source_target_pairs={{0,2},{1,3},{2,0},{3,1},{4,6},{5,7},{6,4},{7,5},{8,10},{9,11},{10,... | collective-permute-start | bytes 983048 | tf_op jit(solution)/shard_map/ppermute | solution.py:224
  76.3 13.3 %collective-permute-done.3.refs_0_.refs_4_ = bf16[5,256,128]{2,1,0:T(8,128)(2,1)S(1)} collective-permute-done((bf16[5,256,128]{2,1,0:T(8,128)(2,1)}, bf16[5,256,128]{2,1,0:T(8,128)(2,1)S(1)}, u32[]{:S(2)}, u32[]{:S(2)}) %collective-permute-start.3) | collective-permute-done | bytes 327712 | tf_op jit(solution)/shard_map/ppermute | solution.py:224
  89.6 1.8 collective-permute-start.8
  91.4 5.2 %collective-permute-done.4.refs_1_.refs_5_ = bf16[5,256,128]{2,1,0:T(8,128)(2,1)S(1)} collective-permute-done((bf16[5,256,128]{2,1,0:T(8,128)(2,1)S(1)}, bf16[5,256,128]{2,1,0:T(8,128)(2,1)S(1)}, u32[]{:S(2)}, u32[]{:S(2)}) %collective-permute-start.4) | collective-permute-done | bytes 327712 | tf_op jit(solution)/shard_map/ppermute | solution.py:224
  96.6 2.3 shard_map.49.refs_4_
  98.9 18.3 %collective-permute-done.7.refs_1_.refs_10_ = bf16[5,256,128]{2,1,0:T(8,128)(2,1)S(1)} collective-permute-done((bf16[5,256,128]{2,1,0:T(8,128)(2,1)}, bf16[5,256,128]{2,1,0:T(8,128)(2,1)S(1)}, u32[]{:S(2)}, u32[]{:S(2)}) %collective-permute-start.7) | collective-permute-done | bytes 327712 | tf_op jit(solution)/shard_map/ppermute | solution.py:224
  117.2 7.6 %collective-permute-done.8.refs_0_.refs_11_ = bf16[5,256,128]{2,1,0:T(8,128)(2,1)S(1)} collective-permute-done((bf16[5,256,128]{2,1,0:T(8,128)(2,1)}, bf16[5,256,128]{2,1,0:T(8,128)(2,1)S(1)}, u32[]{:S(2)}, u32[]{:S(2)}) %collective-permute-start.8) | collective-permute-done | bytes 327712 | tf_op jit(solution)/shard_map/ppermute | solution.py:224
  124.7 2.2 shard_map.50
  127.1 1.7 all-to-all-done.1.refs_12_
  128.8 6.2 %all-to-all-start = ((bf16[8,2,2,5,128,128]{5,4,3,2,1,0:T(8,128)(2,1)}), bf16[8,2,2,5,128,128]{5,4,3,2,1,0:T(8,128)(2,1)}, u32[]{:S(2)}, u32[]{:S(2)}) async-start(bf16[8,2,2,5,128,128]{5,4,3,2,1,0:T(8,128)(2,1)} %shard_map.50), calls=%async_computation | async-start | bytes 10485760 | tf_op jit(solution)/shard_map/all_to_all | solution.py:236
  135.0 1.6 collective-permute-start.9
  136.5 1.9 collective-permute-start.11
  138.5 1.6 collective-permute-start.2
  140.0 1.0 collective-permute-start
  141.1 0.1 fusion
  141.2 0.1 reshape.137
  141.3 0.2 reduce_window_sum.17
  141.5 0.1 select_n.76
  141.6 0.3 select_reduce_fusion
  142.1 0.1 broadcast_in_dim.65
  142.2 0.6 gather_fusion
  142.8 12.4 %collective-permute-done.9.refs_0_ = bf16[5,256,128]{2,1,0:T(8,128)(2,1)S(1)} collective-permute-done((bf16[5,256,128]{2,1,0:T(8,128)(2,1)S(1)}, bf16[5,256,128]{2,1,0:T(8,128)(2,1)S(1)}, u32[]{:S(2)}, u32[]{:S(2)}) %collective-permute-start.9) | collective-permute-done | bytes 327712 | tf_op jit(solution)/shard_map/ppermute | solution.py:224
  155.1 0.7 broadcast_select_fusion.place_ref
  155.8 12.6 %collective-permute-done.10.refs_1_ = bf16[5,256,128]{2,1,0:T(8,128)(2,1)} collective-permute-done((bf16[5,256,128]{2,1,0:T(8,128)(2,1)S(1)}, bf16[5,256,128]{2,1,0:T(8,128)(2,1)}, u32[]{:S(2)}, u32[]{:S(2)}) %collective-permute-start.10) | collective-permute-done | bytes 327712 | tf_op jit(solution)/shard_map/ppermute | solution.py:224
  168.4 13.2 %shard_map.54 = (bf16[5,256,128]{2,1,0:T(8,128)(2,1)}, bf16[5,256,128]{2,1,0:T(8,128)(2,1)}, bf16[5,256,128]{2,1,0:T(8,128)(2,1)}, bf16[5,256,128]{2,1,0:T(8,128)(2,1)}) custom-call(s32[8,10]{1,0:T(8,128)} %broadcast_select_fusion.place_ref, bf16[5,256,128]{2,1,0:T(8,128)(2,1)} %copy-done.29, bf16[5,256,128]{2,1,0:T(8,128)(2,1)} %collective-permute-done.10.refs_1_, ...), custom_call_target="tpu_custom_call" | custom-call | flops 3355443200 | bytes 10485760 | tf_op jit(solution)/shard_map/pallas_call | solution.py:169
  181.7 1.0 collective-permute-done.2.refs_3_
  182.7 1.4 collective-permute-start.19
  184.1 1.8 collective-permute-start.21
  185.9 0.3 collective-permute-start.23
  186.2 2.9 %collective-permute-done.1.refs_2_ = bf16[5,256,128]{2,1,0:T(8,128)(2,1)} collective-permute-done((bf16[5,256,128]{2,1,0:T(8,128)(2,1)S(1)}, bf16[5,256,128]{2,1,0:T(8,128)(2,1)}, u32[]{:S(2)}, u32[]{:S(2)}) %collective-permute-start.1) | collective-permute-done | bytes 327712 | tf_op jit(solution)/shard_map/ppermute | solution.py:224
  189.0 4.9 %all-to-all-done.refs_12_ = bf16[8,2,2,5,128,128]{5,4,3,2,1,0:T(8,128)(2,1)} async-done(((bf16[8,2,2,5,128,128]{5,4,3,2,1,0:T(8,128)(2,1)}), bf16[8,2,2,5,128,128]{5,4,3,2,1,0:T(8,128)(2,1)}, u32[]{:S(2)}, u32[]{:S(2)}) %all-to-all-start) | async-done | bytes 5242912 | tf_op jit(solution)/shard_map/all_to_all | solution.py:236
  193.9 13.2 %shard_map.51 = (bf16[5,256,128]{2,1,0:T(8,128)(2,1)}, bf16[5,256,128]{2,1,0:T(8,128)(2,1)}, bf16[5,256,128]{2,1,0:T(8,128)(2,1)}, bf16[5,256,128]{2,1,0:T(8,128)(2,1)}) custom-call(s32[8,10]{1,0:T(8,128)} %broadcast_select_fusion.place_ref, bf16[5,256,128]{2,1,0:T(8,128)(2,1)} %get-tuple-element.62.refs_0_, bf16[5,256,128]{2,1,0:T(8,128)(2,1)} %copy-done.28, ...), custom_call_target="tpu_custom_call" | custom-call | flops 3355443200 | bytes 10485760 | tf_op jit(solution)/shard_map/pallas_call | solution.py:169
  207.2 3.0 %collective-permute-start.20 = (bf16[5,256,128]{2,1,0:T(8,128)(2,1)}, bf16[5,256,128]{2,1,0:T(8,128)(2,1)S(1)}, u32[]{:S(2)}, u32[]{:S(2)}) collective-permute-start(bf16[5,256,128]{2,1,0:T(8,128)(2,1)} %get-tuple-element.99), channel_id=1, source_target_pairs={{0,2},{1,3},{2,0},{3,1},{4,6},{5,7},{6,4},{7,5},{8,10},{9,11},{10,... | collective-permute-start | bytes 983048 | tf_op jit(solution)/shard_map/ppermute | solution.py:224
  210.3 0.4 collective-permute-start.22
  210.7 20.6 %collective-permute-done.23.refs_7_ = bf16[5,256,128]{2,1,0:T(8,128)(2,1)S(1)} collective-permute-done((bf16[5,256,128]{2,1,0:T(8,128)(2,1)}, bf16[5,256,128]{2,1,0:T(8,128)(2,1)S(1)}, u32[]{:S(2)}, u32[]{:S(2)}) %collective-permute-start.23) | collective-permute-done | bytes 327712 | tf_op jit(solution)/shard_map/ppermute | solution.py:224
  231.3 7.0 %collective-permute-done.20.refs_4_ = bf16[5,256,128]{2,1,0:T(8,128)(2,1)S(1)} collective-permute-done((bf16[5,256,128]{2,1,0:T(8,128)(2,1)}, bf16[5,256,128]{2,1,0:T(8,128)(2,1)S(1)}, u32[]{:S(2)}, u32[]{:S(2)}) %collective-permute-start.20) | collective-permute-done | bytes 327712 | tf_op jit(solution)/shard_map/ppermute | solution.py:224
  238.3 7.5 %collective-permute-done.22.refs_6_ = bf16[5,256,128]{2,1,0:T(8,128)(2,1)S(1)} collective-permute-done((bf16[5,256,128]{2,1,0:T(8,128)(2,1)}, bf16[5,256,128]{2,1,0:T(8,128)(2,1)S(1)}, u32[]{:S(2)}, u32[]{:S(2)}) %collective-permute-start.22) | collective-permute-done | bytes 327712 | tf_op jit(solution)/shard_map/ppermute | solution.py:224
  245.9 1.0 copy-done.17
  246.8 2.1 shard_map.55
  (85 shorter events, 0.6 us)
Async XLA Ops:
  0.0 13.8 %copy-start.18 = (s32[64,10]{0,1:T(8,128)S(1)}, s32[64,10]{0,1:T(8,128)}, u32[]{:S(2)}) copy-start(s32[64,10]{0,1:T(8,128)} %param.7) | copy-start | bytes 7684
  3.3 31.1 %copy-start.2 = (bf16[5,256,128]{2,1,0:T(8,128)(2,1)S(1)}, bf16[5,256,128]{2,1,0:T(8,128)(2,1)}, u32[]{:S(2)}) copy-start(bf16[5,256,128]{2,1,0:T(8,128)(2,1)} %get-tuple-element.87.refs_3_.refs_7_) | copy-start | bytes 983044
  3.3 24.7 %collective-permute-start.12 = (bf16[5,256,128]{2,1,0:T(8,128)(2,1)}, bf16[5,256,128]{2,1,0:T(8,128)(2,1)S(1)}, u32[]{:S(2)}, u32[]{:S(2)}) collective-permute-start(bf16[5,256,128]{2,1,0:T(8,128)(2,1)} %get-tuple-element.84), channel_id=1, source_target_pairs={{0,3},{1,2},{2,1},{3,0},{4,7},{5,6},{6,5},{7,4},{8,11},{9,10},{10,... | collective-permute-start | bytes 983048 | tf_op jit(solution)/shard_map/ppermute | solution.py:224
  4.9 29.5 %collective-permute-start.13 = (bf16[5,256,128]{2,1,0:T(8,128)(2,1)}, bf16[5,256,128]{2,1,0:T(8,128)(2,1)S(1)}, u32[]{:S(2)}, u32[]{:S(2)}) collective-permute-start(bf16[5,256,128]{2,1,0:T(8,128)(2,1)} %get-tuple-element.85), channel_id=1, source_target_pairs={{0,2},{1,3},{2,0},{3,1},{4,6},{5,7},{6,4},{7,5},{8,10},{9,11},{10,... | collective-permute-start | bytes 983048 | tf_op jit(solution)/shard_map/ppermute | solution.py:224
  6.2 28.2 %collective-permute-start.14 = (bf16[5,256,128]{2,1,0:T(8,128)(2,1)}, bf16[5,256,128]{2,1,0:T(8,128)(2,1)S(1)}, u32[]{:S(2)}, u32[]{:S(2)}) collective-permute-start(bf16[5,256,128]{2,1,0:T(8,128)(2,1)} %get-tuple-element.86), channel_id=1, source_target_pairs={{0,1},{1,0},{2,3},{3,2},{4,5},{5,4},{6,7},{7,6},{8,9},{9,8},{10,11... | collective-permute-start | bytes 983048 | tf_op jit(solution)/shard_map/ppermute | solution.py:224
  10.7 51.5 %copy-start.6 = (bf16[5,256,128]{2,1,0:T(8,128)(2,1)S(1)}, bf16[5,256,128]{2,1,0:T(8,128)(2,1)}, u32[]{:S(2)}) copy-start(bf16[5,256,128]{2,1,0:T(8,128)(2,1)} %get-tuple-element.88.refs_3_.refs_8_) | copy-start | bytes 983044
  10.7 26.6 %collective-permute-start.15 = (bf16[5,256,128]{2,1,0:T(8,128)(2,1)}, bf16[5,256,128]{2,1,0:T(8,128)(2,1)S(1)}, u32[]{:S(2)}, u32[]{:S(2)}) collective-permute-start(bf16[5,256,128]{2,1,0:T(8,128)(2,1)} %get-tuple-element.89), channel_id=1, source_target_pairs={{0,1},{1,0},{2,3},{3,2},{4,5},{5,4},{6,7},{7,6},{8,9},{9,8},{10,11... | collective-permute-start | bytes 983048 | tf_op jit(solution)/shard_map/ppermute | solution.py:224
  11.6 44.0 %collective-permute-start.16 = (bf16[5,256,128]{2,1,0:T(8,128)(2,1)}, bf16[5,256,128]{2,1,0:T(8,128)(2,1)S(1)}, u32[]{:S(2)}, u32[]{:S(2)}) collective-permute-start(bf16[5,256,128]{2,1,0:T(8,128)(2,1)} %get-tuple-element.90), channel_id=1, source_target_pairs={{0,2},{1,3},{2,0},{3,1},{4,6},{5,7},{6,4},{7,5},{8,10},{9,11},{10,... | collective-permute-start | bytes 983048 | tf_op jit(solution)/shard_map/ppermute | solution.py:224
  28.0 36.5 %copy-start.3 = (bf16[5,256,128]{2,1,0:T(8,128)(2,1)}, bf16[5,256,128]{2,1,0:T(8,128)(2,1)S(1)}, u32[]{:S(2)}) copy-start(bf16[5,256,128]{2,1,0:T(8,128)(2,1)S(1)} %collective-permute-done.12.refs_0_.refs_4_) | copy-start | bytes 983044
  28.0 34.2 %collective-permute-start.17 = (bf16[5,256,128]{2,1,0:T(8,128)(2,1)}, bf16[5,256,128]{2,1,0:T(8,128)(2,1)S(1)}, u32[]{:S(2)}, u32[]{:S(2)}) collective-permute-start(bf16[5,256,128]{2,1,0:T(8,128)(2,1)} %get-tuple-element.91), channel_id=1, source_target_pairs={{0,3},{1,2},{2,1},{3,0},{4,7},{5,6},{6,5},{7,4},{8,11},{9,10},{10,... | collective-permute-start | bytes 983048 | tf_op jit(solution)/shard_map/ppermute | solution.py:224
  34.4 30.1 %copy-start.4 = (bf16[5,256,128]{2,1,0:T(8,128)(2,1)}, bf16[5,256,128]{2,1,0:T(8,128)(2,1)S(1)}, u32[]{:S(2)}) copy-start(bf16[5,256,128]{2,1,0:T(8,128)(2,1)S(1)} %collective-permute-done.13.refs_1_.refs_5_) | copy-start | bytes 983044
  34.4 30.1 %copy-start.5 = (bf16[5,256,128]{2,1,0:T(8,128)(2,1)}, bf16[5,256,128]{2,1,0:T(8,128)(2,1)S(1)}, u32[]{:S(2)}) copy-start(bf16[5,256,128]{2,1,0:T(8,128)(2,1)S(1)} %collective-permute-done.14.refs_2_.refs_6_) | copy-start | bytes 983044
  37.3 27.2 %copy-start.7 = (bf16[5,256,128]{2,1,0:T(8,128)(2,1)}, bf16[5,256,128]{2,1,0:T(8,128)(2,1)S(1)}, u32[]{:S(2)}) copy-start(bf16[5,256,128]{2,1,0:T(8,128)(2,1)S(1)} %collective-permute-done.15.refs_2_.refs_9_) | copy-start | bytes 983044
  55.6 9.0 %copy-start.8 = (bf16[5,256,128]{2,1,0:T(8,128)(2,1)}, bf16[5,256,128]{2,1,0:T(8,128)(2,1)S(1)}, u32[]{:S(2)}) copy-start(bf16[5,256,128]{2,1,0:T(8,128)(2,1)S(1)} %collective-permute-done.16.refs_1_.refs_10_) | copy-start | bytes 983044
  62.2 2.3 copy-start.10
  64.6 6.8 %copy-start.26 = (bf16[5,256,128]{2,1,0:T(8,128)(2,1)S(1)}, bf16[5,256,128]{2,1,0:T(8,128)(2,1)}, u32[]{:S(2)}) copy-start(bf16[5,256,128]{2,1,0:T(8,128)(2,1)} %get-tuple-element.67) | copy-start | bytes 983044
  64.6 6.8 %copy-start.25 = (bf16[5,256,128]{2,1,0:T(8,128)(2,1)S(1)}, bf16[5,256,128]{2,1,0:T(8,128)(2,1)}, u32[]{:S(2)}) copy-start(bf16[5,256,128]{2,1,0:T(8,128)(2,1)} %get-tuple-element.68) | copy-start | bytes 983044
  64.6 32.0 %copy-start = (bf16[5,256,128]{2,1,0:T(8,128)(2,1)S(1)}, bf16[5,256,128]{2,1,0:T(8,128)(2,1)}, u32[]{:S(2)}) copy-start(bf16[5,256,128]{2,1,0:T(8,128)(2,1)} %get-tuple-element.69.refs_3_.refs_7_) | copy-start | bytes 983044
  64.6 64.2 %all-to-all-start.1 = ((bf16[8,2,2,5,128,128]{5,4,3,2,1,0:T(8,128)(2,1)}), bf16[8,2,2,5,128,128]{5,4,3,2,1,0:T(8,128)(2,1)}, u32[]{:S(2)}, u32[]{:S(2)}) async-start(bf16[8,2,2,5,128,128]{5,4,3,2,1,0:T(8,128)(2,1)} %shard_map.53), calls=%async_computation.1 | async-start | bytes 10485760 | tf_op jit(solution)/shard_map/all_to_all | solution.py:236
  69.8 54.9 %copy-start.1 = (bf16[5,256,128]{2,1,0:T(8,128)(2,1)S(1)}, bf16[5,256,128]{2,1,0:T(8,128)(2,1)}, u32[]{:S(2)}) copy-start(bf16[5,256,128]{2,1,0:T(8,128)(2,1)} %get-tuple-element.70.refs_3_.refs_8_) | copy-start | bytes 983044
  69.8 19.8 %collective-permute-start.3 = (bf16[5,256,128]{2,1,0:T(8,128)(2,1)}, bf16[5,256,128]{2,1,0:T(8,128)(2,1)S(1)}, u32[]{:S(2)}, u32[]{:S(2)}) collective-permute-start(bf16[5,256,128]{2,1,0:T(8,128)(2,1)} %get-tuple-element.66), channel_id=1, source_target_pairs={{0,3},{1,2},{2,1},{3,0},{4,7},{5,6},{6,5},{7,4},{8,11},{9,10},{10,... | collective-permute-start | bytes 983048 | tf_op jit(solution)/shard_map/ppermute | solution.py:224
  71.4 25.2 %collective-permute-start.4 = (bf16[5,256,128]{2,1,0:T(8,128)(2,1)S(1)}, bf16[5,256,128]{2,1,0:T(8,128)(2,1)S(1)}, u32[]{:S(2)}, u32[]{:S(2)}) collective-permute-start(bf16[5,256,128]{2,1,0:T(8,128)(2,1)S(1)} %copy-done.26), channel_id=1, source_target_pairs={{0,2},{1,3},{2,0},{3,1},{4,6},{5,7},{6,4},{7,5},{8,10},{9,11},{10,... | collective-permute-start | bytes 983048 | tf_op jit(solution)/shard_map/ppermute | solution.py:224
  71.4 25.2 %collective-permute-start.5 = (bf16[5,256,128]{2,1,0:T(8,128)(2,1)S(1)}, bf16[5,256,128]{2,1,0:T(8,128)(2,1)S(1)}, u32[]{:S(2)}, u32[]{:S(2)}) collective-permute-start(bf16[5,256,128]{2,1,0:T(8,128)(2,1)S(1)} %copy-done.25), channel_id=1, source_target_pairs={{0,1},{1,0},{2,3},{3,2},{4,5},{5,4},{6,7},{7,6},{8,9},{9,8},{10,11... | collective-permute-start | bytes 983048 | tf_op jit(solution)/shard_map/ppermute | solution.py:224
  73.3 25.6 %collective-permute-start.6 = (bf16[5,256,128]{2,1,0:T(8,128)(2,1)}, bf16[5,256,128]{2,1,0:T(8,128)(2,1)S(1)}, u32[]{:S(2)}, u32[]{:S(2)}) collective-permute-start(bf16[5,256,128]{2,1,0:T(8,128)(2,1)} %get-tuple-element.71), channel_id=1, source_target_pairs={{0,1},{1,0},{2,3},{3,2},{4,5},{5,4},{6,7},{7,6},{8,9},{9,8},{10,11... | collective-permute-start | bytes 983048 | tf_op jit(solution)/shard_map/ppermute | solution.py:224
  73.5 43.7 %collective-permute-start.7 = (bf16[5,256,128]{2,1,0:T(8,128)(2,1)}, bf16[5,256,128]{2,1,0:T(8,128)(2,1)S(1)}, u32[]{:S(2)}, u32[]{:S(2)}) collective-permute-start(bf16[5,256,128]{2,1,0:T(8,128)(2,1)} %get-tuple-element.72), channel_id=1, source_target_pairs={{0,2},{1,3},{2,0},{3,1},{4,6},{5,7},{6,4},{7,5},{8,10},{9,11},{10,... | collective-permute-start | bytes 983048 | tf_op jit(solution)/shard_map/ppermute | solution.py:224
  89.6 37.3 %copy-start.9 = (bf16[5,256,128]{2,1,0:T(8,128)(2,1)}, bf16[5,256,128]{2,1,0:T(8,128)(2,1)S(1)}, u32[]{:S(2)}) copy-start(bf16[5,256,128]{2,1,0:T(8,128)(2,1)S(1)} %collective-permute-done.3.refs_0_.refs_4_) | copy-start | bytes 983044
  89.6 35.1 %collective-permute-start.8 = (bf16[5,256,128]{2,1,0:T(8,128)(2,1)}, bf16[5,256,128]{2,1,0:T(8,128)(2,1)S(1)}, u32[]{:S(2)}, u32[]{:S(2)}) collective-permute-start(bf16[5,256,128]{2,1,0:T(8,128)(2,1)} %get-tuple-element.73), channel_id=1, source_target_pairs={{0,3},{1,2},{2,1},{3,0},{4,7},{5,6},{6,5},{7,4},{8,11},{9,10},{10,... | collective-permute-start | bytes 983048 | tf_op jit(solution)/shard_map/ppermute | solution.py:224
  96.6 30.4 %copy-start.11 = (bf16[5,256,128]{2,1,0:T(8,128)(2,1)}, bf16[5,256,128]{2,1,0:T(8,128)(2,1)S(1)}, u32[]{:S(2)}) copy-start(bf16[5,256,128]{2,1,0:T(8,128)(2,1)S(1)} %collective-permute-done.4.refs_1_.refs_5_) | copy-start | bytes 983044
  96.6 30.4 %copy-start.12 = (bf16[5,256,128]{2,1,0:T(8,128)(2,1)}, bf16[5,256,128]{2,1,0:T(8,128)(2,1)S(1)}, u32[]{:S(2)}) copy-start(bf16[5,256,128]{2,1,0:T(8,128)(2,1)S(1)} %collective-permute-done.5.refs_2_.refs_6_) | copy-start | bytes 983044
  98.9 28.2 %copy-start.13 = (bf16[5,256,128]{2,1,0:T(8,128)(2,1)}, bf16[5,256,128]{2,1,0:T(8,128)(2,1)S(1)}, u32[]{:S(2)}) copy-start(bf16[5,256,128]{2,1,0:T(8,128)(2,1)S(1)} %collective-permute-done.6.refs_2_.refs_9_) | copy-start | bytes 983044
  117.2 9.9 %copy-start.14 = (bf16[5,256,128]{2,1,0:T(8,128)(2,1)}, bf16[5,256,128]{2,1,0:T(8,128)(2,1)S(1)}, u32[]{:S(2)}) copy-start(bf16[5,256,128]{2,1,0:T(8,128)(2,1)S(1)} %collective-permute-done.7.refs_1_.refs_10_) | copy-start | bytes 983044
  124.7 2.3 copy-start.15
  127.0 9.5 %copy-start.22 = (bf16[5,256,128]{2,1,0:T(8,128)(2,1)S(1)}, bf16[5,256,128]{2,1,0:T(8,128)(2,1)}, u32[]{:S(2)}) copy-start(bf16[5,256,128]{2,1,0:T(8,128)(2,1)} %get-tuple-element.82) | copy-start | bytes 983044
  127.1 11.4 %copy-start.21 = (bf16[5,256,128]{2,1,0:T(8,128)(2,1)S(1)}, bf16[5,256,128]{2,1,0:T(8,128)(2,1)}, u32[]{:S(2)}) copy-start(bf16[5,256,128]{2,1,0:T(8,128)(2,1)} %get-tuple-element.65) | copy-start | bytes 983044
  127.1 13.0 %copy-start.20 = (bf16[5,256,128]{2,1,0:T(8,128)(2,1)S(1)}, bf16[5,256,128]{2,1,0:T(8,128)(2,1)}, u32[]{:S(2)}) copy-start(bf16[5,256,128]{2,1,0:T(8,128)(2,1)} %get-tuple-element.63) | copy-start | bytes 983044
  127.1 28.1 %copy-start.19 = (bf16[5,256,128]{2,1,0:T(8,128)(2,1)S(1)}, bf16[5,256,128]{2,1,0:T(8,128)(2,1)}, u32[]{:S(2)}) copy-start(bf16[5,256,128]{2,1,0:T(8,128)(2,1)} %get-tuple-element.64) | copy-start | bytes 983044
  128.8 6.2 %copy-start.24 = (bf16[5,256,128]{2,1,0:T(8,128)(2,1)S(1)}, bf16[5,256,128]{2,1,0:T(8,128)(2,1)}, u32[]{:S(2)}) copy-start(bf16[5,256,128]{2,1,0:T(8,128)(2,1)} %get-tuple-element.79) | copy-start | bytes 983044
  128.8 7.8 %copy-start.23 = (bf16[5,256,128]{2,1,0:T(8,128)(2,1)S(1)}, bf16[5,256,128]{2,1,0:T(8,128)(2,1)}, u32[]{:S(2)}) copy-start(bf16[5,256,128]{2,1,0:T(8,128)(2,1)} %get-tuple-element.81) | copy-start | bytes 983044
  128.8 65.2 %all-to-all-start = ((bf16[8,2,2,5,128,128]{5,4,3,2,1,0:T(8,128)(2,1)}), bf16[8,2,2,5,128,128]{5,4,3,2,1,0:T(8,128)(2,1)}, u32[]{:S(2)}, u32[]{:S(2)}) async-start(bf16[8,2,2,5,128,128]{5,4,3,2,1,0:T(8,128)(2,1)} %shard_map.50), calls=%async_computation | async-start | bytes 10485760 | tf_op jit(solution)/shard_map/all_to_all | solution.py:236
  135.0 20.2 %collective-permute-start.9 = (bf16[5,256,128]{2,1,0:T(8,128)(2,1)S(1)}, bf16[5,256,128]{2,1,0:T(8,128)(2,1)S(1)}, u32[]{:S(2)}, u32[]{:S(2)}) collective-permute-start(bf16[5,256,128]{2,1,0:T(8,128)(2,1)S(1)} %copy-done.24), channel_id=1, source_target_pairs={{0,3},{1,2},{2,1},{3,0},{4,7},{5,6},{6,5},{7,4},{8,11},{9,10},{10,... | collective-permute-start | bytes 983048 | tf_op jit(solution)/shard_map/ppermute | solution.py:224
  136.5 31.9 %collective-permute-start.10 = (bf16[5,256,128]{2,1,0:T(8,128)(2,1)S(1)}, bf16[5,256,128]{2,1,0:T(8,128)(2,1)}, u32[]{:S(2)}, u32[]{:S(2)}) collective-permute-start(bf16[5,256,128]{2,1,0:T(8,128)(2,1)S(1)} %copy-done.23), channel_id=1, source_target_pairs={{0,2},{1,3},{2,0},{3,1},{4,6},{5,7},{6,4},{7,5},{8,10},{9,11},{10,... | collective-permute-start | bytes 983048 | tf_op jit(solution)/shard_map/ppermute | solution.py:224
  136.5 31.9 %collective-permute-start.11 = (bf16[5,256,128]{2,1,0:T(8,128)(2,1)S(1)}, bf16[5,256,128]{2,1,0:T(8,128)(2,1)}, u32[]{:S(2)}, u32[]{:S(2)}) collective-permute-start(bf16[5,256,128]{2,1,0:T(8,128)(2,1)S(1)} %copy-done.22), channel_id=1, source_target_pairs={{0,1},{1,0},{2,3},{3,2},{4,5},{5,4},{6,7},{7,6},{8,9},{9,8},{10,11... | collective-permute-start | bytes 983048 | tf_op jit(solution)/shard_map/ppermute | solution.py:224
  138.5 44.2 %collective-permute-start.2 = (bf16[5,256,128]{2,1,0:T(8,128)(2,1)S(1)}, bf16[5,256,128]{2,1,0:T(8,128)(2,1)S(1)}, u32[]{:S(2)}, u32[]{:S(2)}) collective-permute-start(bf16[5,256,128]{2,1,0:T(8,128)(2,1)S(1)} %copy-done.21), channel_id=1, source_target_pairs={{0,3},{1,2},{2,1},{3,0},{4,7},{5,6},{6,5},{7,4},{8,11},{9,10},{10,... | collective-permute-start | bytes 983048 | tf_op jit(solution)/shard_map/ppermute | solution.py:224
  140.0 46.1 %collective-permute-start = (bf16[5,256,128]{2,1,0:T(8,128)(2,1)S(1)}, bf16[5,256,128]{2,1,0:T(8,128)(2,1)S(1)}, u32[]{:S(2)}, u32[]{:S(2)}) collective-permute-start(bf16[5,256,128]{2,1,0:T(8,128)(2,1)S(1)} %copy-done.20), channel_id=1, source_target_pairs={{0,1},{1,0},{2,3},{3,2},{4,5},{5,4},{6,7},{7,6},{8,9},{9,8},{10,11... | collective-permute-start | bytes 983048 | tf_op jit(solution)/shard_map/ppermute | solution.py:224
  155.1 13.3 %copy-start.29 = (bf16[5,256,128]{2,1,0:T(8,128)(2,1)}, bf16[5,256,128]{2,1,0:T(8,128)(2,1)S(1)}, u32[]{:S(2)}) copy-start(bf16[5,256,128]{2,1,0:T(8,128)(2,1)S(1)} %collective-permute-done.9.refs_0_) | copy-start | bytes 983044
  155.1 33.9 %collective-permute-start.1 = (bf16[5,256,128]{2,1,0:T(8,128)(2,1)S(1)}, bf16[5,256,128]{2,1,0:T(8,128)(2,1)}, u32[]{:S(2)}, u32[]{:S(2)}) collective-permute-start(bf16[5,256,128]{2,1,0:T(8,128)(2,1)S(1)} %copy-done.19), channel_id=1, source_target_pairs={{0,2},{1,3},{2,0},{3,1},{4,6},{5,7},{6,4},{7,5},{8,10},{9,11},{10,... | collective-permute-start | bytes 983048 | tf_op jit(solution)/shard_map/ppermute | solution.py:224
  182.7 11.2 %copy-start.27 = (bf16[5,256,128]{2,1,0:T(8,128)(2,1)}, bf16[5,256,128]{2,1,0:T(8,128)(2,1)S(1)}, u32[]{:S(2)}) copy-start(bf16[5,256,128]{2,1,0:T(8,128)(2,1)S(1)} %collective-permute-done.2.refs_3_) | copy-start | bytes 983044
  182.7 63.2 %copy-start.16 = (bf16[5,256,128]{2,1,0:T(8,128)(2,1)S(1)}, bf16[5,256,128]{2,1,0:T(8,128)(2,1)}, u32[]{:S(2)}) copy-start(bf16[5,256,128]{2,1,0:T(8,128)(2,1)} %get-tuple-element.96.refs_1_) | copy-start | bytes 983044
  182.7 27.6 %collective-permute-start.19 = (bf16[5,256,128]{2,1,0:T(8,128)(2,1)}, bf16[5,256,128]{2,1,0:T(8,128)(2,1)S(1)}, u32[]{:S(2)}, u32[]{:S(2)}) collective-permute-start(bf16[5,256,128]{2,1,0:T(8,128)(2,1)} %get-tuple-element.98), channel_id=1, source_target_pairs={{0,1},{1,0},{2,3},{3,2},{4,5},{5,4},{6,7},{7,6},{8,9},{9,8},{10,11... | collective-permute-start | bytes 983048 | tf_op jit(solution)/shard_map/ppermute | solution.py:224
  184.1 26.7 %collective-permute-start.21 = (bf16[5,256,128]{2,1,0:T(8,128)(2,1)}, bf16[5,256,128]{2,1,0:T(8,128)(2,1)S(1)}, u32[]{:S(2)}, u32[]{:S(2)}) collective-permute-start(bf16[5,256,128]{2,1,0:T(8,128)(2,1)} %get-tuple-element.100), channel_id=1, source_target_pairs={{0,2},{1,3},{2,0},{3,1},{4,6},{5,7},{6,4},{7,5},{8,10},{9,11},{10,... | collective-permute-start | bytes 983048 | tf_op jit(solution)/shard_map/ppermute | solution.py:224
  185.9 45.4 %collective-permute-start.23 = (bf16[5,256,128]{2,1,0:T(8,128)(2,1)}, bf16[5,256,128]{2,1,0:T(8,128)(2,1)S(1)}, u32[]{:S(2)}, u32[]{:S(2)}) collective-permute-start(bf16[5,256,128]{2,1,0:T(8,128)(2,1)} %get-tuple-element.102), channel_id=1, source_target_pairs={{0,3},{1,2},{2,1},{3,0},{4,7},{5,6},{6,5},{7,4},{8,11},{9,10},{10,... | collective-permute-start | bytes 983048 | tf_op jit(solution)/shard_map/ppermute | solution.py:224
  186.2 7.8 %copy-start.28 = (bf16[5,256,128]{2,1,0:T(8,128)(2,1)}, bf16[5,256,128]{2,1,0:T(8,128)(2,1)S(1)}, u32[]{:S(2)}) copy-start(bf16[5,256,128]{2,1,0:T(8,128)(2,1)S(1)} %collective-permute-done.refs_1_) | copy-start | bytes 983044
  207.2 24.1 %collective-permute-start.18 = (bf16[5,256,128]{2,1,0:T(8,128)(2,1)}, bf16[5,256,128]{2,1,0:T(8,128)(2,1)S(1)}, u32[]{:S(2)}, u32[]{:S(2)}) collective-permute-start(bf16[5,256,128]{2,1,0:T(8,128)(2,1)} %get-tuple-element.97), channel_id=1, source_target_pairs={{0,1},{1,0},{2,3},{3,2},{4,5},{5,4},{6,7},{7,6},{8,9},{9,8},{10,11... | collective-permute-start | bytes 983048 | tf_op jit(solution)/shard_map/ppermute | solution.py:224
  207.2 31.1 %collective-permute-start.20 = (bf16[5,256,128]{2,1,0:T(8,128)(2,1)}, bf16[5,256,128]{2,1,0:T(8,128)(2,1)S(1)}, u32[]{:S(2)}, u32[]{:S(2)}) collective-permute-start(bf16[5,256,128]{2,1,0:T(8,128)(2,1)} %get-tuple-element.99), channel_id=1, source_target_pairs={{0,2},{1,3},{2,0},{3,1},{4,6},{5,7},{6,4},{7,5},{8,10},{9,11},{10,... | collective-permute-start | bytes 983048 | tf_op jit(solution)/shard_map/ppermute | solution.py:224
  210.3 35.6 %collective-permute-start.22 = (bf16[5,256,128]{2,1,0:T(8,128)(2,1)}, bf16[5,256,128]{2,1,0:T(8,128)(2,1)S(1)}, u32[]{:S(2)}, u32[]{:S(2)}) collective-permute-start(bf16[5,256,128]{2,1,0:T(8,128)(2,1)} %get-tuple-element.101), channel_id=1, source_target_pairs={{0,3},{1,2},{2,1},{3,0},{4,7},{5,6},{6,5},{7,4},{8,11},{9,10},{10,... | collective-permute-start | bytes 983048 | tf_op jit(solution)/shard_map/ppermute | solution.py:224
  245.9 1.0 copy-start.17

commit v6 on v5

--- a/solution.py
+++ b/solution.py
@@ -122,7 +122,7 @@
     )(picks, *pieces[::-1], *held)
 
 
-def attend(queries, keys, values, far, places, turn):
+def attend(queries, keys, values, far, places, orders):
     partners = len(queries)
     count, rows, size = queries[0].shape
     far_count = len(far)
@@ -133,8 +133,9 @@
     factor = math.log2(math.e) / math.sqrt(size)
 
     def kernel(place_ref, *refs):
-        q_refs = refs[:partners][::turn]
-        k_refs, v_refs = refs[partners : 2 * partners][::-1], refs[2 * partners : 3 * partners]
+        q_refs, k_refs, v_refs = (
+            [refs[i * partners + order.index(k)] for k in range(partners)] for i, order in enumerate(orders)
+        )
         far_refs = refs[3 * partners : 3 * partners + far_count]
         outs, (k_pool, v_pool) = refs[3 * partners + far_count : -2], refs[-2:]
         for k in range(partners):
@@ -176,12 +177,19 @@
             scratch_shapes=[pltpu.VMEM((pool_size, TILE, size), BF16)] * 2,
         ),
         out_shape=[jax.ShapeDtypeStruct((count, rows, size), BF16)] * partners,
+        compiler_params=pltpu.CompilerParams(vmem_limit_bytes=50 * 2**20),
         cost_estimate=pl.CostEstimate(
             flops=pairs * 4 * TILE * TILE * size,
             bytes_accessed=count * 2 * TILE * size * (2 * near + 2 * pool_size),
             transcendentals=pairs * TILE * TILE,
         ),
-    )(places, *queries[::turn], *keys[::-1], *values, *far)
+    )(places, *(side[k] for side, order in zip((queries, keys, values), orders) for k in order), *far)
+
+
+def orders_of(partners, c):
+    up = list(range(partners))
+    down = up[::-1]
+    return [down if c else up, down, up]
 
 
 def plan(key_tiles, my_shard, here, shards, partners, tiles):
@@ -244,7 +252,7 @@
     asked = [exchange(query_parts, c) for c in range(len(chunks))]
     answers = []
     for c in range(len(chunks)):
-        outs, _ = lax.optimization_barrier((attend(asked[c], *ready[c], places, -1 if c else 1), [pieces[-1] for pieces in asked]))
+        outs, _ = lax.optimization_barrier((attend(asked[c], *ready[c], places, orders_of(partners, c)), [pieces[-1] for pieces in asked]))
         answers.append([swap(outs[k], k) for k in range(partners)])
     return from_partners([[answers[c][k] for c in range(len(chunks))] for k in range(partners)], here_arg, chunks, heads)
 

time: 250 us -> 248 us (level)
  waiting for transfers between devices: 155 us -> 149 us
  local copies, waits for them, and re-layouts: 2.39 us -> 7.16 us
    unnamed x61 -> x39, local copies, waits for them, and re-layouts: 1.18 us -> 5.95 us
    ppermute x24, waiting for transfers between devices: 148 us -> 145 us  [swap(): lax.ppermute(piece, 'head', [(i, i ^ k) for i in range(partners)])]
  transfers between devices with their start and end apart: 26 -> 26, of which waited for: 18 -> 17; matrix products, arithmetic and copies ran while one was open for 1% -> 1% of each run, Pallas kernels for 16% -> 16%
where the time goes in v6:
time: 248 us
  waiting for transfers between devices  149 us (60%)
  Pallas kernels  47.7 us (19%)
  starting transfers between devices  42.3 us (17%)
  local copies, waits for them, and re-layouts  7.16 us (3%)
    ppermute x24, waiting for transfers between devices, swap(): lax.ppermute(piece, 'head', [(i, i ^ k) for i in range(partners)])  145 us
    ppermute x24, starting transfers between devices, swap(): lax.ppermute(piece, 'head', [(i, i ^ k) for i in range(partners)])  31 us
    pallas_call x2, Pallas kernels, attend(): pl.pallas_call(kernel, grid_spec=pltpu.PrefetchScalarGridSpec(num_scalar_...  26.8 us
    all_to_all x2, starting transfers between devices, share(): return [lax.all_to_all(sent, 'seq', 0, 0, tiled=True)]  11.3 us
    pallas_call x3, Pallas kernels, by_partner(): pl.pallas_call(kernel, grid_spec=pltpu.PrefetchScalarGridSpec(num_scalar_...  9.76 us
    pallas_call x4, Pallas kernels, pick_tiles(): pl.pallas_call(kernel, in_specs=[pl.BlockSpec(memory_space=pltpu.SMEM)] +...  9.01 us
    unnamed x39, local copies, waits for them, and re-layouts  5.95 us
  transfers between devices with their start and end apart: 26, of which 17 were waited for; matrix products, arithmetic and copies ran while one was open for 1% of the time, Pallas kernels for 16%

profile of v6, /device:TPU:10, one launch (start us, length us, event | category | flops | bytes accessed | tf_op | source)
XLA Modules:
  0.0 247.7 jit_solution(1601207953162465247)
XLA Ops:
  0.0 3.2 %shard_map.47 = (bf16[5,256,128]{2,1,0:T(8,128)(2,1)}, bf16[5,256,128]{2,1,0:T(8,128)(2,1)}, bf16[5,256,128]{2,1,0:T(8,128)(2,1)}, bf16[5,256,128]{2,1,0:T(8,128...) custom-call(s32[1]{0:T(128)} %bitcast.here_ref, ...), custom_call_target="tpu_custom_call" | custom-call | tf_op jit(solution)/shard_map/pallas_call | solution.py:41
  3.2 1.6 collective-permute-start.12
  4.9 1.2 collective-permute-start.13
  6.1 1.2 collective-permute-start.14
  7.4 3.3 %shard_map.48 = (bf16[5,256,128]{2,1,0:T(8,128)(2,1)}, bf16[5,256,128]{2,1,0:T(8,128)(2,1)}, bf16[5,256,128]{2,1,0:T(8,128)(2,1)}, bf16[5,256,128]{2,1,0:T(8,128...) custom-call(s32[1]{0:T(128)} %bitcast.here_ref, ...), custom_call_target="tpu_custom_call" | custom-call | tf_op jit(solution)/shard_map/pallas_call | solution.py:41
  10.6 0.8 collective-permute-start.15
  11.5 2.2 collective-permute-start.16
  13.7 0.1 copy.11
  13.9 0.3 compare_reduce_fusion
  14.2 3.3 %shard_map.46 = (bf16[5,256,128]{2,1,0:T(8,128)(2,1)}, bf16[5,256,128]{2,1,0:T(8,128)(2,1)}, bf16[5,256,128]{2,1,0:T(8,128)(2,1)}, bf16[5,256,128]{2,1,0:T(8,128...) custom-call(s32[1]{0:T(128)} %bitcast.here_ref, ...), custom_call_target="tpu_custom_call" | custom-call | tf_op jit(solution)/shard_map/pallas_call | solution.py:41
  17.4 0.2 reduce_window_sum.18
  17.6 10.4 %collective-permute-done.12.refs_0_.refs_4_ = bf16[5,256,128]{2,1,0:T(8,128)(2,1)S(1)} collective-permute-done((bf16[5,256,128]{2,1,0:T(8,128)(2,1)}, bf16[5,256,128]{2,1,0:T(8,128)(2,1)S(1)}, u32[]{:S(2)}, u32[]{:S(2)}) %collective-permute-start.12) | collective-permute-done | bytes 327712 | tf_op jit(solution)/shard_map/ppermute | solution.py:232
  28.0 1.8 collective-permute-start.17
  29.7 0.1 select_reduce_fusion.1
  30.0 4.4 %collective-permute-done.13.refs_1_.refs_5_ = bf16[5,256,128]{2,1,0:T(8,128)(2,1)S(1)} collective-permute-done((bf16[5,256,128]{2,1,0:T(8,128)(2,1)}, bf16[5,256,128]{2,1,0:T(8,128)(2,1)S(1)}, u32[]{:S(2)}, u32[]{:S(2)}) %collective-permute-start.13) | collective-permute-done | bytes 327712 | tf_op jit(solution)/shard_map/ppermute | solution.py:232
  34.3 2.2 shard_map.52.refs_4_
  36.6 0.7 collective-permute-done.15.refs_2_.refs_9_
  37.3 18.2 %collective-permute-done.16.refs_1_.refs_10_ = bf16[5,256,128]{2,1,0:T(8,128)(2,1)S(1)} collective-permute-done((bf16[5,256,128]{2,1,0:T(8,128)(2,1)}, bf16[5,256,128]{2,1,0:T(8,128)(2,1)S(1)}, u32[]{:S(2)}, u32[]{:S(2)}) %collective-permute-start.16) | collective-permute-done | bytes 327712 | tf_op jit(solution)/shard_map/ppermute | solution.py:232
  55.5 6.7 %collective-permute-done.17.refs_0_.refs_11_ = bf16[5,256,128]{2,1,0:T(8,128)(2,1)S(1)} collective-permute-done((bf16[5,256,128]{2,1,0:T(8,128)(2,1)}, bf16[5,256,128]{2,1,0:T(8,128)(2,1)S(1)}, u32[]{:S(2)}, u32[]{:S(2)}) %collective-permute-start.17) | collective-permute-done | bytes 327712 | tf_op jit(solution)/shard_map/ppermute | solution.py:232
  62.2 2.2 shard_map.53
  64.5 5.2 %all-to-all-start.1 = ((bf16[8,2,2,5,128,128]{5,4,3,2,1,0:T(8,128)(2,1)}), bf16[8,2,2,5,128,128]{5,4,3,2,1,0:T(8,128)(2,1)}, u32[]{:S(2)}, u32[]{:S(2)}) async-start(bf16[8,2,2,5,128,128]{5,4,3,2,1,0:T(8,128)(2,1)} %shard_map.53), calls=%async_computation.1 | async-start | bytes 10485760 | tf_op jit(solution)/shard_map/all_to_all | solution.py:244
  69.7 1.6 collective-permute-start.3
  71.3 1.9 collective-permute-start.5
  73.2 0.1 collective-permute-start.6
  73.3 2.9 %collective-permute-start.7 = (bf16[5,256,128]{2,1,0:T(8,128)(2,1)}, bf16[5,256,128]{2,1,0:T(8,128)(2,1)S(1)}, u32[]{:S(2)}, u32[]{:S(2)}) collective-permute-start(bf16[5,256,128]{2,1,0:T(8,128)(2,1)} %get-tuple-element.72), channel_id=1, source_target_pairs={{0,2},{1,3},{2,0},{3,1},{4,6},{5,7},{6,4},{7,5},{8,10},{9,11},{10,... | collective-permute-start | bytes 983048 | tf_op jit(solution)/shard_map/ppermute | solution.py:232
  76.2 13.3 %collective-permute-done.3.refs_0_.refs_4_ = bf16[5,256,128]{2,1,0:T(8,128)(2,1)S(1)} collective-permute-done((bf16[5,256,128]{2,1,0:T(8,128)(2,1)}, bf16[5,256,128]{2,1,0:T(8,128)(2,1)S(1)}, u32[]{:S(2)}, u32[]{:S(2)}) %collective-permute-start.3) | collective-permute-done | bytes 327712 | tf_op jit(solution)/shard_map/ppermute | solution.py:232
  89.5 1.8 collective-permute-start.8
  91.3 5.3 %collective-permute-done.4.refs_1_.refs_5_ = bf16[5,256,128]{2,1,0:T(8,128)(2,1)S(1)} collective-permute-done((bf16[5,256,128]{2,1,0:T(8,128)(2,1)}, bf16[5,256,128]{2,1,0:T(8,128)(2,1)S(1)}, u32[]{:S(2)}, u32[]{:S(2)}) %collective-permute-start.4) | collective-permute-done | bytes 327712 | tf_op jit(solution)/shard_map/ppermute | solution.py:232
  96.6 2.3 shard_map.49.refs_4_
  98.9 18.1 %collective-permute-done.7.refs_1_.refs_10_ = bf16[5,256,128]{2,1,0:T(8,128)(2,1)S(1)} collective-permute-done((bf16[5,256,128]{2,1,0:T(8,128)(2,1)}, bf16[5,256,128]{2,1,0:T(8,128)(2,1)S(1)}, u32[]{:S(2)}, u32[]{:S(2)}) %collective-permute-start.7) | collective-permute-done | bytes 327712 | tf_op jit(solution)/shard_map/ppermute | solution.py:232
  117.0 7.6 %collective-permute-done.8.refs_0_.refs_11_ = bf16[5,256,128]{2,1,0:T(8,128)(2,1)S(1)} collective-permute-done((bf16[5,256,128]{2,1,0:T(8,128)(2,1)}, bf16[5,256,128]{2,1,0:T(8,128)(2,1)S(1)}, u32[]{:S(2)}, u32[]{:S(2)}) %collective-permute-start.8) | collective-permute-done | bytes 327712 | tf_op jit(solution)/shard_map/ppermute | solution.py:232
  124.6 2.2 shard_map.50
  126.8 0.7 copy-done.8
  127.6 0.7 copy-done.9
  128.3 0.4 all-to-all-done.1.refs_12_
  128.6 6.1 %all-to-all-start = ((bf16[8,2,2,5,128,128]{5,4,3,2,1,0:T(8,128)(2,1)}), bf16[8,2,2,5,128,128]{5,4,3,2,1,0:T(8,128)(2,1)}, u32[]{:S(2)}, u32[]{:S(2)}) async-start(bf16[8,2,2,5,128,128]{5,4,3,2,1,0:T(8,128)(2,1)} %shard_map.50), calls=%async_computation | async-start | bytes 10485760 | tf_op jit(solution)/shard_map/all_to_all | solution.py:244
  134.7 1.6 collective-permute-start.9
  136.3 1.9 collective-permute-start.11
  138.2 1.6 collective-permute-start.2
  139.8 0.9 collective-permute-start
  140.7 0.1 fusion
  140.9 0.2 reduce_window_sum.17
  141.3 0.3 select_reduce_fusion
  141.9 0.6 gather_fusion
  142.4 12.6 %collective-permute-done.9.refs_0_ = bf16[5,256,128]{2,1,0:T(8,128)(2,1)S(1)} collective-permute-done((bf16[5,256,128]{2,1,0:T(8,128)(2,1)S(1)}, bf16[5,256,128]{2,1,0:T(8,128)(2,1)S(1)}, u32[]{:S(2)}, u32[]{:S(2)}) %collective-permute-start.9) | collective-permute-done | bytes 327712 | tf_op jit(solution)/shard_map/ppermute | solution.py:232
  155.1 0.7 copy-done.12
  155.9 12.4 %collective-permute-done.10.refs_1_ = bf16[5,256,128]{2,1,0:T(8,128)(2,1)} collective-permute-done((bf16[5,256,128]{2,1,0:T(8,128)(2,1)}, bf16[5,256,128]{2,1,0:T(8,128)(2,1)}, u32[]{:S(2)}, u32[]{:S(2)}) %collective-permute-start.10) | collective-permute-done | bytes 327712 | tf_op jit(solution)/shard_map/ppermute | solution.py:232
  168.3 1.0 copy-done.11
  169.2 1.0 copy-done.13
  170.2 13.7 %shard_map.54 = (bf16[5,256,128]{2,1,0:T(8,128)(2,1)S(1)}, bf16[5,256,128]{2,1,0:T(8,128)(2,1)}, bf16[5,256,128]{2,1,0:T(8,128)(2,1)}, bf16[5,256,128]{2,1,0:T(8,128)(2,1)}) custom-call(s32[8,10]{1,0:T(8,128)S(1)} %broadcast_select_fusion.place_ref, bf16[5,256,128]{2,1,0:T(8,128)(2,1)S(1)} %copy-done.13, ...), custom_call_target="tpu_custom_call" | custom-call | flops 3355443200 | bytes 10485760 | tf_op jit(solution)/shard_map/pallas_call | solution.py:170
  183.9 2.4 collective-permute-start.19
  186.4 1.4 collective-permute-start.21
  187.7 0.5 collective-permute-start.23
  188.2 0.7 collective-permute-done.1.refs_2_
  188.9 0.7 copy-done.14
  189.6 4.1 %all-to-all-done.refs_12_ = bf16[8,2,2,5,128,128]{5,4,3,2,1,0:T(8,128)(2,1)} async-done(((bf16[8,2,2,5,128,128]{5,4,3,2,1,0:T(8,128)(2,1)}), bf16[8,2,2,5,128,128]{5,4,3,2,1,0:T(8,128)(2,1)}, u32[]{:S(2)}, u32[]{:S(2)}) %all-to-all-start) | async-done | bytes 5242912 | tf_op jit(solution)/shard_map/all_to_all | solution.py:244
  193.7 1.0 copy-done.15
  194.6 13.1 %shard_map.51 = (bf16[5,256,128]{2,1,0:T(8,128)(2,1)S(1)}, bf16[5,256,128]{2,1,0:T(8,128)(2,1)S(1)}, bf16[5,256,128]{2,1,0:T(8,128)(2,1)S(1)}, bf16[5,256,128]{2,1,0:T(8,128)(2,1)S(1)}) custom-call(s32[8,10]{1,0:T(8,128)S(1)} %broadcast_select_fusion.place_ref, bf16[5,256,128]{2,1,0:T(8,128)(2,1)S(1)} %copy-done.10, ...), custom_call_target="tpu_custom_call" | custom-call | flops 3355443200 | bytes 10485760 | tf_op jit(solution)/shard_map/pallas_call | solution.py:170
  207.8 3.0 %collective-permute-start.20 = (bf16[5,256,128]{2,1,0:T(8,128)(2,1)S(1)}, bf16[5,256,128]{2,1,0:T(8,128)(2,1)S(1)}, u32[]{:S(2)}, u32[]{:S(2)}) collective-permute-start(bf16[5,256,128]{2,1,0:T(8,128)(2,1)S(1)} %get-tuple-element.99), channel_id=1, source_target_pairs={{0,2},{1,3},{2,0},{3,1},{4,6},{5,7},{6,4},{7,5},{8,10},{9,11},{10,... | collective-permute-start | bytes 983048 | tf_op jit(solution)/shard_map/ppermute | solution.py:232
  210.9 0.4 collective-permute-start.22
  211.3 19.8 %collective-permute-done.23.refs_7_ = bf16[5,256,128]{2,1,0:T(8,128)(2,1)S(1)} collective-permute-done((bf16[5,256,128]{2,1,0:T(8,128)(2,1)}, bf16[5,256,128]{2,1,0:T(8,128)(2,1)S(1)}, u32[]{:S(2)}, u32[]{:S(2)}) %collective-permute-start.23) | collective-permute-done | bytes 327712 | tf_op jit(solution)/shard_map/ppermute | solution.py:232
  231.2 7.1 %collective-permute-done.20.refs_4_ = bf16[5,256,128]{2,1,0:T(8,128)(2,1)S(1)} collective-permute-done((bf16[5,256,128]{2,1,0:T(8,128)(2,1)S(1)}, bf16[5,256,128]{2,1,0:T(8,128)(2,1)S(1)}, u32[]{:S(2)}, u32[]{:S(2)}) %collective-permute-start.20) | collective-permute-done | bytes 327712 | tf_op jit(solution)/shard_map/ppermute | solution.py:232
  238.2 7.4 %collective-permute-done.22.refs_6_ = bf16[5,256,128]{2,1,0:T(8,128)(2,1)S(1)} collective-permute-done((bf16[5,256,128]{2,1,0:T(8,128)(2,1)S(1)}, bf16[5,256,128]{2,1,0:T(8,128)(2,1)S(1)}, u32[]{:S(2)}, u32[]{:S(2)}) %collective-permute-start.22) | collective-permute-done | bytes 327712 | tf_op jit(solution)/shard_map/ppermute | solution.py:232
  245.6 2.1 shard_map.55
  (63 shorter events, 1.0 us)
Async XLA Ops:
  0.0 13.7 %copy-start.16 = (s32[64,10]{0,1:T(8,128)S(1)}, s32[64,10]{0,1:T(8,128)}, u32[]{:S(2)}) copy-start(s32[64,10]{0,1:T(8,128)} %param.7) | copy-start | bytes 7684
  3.2 31.1 %copy-start.2 = (bf16[5,256,128]{2,1,0:T(8,128)(2,1)S(1)}, bf16[5,256,128]{2,1,0:T(8,128)(2,1)}, u32[]{:S(2)}) copy-start(bf16[5,256,128]{2,1,0:T(8,128)(2,1)} %get-tuple-element.87.refs_3_.refs_7_) | copy-start | bytes 983044
  3.2 24.7 %collective-permute-start.12 = (bf16[5,256,128]{2,1,0:T(8,128)(2,1)}, bf16[5,256,128]{2,1,0:T(8,128)(2,1)S(1)}, u32[]{:S(2)}, u32[]{:S(2)}) collective-permute-start(bf16[5,256,128]{2,1,0:T(8,128)(2,1)} %get-tuple-element.84), channel_id=1, source_target_pairs={{0,3},{1,2},{2,1},{3,0},{4,7},{5,6},{6,5},{7,4},{8,11},{9,10},{10,... | collective-permute-start | bytes 983048 | tf_op jit(solution)/shard_map/ppermute | solution.py:232
  4.9 29.5 %collective-permute-start.13 = (bf16[5,256,128]{2,1,0:T(8,128)(2,1)}, bf16[5,256,128]{2,1,0:T(8,128)(2,1)S(1)}, u32[]{:S(2)}, u32[]{:S(2)}) collective-permute-start(bf16[5,256,128]{2,1,0:T(8,128)(2,1)} %get-tuple-element.85), channel_id=1, source_target_pairs={{0,2},{1,3},{2,0},{3,1},{4,6},{5,7},{6,4},{7,5},{8,10},{9,11},{10,... | collective-permute-start | bytes 983048 | tf_op jit(solution)/shard_map/ppermute | solution.py:232
  6.1 28.2 %collective-permute-start.14 = (bf16[5,256,128]{2,1,0:T(8,128)(2,1)}, bf16[5,256,128]{2,1,0:T(8,128)(2,1)S(1)}, u32[]{:S(2)}, u32[]{:S(2)}) collective-permute-start(bf16[5,256,128]{2,1,0:T(8,128)(2,1)} %get-tuple-element.86), channel_id=1, source_target_pairs={{0,1},{1,0},{2,3},{3,2},{4,5},{5,4},{6,7},{7,6},{8,9},{9,8},{10,11... | collective-permute-start | bytes 983048 | tf_op jit(solution)/shard_map/ppermute | solution.py:232
  10.6 51.6 %copy-start.3 = (bf16[5,256,128]{2,1,0:T(8,128)(2,1)S(1)}, bf16[5,256,128]{2,1,0:T(8,128)(2,1)}, u32[]{:S(2)}) copy-start(bf16[5,256,128]{2,1,0:T(8,128)(2,1)} %get-tuple-element.88.refs_3_.refs_8_) | copy-start | bytes 983044
  10.6 26.6 %collective-permute-start.15 = (bf16[5,256,128]{2,1,0:T(8,128)(2,1)}, bf16[5,256,128]{2,1,0:T(8,128)(2,1)S(1)}, u32[]{:S(2)}, u32[]{:S(2)}) collective-permute-start(bf16[5,256,128]{2,1,0:T(8,128)(2,1)} %get-tuple-element.89), channel_id=1, source_target_pairs={{0,1},{1,0},{2,3},{3,2},{4,5},{5,4},{6,7},{7,6},{8,9},{9,8},{10,11... | collective-permute-start | bytes 983048 | tf_op jit(solution)/shard_map/ppermute | solution.py:232
  11.5 44.0 %collective-permute-start.16 = (bf16[5,256,128]{2,1,0:T(8,128)(2,1)}, bf16[5,256,128]{2,1,0:T(8,128)(2,1)S(1)}, u32[]{:S(2)}, u32[]{:S(2)}) collective-permute-start(bf16[5,256,128]{2,1,0:T(8,128)(2,1)} %get-tuple-element.90), channel_id=1, source_target_pairs={{0,2},{1,3},{2,0},{3,1},{4,6},{5,7},{6,4},{7,5},{8,10},{9,11},{10,... | collective-permute-start | bytes 983048 | tf_op jit(solution)/shard_map/ppermute | solution.py:232
  28.0 34.2 %collective-permute-start.17 = (bf16[5,256,128]{2,1,0:T(8,128)(2,1)}, bf16[5,256,128]{2,1,0:T(8,128)(2,1)S(1)}, u32[]{:S(2)}, u32[]{:S(2)}) collective-permute-start(bf16[5,256,128]{2,1,0:T(8,128)(2,1)} %get-tuple-element.91), channel_id=1, source_target_pairs={{0,3},{1,2},{2,1},{3,0},{4,7},{5,6},{6,5},{7,4},{8,11},{9,10},{10,... | collective-permute-start | bytes 983048 | tf_op jit(solution)/shard_map/ppermute | solution.py:232
  37.2 27.2 %copy-start.4 = (bf16[5,256,128]{2,1,0:T(8,128)(2,1)}, bf16[5,256,128]{2,1,0:T(8,128)(2,1)S(1)}, u32[]{:S(2)}) copy-start(bf16[5,256,128]{2,1,0:T(8,128)(2,1)S(1)} %collective-permute-done.15.refs_2_.refs_9_) | copy-start | bytes 983044
  55.5 8.9 %copy-start.5 = (bf16[5,256,128]{2,1,0:T(8,128)(2,1)}, bf16[5,256,128]{2,1,0:T(8,128)(2,1)S(1)}, u32[]{:S(2)}) copy-start(bf16[5,256,128]{2,1,0:T(8,128)(2,1)S(1)} %collective-permute-done.16.refs_1_.refs_10_) | copy-start | bytes 983044
  62.2 2.3 copy-start.6
  64.5 6.8 %copy-start.18 = (bf16[5,256,128]{2,1,0:T(8,128)(2,1)S(1)}, bf16[5,256,128]{2,1,0:T(8,128)(2,1)}, u32[]{:S(2)}) copy-start(bf16[5,256,128]{2,1,0:T(8,128)(2,1)} %get-tuple-element.68) | copy-start | bytes 983044
  64.5 32.1 %copy-start = (bf16[5,256,128]{2,1,0:T(8,128)(2,1)S(1)}, bf16[5,256,128]{2,1,0:T(8,128)(2,1)}, u32[]{:S(2)}) copy-start(bf16[5,256,128]{2,1,0:T(8,128)(2,1)} %get-tuple-element.69.refs_3_.refs_7_) | copy-start | bytes 983044
  64.5 64.2 %all-to-all-start.1 = ((bf16[8,2,2,5,128,128]{5,4,3,2,1,0:T(8,128)(2,1)}), bf16[8,2,2,5,128,128]{5,4,3,2,1,0:T(8,128)(2,1)}, u32[]{:S(2)}, u32[]{:S(2)}) async-start(bf16[8,2,2,5,128,128]{5,4,3,2,1,0:T(8,128)(2,1)} %shard_map.53), calls=%async_computation.1 | async-start | bytes 10485760 | tf_op jit(solution)/shard_map/all_to_all | solution.py:244
  69.7 54.9 %copy-start.1 = (bf16[5,256,128]{2,1,0:T(8,128)(2,1)S(1)}, bf16[5,256,128]{2,1,0:T(8,128)(2,1)}, u32[]{:S(2)}) copy-start(bf16[5,256,128]{2,1,0:T(8,128)(2,1)} %get-tuple-element.70.refs_3_.refs_8_) | copy-start | bytes 983044
  69.7 19.8 %collective-permute-start.3 = (bf16[5,256,128]{2,1,0:T(8,128)(2,1)}, bf16[5,256,128]{2,1,0:T(8,128)(2,1)S(1)}, u32[]{:S(2)}, u32[]{:S(2)}) collective-permute-start(bf16[5,256,128]{2,1,0:T(8,128)(2,1)} %get-tuple-element.66), channel_id=1, source_target_pairs={{0,3},{1,2},{2,1},{3,0},{4,7},{5,6},{6,5},{7,4},{8,11},{9,10},{10,... | collective-permute-start | bytes 983048 | tf_op jit(solution)/shard_map/ppermute | solution.py:232
  71.3 25.3 %collective-permute-start.4 = (bf16[5,256,128]{2,1,0:T(8,128)(2,1)}, bf16[5,256,128]{2,1,0:T(8,128)(2,1)S(1)}, u32[]{:S(2)}, u32[]{:S(2)}) collective-permute-start(bf16[5,256,128]{2,1,0:T(8,128)(2,1)} %get-tuple-element.67), channel_id=1, source_target_pairs={{0,2},{1,3},{2,0},{3,1},{4,6},{5,7},{6,4},{7,5},{8,10},{9,11},{10,... | collective-permute-start | bytes 983048 | tf_op jit(solution)/shard_map/ppermute | solution.py:232
  71.3 25.3 %collective-permute-start.5 = (bf16[5,256,128]{2,1,0:T(8,128)(2,1)S(1)}, bf16[5,256,128]{2,1,0:T(8,128)(2,1)S(1)}, u32[]{:S(2)}, u32[]{:S(2)}) collective-permute-start(bf16[5,256,128]{2,1,0:T(8,128)(2,1)S(1)} %copy-done.18), channel_id=1, source_target_pairs={{0,1},{1,0},{2,3},{3,2},{4,5},{5,4},{6,7},{7,6},{8,9},{9,8},{10,11... | collective-permute-start | bytes 983048 | tf_op jit(solution)/shard_map/ppermute | solution.py:232
  73.2 25.7 %collective-permute-start.6 = (bf16[5,256,128]{2,1,0:T(8,128)(2,1)}, bf16[5,256,128]{2,1,0:T(8,128)(2,1)S(1)}, u32[]{:S(2)}, u32[]{:S(2)}) collective-permute-start(bf16[5,256,128]{2,1,0:T(8,128)(2,1)} %get-tuple-element.71), channel_id=1, source_target_pairs={{0,1},{1,0},{2,3},{3,2},{4,5},{5,4},{6,7},{7,6},{8,9},{9,8},{10,11... | collective-permute-start | bytes 983048 | tf_op jit(solution)/shard_map/ppermute | solution.py:232
  73.3 43.7 %collective-permute-start.7 = (bf16[5,256,128]{2,1,0:T(8,128)(2,1)}, bf16[5,256,128]{2,1,0:T(8,128)(2,1)S(1)}, u32[]{:S(2)}, u32[]{:S(2)}) collective-permute-start(bf16[5,256,128]{2,1,0:T(8,128)(2,1)} %get-tuple-element.72), channel_id=1, source_target_pairs={{0,2},{1,3},{2,0},{3,1},{4,6},{5,7},{6,4},{7,5},{8,10},{9,11},{10,... | collective-permute-start | bytes 983048 | tf_op jit(solution)/shard_map/ppermute | solution.py:232
  89.5 35.1 %collective-permute-start.8 = (bf16[5,256,128]{2,1,0:T(8,128)(2,1)}, bf16[5,256,128]{2,1,0:T(8,128)(2,1)S(1)}, u32[]{:S(2)}, u32[]{:S(2)}) collective-permute-start(bf16[5,256,128]{2,1,0:T(8,128)(2,1)} %get-tuple-element.73), channel_id=1, source_target_pairs={{0,3},{1,2},{2,1},{3,0},{4,7},{5,6},{6,5},{7,4},{8,11},{9,10},{10,... | collective-permute-start | bytes 983048 | tf_op jit(solution)/shard_map/ppermute | solution.py:232
  98.9 27.9 %copy-start.7 = (bf16[5,256,128]{2,1,0:T(8,128)(2,1)}, bf16[5,256,128]{2,1,0:T(8,128)(2,1)S(1)}, u32[]{:S(2)}) copy-start(bf16[5,256,128]{2,1,0:T(8,128)(2,1)S(1)} %collective-permute-done.6.refs_2_.refs_9_) | copy-start | bytes 983044
  126.8 0.7 copy-start.8
  127.6 0.7 copy-start.9
  128.3 6.4 %copy-start.17 = (bf16[5,256,128]{2,1,0:T(8,128)(2,1)S(1)}, bf16[5,256,128]{2,1,0:T(8,128)(2,1)}, u32[]{:S(2)}) copy-start(bf16[5,256,128]{2,1,0:T(8,128)(2,1)} %get-tuple-element.79) | copy-start | bytes 983044
  128.6 65.0 %all-to-all-start = ((bf16[8,2,2,5,128,128]{5,4,3,2,1,0:T(8,128)(2,1)}), bf16[8,2,2,5,128,128]{5,4,3,2,1,0:T(8,128)(2,1)}, u32[]{:S(2)}, u32[]{:S(2)}) async-start(bf16[8,2,2,5,128,128]{5,4,3,2,1,0:T(8,128)(2,1)} %shard_map.50), calls=%async_computation | async-start | bytes 10485760 | tf_op jit(solution)/shard_map/all_to_all | solution.py:244
  134.7 20.3 %collective-permute-start.9 = (bf16[5,256,128]{2,1,0:T(8,128)(2,1)S(1)}, bf16[5,256,128]{2,1,0:T(8,128)(2,1)S(1)}, u32[]{:S(2)}, u32[]{:S(2)}) collective-permute-start(bf16[5,256,128]{2,1,0:T(8,128)(2,1)S(1)} %copy-done.17), channel_id=1, source_target_pairs={{0,3},{1,2},{2,1},{3,0},{4,7},{5,6},{6,5},{7,4},{8,11},{9,10},{10,... | collective-permute-start | bytes 983048 | tf_op jit(solution)/shard_map/ppermute | solution.py:232
  136.3 32.0 %collective-permute-start.10 = (bf16[5,256,128]{2,1,0:T(8,128)(2,1)}, bf16[5,256,128]{2,1,0:T(8,128)(2,1)}, u32[]{:S(2)}, u32[]{:S(2)}) collective-permute-start(bf16[5,256,128]{2,1,0:T(8,128)(2,1)} %get-tuple-element.81), channel_id=1, source_target_pairs={{0,2},{1,3},{2,0},{3,1},{4,6},{5,7},{6,4},{7,5},{8,10},{9,11},{10,... | collective-permute-start | bytes 983048 | tf_op jit(solution)/shard_map/ppermute | solution.py:232
  136.3 32.0 %collective-permute-start.11 = (bf16[5,256,128]{2,1,0:T(8,128)(2,1)}, bf16[5,256,128]{2,1,0:T(8,128)(2,1)}, u32[]{:S(2)}, u32[]{:S(2)}) collective-permute-start(bf16[5,256,128]{2,1,0:T(8,128)(2,1)} %get-tuple-element.82), channel_id=1, source_target_pairs={{0,1},{1,0},{2,3},{3,2},{4,5},{5,4},{6,7},{7,6},{8,9},{9,8},{10,11... | collective-permute-start | bytes 983048 | tf_op jit(solution)/shard_map/ppermute | solution.py:232
  138.2 45.7 %collective-permute-start.2 = (bf16[5,256,128]{2,1,0:T(8,128)(2,1)}, bf16[5,256,128]{2,1,0:T(8,128)(2,1)}, u32[]{:S(2)}, u32[]{:S(2)}) collective-permute-start(bf16[5,256,128]{2,1,0:T(8,128)(2,1)} %get-tuple-element.65), channel_id=1, source_target_pairs={{0,3},{1,2},{2,1},{3,0},{4,7},{5,6},{6,5},{7,4},{8,11},{9,10},{10,... | collective-permute-start | bytes 983048 | tf_op jit(solution)/shard_map/ppermute | solution.py:232
  139.8 48.4 %collective-permute-start = (bf16[5,256,128]{2,1,0:T(8,128)(2,1)}, bf16[5,256,128]{2,1,0:T(8,128)(2,1)}, u32[]{:S(2)}, u32[]{:S(2)}) collective-permute-start(bf16[5,256,128]{2,1,0:T(8,128)(2,1)} %get-tuple-element.63), channel_id=1, source_target_pairs={{0,1},{1,0},{2,3},{3,2},{4,5},{5,4},{6,7},{7,6},{8,9},{9,8},{10,11... | collective-permute-start | bytes 983048 | tf_op jit(solution)/shard_map/ppermute | solution.py:232
  155.1 0.7 copy-start.12
  155.8 33.1 %collective-permute-start.1 = (bf16[5,256,128]{2,1,0:T(8,128)(2,1)}, bf16[5,256,128]{2,1,0:T(8,128)(2,1)S(1)}, u32[]{:S(2)}, u32[]{:S(2)}) collective-permute-start(bf16[5,256,128]{2,1,0:T(8,128)(2,1)} %get-tuple-element.64), channel_id=1, source_target_pairs={{0,2},{1,3},{2,0},{3,1},{4,6},{5,7},{6,4},{7,5},{8,10},{9,11},{10,... | collective-permute-start | bytes 983048 | tf_op jit(solution)/shard_map/ppermute | solution.py:232
  155.9 37.8 %copy-start.10 = (bf16[5,256,128]{2,1,0:T(8,128)(2,1)S(1)}, bf16[5,256,128]{2,1,0:T(8,128)(2,1)}, u32[]{:S(2)}) copy-start(bf16[5,256,128]{2,1,0:T(8,128)(2,1)} %get-tuple-element.62.refs_0_) | copy-start | bytes 983044
  168.3 1.0 copy-start.11
  169.2 1.0 copy-start.13
  183.9 27.0 %collective-permute-start.19 = (bf16[5,256,128]{2,1,0:T(8,128)(2,1)}, bf16[5,256,128]{2,1,0:T(8,128)(2,1)S(1)}, u32[]{:S(2)}, u32[]{:S(2)}) collective-permute-start(bf16[5,256,128]{2,1,0:T(8,128)(2,1)} %get-tuple-element.98), channel_id=1, source_target_pairs={{0,1},{1,0},{2,3},{3,2},{4,5},{5,4},{6,7},{7,6},{8,9},{9,8},{10,11... | collective-permute-start | bytes 983048 | tf_op jit(solution)/shard_map/ppermute | solution.py:232
  186.4 25.0 %collective-permute-start.21 = (bf16[5,256,128]{2,1,0:T(8,128)(2,1)}, bf16[5,256,128]{2,1,0:T(8,128)(2,1)S(1)}, u32[]{:S(2)}, u32[]{:S(2)}) collective-permute-start(bf16[5,256,128]{2,1,0:T(8,128)(2,1)} %get-tuple-element.100), channel_id=1, source_target_pairs={{0,2},{1,3},{2,0},{3,1},{4,6},{5,7},{6,4},{7,5},{8,10},{9,11},{10,... | collective-permute-start | bytes 983048 | tf_op jit(solution)/shard_map/ppermute | solution.py:232
  187.7 43.5 %collective-permute-start.23 = (bf16[5,256,128]{2,1,0:T(8,128)(2,1)}, bf16[5,256,128]{2,1,0:T(8,128)(2,1)S(1)}, u32[]{:S(2)}, u32[]{:S(2)}) collective-permute-start(bf16[5,256,128]{2,1,0:T(8,128)(2,1)} %get-tuple-element.102), channel_id=1, source_target_pairs={{0,3},{1,2},{2,1},{3,0},{4,7},{5,6},{6,5},{7,4},{8,11},{9,10},{10,... | collective-permute-start | bytes 983048 | tf_op jit(solution)/shard_map/ppermute | solution.py:232
  188.9 0.7 copy-start.14
  193.7 1.0 copy-start.15
  207.8 23.4 %collective-permute-start.18 = (bf16[5,256,128]{2,1,0:T(8,128)(2,1)S(1)}, bf16[5,256,128]{2,1,0:T(8,128)(2,1)S(1)}, u32[]{:S(2)}, u32[]{:S(2)}) collective-permute-start(bf16[5,256,128]{2,1,0:T(8,128)(2,1)S(1)} %get-tuple-element.97), channel_id=1, source_target_pairs={{0,1},{1,0},{2,3},{3,2},{4,5},{5,4},{6,7},{7,6},{8,9},{9,8},{10,11... | collective-permute-start | bytes 983048 | tf_op jit(solution)/shard_map/ppermute | solution.py:232
  207.8 30.4 %collective-permute-start.20 = (bf16[5,256,128]{2,1,0:T(8,128)(2,1)S(1)}, bf16[5,256,128]{2,1,0:T(8,128)(2,1)S(1)}, u32[]{:S(2)}, u32[]{:S(2)}) collective-permute-start(bf16[5,256,128]{2,1,0:T(8,128)(2,1)S(1)} %get-tuple-element.99), channel_id=1, source_target_pairs={{0,2},{1,3},{2,0},{3,1},{4,6},{5,7},{6,4},{7,5},{8,10},{9,11},{10,... | collective-permute-start | bytes 983048 | tf_op jit(solution)/shard_map/ppermute | solution.py:232
  210.9 34.7 %collective-permute-start.22 = (bf16[5,256,128]{2,1,0:T(8,128)(2,1)S(1)}, bf16[5,256,128]{2,1,0:T(8,128)(2,1)S(1)}, u32[]{:S(2)}, u32[]{:S(2)}) collective-permute-start(bf16[5,256,128]{2,1,0:T(8,128)(2,1)S(1)} %get-tuple-element.101), channel_id=1, source_target_pairs={{0,3},{1,2},{2,1},{3,0},{4,7},{5,6},{6,5},{7,4},{8,11},{9,10},{10,... | collective-permute-start | bytes 983048 | tf_op jit(solution)/shard_map/ppermute | solution.py:232

commit v7 on v6

--- a/solution.py
+++ b/solution.py
@@ -10,6 +10,7 @@
 TILE = 128
 CAP = 2
 CHUNKS = 2
+AHEAD = 2
 BF16 = jnp.bfloat16
 F32 = jnp.float32
 
@@ -24,7 +25,7 @@
     return TILE if rows % TILE == 0 else rows
 
 
-def by_partner(array, here, partners, chunks):
+def by_partner(array, here, partners, cuts):
     rows, heads, size = array.shape
     own_heads = heads // partners
     block = row_block(rows)
@@ -32,12 +33,14 @@
     def kernel(here_ref, in_ref, *refs):
         outs, turned = refs[:-1], refs[-1]
         turned[...] = jnp.swapaxes(in_ref[...], 0, 1)
+        at = 0
         for k in range(partners):
             first = (here_ref[0] ^ k) * own_heads
-            for c, (start, count) in enumerate(chunks):
-                outs[k * len(chunks) + c][...] = turned[pl.ds(first + start, count)]
-
-    parts = [count for _ in range(partners) for _, count in chunks]
+            for start, count in cuts[k]:
+                outs[at][...] = turned[pl.ds(first + start, count)]
+                at += 1
+
+    parts = [count for cut in cuts for _, count in cut]
     outs = pl.pallas_call(
         kernel,
         grid_spec=pltpu.PrefetchScalarGridSpec(
@@ -49,7 +52,8 @@
         ),
         out_shape=[jax.ShapeDtypeStruct((count, rows, size), array.dtype) for count in parts],
     )(here, array)
-    return [outs[k * len(chunks) : (k + 1) * len(chunks)] for k in range(partners)]
+    outs = iter(outs)
+    return [[next(outs) for _ in cut] for cut in cuts]
 
 
 def from_partners(pieces, here, chunks, heads):
@@ -124,7 +128,9 @@
 
 def attend(queries, keys, values, far, places, orders):
     partners = len(queries)
-    count, rows, size = queries[0].shape
+    count, rows, size = keys[0].shape
+    rest = list(queries[-1][1:])
+    first = queries[-1][0].shape[0]
     far_count = len(far)
     far_tiles = [part.shape[0] * CAP for part in far]
     tiles = rows // TILE
@@ -133,9 +139,17 @@
     factor = math.log2(math.e) / math.sqrt(size)
 
     def kernel(place_ref, *refs):
+        late, refs = refs[: len(rest)], refs[len(rest) :]
         q_refs, k_refs, v_refs = (
             [refs[i * partners + order.index(k)] for k in range(partners)] for i, order in enumerate(orders)
         )
+        in_late = pl.program_id(0) >= first
+
+        def query_of(k, at):
+            if k < partners - 1 or not late:
+                return q_refs[k][0, at, :]
+            return jnp.where(in_late, late[0][0, at, :], q_refs[k][0, at, :])
+
         far_refs = refs[3 * partners : 3 * partners + far_count]
         outs, (k_pool, v_pool) = refs[3 * partners + far_count : -2], refs[-2:]
         for k in range(partners):
@@ -152,7 +166,7 @@
                 ids = [place_ref[k * tiles + tile, j] for j in range(listed)]
                 key_rows = jnp.concatenate([k_pool[i] for i in ids], axis=0)
                 scores = lax.dot_general(
-                    q_refs[k][0, at, :], key_rows, (((1,), (1,)), ((), ())), preferred_element_type=F32
+                    query_of(k, at), key_rows, (((1,), (1,)), ((), ())), preferred_element_type=F32
                 )
                 row_top = jnp.max(scores, axis=-1, keepdims=True)
                 weights = jnp.exp2((scores - row_top) * factor)
@@ -162,6 +176,8 @@
                 outs[k][0, at, :] = (mixed[:, :size] / mixed[:, size:]).astype(BF16)
 
     head_spec = pl.BlockSpec((1, rows, size), lambda h, _: (h, 0, 0))
+    first_spec = pl.BlockSpec((1, rows, size), lambda h, _: (jnp.minimum(h, first - 1), 0, 0))
+    rest_spec = pl.BlockSpec((1, rows, size), lambda h, _: (jnp.maximum(h - first, 0), 0, 0))
     far_specs = [
         pl.BlockSpec((part.shape[0], 2, CAP, 1, TILE, size), lambda h, _: (0, 0, 0, h, 0, 0)) for part in far
     ]
@@ -172,7 +188,10 @@
         grid_spec=pltpu.PrefetchScalarGridSpec(
             num_scalar_prefetch=1,
             grid=(count,),
-            in_specs=[head_spec] * (3 * partners) + far_specs,
+            in_specs=[rest_spec] * len(rest)
+            + [first_spec if k == partners - 1 else head_spec for k in orders[0]]
+            + [head_spec] * (2 * partners)
+            + far_specs,
             out_specs=[head_spec] * partners,
             scratch_shapes=[pltpu.VMEM((pool_size, TILE, size), BF16)] * 2,
         ),
@@ -183,7 +202,12 @@
             bytes_accessed=count * 2 * TILE * size * (2 * near + 2 * pool_size),
             transcendentals=pairs * TILE * TILE,
         ),
-    )(places, *(side[k] for side, order in zip((queries, keys, values), orders) for k in order), *far)
+    )(
+        places,
+        *rest,
+        *(side[k] for side, order in zip(([part[0] for part in queries], keys, values), orders) for k in order),
+        *far,
+    )
 
 
 def orders_of(partners, c):
@@ -234,25 +258,35 @@
     def exchange(parts, c):
         return [swap(parts[k][c], k) for k in range(partners)]
 
-    key_parts = by_partner(key_vectors, here_arg, partners, chunks)
-    value_parts = by_partner(value_vectors, here_arg, partners, chunks)
-    query_parts = by_partner(queries, here_arg, partners, chunks)
+    cuts = [chunks] * partners
+    key_parts = by_partner(key_vectors, here_arg, partners, cuts)
+    value_parts = by_partner(value_vectors, here_arg, partners, cuts)
+    start, count = chunks[-1]
+    ahead = max(1, count * AHEAD // 5)
+    query_cuts = cuts[:-1] + [chunks[:-1] + [(start, ahead), (start + ahead, count - ahead)]]
+    query_parts = by_partner(queries, here_arg, partners, query_cuts)
     picks, places = plan(key_tiles, my_shard, here, shard_count, partners, tiles)
-
-    def share(keys, values):
+    picks, query_parts = lax.optimization_barrier((picks, query_parts))
+
+    held = [(exchange(key_parts, c), exchange(value_parts, c)) for c in range(len(chunks))]
+    asked = [[[swap(query_parts[k][c], k)] for k in range(partners)] for c in range(len(chunks) - 1)]
+    asked.append([[swap(query_parts[k][len(chunks) - 1], k)] for k in range(partners - 1)])
+    early, _ = lax.optimization_barrier((query_parts[-1][-2], held[0][0][-1]))
+    early = swap(early, partners - 1)
+    asked[-1].append([early, swap(query_parts[-1][-1], partners - 1)])
+
+    def share(c):
+        keys, values = held[c]
         sent = pick_tiles(values, picks, 1, pick_tiles(keys, picks, 0, None))
+        if c == 0:
+            sent, _ = lax.optimization_barrier((sent, early))
         return [lax.all_to_all(sent, "seq", 0, 0, tiled=True)]
 
-    picks, query_parts = lax.optimization_barrier((picks, query_parts))
-    ready = []
-    for c in range(len(chunks)):
-        keys = exchange(key_parts, c)
-        values = exchange(value_parts, c)
-        ready.append((keys, values, share(keys, values)))
-    asked = [exchange(query_parts, c) for c in range(len(chunks))]
+    far = [share(c) for c in range(len(chunks))]
     answers = []
     for c in range(len(chunks)):
-        outs, _ = lax.optimization_barrier((attend(asked[c], *ready[c], places, orders_of(partners, c)), [pieces[-1] for pieces in asked]))
+        outs = attend(asked[c], *held[c], far[c], places, orders_of(partners, c))
+        outs, _ = lax.optimization_barrier((outs, [pieces[-1][-1] for pieces in asked]))
         answers.append([swap(outs[k], k) for k in range(partners)])
     return from_partners([[answers[c][k] for c in range(len(chunks))] for k in range(partners)], here_arg, chunks, heads)
 

time: 248 us -> 244 us (0.984)
  waiting for transfers between devices: 149 us -> 146 us
    ppermute x24 -> x25, waiting for transfers between devices: 145 us -> 137 us  [swap(): lax.ppermute(piece, 'head', [(i, i ^ k) for i in range(partners)])]
    all_to_all x2, waiting for transfers between devices: 4.44 us -> 8.85 us  [share(): return [lax.all_to_all(sent, 'seq', 0, 0, tiled=True)]]
    unnamed x39 -> x47, local copies, waits for them, and re-layouts: 5.95 us -> 6.09 us
    ppermute x24 -> x25, starting transfers between devices: 31 us -> 31.1 us  [swap(): lax.ppermute(piece, 'head', [(i, i ^ k) for i in range(partners)])]
  transfers between devices with their start and end apart: 26 -> 27, of which waited for: 17 -> 17; matrix products, arithmetic and copies ran while one was open for 1% -> 1% of each run, Pallas kernels for 16% -> 16%
where the time goes in v7:
time: 244 us
  waiting for transfers between devices  146 us (60%)
  Pallas kernels  47.9 us (20%)
  starting transfers between devices  41.2 us (17%)
  local copies, waits for them, and re-layouts  7.3 us (3%)
    ppermute x25, waiting for transfers between devices, swap(): lax.ppermute(piece, 'head', [(i, i ^ k) for i in range(partners)])  137 us
    ppermute x25, starting transfers between devices, swap(): lax.ppermute(piece, 'head', [(i, i ^ k) for i in range(partners)])  31.1 us
    pallas_call x2, Pallas kernels, attend(): pl.pallas_call(kernel, grid_spec=pltpu.PrefetchScalarGridSpec(num_scalar_...  26.8 us
    all_to_all x2, starting transfers between devices, share(): return [lax.all_to_all(sent, 'seq', 0, 0, tiled=True)]  10.1 us
    pallas_call x3, Pallas kernels, by_partner(): pl.pallas_call(kernel, grid_spec=pltpu.PrefetchScalarGridSpec(num_scalar_...  9.88 us
    pallas_call x4, Pallas kernels, pick_tiles(): pl.pallas_call(kernel, in_specs=[pl.BlockSpec(memory_space=pltpu.SMEM)] +...  9.14 us
    all_to_all x2, waiting for transfers between devices, share(): return [lax.all_to_all(sent, 'seq', 0, 0, tiled=True)]  8.85 us
    unnamed x47, local copies, waits for them, and re-layouts  6.09 us
  transfers between devices with their start and end apart: 27, of which 17 were waited for; matrix products, arithmetic and copies ran while one was open for 1% of the time, Pallas kernels for 16%

profile of v7, /device:TPU:10, one launch (start us, length us, event | category | flops | bytes accessed | tf_op | source)
XLA Modules:
  0.0 243.6 jit_solution(16053003238359285200)
XLA Ops:
  0.0 3.3 %shard_map.47 = (bf16[5,256,128]{2,1,0:T(8,128)(2,1)}, bf16[5,256,128]{2,1,0:T(8,128)(2,1)}, bf16[5,256,128]{2,1,0:T(8,128)(2,1)}, bf16[5,256,128]{2,1,0:T(8,128...) custom-call(s32[1]{0:T(128)} %bitcast.here_ref, ...), custom_call_target="tpu_custom_call" | custom-call | tf_op jit(solution)/shard_map/pallas_call | solution.py:44
  3.3 1.6 collective-permute-start.13
  5.0 1.2 collective-permute-start.14
  6.2 1.2 collective-permute-start.15
  7.4 3.3 %shard_map.48 = (bf16[5,256,128]{2,1,0:T(8,128)(2,1)}, bf16[5,256,128]{2,1,0:T(8,128)(2,1)}, bf16[5,256,128]{2,1,0:T(8,128)(2,1)}, bf16[5,256,128]{2,1,0:T(8,128...) custom-call(s32[1]{0:T(128)} %bitcast.here_ref, ...), custom_call_target="tpu_custom_call" | custom-call | tf_op jit(solution)/shard_map/pallas_call | solution.py:44
  10.7 0.8 collective-permute-start.16
  11.6 2.2 collective-permute-start.17
  14.0 0.3 compare_reduce_fusion
  14.3 3.3 %shard_map.46 = (bf16[5,256,128]{2,1,0:T(8,128)(2,1)}, bf16[5,256,128]{2,1,0:T(8,128)(2,1)}, bf16[5,256,128]{2,1,0:T(8,128)(2,1)}, bf16[5,256,128]{2,1,0:T(8,128...) custom-call(s32[1]{0:T(128)} %bitcast.here_ref, ...), custom_call_target="tpu_custom_call" | custom-call | tf_op jit(solution)/shard_map/pallas_call | solution.py:44
  17.5 0.2 reduce_window_sum.18
  17.7 10.3 %collective-permute-done.13.refs_0_.refs_5_ = bf16[5,256,128]{2,1,0:T(8,128)(2,1)S(1)} collective-permute-done((bf16[5,256,128]{2,1,0:T(8,128)(2,1)}, bf16[5,256,128]{2,1,0:T(8,128)(2,1)S(1)}, u32[]{:S(2)}, u32[]{:S(2)}) %collective-permute-start.13) | collective-permute-done | bytes 327712 | tf_op jit(solution)/shard_map/ppermute | solution.py:256
  28.0 1.8 collective-permute-start.18
  29.8 0.1 select_reduce_fusion.1
  30.0 4.4 %collective-permute-done.14.refs_1_.refs_6_ = bf16[5,256,128]{2,1,0:T(8,128)(2,1)S(1)} collective-permute-done((bf16[5,256,128]{2,1,0:T(8,128)(2,1)}, bf16[5,256,128]{2,1,0:T(8,128)(2,1)S(1)}, u32[]{:S(2)}, u32[]{:S(2)}) %collective-permute-start.14) | collective-permute-done | bytes 327712 | tf_op jit(solution)/shard_map/ppermute | solution.py:256
  34.4 2.2 shard_map.52.refs_4_
  36.7 0.7 collective-permute-done.16.refs_2_.refs_10_
  37.3 18.2 %collective-permute-done.17.refs_1_.refs_11_ = bf16[5,256,128]{2,1,0:T(8,128)(2,1)S(1)} collective-permute-done((bf16[5,256,128]{2,1,0:T(8,128)(2,1)}, bf16[5,256,128]{2,1,0:T(8,128)(2,1)S(1)}, u32[]{:S(2)}, u32[]{:S(2)}) %collective-permute-start.17) | collective-permute-done | bytes 327712 | tf_op jit(solution)/shard_map/ppermute | solution.py:256
  55.6 6.7 %collective-permute-done.18.refs_0_.refs_12_ = bf16[5,256,128]{2,1,0:T(8,128)(2,1)S(1)} collective-permute-done((bf16[5,256,128]{2,1,0:T(8,128)(2,1)}, bf16[5,256,128]{2,1,0:T(8,128)(2,1)S(1)}, u32[]{:S(2)}, u32[]{:S(2)}) %collective-permute-start.18) | collective-permute-done | bytes 327712 | tf_op jit(solution)/shard_map/ppermute | solution.py:256
  62.2 2.4 shard_map.53
  64.7 5.2 %all-to-all-start.1 = ((bf16[8,2,2,5,128,128]{5,4,3,2,1,0:T(8,128)(2,1)}), bf16[8,2,2,5,128,128]{5,4,3,2,1,0:T(8,128)(2,1)}, u32[]{:S(2)}, u32[]{:S(2)}) async-start(bf16[8,2,2,5,128,128]{5,4,3,2,1,0:T(8,128)(2,1)} %shard_map.53), calls=%async_computation.1 | async-start | bytes 10485760 | tf_op jit(solution)/shard_map/all_to_all | solution.py:283
  69.9 1.6 collective-permute-start.3
  71.5 1.9 collective-permute-start.5
  73.4 0.2 collective-permute-start.6
  73.6 2.9 %collective-permute-start.7 = (bf16[5,256,128]{2,1,0:T(8,128)(2,1)}, bf16[5,256,128]{2,1,0:T(8,128)(2,1)S(1)}, u32[]{:S(2)}, u32[]{:S(2)}) collective-permute-start(bf16[5,256,128]{2,1,0:T(8,128)(2,1)} %get-tuple-element.77), channel_id=1, source_target_pairs={{0,2},{1,3},{2,0},{3,1},{4,6},{5,7},{6,4},{7,5},{8,10},{9,11},{10,... | collective-permute-start | bytes 983048 | tf_op jit(solution)/shard_map/ppermute | solution.py:256
  76.4 13.3 %collective-permute-done.3.refs_0_.refs_4_ = bf16[5,256,128]{2,1,0:T(8,128)(2,1)S(1)} collective-permute-done((bf16[5,256,128]{2,1,0:T(8,128)(2,1)}, bf16[5,256,128]{2,1,0:T(8,128)(2,1)S(1)}, u32[]{:S(2)}, u32[]{:S(2)}) %collective-permute-start.3) | collective-permute-done | bytes 327712 | tf_op jit(solution)/shard_map/ppermute | solution.py:256
  89.7 1.8 collective-permute-start.8
  91.5 5.2 %collective-permute-done.4.refs_1_.refs_5_ = bf16[5,256,128]{2,1,0:T(8,128)(2,1)S(1)} collective-permute-done((bf16[5,256,128]{2,1,0:T(8,128)(2,1)S(1)}, bf16[5,256,128]{2,1,0:T(8,128)(2,1)S(1)}, u32[]{:S(2)}, u32[]{:S(2)}) %collective-permute-start.4) | collective-permute-done | bytes 327712 | tf_op jit(solution)/shard_map/ppermute | solution.py:256
  96.7 0.3 collective-permute-start.9
  96.9 2.3 shard_map.49.refs_4_
  99.2 20.8 %collective-permute-done.7.refs_1_.refs_10_ = bf16[5,256,128]{2,1,0:T(8,128)(2,1)S(1)} collective-permute-done((bf16[5,256,128]{2,1,0:T(8,128)(2,1)}, bf16[5,256,128]{2,1,0:T(8,128)(2,1)S(1)}, u32[]{:S(2)}, u32[]{:S(2)}) %collective-permute-start.7) | collective-permute-done | bytes 327712 | tf_op jit(solution)/shard_map/ppermute | solution.py:256
  120.1 7.6 %collective-permute-done.8.refs_0_.refs_11_ = bf16[5,256,128]{2,1,0:T(8,128)(2,1)S(1)} collective-permute-done((bf16[5,256,128]{2,1,0:T(8,128)(2,1)}, bf16[5,256,128]{2,1,0:T(8,128)(2,1)S(1)}, u32[]{:S(2)}, u32[]{:S(2)}) %collective-permute-start.8) | collective-permute-done | bytes 327712 | tf_op jit(solution)/shard_map/ppermute | solution.py:256
  127.7 2.3 shard_map.50
  130.0 0.4 collective-permute-done.9.refs_1_
  130.4 0.7 copy-done.16
  131.1 4.9 %all-to-all-start = ((bf16[8,2,2,5,128,128]{5,4,3,2,1,0:T(8,128)(2,1)}), bf16[8,2,2,5,128,128]{5,4,3,2,1,0:T(8,128)(2,1)}, u32[]{:S(2)}, u32[]{:S(2)}) async-start(bf16[8,2,2,5,128,128]{5,4,3,2,1,0:T(8,128)(2,1)} %shard_map.50), calls=%async_computation | async-start | bytes 10485760 | tf_op jit(solution)/shard_map/all_to_all | solution.py:283
  136.0 1.8 collective-permute-start.10
  137.8 1.7 collective-permute-start.12
  139.5 1.8 collective-permute-start.2
  141.3 0.9 collective-permute-start
  142.3 0.1 fusion
  142.4 0.2 reduce_window_sum.17
  142.8 0.3 select_reduce_fusion
  143.4 0.6 gather_fusion
  143.9 6.8 %collective-permute-done.10.refs_0_ = bf16[3,256,128]{2,1,0:T(8,128)(2,1)S(1)} collective-permute-done((bf16[3,256,128]{2,1,0:T(8,128)(2,1)S(1)}, bf16[3,256,128]{2,1,0:T(8,128)(2,1)S(1)}, u32[]{:S(2)}, u32[]{:S(2)}) %collective-permute-start.10) | collective-permute-done | bytes 196640 | tf_op jit(solution)/shard_map/ppermute | solution.py:256
  150.9 13.4 %collective-permute-done.11.refs_2_ = bf16[5,256,128]{2,1,0:T(8,128)(2,1)S(1)} collective-permute-done((bf16[5,256,128]{2,1,0:T(8,128)(2,1)}, bf16[5,256,128]{2,1,0:T(8,128)(2,1)S(1)}, u32[]{:S(2)}, u32[]{:S(2)}) %collective-permute-start.11) | collective-permute-done | bytes 327712 | tf_op jit(solution)/shard_map/ppermute | solution.py:256
  164.3 0.7 copy-done.12
  165.0 1.0 copy-done.11
  166.0 1.0 copy-done.13
  167.0 0.9 copy-done.17
  167.9 13.6 %shard_map.54 = (bf16[5,256,128]{2,1,0:T(8,128)(2,1)S(1)}, bf16[5,256,128]{2,1,0:T(8,128)(2,1)}, bf16[5,256,128]{2,1,0:T(8,128)(2,1)}, bf16[5,256,128]{2,1,0:T(8,128)(2,1)}) custom-call(s32[8,10]{1,0:T(8,128)S(1)} %broadcast_select_fusion.place_ref, bf16[3,256,128]{2,1,0:T(8,128)(2,1)S(1)} %collective-permute-done.10.refs_0_, ...), custom_call_target="tpu_custom_call" | custom-call | flops 3355443200 | bytes 10485760 | tf_op jit(solution)/shard_map/pallas_call | solution.py:186
  181.5 2.1 collective-permute-start.20
  183.6 1.3 collective-permute-start.22
  184.9 0.5 collective-permute-start.24
  185.4 0.7 copy-done.14
  186.1 8.9 %all-to-all-done.refs_12_ = bf16[8,2,2,5,128,128]{5,4,3,2,1,0:T(8,128)(2,1)} async-done(((bf16[8,2,2,5,128,128]{5,4,3,2,1,0:T(8,128)(2,1)}), bf16[8,2,2,5,128,128]{5,4,3,2,1,0:T(8,128)(2,1)}, u32[]{:S(2)}, u32[]{:S(2)}) %all-to-all-start) | async-done | bytes 5242912 | tf_op jit(solution)/shard_map/all_to_all | solution.py:283
  195.0 1.0 copy-done.15
  196.0 13.1 %shard_map.51 = (bf16[5,256,128]{2,1,0:T(8,128)(2,1)S(1)}, bf16[5,256,128]{2,1,0:T(8,128)(2,1)S(1)}, bf16[5,256,128]{2,1,0:T(8,128)(2,1)S(1)}, bf16[5,256,128]{2,1,0:T(8,128)(2,1)S(1)}) custom-call(s32[8,10]{1,0:T(8,128)S(1)} %broadcast_select_fusion.place_ref, bf16[5,256,128]{2,1,0:T(8,128)(2,1)S(1)} %copy-done.10, ...), custom_call_target="tpu_custom_call" | custom-call | flops 3355443200 | bytes 10485760 | tf_op jit(solution)/shard_map/pallas_call | solution.py:186
  209.2 3.2 %collective-permute-start.21 = (bf16[5,256,128]{2,1,0:T(8,128)(2,1)S(1)}, bf16[5,256,128]{2,1,0:T(8,128)(2,1)S(1)}, u32[]{:S(2)}, u32[]{:S(2)}) collective-permute-start(bf16[5,256,128]{2,1,0:T(8,128)(2,1)S(1)} %get-tuple-element.107), channel_id=1, source_target_pairs={{0,2},{1,3},{2,0},{3,1},{4,6},{5,7},{6,4},{7,5},{8,10},{9,11},{10,... | collective-permute-start | bytes 983048 | tf_op jit(solution)/shard_map/ppermute | solution.py:256
  212.4 0.3 collective-permute-start.23
  212.7 0.8 collective-permute-done.24.refs_7_
  213.5 9.6 %collective-permute-done.19.refs_2_ = bf16[5,256,128]{2,1,0:T(8,128)(2,1)S(1)} collective-permute-done((bf16[5,256,128]{2,1,0:T(8,128)(2,1)S(1)}, bf16[5,256,128]{2,1,0:T(8,128)(2,1)S(1)}, u32[]{:S(2)}, u32[]{:S(2)}) %collective-permute-start.19) | collective-permute-done | bytes 327712 | tf_op jit(solution)/shard_map/ppermute | solution.py:256
  223.1 11.5 %collective-permute-done.21.refs_4_ = bf16[5,256,128]{2,1,0:T(8,128)(2,1)S(1)} collective-permute-done((bf16[5,256,128]{2,1,0:T(8,128)(2,1)S(1)}, bf16[5,256,128]{2,1,0:T(8,128)(2,1)S(1)}, u32[]{:S(2)}, u32[]{:S(2)}) %collective-permute-start.21) | collective-permute-done | bytes 327712 | tf_op jit(solution)/shard_map/ppermute | solution.py:256
  234.6 6.8 %collective-permute-done.23.refs_6_ = bf16[5,256,128]{2,1,0:T(8,128)(2,1)S(1)} collective-permute-done((bf16[5,256,128]{2,1,0:T(8,128)(2,1)S(1)}, bf16[5,256,128]{2,1,0:T(8,128)(2,1)S(1)}, u32[]{:S(2)}, u32[]{:S(2)}) %collective-permute-start.23) | collective-permute-done | bytes 327712 | tf_op jit(solution)/shard_map/ppermute | solution.py:256
  241.4 2.1 shard_map.55
  (73 shorter events, 1.1 us)
Async XLA Ops:
  0.0 13.8 %copy-start.18 = (s32[64,10]{0,1:T(8,128)S(1)}, s32[64,10]{0,1:T(8,128)}, u32[]{:S(2)}) copy-start(s32[64,10]{0,1:T(8,128)} %param.7) | copy-start | bytes 7684
  3.3 31.1 %copy-start.2 = (bf16[5,256,128]{2,1,0:T(8,128)(2,1)S(1)}, bf16[5,256,128]{2,1,0:T(8,128)(2,1)}, u32[]{:S(2)}) copy-start(bf16[5,256,128]{2,1,0:T(8,128)(2,1)} %get-tuple-element.95.refs_3_.refs_8_) | copy-start | bytes 983044
  3.3 24.7 %collective-permute-start.13 = (bf16[5,256,128]{2,1,0:T(8,128)(2,1)}, bf16[5,256,128]{2,1,0:T(8,128)(2,1)S(1)}, u32[]{:S(2)}, u32[]{:S(2)}) collective-permute-start(bf16[5,256,128]{2,1,0:T(8,128)(2,1)} %get-tuple-element.92), channel_id=1, source_target_pairs={{0,3},{1,2},{2,1},{3,0},{4,7},{5,6},{6,5},{7,4},{8,11},{9,10},{10,... | collective-permute-start | bytes 983048 | tf_op jit(solution)/shard_map/ppermute | solution.py:256
  5.0 29.5 %collective-permute-start.14 = (bf16[5,256,128]{2,1,0:T(8,128)(2,1)}, bf16[5,256,128]{2,1,0:T(8,128)(2,1)S(1)}, u32[]{:S(2)}, u32[]{:S(2)}) collective-permute-start(bf16[5,256,128]{2,1,0:T(8,128)(2,1)} %get-tuple-element.93), channel_id=1, source_target_pairs={{0,2},{1,3},{2,0},{3,1},{4,6},{5,7},{6,4},{7,5},{8,10},{9,11},{10,... | collective-permute-start | bytes 983048 | tf_op jit(solution)/shard_map/ppermute | solution.py:256
  6.2 28.2 %collective-permute-start.15 = (bf16[5,256,128]{2,1,0:T(8,128)(2,1)}, bf16[5,256,128]{2,1,0:T(8,128)(2,1)S(1)}, u32[]{:S(2)}, u32[]{:S(2)}) collective-permute-start(bf16[5,256,128]{2,1,0:T(8,128)(2,1)} %get-tuple-element.94), channel_id=1, source_target_pairs={{0,1},{1,0},{2,3},{3,2},{4,5},{5,4},{6,7},{7,6},{8,9},{9,8},{10,11... | collective-permute-start | bytes 983048 | tf_op jit(solution)/shard_map/ppermute | solution.py:256
  10.7 51.5 %copy-start.3 = (bf16[5,256,128]{2,1,0:T(8,128)(2,1)S(1)}, bf16[5,256,128]{2,1,0:T(8,128)(2,1)}, u32[]{:S(2)}) copy-start(bf16[5,256,128]{2,1,0:T(8,128)(2,1)} %get-tuple-element.96.refs_3_.refs_9_) | copy-start | bytes 983044
  10.7 26.6 %collective-permute-start.16 = (bf16[5,256,128]{2,1,0:T(8,128)(2,1)}, bf16[5,256,128]{2,1,0:T(8,128)(2,1)S(1)}, u32[]{:S(2)}, u32[]{:S(2)}) collective-permute-start(bf16[5,256,128]{2,1,0:T(8,128)(2,1)} %get-tuple-element.97), channel_id=1, source_target_pairs={{0,1},{1,0},{2,3},{3,2},{4,5},{5,4},{6,7},{7,6},{8,9},{9,8},{10,11... | collective-permute-start | bytes 983048 | tf_op jit(solution)/shard_map/ppermute | solution.py:256
  11.6 44.0 %collective-permute-start.17 = (bf16[5,256,128]{2,1,0:T(8,128)(2,1)}, bf16[5,256,128]{2,1,0:T(8,128)(2,1)S(1)}, u32[]{:S(2)}, u32[]{:S(2)}) collective-permute-start(bf16[5,256,128]{2,1,0:T(8,128)(2,1)} %get-tuple-element.98), channel_id=1, source_target_pairs={{0,2},{1,3},{2,0},{3,1},{4,6},{5,7},{6,4},{7,5},{8,10},{9,11},{10,... | collective-permute-start | bytes 983048 | tf_op jit(solution)/shard_map/ppermute | solution.py:256
  28.0 34.2 %collective-permute-start.18 = (bf16[5,256,128]{2,1,0:T(8,128)(2,1)}, bf16[5,256,128]{2,1,0:T(8,128)(2,1)S(1)}, u32[]{:S(2)}, u32[]{:S(2)}) collective-permute-start(bf16[5,256,128]{2,1,0:T(8,128)(2,1)} %get-tuple-element.99), channel_id=1, source_target_pairs={{0,3},{1,2},{2,1},{3,0},{4,7},{5,6},{6,5},{7,4},{8,11},{9,10},{10,... | collective-permute-start | bytes 983048 | tf_op jit(solution)/shard_map/ppermute | solution.py:256
  37.3 27.3 %copy-start.4 = (bf16[5,256,128]{2,1,0:T(8,128)(2,1)}, bf16[5,256,128]{2,1,0:T(8,128)(2,1)S(1)}, u32[]{:S(2)}) copy-start(bf16[5,256,128]{2,1,0:T(8,128)(2,1)S(1)} %collective-permute-done.16.refs_2_.refs_10_) | copy-start | bytes 983044
  55.6 9.1 %copy-start.5 = (bf16[5,256,128]{2,1,0:T(8,128)(2,1)}, bf16[5,256,128]{2,1,0:T(8,128)(2,1)S(1)}, u32[]{:S(2)}) copy-start(bf16[5,256,128]{2,1,0:T(8,128)(2,1)S(1)} %collective-permute-done.17.refs_1_.refs_11_) | copy-start | bytes 983044
  62.2 2.4 copy-start.6
  64.6 6.8 %copy-start.20 = (bf16[5,256,128]{2,1,0:T(8,128)(2,1)S(1)}, bf16[5,256,128]{2,1,0:T(8,128)(2,1)}, u32[]{:S(2)}) copy-start(bf16[5,256,128]{2,1,0:T(8,128)(2,1)} %get-tuple-element.72) | copy-start | bytes 983044
  64.7 6.8 %copy-start.19 = (bf16[5,256,128]{2,1,0:T(8,128)(2,1)S(1)}, bf16[5,256,128]{2,1,0:T(8,128)(2,1)}, u32[]{:S(2)}) copy-start(bf16[5,256,128]{2,1,0:T(8,128)(2,1)} %get-tuple-element.73) | copy-start | bytes 983044
  64.7 32.0 %copy-start.22 = (bf16[2,256,128]{2,1,0:T(8,128)(2,1)S(1)}, bf16[2,256,128]{2,1,0:T(8,128)(2,1)}, u32[]{:S(2)}) copy-start(bf16[2,256,128]{2,1,0:T(8,128)(2,1)} %get-tuple-element.81) | copy-start | bytes 393220
  64.7 32.3 %copy-start = (bf16[5,256,128]{2,1,0:T(8,128)(2,1)S(1)}, bf16[5,256,128]{2,1,0:T(8,128)(2,1)}, u32[]{:S(2)}) copy-start(bf16[5,256,128]{2,1,0:T(8,128)(2,1)} %get-tuple-element.74.refs_3_.refs_7_) | copy-start | bytes 983044
  64.7 66.4 %all-to-all-start.1 = ((bf16[8,2,2,5,128,128]{5,4,3,2,1,0:T(8,128)(2,1)}), bf16[8,2,2,5,128,128]{5,4,3,2,1,0:T(8,128)(2,1)}, u32[]{:S(2)}, u32[]{:S(2)}) async-start(bf16[8,2,2,5,128,128]{5,4,3,2,1,0:T(8,128)(2,1)} %shard_map.53), calls=%async_computation.1 | async-start | bytes 10485760 | tf_op jit(solution)/shard_map/all_to_all | solution.py:283
  69.9 57.8 %copy-start.1 = (bf16[5,256,128]{2,1,0:T(8,128)(2,1)S(1)}, bf16[5,256,128]{2,1,0:T(8,128)(2,1)}, u32[]{:S(2)}) copy-start(bf16[5,256,128]{2,1,0:T(8,128)(2,1)} %get-tuple-element.75.refs_3_.refs_8_) | copy-start | bytes 983044
  69.9 19.8 %collective-permute-start.3 = (bf16[5,256,128]{2,1,0:T(8,128)(2,1)}, bf16[5,256,128]{2,1,0:T(8,128)(2,1)S(1)}, u32[]{:S(2)}, u32[]{:S(2)}) collective-permute-start(bf16[5,256,128]{2,1,0:T(8,128)(2,1)} %get-tuple-element.71), channel_id=1, source_target_pairs={{0,3},{1,2},{2,1},{3,0},{4,7},{5,6},{6,5},{7,4},{8,11},{9,10},{10,... | collective-permute-start | bytes 983048 | tf_op jit(solution)/shard_map/ppermute | solution.py:256
  71.5 25.2 %collective-permute-start.4 = (bf16[5,256,128]{2,1,0:T(8,128)(2,1)S(1)}, bf16[5,256,128]{2,1,0:T(8,128)(2,1)S(1)}, u32[]{:S(2)}, u32[]{:S(2)}) collective-permute-start(bf16[5,256,128]{2,1,0:T(8,128)(2,1)S(1)} %copy-done.20), channel_id=1, source_target_pairs={{0,2},{1,3},{2,0},{3,1},{4,6},{5,7},{6,4},{7,5},{8,10},{9,11},{10,... | collective-permute-start | bytes 983048 | tf_op jit(solution)/shard_map/ppermute | solution.py:256
  71.5 25.4 %collective-permute-start.5 = (bf16[5,256,128]{2,1,0:T(8,128)(2,1)S(1)}, bf16[5,256,128]{2,1,0:T(8,128)(2,1)S(1)}, u32[]{:S(2)}, u32[]{:S(2)}) collective-permute-start(bf16[5,256,128]{2,1,0:T(8,128)(2,1)S(1)} %copy-done.19), channel_id=1, source_target_pairs={{0,1},{1,0},{2,3},{3,2},{4,5},{5,4},{6,7},{7,6},{8,9},{9,8},{10,11... | collective-permute-start | bytes 983048 | tf_op jit(solution)/shard_map/ppermute | solution.py:256
  73.4 25.8 %collective-permute-start.6 = (bf16[5,256,128]{2,1,0:T(8,128)(2,1)}, bf16[5,256,128]{2,1,0:T(8,128)(2,1)S(1)}, u32[]{:S(2)}, u32[]{:S(2)}) collective-permute-start(bf16[5,256,128]{2,1,0:T(8,128)(2,1)} %get-tuple-element.76), channel_id=1, source_target_pairs={{0,1},{1,0},{2,3},{3,2},{4,5},{5,4},{6,7},{7,6},{8,9},{9,8},{10,11... | collective-permute-start | bytes 983048 | tf_op jit(solution)/shard_map/ppermute | solution.py:256
  73.6 46.5 %collective-permute-start.7 = (bf16[5,256,128]{2,1,0:T(8,128)(2,1)}, bf16[5,256,128]{2,1,0:T(8,128)(2,1)S(1)}, u32[]{:S(2)}, u32[]{:S(2)}) collective-permute-start(bf16[5,256,128]{2,1,0:T(8,128)(2,1)} %get-tuple-element.77), channel_id=1, source_target_pairs={{0,2},{1,3},{2,0},{3,1},{4,6},{5,7},{6,4},{7,5},{8,10},{9,11},{10,... | collective-permute-start | bytes 983048 | tf_op jit(solution)/shard_map/ppermute | solution.py:256
  89.7 38.0 %collective-permute-start.8 = (bf16[5,256,128]{2,1,0:T(8,128)(2,1)}, bf16[5,256,128]{2,1,0:T(8,128)(2,1)S(1)}, u32[]{:S(2)}, u32[]{:S(2)}) collective-permute-start(bf16[5,256,128]{2,1,0:T(8,128)(2,1)} %get-tuple-element.78), channel_id=1, source_target_pairs={{0,3},{1,2},{2,1},{3,0},{4,7},{5,6},{6,5},{7,4},{8,11},{9,10},{10,... | collective-permute-start | bytes 983048 | tf_op jit(solution)/shard_map/ppermute | solution.py:256
  96.7 33.8 %collective-permute-start.9 = (bf16[2,256,128]{2,1,0:T(8,128)(2,1)S(1)}, bf16[2,256,128]{2,1,0:T(8,128)(2,1)S(1)}, u32[]{:S(2)}, u32[]{:S(2)}) collective-permute-start(bf16[2,256,128]{2,1,0:T(8,128)(2,1)S(1)} %copy-done.22), channel_id=1, source_target_pairs={{0,3},{1,2},{2,1},{3,0},{4,7},{5,6},{6,5},{7,4},{8,11},{9,10},{10,... | collective-permute-start | bytes 393224 | tf_op jit(solution)/shard_map/ppermute | solution.py:256
  99.2 30.8 %copy-start.7 = (bf16[5,256,128]{2,1,0:T(8,128)(2,1)}, bf16[5,256,128]{2,1,0:T(8,128)(2,1)S(1)}, u32[]{:S(2)}) copy-start(bf16[5,256,128]{2,1,0:T(8,128)(2,1)S(1)} %collective-permute-done.6.refs_2_.refs_9_) | copy-start | bytes 983044
  120.1 9.9 %copy-start.8 = (bf16[5,256,128]{2,1,0:T(8,128)(2,1)}, bf16[5,256,128]{2,1,0:T(8,128)(2,1)S(1)}, u32[]{:S(2)}) copy-start(bf16[5,256,128]{2,1,0:T(8,128)(2,1)S(1)} %collective-permute-done.7.refs_1_.refs_10_) | copy-start | bytes 983044
  127.7 2.3 copy-start.9
  130.0 6.0 %copy-start.21 = (bf16[3,256,128]{2,1,0:T(8,128)(2,1)S(1)}, bf16[3,256,128]{2,1,0:T(8,128)(2,1)}, u32[]{:S(2)}) copy-start(bf16[3,256,128]{2,1,0:T(8,128)(2,1)} %get-tuple-element.87) | copy-start | bytes 589828
  130.4 0.7 copy-start.16
  131.1 63.9 %all-to-all-start = ((bf16[8,2,2,5,128,128]{5,4,3,2,1,0:T(8,128)(2,1)}), bf16[8,2,2,5,128,128]{5,4,3,2,1,0:T(8,128)(2,1)}, u32[]{:S(2)}, u32[]{:S(2)}) async-start(bf16[8,2,2,5,128,128]{5,4,3,2,1,0:T(8,128)(2,1)} %shard_map.50), calls=%async_computation | async-start | bytes 10485760 | tf_op jit(solution)/shard_map/all_to_all | solution.py:283
  136.0 14.8 %collective-permute-start.10 = (bf16[3,256,128]{2,1,0:T(8,128)(2,1)S(1)}, bf16[3,256,128]{2,1,0:T(8,128)(2,1)S(1)}, u32[]{:S(2)}, u32[]{:S(2)}) collective-permute-start(bf16[3,256,128]{2,1,0:T(8,128)(2,1)S(1)} %copy-done.21), channel_id=1, source_target_pairs={{0,3},{1,2},{2,1},{3,0},{4,7},{5,6},{6,5},{7,4},{8,11},{9,10},{10,... | collective-permute-start | bytes 589832 | tf_op jit(solution)/shard_map/ppermute | solution.py:256
  137.8 26.5 %collective-permute-start.11 = (bf16[5,256,128]{2,1,0:T(8,128)(2,1)}, bf16[5,256,128]{2,1,0:T(8,128)(2,1)S(1)}, u32[]{:S(2)}, u32[]{:S(2)}) collective-permute-start(bf16[5,256,128]{2,1,0:T(8,128)(2,1)} %get-tuple-element.89), channel_id=1, source_target_pairs={{0,2},{1,3},{2,0},{3,1},{4,6},{5,7},{6,4},{7,5},{8,10},{9,11},{10,... | collective-permute-start | bytes 983048 | tf_op jit(solution)/shard_map/ppermute | solution.py:256
  137.8 27.2 %collective-permute-start.12 = (bf16[5,256,128]{2,1,0:T(8,128)(2,1)}, bf16[5,256,128]{2,1,0:T(8,128)(2,1)}, u32[]{:S(2)}, u32[]{:S(2)}) collective-permute-start(bf16[5,256,128]{2,1,0:T(8,128)(2,1)} %get-tuple-element.90), channel_id=1, source_target_pairs={{0,1},{1,0},{2,3},{3,2},{4,5},{5,4},{6,7},{7,6},{8,9},{9,8},{10,11... | collective-permute-start | bytes 983048 | tf_op jit(solution)/shard_map/ppermute | solution.py:256
  139.5 42.0 %collective-permute-start.2 = (bf16[5,256,128]{2,1,0:T(8,128)(2,1)}, bf16[5,256,128]{2,1,0:T(8,128)(2,1)}, u32[]{:S(2)}, u32[]{:S(2)}) collective-permute-start(bf16[5,256,128]{2,1,0:T(8,128)(2,1)} %get-tuple-element.70), channel_id=1, source_target_pairs={{0,3},{1,2},{2,1},{3,0},{4,7},{5,6},{6,5},{7,4},{8,11},{9,10},{10,... | collective-permute-start | bytes 983048 | tf_op jit(solution)/shard_map/ppermute | solution.py:256
  141.3 44.1 %collective-permute-start = (bf16[5,256,128]{2,1,0:T(8,128)(2,1)}, bf16[5,256,128]{2,1,0:T(8,128)(2,1)}, u32[]{:S(2)}, u32[]{:S(2)}) collective-permute-start(bf16[5,256,128]{2,1,0:T(8,128)(2,1)} %get-tuple-element.68), channel_id=1, source_target_pairs={{0,1},{1,0},{2,3},{3,2},{4,5},{5,4},{6,7},{7,6},{8,9},{9,8},{10,11... | collective-permute-start | bytes 983048 | tf_op jit(solution)/shard_map/ppermute | solution.py:256
  150.8 34.6 %collective-permute-start.1 = (bf16[5,256,128]{2,1,0:T(8,128)(2,1)}, bf16[5,256,128]{2,1,0:T(8,128)(2,1)S(1)}, u32[]{:S(2)}, u32[]{:S(2)}) collective-permute-start(bf16[5,256,128]{2,1,0:T(8,128)(2,1)} %get-tuple-element.69), channel_id=1, source_target_pairs={{0,2},{1,3},{2,0},{3,1},{4,6},{5,7},{6,4},{7,5},{8,10},{9,11},{10,... | collective-permute-start | bytes 983048 | tf_op jit(solution)/shard_map/ppermute | solution.py:256
  150.9 44.1 %copy-start.10 = (bf16[5,256,128]{2,1,0:T(8,128)(2,1)S(1)}, bf16[5,256,128]{2,1,0:T(8,128)(2,1)}, u32[]{:S(2)}) copy-start(bf16[5,256,128]{2,1,0:T(8,128)(2,1)} %get-tuple-element.67.refs_0_) | copy-start | bytes 983044
  164.3 0.7 copy-start.12
  165.0 1.0 copy-start.11
  166.0 1.0 copy-start.13
  167.0 0.9 copy-start.17
  181.5 30.9 %collective-permute-start.20 = (bf16[5,256,128]{2,1,0:T(8,128)(2,1)}, bf16[5,256,128]{2,1,0:T(8,128)(2,1)S(1)}, u32[]{:S(2)}, u32[]{:S(2)}) collective-permute-start(bf16[5,256,128]{2,1,0:T(8,128)(2,1)} %get-tuple-element.106), channel_id=1, source_target_pairs={{0,1},{1,0},{2,3},{3,2},{4,5},{5,4},{6,7},{7,6},{8,9},{9,8},{10,11... | collective-permute-start | bytes 983048 | tf_op jit(solution)/shard_map/ppermute | solution.py:256
  183.6 29.0 %collective-permute-start.22 = (bf16[5,256,128]{2,1,0:T(8,128)(2,1)}, bf16[5,256,128]{2,1,0:T(8,128)(2,1)S(1)}, u32[]{:S(2)}, u32[]{:S(2)}) collective-permute-start(bf16[5,256,128]{2,1,0:T(8,128)(2,1)} %get-tuple-element.108), channel_id=1, source_target_pairs={{0,2},{1,3},{2,0},{3,1},{4,6},{5,7},{6,4},{7,5},{8,10},{9,11},{10,... | collective-permute-start | bytes 983048 | tf_op jit(solution)/shard_map/ppermute | solution.py:256
  184.9 28.6 %collective-permute-start.24 = (bf16[5,256,128]{2,1,0:T(8,128)(2,1)}, bf16[5,256,128]{2,1,0:T(8,128)(2,1)S(1)}, u32[]{:S(2)}, u32[]{:S(2)}) collective-permute-start(bf16[5,256,128]{2,1,0:T(8,128)(2,1)} %get-tuple-element.110), channel_id=1, source_target_pairs={{0,3},{1,2},{2,1},{3,0},{4,7},{5,6},{6,5},{7,4},{8,11},{9,10},{10,... | collective-permute-start | bytes 983048 | tf_op jit(solution)/shard_map/ppermute | solution.py:256
  185.4 0.7 copy-start.14
  195.0 1.0 copy-start.15
  209.1 14.0 %collective-permute-start.19 = (bf16[5,256,128]{2,1,0:T(8,128)(2,1)S(1)}, bf16[5,256,128]{2,1,0:T(8,128)(2,1)S(1)}, u32[]{:S(2)}, u32[]{:S(2)}) collective-permute-start(bf16[5,256,128]{2,1,0:T(8,128)(2,1)S(1)} %get-tuple-element.105), channel_id=1, source_target_pairs={{0,1},{1,0},{2,3},{3,2},{4,5},{5,4},{6,7},{7,6},{8,9},{9,8},{10,11... | collective-permute-start | bytes 983048 | tf_op jit(solution)/shard_map/ppermute | solution.py:256
  209.2 25.4 %collective-permute-start.21 = (bf16[5,256,128]{2,1,0:T(8,128)(2,1)S(1)}, bf16[5,256,128]{2,1,0:T(8,128)(2,1)S(1)}, u32[]{:S(2)}, u32[]{:S(2)}) collective-permute-start(bf16[5,256,128]{2,1,0:T(8,128)(2,1)S(1)} %get-tuple-element.107), channel_id=1, source_target_pairs={{0,2},{1,3},{2,0},{3,1},{4,6},{5,7},{6,4},{7,5},{8,10},{9,11},{10,... | collective-permute-start | bytes 983048 | tf_op jit(solution)/shard_map/ppermute | solution.py:256
  212.4 29.0 %collective-permute-start.23 = (bf16[5,256,128]{2,1,0:T(8,128)(2,1)S(1)}, bf16[5,256,128]{2,1,0:T(8,128)(2,1)S(1)}, u32[]{:S(2)}, u32[]{:S(2)}) collective-permute-start(bf16[5,256,128]{2,1,0:T(8,128)(2,1)S(1)} %get-tuple-element.109), channel_id=1, source_target_pairs={{0,3},{1,2},{2,1},{3,0},{4,7},{5,6},{6,5},{7,4},{8,11},{9,10},{10,... | collective-permute-start | bytes 983048 | tf_op jit(solution)/shard_map/ppermute | solution.py:256

commit v8 on v7

--- a/solution.py
+++ b/solution.py
@@ -286,7 +286,7 @@
     answers = []
     for c in range(len(chunks)):
         outs = attend(asked[c], *held[c], far[c], places, orders_of(partners, c))
-        outs, _ = lax.optimization_barrier((outs, [pieces[-1][-1] for pieces in asked]))
+        outs, _ = lax.optimization_barrier((outs, [pieces[-1][-1] for pieces in asked] + [asked[0][1][0]]))
         answers.append([swap(outs[k], k) for k in range(partners)])
     return from_partners([[answers[c][k] for c in range(len(chunks))] for k in range(partners)], here_arg, chunks, heads)
 

time: 244 us -> 244 us (level)
    ppermute x25, waiting for transfers between devices: 137 us -> 139 us  [swap(): lax.ppermute(piece, 'head', [(i, i ^ k) for i in range(partners)])]
    unnamed x47 -> x45, local copies, waits for them, and re-layouts: 6.09 us -> 6.07 us
  transfers between devices with their start and end apart: 27 -> 27, of which waited for: 17 -> 19; matrix products, arithmetic and copies ran while one was open for 1% -> 1% of each run, Pallas kernels for 16% -> 16%
where the time goes in v8:
time: 244 us
  waiting for transfers between devices  147 us (60%)
  Pallas kernels  47.7 us (20%)
  starting transfers between devices  39.9 us (16%)
  local copies, waits for them, and re-layouts  7.28 us (3%)
    ppermute x25, waiting for transfers between devices, swap(): lax.ppermute(piece, 'head', [(i, i ^ k) for i in range(partners)])  139 us
    ppermute x25, starting transfers between devices, swap(): lax.ppermute(piece, 'head', [(i, i ^ k) for i in range(partners)])  29.8 us
    pallas_call x2, Pallas kernels, attend(): pl.pallas_call(kernel, grid_spec=pltpu.PrefetchScalarGridSpec(num_scalar_...  26.8 us
    all_to_all x2, starting transfers between devices, share(): return [lax.all_to_all(sent, 'seq', 0, 0, tiled=True)]  10.1 us
    pallas_call x3, Pallas kernels, by_partner(): pl.pallas_call(kernel, grid_spec=pltpu.PrefetchScalarGridSpec(num_scalar_...  9.75 us
    pallas_call x4, Pallas kernels, pick_tiles(): pl.pallas_call(kernel, in_specs=[pl.BlockSpec(memory_space=pltpu.SMEM)] +...  9.06 us
    all_to_all x2, waiting for transfers between devices, share(): return [lax.all_to_all(sent, 'seq', 0, 0, tiled=True)]  7.87 us
    unnamed x45, local copies, waits for them, and re-layouts  6.07 us
  transfers between devices with their start and end apart: 27, of which 19 were waited for; matrix products, arithmetic and copies ran while one was open for 1% of the time, Pallas kernels for 16%

profile of v8, /device:TPU:10, one launch (start us, length us, event | category | flops | bytes accessed | tf_op | source)
XLA Modules:
  0.0 243.7 jit_solution(173367039068369430)
XLA Ops:
  0.0 3.2 %shard_map.47 = (bf16[5,256,128]{2,1,0:T(8,128)(2,1)}, bf16[5,256,128]{2,1,0:T(8,128)(2,1)}, bf16[5,256,128]{2,1,0:T(8,128)(2,1)}, bf16[5,256,128]{2,1,0:T(8,128...) custom-call(s32[1]{0:T(128)} %bitcast.here_ref, ...), custom_call_target="tpu_custom_call" | custom-call | tf_op jit(solution)/shard_map/pallas_call | solution.py:44
  3.2 1.6 collective-permute-start.13
  4.9 1.2 collective-permute-start.14
  6.1 1.2 collective-permute-start.15
  7.4 3.3 %shard_map.48 = (bf16[5,256,128]{2,1,0:T(8,128)(2,1)}, bf16[5,256,128]{2,1,0:T(8,128)(2,1)}, bf16[5,256,128]{2,1,0:T(8,128)(2,1)}, bf16[5,256,128]{2,1,0:T(8,128...) custom-call(s32[1]{0:T(128)} %bitcast.here_ref, ...), custom_call_target="tpu_custom_call" | custom-call | tf_op jit(solution)/shard_map/pallas_call | solution.py:44
  10.6 0.8 collective-permute-start.16
  11.5 2.2 collective-permute-start.17
  13.9 0.3 compare_reduce_fusion
  14.2 3.2 %shard_map.46 = (bf16[5,256,128]{2,1,0:T(8,128)(2,1)}, bf16[5,256,128]{2,1,0:T(8,128)(2,1)}, bf16[5,256,128]{2,1,0:T(8,128)(2,1)}, bf16[5,256,128]{2,1,0:T(8,128...) custom-call(s32[1]{0:T(128)} %bitcast.here_ref, ...), custom_call_target="tpu_custom_call" | custom-call | tf_op jit(solution)/shard_map/pallas_call | solution.py:44
  17.4 0.2 reduce_window_sum.18
  17.6 10.4 %collective-permute-done.13.refs_0_.refs_5_ = bf16[5,256,128]{2,1,0:T(8,128)(2,1)S(1)} collective-permute-done((bf16[5,256,128]{2,1,0:T(8,128)(2,1)}, bf16[5,256,128]{2,1,0:T(8,128)(2,1)S(1)}, u32[]{:S(2)}, u32[]{:S(2)}) %collective-permute-start.13) | collective-permute-done | bytes 327712 | tf_op jit(solution)/shard_map/ppermute | solution.py:256
  28.0 1.8 collective-permute-start.18
  29.7 0.1 select_reduce_fusion.1
  30.0 4.4 %collective-permute-done.14.refs_1_.refs_6_ = bf16[5,256,128]{2,1,0:T(8,128)(2,1)S(1)} collective-permute-done((bf16[5,256,128]{2,1,0:T(8,128)(2,1)}, bf16[5,256,128]{2,1,0:T(8,128)(2,1)S(1)}, u32[]{:S(2)}, u32[]{:S(2)}) %collective-permute-start.14) | collective-permute-done | bytes 327712 | tf_op jit(solution)/shard_map/ppermute | solution.py:256
  34.3 2.2 shard_map.52.refs_4_
  36.6 0.7 collective-permute-done.16.refs_2_.refs_10_
  37.2 18.2 %collective-permute-done.17.refs_1_.refs_11_ = bf16[5,256,128]{2,1,0:T(8,128)(2,1)S(1)} collective-permute-done((bf16[5,256,128]{2,1,0:T(8,128)(2,1)}, bf16[5,256,128]{2,1,0:T(8,128)(2,1)S(1)}, u32[]{:S(2)}, u32[]{:S(2)}) %collective-permute-start.17) | collective-permute-done | bytes 327712 | tf_op jit(solution)/shard_map/ppermute | solution.py:256
  55.5 6.7 %collective-permute-done.18.refs_0_.refs_12_ = bf16[5,256,128]{2,1,0:T(8,128)(2,1)S(1)} collective-permute-done((bf16[5,256,128]{2,1,0:T(8,128)(2,1)}, bf16[5,256,128]{2,1,0:T(8,128)(2,1)S(1)}, u32[]{:S(2)}, u32[]{:S(2)}) %collective-permute-start.18) | collective-permute-done | bytes 327712 | tf_op jit(solution)/shard_map/ppermute | solution.py:256
  62.2 2.3 shard_map.53
  64.6 5.2 %all-to-all-start.1 = ((bf16[8,2,2,5,128,128]{5,4,3,2,1,0:T(8,128)(2,1)}), bf16[8,2,2,5,128,128]{5,4,3,2,1,0:T(8,128)(2,1)}, u32[]{:S(2)}, u32[]{:S(2)}) async-start(bf16[8,2,2,5,128,128]{5,4,3,2,1,0:T(8,128)(2,1)} %shard_map.53), calls=%async_computation.1 | async-start | bytes 10485760 | tf_op jit(solution)/shard_map/all_to_all | solution.py:283
  69.8 1.6 collective-permute-start.3
  71.4 1.9 collective-permute-start.5
  73.3 0.2 collective-permute-start.6
  73.5 2.9 %collective-permute-start.7 = (bf16[5,256,128]{2,1,0:T(8,128)(2,1)}, bf16[5,256,128]{2,1,0:T(8,128)(2,1)S(1)}, u32[]{:S(2)}, u32[]{:S(2)}) collective-permute-start(bf16[5,256,128]{2,1,0:T(8,128)(2,1)} %get-tuple-element.77), channel_id=1, source_target_pairs={{0,2},{1,3},{2,0},{3,1},{4,6},{5,7},{6,4},{7,5},{8,10},{9,11},{10,... | collective-permute-start | bytes 983048 | tf_op jit(solution)/shard_map/ppermute | solution.py:256
  76.3 13.3 %collective-permute-done.3.refs_0_.refs_4_ = bf16[5,256,128]{2,1,0:T(8,128)(2,1)S(1)} collective-permute-done((bf16[5,256,128]{2,1,0:T(8,128)(2,1)}, bf16[5,256,128]{2,1,0:T(8,128)(2,1)S(1)}, u32[]{:S(2)}, u32[]{:S(2)}) %collective-permute-start.3) | collective-permute-done | bytes 327712 | tf_op jit(solution)/shard_map/ppermute | solution.py:256
  89.6 1.8 collective-permute-start.8
  91.4 5.2 %collective-permute-done.4.refs_1_.refs_5_ = bf16[5,256,128]{2,1,0:T(8,128)(2,1)S(1)} collective-permute-done((bf16[5,256,128]{2,1,0:T(8,128)(2,1)S(1)}, bf16[5,256,128]{2,1,0:T(8,128)(2,1)S(1)}, u32[]{:S(2)}, u32[]{:S(2)}) %collective-permute-start.4) | collective-permute-done | bytes 327712 | tf_op jit(solution)/shard_map/ppermute | solution.py:256
  96.6 0.3 collective-permute-start.9
  96.8 2.3 shard_map.49.refs_4_
  99.1 20.8 %collective-permute-done.7.refs_1_.refs_10_ = bf16[5,256,128]{2,1,0:T(8,128)(2,1)S(1)} collective-permute-done((bf16[5,256,128]{2,1,0:T(8,128)(2,1)}, bf16[5,256,128]{2,1,0:T(8,128)(2,1)S(1)}, u32[]{:S(2)}, u32[]{:S(2)}) %collective-permute-start.7) | collective-permute-done | bytes 327712 | tf_op jit(solution)/shard_map/ppermute | solution.py:256
  120.0 7.6 %collective-permute-done.8.refs_0_.refs_11_ = bf16[5,256,128]{2,1,0:T(8,128)(2,1)S(1)} collective-permute-done((bf16[5,256,128]{2,1,0:T(8,128)(2,1)}, bf16[5,256,128]{2,1,0:T(8,128)(2,1)S(1)}, u32[]{:S(2)}, u32[]{:S(2)}) %collective-permute-start.8) | collective-permute-done | bytes 327712 | tf_op jit(solution)/shard_map/ppermute | solution.py:256
  127.6 2.2 shard_map.50
  129.9 0.5 collective-permute-done.9.refs_1_
  130.3 0.7 copy-done.16
  131.0 4.9 %all-to-all-start = ((bf16[8,2,2,5,128,128]{5,4,3,2,1,0:T(8,128)(2,1)}), bf16[8,2,2,5,128,128]{5,4,3,2,1,0:T(8,128)(2,1)}, u32[]{:S(2)}, u32[]{:S(2)}) async-start(bf16[8,2,2,5,128,128]{5,4,3,2,1,0:T(8,128)(2,1)} %shard_map.50), calls=%async_computation | async-start | bytes 10485760 | tf_op jit(solution)/shard_map/all_to_all | solution.py:283
  135.9 1.8 collective-permute-start.10
  137.7 1.7 collective-permute-start.12
  139.4 0.3 collective-permute-start
  139.7 1.5 collective-permute-start.2
  141.4 0.2 reduce_window_sum.17
  141.8 0.3 select_reduce_fusion
  142.4 0.6 gather_fusion
  143.0 7.8 %collective-permute-done.10.refs_0_ = bf16[3,256,128]{2,1,0:T(8,128)(2,1)S(1)} collective-permute-done((bf16[3,256,128]{2,1,0:T(8,128)(2,1)}, bf16[3,256,128]{2,1,0:T(8,128)(2,1)S(1)}, u32[]{:S(2)}, u32[]{:S(2)}) %collective-permute-start.10) | collective-permute-done | bytes 196640 | tf_op jit(solution)/shard_map/ppermute | solution.py:256
  150.9 6.5 %collective-permute-done.11.refs_2_ = bf16[5,256,128]{2,1,0:T(8,128)(2,1)S(1)} collective-permute-done((bf16[5,256,128]{2,1,0:T(8,128)(2,1)}, bf16[5,256,128]{2,1,0:T(8,128)(2,1)S(1)}, u32[]{:S(2)}, u32[]{:S(2)}) %collective-permute-start.11) | collective-permute-done | bytes 327712 | tf_op jit(solution)/shard_map/ppermute | solution.py:256
  157.3 0.7 copy-done.12
  158.1 1.0 copy-done.11
  159.0 1.0 copy-done.13
  160.0 0.9 copy-done.17
  160.9 13.6 %shard_map.54 = (bf16[5,256,128]{2,1,0:T(8,128)(2,1)S(1)}, bf16[5,256,128]{2,1,0:T(8,128)(2,1)}, bf16[5,256,128]{2,1,0:T(8,128)(2,1)}, bf16[5,256,128]{2,1,0:T(8,128)(2,1)}) custom-call(s32[8,10]{1,0:T(8,128)S(1)} %broadcast_select_fusion.place_ref, bf16[3,256,128]{2,1,0:T(8,128)(2,1)S(1)} %collective-permute-done.10.refs_0_, ...), custom_call_target="tpu_custom_call" | custom-call | flops 3355443200 | bytes 10485760 | tf_op jit(solution)/shard_map/pallas_call | solution.py:186
  174.5 4.6 %collective-permute-done.2.refs_3_ = bf16[5,256,128]{2,1,0:T(8,128)(2,1)} collective-permute-done((bf16[5,256,128]{2,1,0:T(8,128)(2,1)}, bf16[5,256,128]{2,1,0:T(8,128)(2,1)}, u32[]{:S(2)}, u32[]{:S(2)}) %collective-permute-start.2) | collective-permute-done | bytes 327712 | tf_op jit(solution)/shard_map/ppermute | solution.py:256
  179.1 3.2 %collective-permute-start.22 = (bf16[5,256,128]{2,1,0:T(8,128)(2,1)}, bf16[5,256,128]{2,1,0:T(8,128)(2,1)S(1)}, u32[]{:S(2)}, u32[]{:S(2)}) collective-permute-start(bf16[5,256,128]{2,1,0:T(8,128)(2,1)} %get-tuple-element.108), channel_id=1, source_target_pairs={{0,2},{1,3},{2,0},{3,1},{4,6},{5,7},{6,4},{7,5},{8,10},{9,11},{10,... | collective-permute-start | bytes 983048 | tf_op jit(solution)/shard_map/ppermute | solution.py:256
  182.3 0.3 collective-permute-start.24
  182.6 3.7 %collective-permute-done.1.refs_2_ = bf16[5,256,128]{2,1,0:T(8,128)(2,1)S(1)} collective-permute-done((bf16[5,256,128]{2,1,0:T(8,128)(2,1)}, bf16[5,256,128]{2,1,0:T(8,128)(2,1)S(1)}, u32[]{:S(2)}, u32[]{:S(2)}) %collective-permute-start.1) | collective-permute-done | bytes 327712 | tf_op jit(solution)/shard_map/ppermute | solution.py:256
  186.3 0.7 copy-done.14
  187.0 7.9 %all-to-all-done.refs_12_ = bf16[8,2,2,5,128,128]{5,4,3,2,1,0:T(8,128)(2,1)} async-done(((bf16[8,2,2,5,128,128]{5,4,3,2,1,0:T(8,128)(2,1)}), bf16[8,2,2,5,128,128]{5,4,3,2,1,0:T(8,128)(2,1)}, u32[]{:S(2)}, u32[]{:S(2)}) %all-to-all-start) | async-done | bytes 5242912 | tf_op jit(solution)/shard_map/all_to_all | solution.py:283
  194.9 1.0 copy-done.15
  195.8 13.1 %shard_map.51 = (bf16[5,256,128]{2,1,0:T(8,128)(2,1)S(1)}, bf16[5,256,128]{2,1,0:T(8,128)(2,1)S(1)}, bf16[5,256,128]{2,1,0:T(8,128)(2,1)S(1)}, bf16[5,256,128]{2,1,0:T(8,128)(2,1)S(1)}) custom-call(s32[8,10]{1,0:T(8,128)S(1)} %broadcast_select_fusion.place_ref, bf16[5,256,128]{2,1,0:T(8,128)(2,1)S(1)} %copy-done.10, ...), custom_call_target="tpu_custom_call" | custom-call | flops 3355443200 | bytes 10485760 | tf_op jit(solution)/shard_map/pallas_call | solution.py:186
  209.1 3.2 %collective-permute-start.21 = (bf16[5,256,128]{2,1,0:T(8,128)(2,1)S(1)}, bf16[5,256,128]{2,1,0:T(8,128)(2,1)S(1)}, u32[]{:S(2)}, u32[]{:S(2)}) collective-permute-start(bf16[5,256,128]{2,1,0:T(8,128)(2,1)S(1)} %get-tuple-element.107), channel_id=1, source_target_pairs={{0,2},{1,3},{2,0},{3,1},{4,6},{5,7},{6,4},{7,5},{8,10},{9,11},{10,... | collective-permute-start | bytes 983048 | tf_op jit(solution)/shard_map/ppermute | solution.py:256
  212.3 0.3 collective-permute-start.23
  212.5 1.3 collective-permute-done.24.refs_7_
  213.8 9.2 %collective-permute-done.19.refs_2_ = bf16[5,256,128]{2,1,0:T(8,128)(2,1)S(1)} collective-permute-done((bf16[5,256,128]{2,1,0:T(8,128)(2,1)S(1)}, bf16[5,256,128]{2,1,0:T(8,128)(2,1)S(1)}, u32[]{:S(2)}, u32[]{:S(2)}) %collective-permute-start.19) | collective-permute-done | bytes 327712 | tf_op jit(solution)/shard_map/ppermute | solution.py:256
  223.0 11.5 %collective-permute-done.21.refs_4_ = bf16[5,256,128]{2,1,0:T(8,128)(2,1)S(1)} collective-permute-done((bf16[5,256,128]{2,1,0:T(8,128)(2,1)S(1)}, bf16[5,256,128]{2,1,0:T(8,128)(2,1)S(1)}, u32[]{:S(2)}, u32[]{:S(2)}) %collective-permute-start.21) | collective-permute-done | bytes 327712 | tf_op jit(solution)/shard_map/ppermute | solution.py:256
  234.5 7.0 %collective-permute-done.23.refs_6_ = bf16[5,256,128]{2,1,0:T(8,128)(2,1)S(1)} collective-permute-done((bf16[5,256,128]{2,1,0:T(8,128)(2,1)S(1)}, bf16[5,256,128]{2,1,0:T(8,128)(2,1)S(1)}, u32[]{:S(2)}, u32[]{:S(2)}) %collective-permute-start.23) | collective-permute-done | bytes 327712 | tf_op jit(solution)/shard_map/ppermute | solution.py:256
  241.5 2.1 shard_map.55
  (71 shorter events, 1.2 us)
Async XLA Ops:
  0.0 13.7 %copy-start.18 = (s32[64,10]{0,1:T(8,128)S(1)}, s32[64,10]{0,1:T(8,128)}, u32[]{:S(2)}) copy-start(s32[64,10]{0,1:T(8,128)} %param.7) | copy-start | bytes 7684
  3.2 31.1 %copy-start.2 = (bf16[5,256,128]{2,1,0:T(8,128)(2,1)S(1)}, bf16[5,256,128]{2,1,0:T(8,128)(2,1)}, u32[]{:S(2)}) copy-start(bf16[5,256,128]{2,1,0:T(8,128)(2,1)} %get-tuple-element.95.refs_3_.refs_8_) | copy-start | bytes 983044
  3.2 24.7 %collective-permute-start.13 = (bf16[5,256,128]{2,1,0:T(8,128)(2,1)}, bf16[5,256,128]{2,1,0:T(8,128)(2,1)S(1)}, u32[]{:S(2)}, u32[]{:S(2)}) collective-permute-start(bf16[5,256,128]{2,1,0:T(8,128)(2,1)} %get-tuple-element.92), channel_id=1, source_target_pairs={{0,3},{1,2},{2,1},{3,0},{4,7},{5,6},{6,5},{7,4},{8,11},{9,10},{10,... | collective-permute-start | bytes 983048 | tf_op jit(solution)/shard_map/ppermute | solution.py:256
  4.9 29.5 %collective-permute-start.14 = (bf16[5,256,128]{2,1,0:T(8,128)(2,1)}, bf16[5,256,128]{2,1,0:T(8,128)(2,1)S(1)}, u32[]{:S(2)}, u32[]{:S(2)}) collective-permute-start(bf16[5,256,128]{2,1,0:T(8,128)(2,1)} %get-tuple-element.93), channel_id=1, source_target_pairs={{0,2},{1,3},{2,0},{3,1},{4,6},{5,7},{6,4},{7,5},{8,10},{9,11},{10,... | collective-permute-start | bytes 983048 | tf_op jit(solution)/shard_map/ppermute | solution.py:256
  6.1 28.2 %collective-permute-start.15 = (bf16[5,256,128]{2,1,0:T(8,128)(2,1)}, bf16[5,256,128]{2,1,0:T(8,128)(2,1)S(1)}, u32[]{:S(2)}, u32[]{:S(2)}) collective-permute-start(bf16[5,256,128]{2,1,0:T(8,128)(2,1)} %get-tuple-element.94), channel_id=1, source_target_pairs={{0,1},{1,0},{2,3},{3,2},{4,5},{5,4},{6,7},{7,6},{8,9},{9,8},{10,11... | collective-permute-start | bytes 983048 | tf_op jit(solution)/shard_map/ppermute | solution.py:256
  10.6 51.5 %copy-start.3 = (bf16[5,256,128]{2,1,0:T(8,128)(2,1)S(1)}, bf16[5,256,128]{2,1,0:T(8,128)(2,1)}, u32[]{:S(2)}) copy-start(bf16[5,256,128]{2,1,0:T(8,128)(2,1)} %get-tuple-element.96.refs_3_.refs_9_) | copy-start | bytes 983044
  10.6 26.6 %collective-permute-start.16 = (bf16[5,256,128]{2,1,0:T(8,128)(2,1)}, bf16[5,256,128]{2,1,0:T(8,128)(2,1)S(1)}, u32[]{:S(2)}, u32[]{:S(2)}) collective-permute-start(bf16[5,256,128]{2,1,0:T(8,128)(2,1)} %get-tuple-element.97), channel_id=1, source_target_pairs={{0,1},{1,0},{2,3},{3,2},{4,5},{5,4},{6,7},{7,6},{8,9},{9,8},{10,11... | collective-permute-start | bytes 983048 | tf_op jit(solution)/shard_map/ppermute | solution.py:256
  11.5 44.0 %collective-permute-start.17 = (bf16[5,256,128]{2,1,0:T(8,128)(2,1)}, bf16[5,256,128]{2,1,0:T(8,128)(2,1)S(1)}, u32[]{:S(2)}, u32[]{:S(2)}) collective-permute-start(bf16[5,256,128]{2,1,0:T(8,128)(2,1)} %get-tuple-element.98), channel_id=1, source_target_pairs={{0,2},{1,3},{2,0},{3,1},{4,6},{5,7},{6,4},{7,5},{8,10},{9,11},{10,... | collective-permute-start | bytes 983048 | tf_op jit(solution)/shard_map/ppermute | solution.py:256
  28.0 34.2 %collective-permute-start.18 = (bf16[5,256,128]{2,1,0:T(8,128)(2,1)}, bf16[5,256,128]{2,1,0:T(8,128)(2,1)S(1)}, u32[]{:S(2)}, u32[]{:S(2)}) collective-permute-start(bf16[5,256,128]{2,1,0:T(8,128)(2,1)} %get-tuple-element.99), channel_id=1, source_target_pairs={{0,3},{1,2},{2,1},{3,0},{4,7},{5,6},{6,5},{7,4},{8,11},{9,10},{10,... | collective-permute-start | bytes 983048 | tf_op jit(solution)/shard_map/ppermute | solution.py:256
  37.2 27.3 %copy-start.4 = (bf16[5,256,128]{2,1,0:T(8,128)(2,1)}, bf16[5,256,128]{2,1,0:T(8,128)(2,1)S(1)}, u32[]{:S(2)}) copy-start(bf16[5,256,128]{2,1,0:T(8,128)(2,1)S(1)} %collective-permute-done.16.refs_2_.refs_10_) | copy-start | bytes 983044
  55.5 9.0 %copy-start.5 = (bf16[5,256,128]{2,1,0:T(8,128)(2,1)}, bf16[5,256,128]{2,1,0:T(8,128)(2,1)S(1)}, u32[]{:S(2)}) copy-start(bf16[5,256,128]{2,1,0:T(8,128)(2,1)S(1)} %collective-permute-done.17.refs_1_.refs_11_) | copy-start | bytes 983044
  62.2 2.4 copy-start.6
  64.5 6.8 %copy-start.20 = (bf16[5,256,128]{2,1,0:T(8,128)(2,1)S(1)}, bf16[5,256,128]{2,1,0:T(8,128)(2,1)}, u32[]{:S(2)}) copy-start(bf16[5,256,128]{2,1,0:T(8,128)(2,1)} %get-tuple-element.72) | copy-start | bytes 983044
  64.5 6.8 %copy-start.19 = (bf16[5,256,128]{2,1,0:T(8,128)(2,1)S(1)}, bf16[5,256,128]{2,1,0:T(8,128)(2,1)}, u32[]{:S(2)}) copy-start(bf16[5,256,128]{2,1,0:T(8,128)(2,1)} %get-tuple-element.73) | copy-start | bytes 983044
  64.6 32.0 %copy-start.21 = (bf16[2,256,128]{2,1,0:T(8,128)(2,1)S(1)}, bf16[2,256,128]{2,1,0:T(8,128)(2,1)}, u32[]{:S(2)}) copy-start(bf16[2,256,128]{2,1,0:T(8,128)(2,1)} %get-tuple-element.81) | copy-start | bytes 393220
  64.6 32.3 %copy-start = (bf16[5,256,128]{2,1,0:T(8,128)(2,1)S(1)}, bf16[5,256,128]{2,1,0:T(8,128)(2,1)}, u32[]{:S(2)}) copy-start(bf16[5,256,128]{2,1,0:T(8,128)(2,1)} %get-tuple-element.74.refs_3_.refs_7_) | copy-start | bytes 983044
  64.6 66.4 %all-to-all-start.1 = ((bf16[8,2,2,5,128,128]{5,4,3,2,1,0:T(8,128)(2,1)}), bf16[8,2,2,5,128,128]{5,4,3,2,1,0:T(8,128)(2,1)}, u32[]{:S(2)}, u32[]{:S(2)}) async-start(bf16[8,2,2,5,128,128]{5,4,3,2,1,0:T(8,128)(2,1)} %shard_map.53), calls=%async_computation.1 | async-start | bytes 10485760 | tf_op jit(solution)/shard_map/all_to_all | solution.py:283
  69.8 57.8 %copy-start.1 = (bf16[5,256,128]{2,1,0:T(8,128)(2,1)S(1)}, bf16[5,256,128]{2,1,0:T(8,128)(2,1)}, u32[]{:S(2)}) copy-start(bf16[5,256,128]{2,1,0:T(8,128)(2,1)} %get-tuple-element.75.refs_3_.refs_8_) | copy-start | bytes 983044
  69.8 19.8 %collective-permute-start.3 = (bf16[5,256,128]{2,1,0:T(8,128)(2,1)}, bf16[5,256,128]{2,1,0:T(8,128)(2,1)S(1)}, u32[]{:S(2)}, u32[]{:S(2)}) collective-permute-start(bf16[5,256,128]{2,1,0:T(8,128)(2,1)} %get-tuple-element.71), channel_id=1, source_target_pairs={{0,3},{1,2},{2,1},{3,0},{4,7},{5,6},{6,5},{7,4},{8,11},{9,10},{10,... | collective-permute-start | bytes 983048 | tf_op jit(solution)/shard_map/ppermute | solution.py:256
  71.4 25.2 %collective-permute-start.4 = (bf16[5,256,128]{2,1,0:T(8,128)(2,1)S(1)}, bf16[5,256,128]{2,1,0:T(8,128)(2,1)S(1)}, u32[]{:S(2)}, u32[]{:S(2)}) collective-permute-start(bf16[5,256,128]{2,1,0:T(8,128)(2,1)S(1)} %copy-done.20), channel_id=1, source_target_pairs={{0,2},{1,3},{2,0},{3,1},{4,6},{5,7},{6,4},{7,5},{8,10},{9,11},{10,... | collective-permute-start | bytes 983048 | tf_op jit(solution)/shard_map/ppermute | solution.py:256
  71.4 25.4 %collective-permute-start.5 = (bf16[5,256,128]{2,1,0:T(8,128)(2,1)S(1)}, bf16[5,256,128]{2,1,0:T(8,128)(2,1)S(1)}, u32[]{:S(2)}, u32[]{:S(2)}) collective-permute-start(bf16[5,256,128]{2,1,0:T(8,128)(2,1)S(1)} %copy-done.19), channel_id=1, source_target_pairs={{0,1},{1,0},{2,3},{3,2},{4,5},{5,4},{6,7},{7,6},{8,9},{9,8},{10,11... | collective-permute-start | bytes 983048 | tf_op jit(solution)/shard_map/ppermute | solution.py:256
  73.3 25.8 %collective-permute-start.6 = (bf16[5,256,128]{2,1,0:T(8,128)(2,1)}, bf16[5,256,128]{2,1,0:T(8,128)(2,1)S(1)}, u32[]{:S(2)}, u32[]{:S(2)}) collective-permute-start(bf16[5,256,128]{2,1,0:T(8,128)(2,1)} %get-tuple-element.76), channel_id=1, source_target_pairs={{0,1},{1,0},{2,3},{3,2},{4,5},{5,4},{6,7},{7,6},{8,9},{9,8},{10,11... | collective-permute-start | bytes 983048 | tf_op jit(solution)/shard_map/ppermute | solution.py:256
  73.5 46.5 %collective-permute-start.7 = (bf16[5,256,128]{2,1,0:T(8,128)(2,1)}, bf16[5,256,128]{2,1,0:T(8,128)(2,1)S(1)}, u32[]{:S(2)}, u32[]{:S(2)}) collective-permute-start(bf16[5,256,128]{2,1,0:T(8,128)(2,1)} %get-tuple-element.77), channel_id=1, source_target_pairs={{0,2},{1,3},{2,0},{3,1},{4,6},{5,7},{6,4},{7,5},{8,10},{9,11},{10,... | collective-permute-start | bytes 983048 | tf_op jit(solution)/shard_map/ppermute | solution.py:256
  89.6 38.0 %collective-permute-start.8 = (bf16[5,256,128]{2,1,0:T(8,128)(2,1)}, bf16[5,256,128]{2,1,0:T(8,128)(2,1)S(1)}, u32[]{:S(2)}, u32[]{:S(2)}) collective-permute-start(bf16[5,256,128]{2,1,0:T(8,128)(2,1)} %get-tuple-element.78), channel_id=1, source_target_pairs={{0,3},{1,2},{2,1},{3,0},{4,7},{5,6},{6,5},{7,4},{8,11},{9,10},{10,... | collective-permute-start | bytes 983048 | tf_op jit(solution)/shard_map/ppermute | solution.py:256
  96.6 33.8 %collective-permute-start.9 = (bf16[2,256,128]{2,1,0:T(8,128)(2,1)S(1)}, bf16[2,256,128]{2,1,0:T(8,128)(2,1)S(1)}, u32[]{:S(2)}, u32[]{:S(2)}) collective-permute-start(bf16[2,256,128]{2,1,0:T(8,128)(2,1)S(1)} %copy-done.21), channel_id=1, source_target_pairs={{0,3},{1,2},{2,1},{3,0},{4,7},{5,6},{6,5},{7,4},{8,11},{9,10},{10,... | collective-permute-start | bytes 393224 | tf_op jit(solution)/shard_map/ppermute | solution.py:256
  99.1 30.7 %copy-start.7 = (bf16[5,256,128]{2,1,0:T(8,128)(2,1)}, bf16[5,256,128]{2,1,0:T(8,128)(2,1)S(1)}, u32[]{:S(2)}) copy-start(bf16[5,256,128]{2,1,0:T(8,128)(2,1)S(1)} %collective-permute-done.6.refs_2_.refs_9_) | copy-start | bytes 983044
  120.0 9.9 %copy-start.8 = (bf16[5,256,128]{2,1,0:T(8,128)(2,1)}, bf16[5,256,128]{2,1,0:T(8,128)(2,1)S(1)}, u32[]{:S(2)}) copy-start(bf16[5,256,128]{2,1,0:T(8,128)(2,1)S(1)} %collective-permute-done.7.refs_1_.refs_10_) | copy-start | bytes 983044
  127.6 2.2 copy-start.9
  130.3 0.7 copy-start.16
  131.0 63.9 %all-to-all-start = ((bf16[8,2,2,5,128,128]{5,4,3,2,1,0:T(8,128)(2,1)}), bf16[8,2,2,5,128,128]{5,4,3,2,1,0:T(8,128)(2,1)}, u32[]{:S(2)}, u32[]{:S(2)}) async-start(bf16[8,2,2,5,128,128]{5,4,3,2,1,0:T(8,128)(2,1)} %shard_map.50), calls=%async_computation | async-start | bytes 10485760 | tf_op jit(solution)/shard_map/all_to_all | solution.py:283
  135.9 15.0 %collective-permute-start.10 = (bf16[3,256,128]{2,1,0:T(8,128)(2,1)}, bf16[3,256,128]{2,1,0:T(8,128)(2,1)S(1)}, u32[]{:S(2)}, u32[]{:S(2)}) collective-permute-start(bf16[3,256,128]{2,1,0:T(8,128)(2,1)} %get-tuple-element.87), channel_id=1, source_target_pairs={{0,3},{1,2},{2,1},{3,0},{4,7},{5,6},{6,5},{7,4},{8,11},{9,10},{10,... | collective-permute-start | bytes 589832 | tf_op jit(solution)/shard_map/ppermute | solution.py:256
  137.7 19.7 %collective-permute-start.11 = (bf16[5,256,128]{2,1,0:T(8,128)(2,1)}, bf16[5,256,128]{2,1,0:T(8,128)(2,1)S(1)}, u32[]{:S(2)}, u32[]{:S(2)}) collective-permute-start(bf16[5,256,128]{2,1,0:T(8,128)(2,1)} %get-tuple-element.89), channel_id=1, source_target_pairs={{0,2},{1,3},{2,0},{3,1},{4,6},{5,7},{6,4},{7,5},{8,10},{9,11},{10,... | collective-permute-start | bytes 983048 | tf_op jit(solution)/shard_map/ppermute | solution.py:256
  137.7 20.4 %collective-permute-start.12 = (bf16[5,256,128]{2,1,0:T(8,128)(2,1)}, bf16[5,256,128]{2,1,0:T(8,128)(2,1)}, u32[]{:S(2)}, u32[]{:S(2)}) collective-permute-start(bf16[5,256,128]{2,1,0:T(8,128)(2,1)} %get-tuple-element.90), channel_id=1, source_target_pairs={{0,1},{1,0},{2,3},{3,2},{4,5},{5,4},{6,7},{7,6},{8,9},{9,8},{10,11... | collective-permute-start | bytes 983048 | tf_op jit(solution)/shard_map/ppermute | solution.py:256
  139.4 35.2 %collective-permute-start = (bf16[5,256,128]{2,1,0:T(8,128)(2,1)}, bf16[5,256,128]{2,1,0:T(8,128)(2,1)}, u32[]{:S(2)}, u32[]{:S(2)}) collective-permute-start(bf16[5,256,128]{2,1,0:T(8,128)(2,1)} %get-tuple-element.68), channel_id=1, source_target_pairs={{0,1},{1,0},{2,3},{3,2},{4,5},{5,4},{6,7},{7,6},{8,9},{9,8},{10,11... | collective-permute-start | bytes 983048 | tf_op jit(solution)/shard_map/ppermute | solution.py:256
  139.7 39.4 %collective-permute-start.2 = (bf16[5,256,128]{2,1,0:T(8,128)(2,1)}, bf16[5,256,128]{2,1,0:T(8,128)(2,1)}, u32[]{:S(2)}, u32[]{:S(2)}) collective-permute-start(bf16[5,256,128]{2,1,0:T(8,128)(2,1)} %get-tuple-element.70), channel_id=1, source_target_pairs={{0,3},{1,2},{2,1},{3,0},{4,7},{5,6},{6,5},{7,4},{8,11},{9,10},{10,... | collective-permute-start | bytes 983048 | tf_op jit(solution)/shard_map/ppermute | solution.py:256
  143.0 51.8 %copy-start.10 = (bf16[5,256,128]{2,1,0:T(8,128)(2,1)S(1)}, bf16[5,256,128]{2,1,0:T(8,128)(2,1)}, u32[]{:S(2)}) copy-start(bf16[5,256,128]{2,1,0:T(8,128)(2,1)} %get-tuple-element.67.refs_0_) | copy-start | bytes 983044
  150.9 35.4 %collective-permute-start.1 = (bf16[5,256,128]{2,1,0:T(8,128)(2,1)}, bf16[5,256,128]{2,1,0:T(8,128)(2,1)S(1)}, u32[]{:S(2)}, u32[]{:S(2)}) collective-permute-start(bf16[5,256,128]{2,1,0:T(8,128)(2,1)} %get-tuple-element.69), channel_id=1, source_target_pairs={{0,2},{1,3},{2,0},{3,1},{4,6},{5,7},{6,4},{7,5},{8,10},{9,11},{10,... | collective-permute-start | bytes 983048 | tf_op jit(solution)/shard_map/ppermute | solution.py:256
  157.3 0.7 copy-start.12
  158.1 1.0 copy-start.11
  159.0 1.0 copy-start.13
  160.0 0.9 copy-start.17
  179.1 33.2 %collective-permute-start.20 = (bf16[5,256,128]{2,1,0:T(8,128)(2,1)}, bf16[5,256,128]{2,1,0:T(8,128)(2,1)S(1)}, u32[]{:S(2)}, u32[]{:S(2)}) collective-permute-start(bf16[5,256,128]{2,1,0:T(8,128)(2,1)} %get-tuple-element.106), channel_id=1, source_target_pairs={{0,1},{1,0},{2,3},{3,2},{4,5},{5,4},{6,7},{7,6},{8,9},{9,8},{10,11... | collective-permute-start | bytes 983048 | tf_op jit(solution)/shard_map/ppermute | solution.py:256
  179.1 33.4 %collective-permute-start.22 = (bf16[5,256,128]{2,1,0:T(8,128)(2,1)}, bf16[5,256,128]{2,1,0:T(8,128)(2,1)S(1)}, u32[]{:S(2)}, u32[]{:S(2)}) collective-permute-start(bf16[5,256,128]{2,1,0:T(8,128)(2,1)} %get-tuple-element.108), channel_id=1, source_target_pairs={{0,2},{1,3},{2,0},{3,1},{4,6},{5,7},{6,4},{7,5},{8,10},{9,11},{10,... | collective-permute-start | bytes 983048 | tf_op jit(solution)/shard_map/ppermute | solution.py:256
  182.3 31.5 %collective-permute-start.24 = (bf16[5,256,128]{2,1,0:T(8,128)(2,1)}, bf16[5,256,128]{2,1,0:T(8,128)(2,1)S(1)}, u32[]{:S(2)}, u32[]{:S(2)}) collective-permute-start(bf16[5,256,128]{2,1,0:T(8,128)(2,1)} %get-tuple-element.110), channel_id=1, source_target_pairs={{0,3},{1,2},{2,1},{3,0},{4,7},{5,6},{6,5},{7,4},{8,11},{9,10},{10,... | collective-permute-start | bytes 983048 | tf_op jit(solution)/shard_map/ppermute | solution.py:256
  186.3 0.7 copy-start.14
  194.9 1.0 copy-start.15
  209.0 14.0 %collective-permute-start.19 = (bf16[5,256,128]{2,1,0:T(8,128)(2,1)S(1)}, bf16[5,256,128]{2,1,0:T(8,128)(2,1)S(1)}, u32[]{:S(2)}, u32[]{:S(2)}) collective-permute-start(bf16[5,256,128]{2,1,0:T(8,128)(2,1)S(1)} %get-tuple-element.105), channel_id=1, source_target_pairs={{0,1},{1,0},{2,3},{3,2},{4,5},{5,4},{6,7},{7,6},{8,9},{9,8},{10,11... | collective-permute-start | bytes 983048 | tf_op jit(solution)/shard_map/ppermute | solution.py:256
  209.1 25.4 %collective-permute-start.21 = (bf16[5,256,128]{2,1,0:T(8,128)(2,1)S(1)}, bf16[5,256,128]{2,1,0:T(8,128)(2,1)S(1)}, u32[]{:S(2)}, u32[]{:S(2)}) collective-permute-start(bf16[5,256,128]{2,1,0:T(8,128)(2,1)S(1)} %get-tuple-element.107), channel_id=1, source_target_pairs={{0,2},{1,3},{2,0},{3,1},{4,6},{5,7},{6,4},{7,5},{8,10},{9,11},{10,... | collective-permute-start | bytes 983048 | tf_op jit(solution)/shard_map/ppermute | solution.py:256
  212.3 29.2 %collective-permute-start.23 = (bf16[5,256,128]{2,1,0:T(8,128)(2,1)S(1)}, bf16[5,256,128]{2,1,0:T(8,128)(2,1)S(1)}, u32[]{:S(2)}, u32[]{:S(2)}) collective-permute-start(bf16[5,256,128]{2,1,0:T(8,128)(2,1)S(1)} %get-tuple-element.109), channel_id=1, source_target_pairs={{0,3},{1,2},{2,1},{3,0},{4,7},{5,6},{6,5},{7,4},{8,11},{9,10},{10,... | collective-permute-start | bytes 983048 | tf_op jit(solution)/shard_map/ppermute | solution.py:256
